TPU v7x, 32 devices: a whole 2x2x4 slice. The times are simulated.
32 devices in a mesh: parts: 2 (over x), sub: 16 (over z, y, core).
Axes of the slice: x: 2, y: 2, z: 4, core: 2. Of those that a mesh axis runs over, the one named last changes fastest.
Arguments:
- right_side: float32 [32768, 256], P(('parts', 'sub')), parts along dimension 0, may hold values from -6 to 6
- face_weight: float32 [64, 512], P(('parts', 'sub')), parts along dimension 0, may hold values from 0.2 to 0.8
- schur: bfloat16 [65536, 1024], P(('parts', 'sub')), parts along dimension 0, as said below
- neumann: bfloat16 [65536, 1024], P(('parts', 'sub')), parts along dimension 0
- constraint: bfloat16 [2048, 512], P(('parts', 'sub')), parts along dimension 0, may hold values from -0.25 to 0.25
- coarse_inverse: bfloat16 [2048, 1024], P(('parts', 'sub')), parts along dimension 0
Outputs:
- solution: float32 [32768, 256], P(('parts', 'sub')), parts along dimension 0
- residual: float32 [32768, 256], P(('parts', 'sub')), parts along dimension 0
There are 2 independent parts, one for each index of `parts`. A program takes and returns all parts, laid end to end along the dimension named above; each array names one. Nothing has to cross between parts.
Inputs may be any that keep to these rules, and one draw needn't show every extreme that they name: schur, neumann and coarse_inverse are symmetric, and each block schur_j, neumann_j and the whole coarse_inverse is positive definite.
All inputs are finite; a program needn't handle non-finite values.
Results may differ from a plain program's by a relative error of at most 0.0091.
Values may be sent and summed in bfloat16 or wider, within the bound.
No kernel may reach another device: no remote copies, remote signals or barrier semaphores. Data moves between devices by JAX's collectives and lax.ppermute only.
A program may use at most 64 MiB of HBM per device.

v0:
```python
import jax
import jax.numpy as jnp
from jax import lax
from jax.sharding import PartitionSpec as P

NF = 512
NCF = 32
R = 256
ITERS = 2
NI = 1024


def from_behind(block, axis, distance):
    devices = range(lax.axis_size(axis))
    route = [((i - distance) % len(devices), i) for i in devices]
    return lax.ppermute(block, axis, route)


def couple(matrices, left_part, right_part):
    stacked = jnp.concatenate([left_part, right_part], axis=1)
    return jnp.einsum("sij,sjr->sir", matrices, stacked, preferred_element_type=jnp.float32)


def previous_faces(face_rows):
    last_face = from_behind(face_rows[-1:], "sub", 1)
    return jnp.concatenate([last_face, face_rows[:-1]], axis=0)


def following_halves(halves):
    first_half = from_behind(halves[:1], "sub", -1)
    return jnp.concatenate([halves[1:], first_half], axis=0)


def column_sum(first_vector, second_vector):
    return lax.psum(jnp.sum(first_vector * second_vector, axis=(0, 1)), "sub")


def schur_apply(blocks, vector):
    rounded = vector.astype(jnp.bfloat16)
    output = couple(blocks, previous_faces(rounded), rounded)
    return output[:, NF:] + following_halves(output[:, :NF])


def coarse_apply(coarse_inverse, coarse_input):
    return jnp.dot(
        coarse_inverse,
        lax.all_gather(coarse_input, "sub", axis=0, tiled=True),
        preferred_element_type=jnp.float32,
    )


def precondition(neumann_blocks, weights, rows_constraint, coarse_inverse, vector):
    coarse_input = jnp.einsum(
        "sqf,sfr->sqr",
        rows_constraint,
        vector.astype(jnp.bfloat16),
        preferred_element_type=jnp.float32,
    ).astype(jnp.bfloat16)
    coarse_input = coarse_input.reshape(-1, vector.shape[2])
    coarse_solution = coarse_apply(coarse_inverse, coarse_input).astype(jnp.bfloat16)
    right_part = (weights * vector).astype(jnp.bfloat16)
    left_source = ((1.0 - weights) * vector).astype(jnp.bfloat16)
    output = couple(neumann_blocks, previous_faces(left_source), right_part)
    local_part = weights * output[:, NF:] + (1.0 - weights) * following_halves(output[:, :NF])
    coarse_solution = coarse_solution.reshape(
        rows_constraint.shape[0], rows_constraint.shape[1], -1
    )
    correction = jnp.einsum(
        "sqf,sqr->sfr", rows_constraint, coarse_solution, preferred_element_type=jnp.float32
    )
    return local_part + correction


def shards(right_side, face_weight, schur, neumann, constraint, coarse_inverse):
    local_subs = face_weight.shape[0]
    schur_blocks = schur.reshape(local_subs, NI, NI)
    neumann_blocks = neumann.reshape(local_subs, NI, NI)
    rows_constraint = constraint.reshape(local_subs, NCF, NF)
    weights = face_weight.reshape(local_subs, NF, 1)
    residual = right_side.reshape(local_subs, NF, R)
    solution = jnp.zeros_like(residual)
    precond = precondition(neumann_blocks, weights, rows_constraint, coarse_inverse, residual)
    direction = precond
    norm_now = column_sum(residual, precond)
    for iteration in range(ITERS):
        product_image = schur_apply(schur_blocks, direction)
        step_size = norm_now / column_sum(direction, product_image)
        solution = solution + step_size * direction
        residual = residual - step_size * product_image
        if iteration + 1 < ITERS:
            precond = precondition(
                neumann_blocks, weights, rows_constraint, coarse_inverse, residual
            )
            norm_next = column_sum(residual, precond)
            direction = precond + norm_next / norm_now * direction
            norm_now = norm_next
    return (solution.reshape(local_subs * NF, R), residual.reshape(local_subs * NF, R))


def solution(mesh):
    in_specs = (
        P(("parts", "sub"), None),
        P(("parts", "sub"), None),
        P(("parts", "sub"), None),
        P(("parts", "sub"), None),
        P(("parts", "sub"), None),
        P(("parts", "sub"), None),
    )
    out_specs = (P(("parts", "sub"), None), P(("parts", "sub"), None))
    return jax.shard_map(shards, mesh=mesh, in_specs=in_specs, out_specs=out_specs, check_vma=False)
```

profile of v0, /device:TPU:0, one launch (start us, length us, event | category | flops | bytes accessed | tf_op | source)
XLA Modules:
  0.0 221.8 jit_solution(4742571203874210738)
XLA Ops:
  0.6 0.0 copy-start
  0.7 0.8 broadcast_subtract_fusion
  1.4 1.6 copy.12
  3.0 0.2 multiply_convert_fusion.3
  3.2 0.5 collective-permute-start
  3.7 9.0 %collective-permute-done = bf16[1,512,256]{1,2,0:T(8,128)(2,1)S(1)} collective-permute-done((bf16[1,512,256]{1,2,0:T(8,128)(2,1)S(1)}, bf16[1,512,256]{1,2,0:T(8,128)(2,1)S(1)}, u32[]{:S(2)}, u32[]{:S(2)}) %collective-permute-start) | collective-permute-done | bytes 262176 | tf_op jit(solution)/shard_map/ppermute | solution.py:16
  12.8 3.5 %convolution_bitcast_fusion.3 = f32[2,1024,256]{1,2,0:T(8,128)S(1)} fusion(bf16[2,1024,1024]{2,1,0:T(8,128)(2,1)} %bitcast.54, bf16[2,512,256]{1,2,0:T(8,128)(2,1)S(1)} %get-tuple-element.21, bf16[1,512,256]{1,2,0:T(8,128)(2,1)S(1)} %get-tuple-element.29, bf16[1,512,256]{1,2,0:T(8,128)(2,1)S(1)} %collective-permute-done), kind=kOutput, calls=%fused_computation.3 | convolution fusion | flops 1076887552 | bytes 7340032 | tf_op jit(solution)/shard_map/sij,sjr->sir/dot_general | solution.py:21
  16.3 0.1 fusion.37
  16.4 0.1 collective-permute-start.1
  16.4 1.0 copy-done.5
  17.5 0.2 convolution_convert_fusion.3
  17.7 23.7 %all_gather.6 = bf16[1024,256]{1,0:T(8,128)(2,1)S(1)} all-gather(bf16[64,256]{1,0:T(8,128)(2,1)S(1)} %bitcast.52), channel_id=1, replica_groups=mesh['parts'=2,'sub'=16] {'sub'}, dimensions={0}, use_global_device_ids=true | all-gather | bytes 557056 | tf_op jit(solution)/shard_map/all_gather | solution.py:47
  41.4 0.2 convolution_convert_fusion.1
  41.6 0.4 fusion.32
  42.0 0.4 collective-permute-start.2
  42.4 8.2 %collective-permute-done.2 = bf16[1,512,256]{1,2,0:T(8,128)(2,1)S(1)} collective-permute-done((bf16[1,512,256]{1,2,0:T(8,128)(2,1)S(1)}, bf16[1,512,256]{1,2,0:T(8,128)(2,1)S(1)}, u32[]{:S(2)}, u32[]{:S(2)}) %collective-permute-start.2) | collective-permute-done | bytes 262176 | tf_op jit(solution)/shard_map/ppermute | solution.py:16
  50.6 1.3 convolution_bitcast_fusion.2
  51.9 0.1 fusion.36
  52.0 0.1 collective-permute-start.3
  52.1 6.7 %collective-permute-done.3 = f32[1,512,256]{1,2,0:T(8,128)S(1)} collective-permute-done((f32[1,512,256]{1,2,0:T(8,128)S(1)}, f32[1,512,256]{1,2,0:T(8,128)S(1)}, u32[]{:S(2)}, u32[]{:S(2)}) %collective-permute-start.3) | collective-permute-done | bytes 524320 | tf_op jit(solution)/shard_map/ppermute | solution.py:16
  58.8 0.5 multiply_reduce_fusion.2
  59.2 0.3 copy-done.7
  59.5 34.1 %all-reduce = (f32[256]{0:T(256)S(1)}, f32[256]{0:T(256)S(1)}) all-reduce(f32[256]{0:T(256)S(1)} %get-tuple-element.3, f32[256]{0:T(256)S(1)} %get-tuple-element.2), channel_id=1, replica_groups=mesh['parts'=2,'sub'=16] {'sub'}, use_global_device_ids=true, to_apply=%region_1.0 | all-reduce | flops 512 | bytes 4096 | tf_op jit(solution)/shard_map/psum | solution.py:35
  93.7 1.9 multiply_convert_fusion.1
  95.6 0.1 collective-permute-start.4
  95.7 0.1 multiply_convert_fusion
  95.8 8.5 %collective-permute-done.4 = bf16[1,512,256]{1,2,0:T(8,128)(2,1)S(1)} collective-permute-done((bf16[1,512,256]{1,2,0:T(8,128)(2,1)S(1)}, bf16[1,512,256]{1,2,0:T(8,128)(2,1)S(1)}, u32[]{:S(2)}, u32[]{:S(2)}) %collective-permute-start.4) | collective-permute-done | bytes 262176 | tf_op jit(solution)/shard_map/ppermute | solution.py:16
  104.3 1.3 convolution_bitcast_fusion.1
  105.6 0.1 fusion.35
  105.7 0.1 collective-permute-start.5
  105.7 0.3 convolution_convert_fusion.2
  106.0 23.7 %all_gather.7 = bf16[1024,256]{1,0:T(8,128)(2,1)S(1)} all-gather(bf16[64,256]{1,0:T(8,128)(2,1)S(1)} %bitcast.53), channel_id=1, replica_groups=mesh['parts'=2,'sub'=16] {'sub'}, dimensions={0}, use_global_device_ids=true | all-gather | bytes 557056 | tf_op jit(solution)/shard_map/all_gather | solution.py:47
  129.7 0.2 convolution_convert_fusion
  129.9 0.5 multiply_reduce_fusion.1
  130.4 29.8 %psum.30 = f32[256]{0:T(256)S(1)} all-reduce(f32[256]{0:T(256)S(1)} %get-tuple-element.6), channel_id=1, replica_groups=mesh['parts'=2,'sub'=16] {'sub'}, use_global_device_ids=true, to_apply=%region_5.0 | all-reduce | flops 256 | bytes 2048 | tf_op jit(solution)/shard_map/psum | solution.py:35
  160.2 0.2 fusion.30
  160.5 0.1 collective-permute-start.6
  160.5 8.5 %collective-permute-done.6 = bf16[1,512,256]{1,2,0:T(8,128)(2,1)S(1)} collective-permute-done((bf16[1,512,256]{1,2,0:T(8,128)(2,1)S(1)}, bf16[1,512,256]{1,2,0:T(8,128)(2,1)S(1)}, u32[]{:S(2)}, u32[]{:S(2)}) %collective-permute-start.6) | collective-permute-done | bytes 262176 | tf_op jit(solution)/shard_map/ppermute | solution.py:16
  169.0 3.5 %convolution_bitcast_fusion = f32[2,1024,256]{1,2,0:T(8,128)S(1)} fusion(bf16[2,1024,1024]{2,1,0:T(8,128)(2,1)} %bitcast.56, bf16[2,512,256]{1,2,0:T(8,128)(2,1)S(1)} %fusion.30, bf16[1,512,256]{1,2,0:T(8,128)(2,1)S(1)} %get-tuple-element.23, bf16[1,512,256]{1,2,0:T(8,128)(2,1)S(1)} %collective-permute-done.6), kind=kOutput, calls=%fused_computation | convolution fusion | flops 1076887552 | bytes 7340032 | tf_op jit(solution)/shard_map/sij,sjr->sir/dot_general | solution.py:21
  172.5 0.1 fusion.34
  172.6 0.1 collective-permute-start.7
  172.7 6.7 %collective-permute-done.7 = f32[1,512,256]{1,2,0:T(8,128)S(1)} collective-permute-done((f32[1,512,256]{1,2,0:T(8,128)S(1)}, f32[1,512,256]{1,2,0:T(8,128)S(1)}, u32[]{:S(2)}, u32[]{:S(2)}) %collective-permute-start.7) | collective-permute-done | bytes 524320 | tf_op jit(solution)/shard_map/ppermute | solution.py:16
  179.4 0.8 copy-done.8
  180.2 0.4 multiply_reduce_fusion
  180.5 34.1 %psum.31 = f32[256]{0:T(256)S(1)} all-reduce(f32[256]{0:T(256)S(1)} %multiply_reduce_fusion), channel_id=1, replica_groups=mesh['parts'=2,'sub'=16] {'sub'}, use_global_device_ids=true, to_apply=%region_7.0 | all-reduce | flops 256 | bytes 2048 | tf_op jit(solution)/shard_map/psum | solution.py:35
  214.7 3.2 %multiply_subtract_fusion = (f32[2,512,256]{1,2,0:T(8,128)}, f32[2,512,256]{1,2,0:T(8,128)}) fusion(f32[2,512,256]{1,2,0:T(8,128)S(1)} %get-tuple-element.9, f32[256]{0:T(256)S(1)} %div.11, f32[1,512,256]{1,2,0:T(8,128)} %copy-done.8, f32[1,512,256]{1,2,0:T(8,128)} %copy-done.4, f32[2,1024,256]{1,2,0:T(8,128)} %copy-done.2, ...), kind=kLoop, calls=%fused_computation.40 | loop fusion | flops 2359296 | bytes 7343104 | tf_op jit(solution)/shard_map/sub | solution.py:89
  217.9 2.6 %copy.16 = f32[2,512,256]{2,1,0:T(8,128)} copy(f32[2,512,256]{1,2,0:T(8,128)} %get-tuple-element.30) | data formatting | bytes 2097152 | tf_op jit(solution)/shard_map/sub | solution.py:89
  220.5 1.3 copy.15
  (31 shorter events, 0.2 us)
Async XLA Ops:
  0.6 40.8 %copy-start = (bf16[64,1024]{1,0:T(8,128)(2,1)S(1)}, bf16[64,1024]{1,0:T(8,128)(2,1)}, u32[]{:S(2)}) copy-start(bf16[64,1024]{1,0:T(8,128)(2,1)} %param.11) | copy-start | bytes 393220
  0.6 2.3 %copy-start.10 = (f32[2,512]{1,0:T(2,128)S(1)}, f32[2,512]{1,0:T(2,128)}, u32[]{:S(2)}) copy-start(f32[2,512]{1,0:T(2,128)} %param.7) | copy-start | bytes 12292
  3.2 9.6 %collective-permute-start = (bf16[1,512,256]{1,2,0:T(8,128)(2,1)S(1)}, bf16[1,512,256]{1,2,0:T(8,128)(2,1)S(1)}, u32[]{:S(2)}, u32[]{:S(2)}) collective-permute-start(bf16[1,512,256]{1,2,0:T(8,128)(2,1)S(1)} %get-tuple-element.28), channel_id=1, source_target_pairs={{15,0},{0,1},{1,2},{2,3},{3,4},{4,5},{5,6},{6,7},{7,8},{8,9},{9,10... | collective-permute-start | bytes 786440 | tf_op jit(solution)/shard_map/ppermute | solution.py:16
  16.2 1.2 copy-start.5
  16.3 1.2 copy-start.9
  16.4 25.2 %collective-permute-start.1 = (f32[1,512,256]{1,2,0:T(8,128)S(1)}, f32[1,512,256]{1,2,0:T(8,128)S(1)}, u32[]{:S(2)}, u32[]{:S(2)}) collective-permute-start(f32[1,512,256]{1,2,0:T(8,128)S(1)} %get-tuple-element.19), channel_id=1, source_target_pairs={{1,0},{2,1},{3,2},{4,3},{5,4},{6,5},{7,6},{8,7},{9,8},{10,9},{11,1... | collective-permute-start | bytes 1572872 | tf_op jit(solution)/shard_map/ppermute | solution.py:16
  41.6 9.0 %copy-start.12 = (bf16[2048,1024]{1,0:T(8,128)(2,1)S(1)}, bf16[2048,1024]{1,0:T(8,128)(2,1)}, u32[]{:S(2)}) copy-start(bf16[2048,1024]{1,0:T(8,128)(2,1)} %param.8) | copy-start | bytes 12582916
  42.0 8.5 %collective-permute-start.2 = (bf16[1,512,256]{1,2,0:T(8,128)(2,1)S(1)}, bf16[1,512,256]{1,2,0:T(8,128)(2,1)S(1)}, u32[]{:S(2)}, u32[]{:S(2)}) collective-permute-start(bf16[1,512,256]{1,2,0:T(8,128)(2,1)S(1)} %get-tuple-element.26), channel_id=1, source_target_pairs={{15,0},{0,1},{1,2},{2,3},{3,4},{4,5},{5,6},{6,7},{7,8},{8,9},{9,10... | collective-permute-start | bytes 786440 | tf_op jit(solution)/shard_map/ppermute | solution.py:16
  51.9 7.3 %copy-start.1 = (f32[2,1024,256]{1,2,0:T(8,128)}, f32[2,1024,256]{1,2,0:T(8,128)S(1)}, u32[]{:S(2)}) copy-start(f32[2,1024,256]{1,2,0:T(8,128)S(1)} %convolution_bitcast_fusion.2) | copy-start | bytes 6291460
  52.0 7.2 %copy-start.3 = (f32[1,512,256]{1,2,0:T(8,128)}, f32[1,512,256]{1,2,0:T(8,128)S(1)}, u32[]{:S(2)}) copy-start(f32[1,512,256]{1,2,0:T(8,128)S(1)} %get-tuple-element.16) | copy-start | bytes 1572868
  52.0 6.8 %collective-permute-start.3 = (f32[1,512,256]{1,2,0:T(8,128)S(1)}, f32[1,512,256]{1,2,0:T(8,128)S(1)}, u32[]{:S(2)}, u32[]{:S(2)}) collective-permute-start(f32[1,512,256]{1,2,0:T(8,128)S(1)} %get-tuple-element.17), channel_id=1, source_target_pairs={{1,0},{2,1},{3,2},{4,3},{5,4},{6,5},{7,6},{8,7},{9,8},{10,9},{11,1... | collective-permute-start | bytes 1572872 | tf_op jit(solution)/shard_map/ppermute | solution.py:16
  58.8 0.8 copy-start.7
  93.7 10.6 %copy-start.11 = (bf16[2048,1024]{1,0:T(8,128)(2,1)S(1)}, bf16[2048,1024]{1,0:T(8,128)(2,1)}, u32[]{:S(2)}) copy-start(bf16[2048,1024]{1,0:T(8,128)(2,1)} %param.9) | copy-start | bytes 12582916
  95.6 8.7 %collective-permute-start.4 = (bf16[1,512,256]{1,2,0:T(8,128)(2,1)S(1)}, bf16[1,512,256]{1,2,0:T(8,128)(2,1)S(1)}, u32[]{:S(2)}, u32[]{:S(2)}) collective-permute-start(bf16[1,512,256]{1,2,0:T(8,128)(2,1)S(1)} %get-tuple-element.24), channel_id=1, source_target_pairs={{15,0},{0,1},{1,2},{2,3},{3,4},{4,5},{5,6},{6,7},{7,8},{8,9},{9,10... | collective-permute-start | bytes 786440 | tf_op jit(solution)/shard_map/ppermute | solution.py:16
  105.7 24.3 %collective-permute-start.5 = (f32[1,512,256]{1,2,0:T(8,128)S(1)}, f32[1,512,256]{1,2,0:T(8,128)S(1)}, u32[]{:S(2)}, u32[]{:S(2)}) collective-permute-start(f32[1,512,256]{1,2,0:T(8,128)S(1)} %get-tuple-element.15), channel_id=1, source_target_pairs={{1,0},{2,1},{3,2},{4,3},{5,4},{6,5},{7,6},{8,7},{9,8},{10,9},{11,1... | collective-permute-start | bytes 1572872 | tf_op jit(solution)/shard_map/ppermute | solution.py:16
  160.5 8.5 %collective-permute-start.6 = (bf16[1,512,256]{1,2,0:T(8,128)(2,1)S(1)}, bf16[1,512,256]{1,2,0:T(8,128)(2,1)S(1)}, u32[]{:S(2)}, u32[]{:S(2)}) collective-permute-start(bf16[1,512,256]{1,2,0:T(8,128)(2,1)S(1)} %get-tuple-element.22), channel_id=1, source_target_pairs={{15,0},{0,1},{1,2},{2,3},{3,4},{4,5},{5,6},{6,7},{7,8},{8,9},{9,10... | collective-permute-start | bytes 786440 | tf_op jit(solution)/shard_map/ppermute | solution.py:16
  172.5 6.9 %copy-start.2 = (f32[2,1024,256]{1,2,0:T(8,128)}, f32[2,1024,256]{1,2,0:T(8,128)S(1)}, u32[]{:S(2)}) copy-start(f32[2,1024,256]{1,2,0:T(8,128)S(1)} %convolution_bitcast_fusion) | copy-start | bytes 6291460
  172.6 6.8 %copy-start.4 = (f32[1,512,256]{1,2,0:T(8,128)}, f32[1,512,256]{1,2,0:T(8,128)S(1)}, u32[]{:S(2)}) copy-start(f32[1,512,256]{1,2,0:T(8,128)S(1)} %get-tuple-element.12) | copy-start | bytes 1572868
  172.6 6.8 %collective-permute-start.7 = (f32[1,512,256]{1,2,0:T(8,128)S(1)}, f32[1,512,256]{1,2,0:T(8,128)S(1)}, u32[]{:S(2)}, u32[]{:S(2)}) collective-permute-start(f32[1,512,256]{1,2,0:T(8,128)S(1)} %get-tuple-element.13), channel_id=1, source_target_pairs={{1,0},{2,1},{3,2},{4,3},{5,4},{6,5},{7,6},{8,7},{9,8},{10,9},{11,1... | collective-permute-start | bytes 1572872 | tf_op jit(solution)/shard_map/ppermute | solution.py:16
  179.4 0.8 copy-start.8
  217.9 2.6 %copy-start.6 = (f32[2,512,256]{1,2,0:T(8,128)S(1)}, f32[2,512,256]{1,2,0:T(8,128)}, u32[]{:S(2)}) copy-start(f32[2,512,256]{1,2,0:T(8,128)} %get-tuple-element.31) | copy-start | bytes 3145732
where the time goes:
time: 222 us
  blocking collectives  146 us (66%)
  waiting for transfers between devices  47.5 us (21%)
  matrix products  11.2 us (5%)
  local copies, waits for them, and re-layouts  8.15 us (4%)
  other arithmetic  7.23 us (3%)
    psum x3, blocking collectives, column_sum(): return lax.psum(jnp.sum(first_vector * second_vector, axis=(0, 1)), 'sub')  98.1 us
    ppermute x8, waiting for transfers between devices, from_behind(): return lax.ppermute(block, axis, route)  47.5 us
    all_gather x2, blocking collectives, coarse_apply(): lax.all_gather(coarse_input, 'sub', axis=0, tiled=True)  47.5 us
    dot_general x4, matrix products, couple(): jnp.einsum('sij,sjr->sir', matrices, stacked, preferred_element_type=jnp....  9.51 us
  transfers between devices with their start and end apart: 8, of which 6 were waited for; matrix products, arithmetic and copies ran while one was open for 0% of the time, Pallas kernels for 0%

commit v1 on v0

v1 whole, which is shorter than its diff:
```python
import jax
import jax.numpy as jnp
from jax import lax
from jax.sharding import PartitionSpec as P

AXIS = "sub"
BF16 = jnp.bfloat16
F32 = jnp.float32


def shifted(block, distance):
    n = lax.axis_size(AXIS)
    return lax.ppermute(block, AXIS, [((i - distance) % n, i) for i in range(n)])


def partner_block(block):
    n = lax.axis_size(AXIS)
    return lax.ppermute(block, AXIS, [(i, i ^ 1) for i in range(n)])


def gather_relative(block):
    n = lax.axis_size(AXIS)
    if n % 2:
        return jnp.concatenate([block] + [shifted(block, k) for k in range(1, n)], axis=0)
    same = jnp.concatenate([block] + [shifted(block, 2 * k) for k in range(1, n // 2)], axis=0)
    return jnp.concatenate([same, partner_block(same)], axis=0)


def relative_columns(rows):
    n = lax.axis_size(AXIS)
    me = lax.axis_index(AXIS)
    count, width = rows.shape[0], rows.shape[1] // n
    group = 1 if n % 2 else 2
    pairs = rows.reshape(count, n // group, group, width)[:, ::-1]
    first = n // group - 1 - me // group
    doubled = jnp.concatenate([pairs, pairs], axis=1)
    turned = lax.dynamic_slice_in_dim(doubled, first, n // group, axis=1)
    if group == 2:
        turned = jnp.where(me % 2 == 0, turned, turned[:, :, ::-1])
    return turned.transpose(0, 2, 1, 3).reshape(count, n * width)


def sum_all(block):
    n = lax.axis_size(AXIS)
    total = block
    for k in range(1, n):
        total = total + shifted(block, k)
    return total


def dot(a, b):
    return jnp.dot(a, b, preferred_element_type=F32)


def split_dot(a, b):
    high = lax.reduce_precision(b, 8, 7)
    return dot(a, high.astype(BF16)) + dot(a, (b - high).astype(BF16))


def combine(first, second, back, forward):
    faces = [first[0] + forward]
    for j in range(1, len(first)):
        faces.append(second[j - 1] + first[j])
    faces.append(second[-1] + back)
    return faces


def exchange(first, second):
    back = shifted(first[0].astype(BF16), -1).astype(F32)
    forward = shifted(second[-1].astype(BF16), 1).astype(F32)
    return combine(first, second, back, forward)


def shards(right_side, face_weight, schur, neumann, constraint, coarse_inverse):
    subs, nf = face_weight.shape
    ni = 2 * nf
    ncf = constraint.shape[0] // subs
    columns = right_side.shape[1]
    schur_blocks = [schur[j * ni : (j + 1) * ni] for j in range(subs)]
    neumann_blocks = [neumann[j * ni : (j + 1) * ni] for j in range(subs)]
    load = [right_side[j * nf : (j + 1) * nf] for j in range(subs)]
    own_rows = [constraint[j * ncf : (j + 1) * ncf] for j in range(subs)]

    coarse = jnp.concatenate([dot(own_rows[j], load[j].astype(BF16)) for j in range(subs)], axis=0).astype(BF16)
    weight = [face_weight[j].reshape(nf, 1) for j in range(subs)]
    halo_source = shifted(((1.0 - weight[-1]) * load[-1]).astype(BF16), 1)
    coarse_all = gather_relative(coarse)
    weight = [shifted(face_weight[-1:], 1).reshape(nf, 1)] + weight
    rows = [shifted(own_rows[-1], 1)] + own_rows
    inverse = relative_columns(jnp.concatenate([shifted(coarse_inverse[-ncf:], 1), coarse_inverse], axis=0))

    def neumann_halves(left, right):
        first, second = [], []
        for j in range(subs):
            product = dot(neumann_blocks[j], jnp.concatenate([left[j], right[j]], axis=0))
            first.append((1.0 - weight[j]) * product[:nf])
            second.append(weight[j + 1] * product[nf:])
        return first, second

    def add_coarse(faces, coarse_all):
        x = dot(inverse, coarse_all)
        return [face + split_dot(rows[j].T, x[j * ncf : (j + 1) * ncf]) for j, face in enumerate(faces)]

    def schur_halves(faces):
        first, second = [], []
        for j in range(subs):
            product = split_dot(schur_blocks[j], jnp.concatenate([faces[j], faces[j + 1]], axis=0))
            first.append(product[:nf])
            second.append(product[nf:])
        return first, second

    def energy(faces, first, second):
        total = 0.0
        for j in range(subs):
            total = total + jnp.sum(faces[j] * first[j], axis=0) + jnp.sum(faces[j + 1] * second[j], axis=0)
        return total

    def inner(a, b):
        return sum(jnp.sum(x * y, axis=0) for x, y in zip(a, b))

    left = [halo_source] + [((1.0 - weight[j + 1]) * load[j]).astype(BF16) for j in range(subs - 1)]
    right = [(weight[j + 1] * load[j]).astype(BF16) for j in range(subs)]
    z = add_coarse(exchange(*neumann_halves(left, right)), coarse_all)
    first, second = schur_halves(z)
    load_z, z_image = inner(load, z[1:]), energy(z, first, second)
    coarse_back = shifted(split_dot(rows[0], first[0]), -1)
    parts = [split_dot(rows[j], second[j - 1] + first[j]) for j in range(1, subs)]
    parts.append(split_dot(rows[subs], second[-1]) + coarse_back)
    coarse_all = gather_relative(jnp.concatenate(parts, axis=0).astype(BF16))
    image = exchange(first, second)
    left = [((1.0 - weight[j]) * image[j]).astype(BF16) for j in range(subs)]
    right = [(weight[j + 1] * image[j + 1]).astype(BF16) for j in range(subs)]
    y = add_coarse(exchange(*neumann_halves(left, right)), coarse_all)
    first, second = schur_halves(y)
    image_y, y_image = inner(image[1:], y[1:]), energy(y, first, second)
    a, b, c, d = sum_all(jnp.stack([load_z, z_image, image_y, y_image], axis=0))
    image_y_faces = exchange(first, second)[1:]

    step = a / b
    grow = step * (c / b)
    next_step = (grow - 1.0) / ((d - c * (c / b)) * (step / b))
    s = step + next_step * grow
    t = step * next_step
    solution = jnp.concatenate([s * z[j + 1] - t * y[j + 1] for j in range(subs)], axis=0)
    residual = jnp.concatenate([load[j] - s * image[j + 1] + t * image_y_faces[j] for j in range(subs)], axis=0)
    return solution, residual


def solution(mesh):
    specs = P(("parts", AXIS), None)
    return jax.shard_map(shards, mesh=mesh, in_specs=(specs,) * 6, out_specs=(specs, specs), check_vma=False)
```

time: 222 us -> 117 us (0.53)
  blocking collectives: 146 us -> 0 us
  starting transfers between devices: 1.24 us -> 48.2 us
  waiting for transfers between devices: 47.5 us -> 33.8 us
  matrix products: 11.2 us -> 18.7 us
  other arithmetic: 7.23 us -> 4.14 us
    psum x3 -> x0, blocking collectives: 98.1 us -> none  [column_sum(): return lax.psum(jnp.sum(first_vector * second_vector, axis=(0, 1)), 'sub')]
    all_gather x2 -> x0, blocking collectives: 47.5 us -> none  [coarse_apply(): lax.all_gather(coarse_input, 'sub', axis=0, tiled=True)]
    ppermute x8 -> x43, starting transfers between devices: 1.24 us -> 48.2 us  [the longest x41 47.3 us: shifted(): lax.ppermute(block, AXIS, [((i - distance) % n, i) for i in range(n)])]
    ppermute x8 -> x43, waiting for transfers between devices: 47.5 us -> 33.8 us  [the longest x41 33 us: shifted(): lax.ppermute(block, AXIS, [((i - distance) % n, i) for i in range(n)])]
    dot_general x10 -> x34, matrix products: 11.2 us -> 18.7 us  [dot(): return jnp.dot(a, b, preferred_element_type=F32)]
    unnamed x26 -> x28, local copies, waits for them, and re-layouts: 2.19 us -> 6.96 us
    sub x2 -> x3, other arithmetic: 3.99 us -> 0.01 us  [the longest x2 0.01 us: neumann_halves(): first.append((1.0 - weight[j]) * product[:nf])]
    sub x1 -> x0, local copies, waits for them, and re-layouts: 2.62 us -> none  [shards(): residual = residual - step_size * product_image]
  transfers between devices with their start and end apart: 8 -> 43, of which waited for: 6 -> 15; matrix products, arithmetic and copies ran while one was open for 0% -> 18% of each run, Pallas kernels for 0% -> 0%
where the time goes in v1:
time: 117 us
  starting transfers between devices  48.2 us (41%)
  waiting for transfers between devices  33.8 us (29%)
  matrix products  18.7 us (16%)
  local copies, waits for them, and re-layouts  10.3 us (9%)
  other arithmetic  4.14 us (4%)
  between operations  1.4 us (1%)
    ppermute x41, starting transfers between devices, shifted(): lax.ppermute(block, AXIS, [((i - distance) % n, i) for i in range(n)])  47.3 us
    ppermute x41, waiting for transfers between devices, shifted(): lax.ppermute(block, AXIS, [((i - distance) % n, i) for i in range(n)])  33 us
    dot_general x34, matrix products, dot(): return jnp.dot(a, b, preferred_element_type=F32)  18.7 us
    unnamed x28, local copies, waits for them, and re-layouts  6.96 us
  transfers between devices with their start and end apart: 43, of which 15 were waited for; matrix products, arithmetic and copies ran while one was open for 18% of the time, Pallas kernels for 0%

profile of v1, /device:TPU:0, one launch (start us, length us, event | category | flops | bytes accessed | tf_op | source)
XLA Modules:
  0.0 116.6 jit_solution(14790203720137676024)
XLA Ops:
  0.6 1.3 %fusion.134 = (f32[512,256]{1,0:T(8,128)S(1)}, f32[512,256]{1,0:T(8,128)S(1)}) fusion(f32[1024,256]{1,0:T(8,128)} %param.6), kind=kLoop, calls=%fused_computation.256 | loop fusion | bytes 2097152 | tf_op jit(solution)/shard_map/slice | solution.py:81
  2.4 0.8 constant_dynamic-update-slice_fusion.8
  3.2 0.8 constant_dynamic-update-slice_fusion.7
  4.0 3.0 %collective-permute-start.2 = (bf16[64,256]{1,0:T(8,128)(2,1)S(1)}, bf16[64,256]{1,0:T(8,128)(2,1)S(1)}, u32[]{:S(2)}, u32[]{:S(2)}) collective-permute-start(bf16[64,256]{1,0:T(8,128)(2,1)S(1)} %pad_maximum_fusion.7), channel_id=1, source_target_pairs={{14,0},{15,1},{0,2},{1,3},{2,4},{3,5},{4,6},{5,7},{6,8},{7,9},{8,1... | collective-permute-start | bytes 98312 | tf_op jit(solution)/shard_map/ppermute | solution.py:13
  7.0 1.6 %collective-permute-start.3 = (bf16[64,256]{1,0:T(8,128)(2,1)S(1)}, bf16[64,256]{1,0:T(8,128)(2,1)S(1)}, u32[]{:S(2)}, u32[]{:S(2)}) collective-permute-start(bf16[64,256]{1,0:T(8,128)(2,1)S(1)} %pad_maximum_fusion.7), channel_id=1, source_target_pairs={{12,0},{13,1},{14,2},{15,3},{0,4},{1,5},{2,6},{3,7},{4,8},{5,9},{6... | collective-permute-start | bytes 98312 | tf_op jit(solution)/shard_map/ppermute | solution.py:13
  8.5 2.5 %collective-permute-start.4 = (bf16[64,256]{1,0:T(8,128)(2,1)S(1)}, bf16[64,256]{1,0:T(8,128)(2,1)S(1)}, u32[]{:S(2)}, u32[]{:S(2)}) collective-permute-start(bf16[64,256]{1,0:T(8,128)(2,1)S(1)} %pad_maximum_fusion.7), channel_id=1, source_target_pairs={{10,0},{11,1},{12,2},{13,3},{14,4},{15,5},{0,6},{1,7},{2,8},{3,9},... | collective-permute-start | bytes 98312 | tf_op jit(solution)/shard_map/ppermute | solution.py:13
  11.1 1.2 %collective-permute-start.5 = (bf16[64,256]{1,0:T(8,128)(2,1)S(1)}, bf16[64,256]{1,0:T(8,128)(2,1)S(1)}, u32[]{:S(2)}, u32[]{:S(2)}) collective-permute-start(bf16[64,256]{1,0:T(8,128)(2,1)S(1)} %pad_maximum_fusion.7), channel_id=1, source_target_pairs={{8,0},{9,1},{10,2},{11,3},{12,4},{13,5},{14,6},{15,7},{0,8},{1,9},... | collective-permute-start | bytes 98312 | tf_op jit(solution)/shard_map/ppermute | solution.py:13
  12.4 0.8 multiply_convert_fusion.6
  13.9 2.4 %fusion.14 = f32[1024,256]{0,1:T(8,128)S(1)} fusion(bf16[2048,1024]{1,0:T(8,128)(2,1)} %param.9, bf16[512,256]{0,1:T(8,128)(2,1)S(1)} %get-tuple-element.44, bf16[512,256]{0,1:T(8,128)(2,1)S(1)} %get-tuple-element.46), kind=kOutput, calls=%fused_computation.18 | convolution fusion | flops 537919488 | bytes 3670016 | tf_op jit(solution)/shard_map/dot_general | solution.py:52
  16.7 1.4 %collective-permute-done.10 = f32[1,512]{1,0:T(1,128)S(1)} collective-permute-done((f32[1,512]{1,0:T(1,128)S(1)}, f32[1,512]{1,0:T(1,128)S(1)}, u32[]{:S(2)}, u32[]{:S(2)}) %collective-permute-start.10) | collective-permute-done | bytes 2080 | tf_op jit(solution)/shard_map/ppermute | solution.py:13
  18.1 1.3 %collective-permute-start.6 = (bf16[64,256]{1,0:T(8,128)(2,1)S(1)}, bf16[64,256]{1,0:T(8,128)(2,1)S(1)}, u32[]{:S(2)}, u32[]{:S(2)}) collective-permute-start(bf16[64,256]{1,0:T(8,128)(2,1)S(1)} %pad_maximum_fusion.7), channel_id=1, source_target_pairs={{6,0},{7,1},{8,2},{9,3},{10,4},{11,5},{12,6},{13,7},{14,8},{15,9},... | collective-permute-start | bytes 98312 | tf_op jit(solution)/shard_map/ppermute | solution.py:13
  19.4 1.3 %collective-permute-start.7 = (bf16[64,256]{1,0:T(8,128)(2,1)S(1)}, bf16[64,256]{1,0:T(8,128)(2,1)S(1)}, u32[]{:S(2)}, u32[]{:S(2)}) collective-permute-start(bf16[64,256]{1,0:T(8,128)(2,1)S(1)} %pad_maximum_fusion.7), channel_id=1, source_target_pairs={{4,0},{5,1},{6,2},{7,3},{8,4},{9,5},{10,6},{11,7},{12,8},{13,9},{1... | collective-permute-start | bytes 98312 | tf_op jit(solution)/shard_map/ppermute | solution.py:13
  21.4 1.4 %collective-permute-start.8 = (bf16[64,256]{1,0:T(8,128)(2,1)S(1)}, bf16[64,256]{1,0:T(8,128)(2,1)S(1)}, u32[]{:S(2)}, u32[]{:S(2)}) collective-permute-start(bf16[64,256]{1,0:T(8,128)(2,1)S(1)} %pad_maximum_fusion.7), channel_id=1, source_target_pairs={{2,0},{3,1},{4,2},{5,3},{6,4},{7,5},{8,6},{9,7},{10,8},{11,9},{12,... | collective-permute-start | bytes 98312 | tf_op jit(solution)/shard_map/ppermute | solution.py:13
  25.4 0.8 collective-permute-start.13
  28.0 0.9 collective-permute-start.9
  28.9 3.0 %collective-permute-done.1 = bf16[32,1024]{0,1:T(8,128)(2,1)S(1)} collective-permute-done((bf16[32,1024]{0,1:T(8,128)(2,1)S(1)}, bf16[32,1024]{0,1:T(8,128)(2,1)S(1)}, u32[]{:S(2)}, u32[]{:S(2)}) %collective-permute-start.1) | collective-permute-done | bytes 65568 | tf_op jit(solution)/shard_map/ppermute | solution.py:13
  32.3 2.5 %collective-permute-done = bf16[512,256]{0,1:T(8,128)(2,1)} collective-permute-done((bf16[512,256]{0,1:T(8,128)(2,1)}, bf16[512,256]{0,1:T(8,128)(2,1)}, u32[]{:S(2)}, u32[]{:S(2)}) %collective-permute-start) | collective-permute-done | bytes 262176 | tf_op jit(solution)/shard_map/ppermute | solution.py:13
  34.8 2.5 %fusion.8 = f32[1024,256]{0,1:T(8,128)S(1)} fusion(bf16[2048,1024]{1,0:T(8,128)(2,1)} %param.9, bf16[512,256]{0,1:T(8,128)(2,1)} %get-tuple-element.45, bf16[512,256]{0,1:T(8,128)(2,1)} %collective-permute-done), kind=kOutput, calls=%fused_computation.16 | convolution fusion | flops 537919488 | bytes 3670016 | tf_op jit(solution)/shard_map/dot_general | solution.py:52
  37.5 1.1 constant_dynamic-update-slice_fusion.9
  40.2 1.2 collective-permute-done.11
  42.3 0.8 fusion.22
  43.6 8.3 %collective-permute-done.12 = bf16[512,256]{0,1:T(8,128)(2,1)S(1)} collective-permute-done((bf16[512,256]{0,1:T(8,128)(2,1)S(1)}, bf16[512,256]{0,1:T(8,128)(2,1)S(1)}, u32[]{:S(2)}, u32[]{:S(2)}) %collective-permute-start.12) | collective-permute-done | bytes 262176 | tf_op jit(solution)/shard_map/ppermute | solution.py:13
  52.1 0.8 fusion.34
  52.9 0.8 fusion.23
  54.8 3.0 %collective-permute-done.15 = bf16[512,256]{0,1:T(8,128)(2,1)S(1)} collective-permute-done((bf16[512,256]{0,1:T(8,128)(2,1)S(1)}, bf16[512,256]{0,1:T(8,128)(2,1)S(1)}, u32[]{:S(2)}, u32[]{:S(2)}) %collective-permute-start.15) | collective-permute-done | bytes 262176 | tf_op jit(solution)/shard_map/ppermute | solution.py:13
  58.7 5.1 %collective-permute-start.20 = (bf16[64,256]{1,0:T(8,128)(2,1)S(1)}, bf16[64,256]{1,0:T(8,128)(2,1)S(1)}, u32[]{:S(2)}, u32[]{:S(2)}) collective-permute-start(bf16[64,256]{1,0:T(8,128)(2,1)S(1)} %pad_maximum_fusion.8), channel_id=1, source_target_pairs={{8,0},{9,1},{10,2},{11,3},{12,4},{13,5},{14,6},{15,7},{0,8},{1,9},... | collective-permute-start | bytes 98312 | tf_op jit(solution)/shard_map/ppermute | solution.py:13
  64.8 0.8 collective-permute-done.17
  65.6 2.2 %collective-permute-start.22 = (bf16[64,256]{1,0:T(8,128)(2,1)S(1)}, bf16[64,256]{1,0:T(8,128)(2,1)S(1)}, u32[]{:S(2)}, u32[]{:S(2)}) collective-permute-start(bf16[64,256]{1,0:T(8,128)(2,1)S(1)} %pad_maximum_fusion.8), channel_id=1, source_target_pairs={{4,0},{5,1},{6,2},{7,3},{8,4},{9,5},{10,6},{11,7},{12,8},{13,9},{1... | collective-permute-start | bytes 98312 | tf_op jit(solution)/shard_map/ppermute | solution.py:13
  67.8 1.5 %collective-permute-start.23 = (bf16[64,256]{1,0:T(8,128)(2,1)S(1)}, bf16[64,256]{1,0:T(8,128)(2,1)S(1)}, u32[]{:S(2)}, u32[]{:S(2)}) collective-permute-start(bf16[64,256]{1,0:T(8,128)(2,1)S(1)} %pad_maximum_fusion.8), channel_id=1, source_target_pairs={{2,0},{3,1},{4,2},{5,3},{6,4},{7,5},{8,6},{9,7},{10,8},{11,9},{12,... | collective-permute-start | bytes 98312 | tf_op jit(solution)/shard_map/ppermute | solution.py:13
  69.3 1.6 %collective-permute-start.25 = (bf16[512,256]{0,1:T(8,128)(2,1)S(1)}, bf16[512,256]{0,1:T(8,128)(2,1)S(1)}, u32[]{:S(2)}, u32[]{:S(2)}) collective-permute-start(bf16[512,256]{0,1:T(8,128)(2,1)S(1)} %fusion.76), channel_id=1, source_target_pairs={{1,0},{2,1},{3,2},{4,3},{5,4},{6,5},{7,6},{8,7},{9,8},{10,9},{11,1... | collective-permute-start | bytes 786440 | tf_op jit(solution)/shard_map/ppermute | solution.py:13
  70.9 0.8 collective-permute-done.23
  71.7 0.8 fusion.17
  76.8 0.9 collective-permute-start.26
  77.9 7.6 %collective-permute-done.26 = bf16[512,256]{0,1:T(8,128)(2,1)S(1)} collective-permute-done((bf16[512,256]{0,1:T(8,128)(2,1)S(1)}, bf16[512,256]{0,1:T(8,128)(2,1)S(1)}, u32[]{:S(2)}, u32[]{:S(2)}) %collective-permute-start.26) | collective-permute-done | bytes 262176 | tf_op jit(solution)/shard_map/ppermute | solution.py:13
  87.7 1.2 %collective-permute-start.40 = (f32[4,256]{1,0:T(4,128)S(1)}, f32[4,256]{1,0:T(4,128)S(1)}, u32[]{:S(2)}, u32[]{:S(2)}) collective-permute-start(f32[4,256]{1,0:T(4,128)S(1)} %pad_maximum_fusion.9), channel_id=1, source_target_pairs={{2,0},{3,1},{4,2},{5,3},{6,4},{7,5},{8,6},{9,7},{10,8},{11,9},{12,... | collective-permute-start | bytes 12296 | tf_op jit(solution)/shard_map/ppermute | solution.py:13
  88.9 2.4 %collective-permute-start.38 = (f32[4,256]{1,0:T(4,128)S(1)}, f32[4,256]{1,0:T(4,128)S(1)}, u32[]{:S(2)}, u32[]{:S(2)}) collective-permute-start(f32[4,256]{1,0:T(4,128)S(1)} %pad_maximum_fusion.9), channel_id=1, source_target_pairs={{4,0},{5,1},{6,2},{7,3},{8,4},{9,5},{10,6},{11,7},{12,8},{13,9},{1... | collective-permute-start | bytes 12296 | tf_op jit(solution)/shard_map/ppermute | solution.py:13
  91.3 2.1 %collective-permute-start.36 = (f32[4,256]{1,0:T(4,128)S(1)}, f32[4,256]{1,0:T(4,128)S(1)}, u32[]{:S(2)}, u32[]{:S(2)}) collective-permute-start(f32[4,256]{1,0:T(4,128)S(1)} %pad_maximum_fusion.9), channel_id=1, source_target_pairs={{6,0},{7,1},{8,2},{9,3},{10,4},{11,5},{12,6},{13,7},{14,8},{15,9},... | collective-permute-start | bytes 12296 | tf_op jit(solution)/shard_map/ppermute | solution.py:13
  93.9 1.2 collective-permute-start.34
  95.1 2.3 %collective-permute-start.33 = (f32[4,256]{1,0:T(4,128)S(1)}, f32[4,256]{1,0:T(4,128)S(1)}, u32[]{:S(2)}, u32[]{:S(2)}) collective-permute-start(f32[4,256]{1,0:T(4,128)S(1)} %pad_maximum_fusion.9), channel_id=1, source_target_pairs={{9,0},{10,1},{11,2},{12,3},{13,4},{14,5},{15,6},{0,7},{1,8},{2,9},... | collective-permute-start | bytes 12296 | tf_op jit(solution)/shard_map/ppermute | solution.py:13
  97.3 1.9 %collective-permute-start.32 = (f32[4,256]{1,0:T(4,128)S(1)}, f32[4,256]{1,0:T(4,128)S(1)}, u32[]{:S(2)}, u32[]{:S(2)}) collective-permute-start(f32[4,256]{1,0:T(4,128)S(1)} %pad_maximum_fusion.9), channel_id=1, source_target_pairs={{10,0},{11,1},{12,2},{13,3},{14,4},{15,5},{0,6},{1,7},{2,8},{3,9},... | collective-permute-start | bytes 12296 | tf_op jit(solution)/shard_map/ppermute | solution.py:13
  99.8 2.1 %collective-permute-start.30 = (f32[4,256]{1,0:T(4,128)S(1)}, f32[4,256]{1,0:T(4,128)S(1)}, u32[]{:S(2)}, u32[]{:S(2)}) collective-permute-start(f32[4,256]{1,0:T(4,128)S(1)} %pad_maximum_fusion.9), channel_id=1, source_target_pairs={{12,0},{13,1},{14,2},{15,3},{0,4},{1,5},{2,6},{3,7},{4,8},{5,9},{6... | collective-permute-start | bytes 12296 | tf_op jit(solution)/shard_map/ppermute | solution.py:13
  101.9 2.1 %collective-permute-start.29 = (f32[4,256]{1,0:T(4,128)S(1)}, f32[4,256]{1,0:T(4,128)S(1)}, u32[]{:S(2)}, u32[]{:S(2)}) collective-permute-start(f32[4,256]{1,0:T(4,128)S(1)} %pad_maximum_fusion.9), channel_id=1, source_target_pairs={{13,0},{14,1},{15,2},{0,3},{1,4},{2,5},{3,6},{4,7},{5,8},{6,9},{7,... | collective-permute-start | bytes 12296 | tf_op jit(solution)/shard_map/ppermute | solution.py:13
  104.0 0.8 collective-permute-start.28
  104.9 4.5 %collective-permute-start.42 = (bf16[512,256]{0,1:T(8,128)(2,1)S(1)}, bf16[512,256]{0,1:T(8,128)(2,1)S(1)}, u32[]{:S(2)}, u32[]{:S(2)}) collective-permute-start(bf16[512,256]{0,1:T(8,128)(2,1)S(1)} %slice.312), channel_id=1, source_target_pairs={{1,0},{2,1},{3,2},{4,3},{5,4},{6,5},{7,6},{8,7},{9,8},{10,9},{11,1... | collective-permute-start | bytes 786440 | tf_op jit(solution)/shard_map/ppermute | solution.py:13
  109.4 1.0 collective-permute-done.28
  110.6 2.6 %collective-permute-done.42 = bf16[512,256]{0,1:T(8,128)(2,1)S(1)} collective-permute-done((bf16[512,256]{0,1:T(8,128)(2,1)S(1)}, bf16[512,256]{0,1:T(8,128)(2,1)S(1)}, u32[]{:S(2)}, u32[]{:S(2)}) %collective-permute-start.42) | collective-permute-done | bytes 262176 | tf_op jit(solution)/shard_map/ppermute | solution.py:13
  113.9 1.3 %copy.17 = f32[1024,256]{1,0:T(8,128)} copy(f32[1024,256]{0,1:T(8,128)S(1)} %get-tuple-element.88) | data formatting | bytes 2097152
  115.3 1.3 %copy.18 = f32[1024,256]{1,0:T(8,128)} copy(f32[1024,256]{0,1:T(8,128)S(1)} %get-tuple-element.89) | data formatting | bytes 2097152
  (141 shorter events, 21.9 us)
Async XLA Ops:
  0.6 1.7 %copy-start = (bf16[64,512]{1,0:T(8,128)(2,1)S(1)}, bf16[64,512]{1,0:T(8,128)(2,1)}, u32[]{:S(2)}) copy-start(bf16[64,512]{1,0:T(8,128)(2,1)} %param.10) | copy-start | bytes 196612
  0.6 11.7 %copy-start.2 = (f32[2,512]{1,0:T(2,128)S(1)}, f32[2,512]{1,0:T(2,128)}, u32[]{:S(2)}) copy-start(f32[2,512]{1,0:T(2,128)} %param.7) | copy-start | bytes 12292
  2.4 14.0 %copy-start.1 = (bf16[64,1024]{1,0:T(8,128)(2,1)S(1)}, bf16[64,1024]{1,0:T(8,128)(2,1)}, u32[]{:S(2)}) copy-start(bf16[64,1024]{1,0:T(8,128)(2,1)} %param.11) | copy-start | bytes 393220
  4.0 15.4 %collective-permute-start.2 = (bf16[64,256]{1,0:T(8,128)(2,1)S(1)}, bf16[64,256]{1,0:T(8,128)(2,1)S(1)}, u32[]{:S(2)}, u32[]{:S(2)}) collective-permute-start(bf16[64,256]{1,0:T(8,128)(2,1)S(1)} %pad_maximum_fusion.7), channel_id=1, source_target_pairs={{14,0},{15,1},{0,2},{1,3},{2,4},{3,5},{4,6},{5,7},{6,8},{7,9},{8,1... | collective-permute-start | bytes 98312 | tf_op jit(solution)/shard_map/ppermute | solution.py:13
  7.0 14.4 %collective-permute-start.3 = (bf16[64,256]{1,0:T(8,128)(2,1)S(1)}, bf16[64,256]{1,0:T(8,128)(2,1)S(1)}, u32[]{:S(2)}, u32[]{:S(2)}) collective-permute-start(bf16[64,256]{1,0:T(8,128)(2,1)S(1)} %pad_maximum_fusion.7), channel_id=1, source_target_pairs={{12,0},{13,1},{14,2},{15,3},{0,4},{1,5},{2,6},{3,7},{4,8},{5,9},{6... | collective-permute-start | bytes 98312 | tf_op jit(solution)/shard_map/ppermute | solution.py:13
  8.5 14.9 %collective-permute-start.4 = (bf16[64,256]{1,0:T(8,128)(2,1)S(1)}, bf16[64,256]{1,0:T(8,128)(2,1)S(1)}, u32[]{:S(2)}, u32[]{:S(2)}) collective-permute-start(bf16[64,256]{1,0:T(8,128)(2,1)S(1)} %pad_maximum_fusion.7), channel_id=1, source_target_pairs={{10,0},{11,1},{12,2},{13,3},{14,4},{15,5},{0,6},{1,7},{2,8},{3,9},... | collective-permute-start | bytes 98312 | tf_op jit(solution)/shard_map/ppermute | solution.py:13
  11.1 13.0 %collective-permute-start.5 = (bf16[64,256]{1,0:T(8,128)(2,1)S(1)}, bf16[64,256]{1,0:T(8,128)(2,1)S(1)}, u32[]{:S(2)}, u32[]{:S(2)}) collective-permute-start(bf16[64,256]{1,0:T(8,128)(2,1)S(1)} %pad_maximum_fusion.7), channel_id=1, source_target_pairs={{8,0},{9,1},{10,2},{11,3},{12,4},{13,5},{14,6},{15,7},{0,8},{1,9},... | collective-permute-start | bytes 98312 | tf_op jit(solution)/shard_map/ppermute | solution.py:13
  12.3 5.8 %collective-permute-start.10 = (f32[1,512]{1,0:T(1,128)S(1)}, f32[1,512]{1,0:T(1,128)S(1)}, u32[]{:S(2)}, u32[]{:S(2)}) collective-permute-start(f32[1,512]{1,0:T(1,128)S(1)} %get-tuple-element.82), channel_id=1, source_target_pairs={{15,0},{0,1},{1,2},{2,3},{3,4},{4,5},{5,6},{6,7},{7,8},{8,9},{9,10... | collective-permute-start | bytes 6152 | tf_op jit(solution)/shard_map/ppermute | solution.py:13
  18.1 7.3 %collective-permute-start.6 = (bf16[64,256]{1,0:T(8,128)(2,1)S(1)}, bf16[64,256]{1,0:T(8,128)(2,1)S(1)}, u32[]{:S(2)}, u32[]{:S(2)}) collective-permute-start(bf16[64,256]{1,0:T(8,128)(2,1)S(1)} %pad_maximum_fusion.7), channel_id=1, source_target_pairs={{6,0},{7,1},{8,2},{9,3},{10,4},{11,5},{12,6},{13,7},{14,8},{15,9},... | collective-permute-start | bytes 98312 | tf_op jit(solution)/shard_map/ppermute | solution.py:13
  19.4 7.4 %collective-permute-start.7 = (bf16[64,256]{1,0:T(8,128)(2,1)S(1)}, bf16[64,256]{1,0:T(8,128)(2,1)S(1)}, u32[]{:S(2)}, u32[]{:S(2)}) collective-permute-start(bf16[64,256]{1,0:T(8,128)(2,1)S(1)} %pad_maximum_fusion.7), channel_id=1, source_target_pairs={{4,0},{5,1},{6,2},{7,3},{8,4},{9,5},{10,6},{11,7},{12,8},{13,9},{1... | collective-permute-start | bytes 98312 | tf_op jit(solution)/shard_map/ppermute | solution.py:13
  21.4 6.0 %collective-permute-start.8 = (bf16[64,256]{1,0:T(8,128)(2,1)S(1)}, bf16[64,256]{1,0:T(8,128)(2,1)S(1)}, u32[]{:S(2)}, u32[]{:S(2)}) collective-permute-start(bf16[64,256]{1,0:T(8,128)(2,1)S(1)} %pad_maximum_fusion.7), channel_id=1, source_target_pairs={{2,0},{3,1},{4,2},{5,3},{6,4},{7,5},{8,6},{9,7},{10,8},{11,9},{12,... | collective-permute-start | bytes 98312 | tf_op jit(solution)/shard_map/ppermute | solution.py:13
  23.4 8.5 %collective-permute-start.1 = (bf16[32,1024]{0,1:T(8,128)(2,1)S(1)}, bf16[32,1024]{0,1:T(8,128)(2,1)S(1)}, u32[]{:S(2)}, u32[]{:S(2)}) collective-permute-start(bf16[32,1024]{0,1:T(8,128)(2,1)S(1)} %slice.135), channel_id=1, source_target_pairs={{15,0},{0,1},{1,2},{2,3},{3,4},{4,5},{5,6},{6,7},{7,8},{8,9},{9,10... | collective-permute-start | bytes 196616 | tf_op jit(solution)/shard_map/ppermute | solution.py:13
  24.0 10.8 %collective-permute-start = (bf16[512,256]{0,1:T(8,128)(2,1)}, bf16[512,256]{0,1:T(8,128)(2,1)}, u32[]{:S(2)}, u32[]{:S(2)}) collective-permute-start(bf16[512,256]{0,1:T(8,128)(2,1)} %get-tuple-element.43), channel_id=1, source_target_pairs={{15,0},{0,1},{1,2},{2,3},{3,4},{4,5},{5,6},{6,7},{7,8},{8,9},{9,10... | collective-permute-start | bytes 786440 | tf_op jit(solution)/shard_map/ppermute | solution.py:13
  25.4 14.3 %collective-permute-start.13 = (bf16[32,512]{1,0:T(8,128)(2,1)S(1)}, bf16[32,512]{1,0:T(8,128)(2,1)S(1)}, u32[]{:S(2)}, u32[]{:S(2)}) collective-permute-start(bf16[32,512]{1,0:T(8,128)(2,1)S(1)} %slice.110), channel_id=1, source_target_pairs={{15,0},{0,1},{1,2},{2,3},{3,4},{4,5},{5,6},{6,7},{7,8},{8,9},{9,10... | collective-permute-start | bytes 98312 | tf_op jit(solution)/shard_map/ppermute | solution.py:13
  28.0 9.4 %collective-permute-start.9 = (bf16[512,256]{1,0:T(8,128)(2,1)}, bf16[512,256]{1,0:T(8,128)(2,1)}, u32[]{:S(2)}, u32[]{:S(2)}) collective-permute-start(bf16[512,256]{1,0:T(8,128)(2,1)} %get-tuple-element.61), channel_id=1, source_target_pairs={{0,1},{1,0},{2,3},{3,2},{4,5},{5,4},{6,7},{7,6},{8,9},{9,8},{10,11... | collective-permute-start | bytes 786440 | tf_op jit(solution)/shard_map/ppermute | solution.py:18
  37.4 3.9 %collective-permute-start.11 = (bf16[512,256]{0,1:T(8,128)(2,1)S(1)}, bf16[512,256]{0,1:T(8,128)(2,1)S(1)}, u32[]{:S(2)}, u32[]{:S(2)}) collective-permute-start(bf16[512,256]{0,1:T(8,128)(2,1)S(1)} %fusion.74), channel_id=1, source_target_pairs={{1,0},{2,1},{3,2},{4,3},{5,4},{6,5},{7,6},{8,7},{9,8},{10,9},{11,1... | collective-permute-start | bytes 786440 | tf_op jit(solution)/shard_map/ppermute | solution.py:13
  37.5 4.0 %copy-start.4 = (bf16[2048,1024]{1,0:T(8,128)(2,1)S(1)}, bf16[2048,1024]{1,0:T(8,128)(2,1)}, u32[]{:S(2)}) copy-start(bf16[2048,1024]{1,0:T(8,128)(2,1)} %param.8) | copy-start | bytes 12582916
  43.0 8.8 %collective-permute-start.12 = (bf16[512,256]{0,1:T(8,128)(2,1)S(1)}, bf16[512,256]{0,1:T(8,128)(2,1)S(1)}, u32[]{:S(2)}, u32[]{:S(2)}) collective-permute-start(bf16[512,256]{0,1:T(8,128)(2,1)S(1)} %get-tuple-element.38), channel_id=1, source_target_pairs={{15,0},{0,1},{1,2},{2,3},{3,4},{4,5},{5,6},{6,7},{7,8},{8,9},{9,10... | collective-permute-start | bytes 786440 | tf_op jit(solution)/shard_map/ppermute | solution.py:13
  43.3 11.4 %collective-permute-start.14 = (bf16[512,256]{0,1:T(8,128)(2,1)S(1)}, bf16[512,256]{0,1:T(8,128)(2,1)S(1)}, u32[]{:S(2)}, u32[]{:S(2)}) collective-permute-start(bf16[512,256]{0,1:T(8,128)(2,1)S(1)} %slice.313), channel_id=1, source_target_pairs={{15,0},{0,1},{1,2},{2,3},{3,4},{4,5},{5,6},{6,7},{7,8},{8,9},{9,10... | collective-permute-start | bytes 786440 | tf_op jit(solution)/shard_map/ppermute | solution.py:13
  53.7 10.2 %copy-start.3 = (bf16[2048,1024]{1,0:T(8,128)(2,1)S(1)}, bf16[2048,1024]{1,0:T(8,128)(2,1)}, u32[]{:S(2)}) copy-start(bf16[2048,1024]{1,0:T(8,128)(2,1)} %param.9) | copy-start | bytes 12582916
  53.8 4.0 %collective-permute-start.15 = (bf16[512,256]{0,1:T(8,128)(2,1)S(1)}, bf16[512,256]{0,1:T(8,128)(2,1)S(1)}, u32[]{:S(2)}, u32[]{:S(2)}) collective-permute-start(bf16[512,256]{0,1:T(8,128)(2,1)S(1)} %slice.314), channel_id=1, source_target_pairs={{1,0},{2,1},{3,2},{4,3},{5,4},{6,5},{7,6},{8,7},{9,8},{10,9},{11,1... | collective-permute-start | bytes 786440 | tf_op jit(solution)/shard_map/ppermute | solution.py:13
  54.2 4.3 %collective-permute-start.16 = (f32[32,256]{1,0:T(8,128)S(1)}, f32[32,256]{1,0:T(8,128)S(1)}, u32[]{:S(2)}, u32[]{:S(2)}) collective-permute-start(f32[32,256]{1,0:T(8,128)S(1)} %fusion.44), channel_id=1, source_target_pairs={{1,0},{2,1},{3,2},{4,3},{5,4},{6,5},{7,6},{8,7},{9,8},{10,9},{11,1... | collective-permute-start | bytes 98312 | tf_op jit(solution)/shard_map/ppermute | solution.py:13
  58.5 7.1 %collective-permute-start.17 = (bf16[64,256]{1,0:T(8,128)(2,1)S(1)}, bf16[64,256]{1,0:T(8,128)(2,1)S(1)}, u32[]{:S(2)}, u32[]{:S(2)}) collective-permute-start(bf16[64,256]{1,0:T(8,128)(2,1)S(1)} %pad_maximum_fusion.8), channel_id=1, source_target_pairs={{14,0},{15,1},{0,2},{1,3},{2,4},{3,5},{4,6},{5,7},{6,8},{7,9},{8,1... | collective-permute-start | bytes 98312 | tf_op jit(solution)/shard_map/ppermute | solution.py:13
  58.6 9.2 %collective-permute-start.18 = (bf16[64,256]{1,0:T(8,128)(2,1)S(1)}, bf16[64,256]{1,0:T(8,128)(2,1)S(1)}, u32[]{:S(2)}, u32[]{:S(2)}) collective-permute-start(bf16[64,256]{1,0:T(8,128)(2,1)S(1)} %pad_maximum_fusion.8), channel_id=1, source_target_pairs={{12,0},{13,1},{14,2},{15,3},{0,4},{1,5},{2,6},{3,7},{4,8},{5,9},{6... | collective-permute-start | bytes 98312 | tf_op jit(solution)/shard_map/ppermute | solution.py:13
  58.7 10.6 %collective-permute-start.19 = (bf16[64,256]{1,0:T(8,128)(2,1)S(1)}, bf16[64,256]{1,0:T(8,128)(2,1)S(1)}, u32[]{:S(2)}, u32[]{:S(2)}) collective-permute-start(bf16[64,256]{1,0:T(8,128)(2,1)S(1)} %pad_maximum_fusion.8), channel_id=1, source_target_pairs={{10,0},{11,1},{12,2},{13,3},{14,4},{15,5},{0,6},{1,7},{2,8},{3,9},... | collective-permute-start | bytes 98312 | tf_op jit(solution)/shard_map/ppermute | solution.py:13
  58.7 12.1 %collective-permute-start.20 = (bf16[64,256]{1,0:T(8,128)(2,1)S(1)}, bf16[64,256]{1,0:T(8,128)(2,1)S(1)}, u32[]{:S(2)}, u32[]{:S(2)}) collective-permute-start(bf16[64,256]{1,0:T(8,128)(2,1)S(1)} %pad_maximum_fusion.8), channel_id=1, source_target_pairs={{8,0},{9,1},{10,2},{11,3},{12,4},{13,5},{14,6},{15,7},{0,8},{1,9},... | collective-permute-start | bytes 98312 | tf_op jit(solution)/shard_map/ppermute | solution.py:13
  63.9 7.0 %collective-permute-start.21 = (bf16[64,256]{1,0:T(8,128)(2,1)S(1)}, bf16[64,256]{1,0:T(8,128)(2,1)S(1)}, u32[]{:S(2)}, u32[]{:S(2)}) collective-permute-start(bf16[64,256]{1,0:T(8,128)(2,1)S(1)} %pad_maximum_fusion.8), channel_id=1, source_target_pairs={{6,0},{7,1},{8,2},{9,3},{10,4},{11,5},{12,6},{13,7},{14,8},{15,9},... | collective-permute-start | bytes 98312 | tf_op jit(solution)/shard_map/ppermute | solution.py:13
  65.6 5.3 %collective-permute-start.22 = (bf16[64,256]{1,0:T(8,128)(2,1)S(1)}, bf16[64,256]{1,0:T(8,128)(2,1)S(1)}, u32[]{:S(2)}, u32[]{:S(2)}) collective-permute-start(bf16[64,256]{1,0:T(8,128)(2,1)S(1)} %pad_maximum_fusion.8), channel_id=1, source_target_pairs={{4,0},{5,1},{6,2},{7,3},{8,4},{9,5},{10,6},{11,7},{12,8},{13,9},{1... | collective-permute-start | bytes 98312 | tf_op jit(solution)/shard_map/ppermute | solution.py:13
  67.8 4.0 %collective-permute-start.23 = (bf16[64,256]{1,0:T(8,128)(2,1)S(1)}, bf16[64,256]{1,0:T(8,128)(2,1)S(1)}, u32[]{:S(2)}, u32[]{:S(2)}) collective-permute-start(bf16[64,256]{1,0:T(8,128)(2,1)S(1)} %pad_maximum_fusion.8), channel_id=1, source_target_pairs={{2,0},{3,1},{4,2},{5,3},{6,4},{7,5},{8,6},{9,7},{10,8},{11,9},{12,... | collective-permute-start | bytes 98312 | tf_op jit(solution)/shard_map/ppermute | solution.py:13
  69.3 5.5 %collective-permute-start.25 = (bf16[512,256]{0,1:T(8,128)(2,1)S(1)}, bf16[512,256]{0,1:T(8,128)(2,1)S(1)}, u32[]{:S(2)}, u32[]{:S(2)}) collective-permute-start(bf16[512,256]{0,1:T(8,128)(2,1)S(1)} %fusion.76), channel_id=1, source_target_pairs={{1,0},{2,1},{3,2},{4,3},{5,4},{6,5},{7,6},{8,7},{9,8},{10,9},{11,1... | collective-permute-start | bytes 786440 | tf_op jit(solution)/shard_map/ppermute | solution.py:13
  71.7 1.5 %collective-permute-start.24 = (bf16[512,256]{1,0:T(8,128)(2,1)S(1)}, bf16[512,256]{1,0:T(8,128)(2,1)S(1)}, u32[]{:S(2)}, u32[]{:S(2)}) collective-permute-start(bf16[512,256]{1,0:T(8,128)(2,1)S(1)} %get-tuple-element.47), channel_id=1, source_target_pairs={{0,1},{1,0},{2,3},{3,2},{4,5},{5,4},{6,7},{7,6},{8,9},{9,8},{10,11... | collective-permute-start | bytes 786440 | tf_op jit(solution)/shard_map/ppermute | solution.py:18
  76.8 8.7 %collective-permute-start.26 = (bf16[512,256]{0,1:T(8,128)(2,1)S(1)}, bf16[512,256]{0,1:T(8,128)(2,1)S(1)}, u32[]{:S(2)}, u32[]{:S(2)}) collective-permute-start(bf16[512,256]{0,1:T(8,128)(2,1)S(1)} %get-tuple-element.36), channel_id=1, source_target_pairs={{15,0},{0,1},{1,2},{2,3},{3,4},{4,5},{5,6},{6,7},{7,8},{8,9},{9,10... | collective-permute-start | bytes 786440 | tf_op jit(solution)/shard_map/ppermute | solution.py:13
  87.6 3.6 %collective-permute-start.41 = (f32[4,256]{1,0:T(4,128)S(1)}, f32[4,256]{1,0:T(4,128)S(1)}, u32[]{:S(2)}, u32[]{:S(2)}) collective-permute-start(f32[4,256]{1,0:T(4,128)S(1)} %pad_maximum_fusion.9), channel_id=1, source_target_pairs={{1,0},{2,1},{3,2},{4,3},{5,4},{6,5},{7,6},{8,7},{9,8},{10,9},{11,1... | collective-permute-start | bytes 12296 | tf_op jit(solution)/shard_map/ppermute | solution.py:13
  87.7 5.6 %collective-permute-start.40 = (f32[4,256]{1,0:T(4,128)S(1)}, f32[4,256]{1,0:T(4,128)S(1)}, u32[]{:S(2)}, u32[]{:S(2)}) collective-permute-start(f32[4,256]{1,0:T(4,128)S(1)} %pad_maximum_fusion.9), channel_id=1, source_target_pairs={{2,0},{3,1},{4,2},{5,3},{6,4},{7,5},{8,6},{9,7},{10,8},{11,9},{12,... | collective-permute-start | bytes 12296 | tf_op jit(solution)/shard_map/ppermute | solution.py:13
  88.9 5.0 %collective-permute-start.39 = (f32[4,256]{1,0:T(4,128)S(1)}, f32[4,256]{1,0:T(4,128)S(1)}, u32[]{:S(2)}, u32[]{:S(2)}) collective-permute-start(f32[4,256]{1,0:T(4,128)S(1)} %pad_maximum_fusion.9), channel_id=1, source_target_pairs={{3,0},{4,1},{5,2},{6,3},{7,4},{8,5},{9,6},{10,7},{11,8},{12,9},{13... | collective-permute-start | bytes 12296 | tf_op jit(solution)/shard_map/ppermute | solution.py:13
  88.9 6.2 %collective-permute-start.38 = (f32[4,256]{1,0:T(4,128)S(1)}, f32[4,256]{1,0:T(4,128)S(1)}, u32[]{:S(2)}, u32[]{:S(2)}) collective-permute-start(f32[4,256]{1,0:T(4,128)S(1)} %pad_maximum_fusion.9), channel_id=1, source_target_pairs={{4,0},{5,1},{6,2},{7,3},{8,4},{9,5},{10,6},{11,7},{12,8},{13,9},{1... | collective-permute-start | bytes 12296 | tf_op jit(solution)/shard_map/ppermute | solution.py:13
  91.2 6.1 %collective-permute-start.37 = (f32[4,256]{1,0:T(4,128)S(1)}, f32[4,256]{1,0:T(4,128)S(1)}, u32[]{:S(2)}, u32[]{:S(2)}) collective-permute-start(f32[4,256]{1,0:T(4,128)S(1)} %pad_maximum_fusion.9), channel_id=1, source_target_pairs={{5,0},{6,1},{7,2},{8,3},{9,4},{10,5},{11,6},{12,7},{13,8},{14,9},{... | collective-permute-start | bytes 12296 | tf_op jit(solution)/shard_map/ppermute | solution.py:13
  91.3 8.0 %collective-permute-start.36 = (f32[4,256]{1,0:T(4,128)S(1)}, f32[4,256]{1,0:T(4,128)S(1)}, u32[]{:S(2)}, u32[]{:S(2)}) collective-permute-start(f32[4,256]{1,0:T(4,128)S(1)} %pad_maximum_fusion.9), channel_id=1, source_target_pairs={{6,0},{7,1},{8,2},{9,3},{10,4},{11,5},{12,6},{13,7},{14,8},{15,9},... | collective-permute-start | bytes 12296 | tf_op jit(solution)/shard_map/ppermute | solution.py:13
  93.3 6.5 %collective-permute-start.35 = (f32[4,256]{1,0:T(4,128)S(1)}, f32[4,256]{1,0:T(4,128)S(1)}, u32[]{:S(2)}, u32[]{:S(2)}) collective-permute-start(f32[4,256]{1,0:T(4,128)S(1)} %pad_maximum_fusion.9), channel_id=1, source_target_pairs={{7,0},{8,1},{9,2},{10,3},{11,4},{12,5},{13,6},{14,7},{15,8},{0,9},... | collective-permute-start | bytes 12296 | tf_op jit(solution)/shard_map/ppermute | solution.py:13
  93.9 8.0 %collective-permute-start.34 = (f32[4,256]{1,0:T(4,128)S(1)}, f32[4,256]{1,0:T(4,128)S(1)}, u32[]{:S(2)}, u32[]{:S(2)}) collective-permute-start(f32[4,256]{1,0:T(4,128)S(1)} %pad_maximum_fusion.9), channel_id=1, source_target_pairs={{8,0},{9,1},{10,2},{11,3},{12,4},{13,5},{14,6},{15,7},{0,8},{1,9},... | collective-permute-start | bytes 12296 | tf_op jit(solution)/shard_map/ppermute | solution.py:13
  95.1 8.9 %collective-permute-start.33 = (f32[4,256]{1,0:T(4,128)S(1)}, f32[4,256]{1,0:T(4,128)S(1)}, u32[]{:S(2)}, u32[]{:S(2)}) collective-permute-start(f32[4,256]{1,0:T(4,128)S(1)} %pad_maximum_fusion.9), channel_id=1, source_target_pairs={{9,0},{10,1},{11,2},{12,3},{13,4},{14,5},{15,6},{0,7},{1,8},{2,9},... | collective-permute-start | bytes 12296 | tf_op jit(solution)/shard_map/ppermute | solution.py:13
  97.3 7.5 %collective-permute-start.32 = (f32[4,256]{1,0:T(4,128)S(1)}, f32[4,256]{1,0:T(4,128)S(1)}, u32[]{:S(2)}, u32[]{:S(2)}) collective-permute-start(f32[4,256]{1,0:T(4,128)S(1)} %pad_maximum_fusion.9), channel_id=1, source_target_pairs={{10,0},{11,1},{12,2},{13,3},{14,4},{15,5},{0,6},{1,7},{2,8},{3,9},... | collective-permute-start | bytes 12296 | tf_op jit(solution)/shard_map/ppermute | solution.py:13
  99.2 5.7 %collective-permute-start.31 = (f32[4,256]{1,0:T(4,128)S(1)}, f32[4,256]{1,0:T(4,128)S(1)}, u32[]{:S(2)}, u32[]{:S(2)}) collective-permute-start(f32[4,256]{1,0:T(4,128)S(1)} %pad_maximum_fusion.9), channel_id=1, source_target_pairs={{11,0},{12,1},{13,2},{14,3},{15,4},{0,5},{1,6},{2,7},{3,8},{4,9},{... | collective-permute-start | bytes 12296 | tf_op jit(solution)/shard_map/ppermute | solution.py:13
  99.8 9.5 %collective-permute-start.30 = (f32[4,256]{1,0:T(4,128)S(1)}, f32[4,256]{1,0:T(4,128)S(1)}, u32[]{:S(2)}, u32[]{:S(2)}) collective-permute-start(f32[4,256]{1,0:T(4,128)S(1)} %pad_maximum_fusion.9), channel_id=1, source_target_pairs={{12,0},{13,1},{14,2},{15,3},{0,4},{1,5},{2,6},{3,7},{4,8},{5,9},{6... | collective-permute-start | bytes 12296 | tf_op jit(solution)/shard_map/ppermute | solution.py:13
  101.9 7.5 %collective-permute-start.29 = (f32[4,256]{1,0:T(4,128)S(1)}, f32[4,256]{1,0:T(4,128)S(1)}, u32[]{:S(2)}, u32[]{:S(2)}) collective-permute-start(f32[4,256]{1,0:T(4,128)S(1)} %pad_maximum_fusion.9), channel_id=1, source_target_pairs={{13,0},{14,1},{15,2},{0,3},{1,4},{2,5},{3,6},{4,7},{5,8},{6,9},{7,... | collective-permute-start | bytes 12296 | tf_op jit(solution)/shard_map/ppermute | solution.py:13
  104.0 6.4 %collective-permute-start.28 = (f32[4,256]{1,0:T(4,128)S(1)}, f32[4,256]{1,0:T(4,128)S(1)}, u32[]{:S(2)}, u32[]{:S(2)}) collective-permute-start(f32[4,256]{1,0:T(4,128)S(1)} %pad_maximum_fusion.9), channel_id=1, source_target_pairs={{14,0},{15,1},{0,2},{1,3},{2,4},{3,5},{4,6},{5,7},{6,8},{7,9},{8,1... | collective-permute-start | bytes 12296 | tf_op jit(solution)/shard_map/ppermute | solution.py:13
  104.8 5.7 %collective-permute-start.27 = (f32[4,256]{1,0:T(4,128)S(1)}, f32[4,256]{1,0:T(4,128)S(1)}, u32[]{:S(2)}, u32[]{:S(2)}) collective-permute-start(f32[4,256]{1,0:T(4,128)S(1)} %pad_maximum_fusion.9), channel_id=1, source_target_pairs={{15,0},{0,1},{1,2},{2,3},{3,4},{4,5},{5,6},{6,7},{7,8},{8,9},{9,10... | collective-permute-start | bytes 12296 | tf_op jit(solution)/shard_map/ppermute | solution.py:13
  104.9 8.4 %collective-permute-start.42 = (bf16[512,256]{0,1:T(8,128)(2,1)S(1)}, bf16[512,256]{0,1:T(8,128)(2,1)S(1)}, u32[]{:S(2)}, u32[]{:S(2)}) collective-permute-start(bf16[512,256]{0,1:T(8,128)(2,1)S(1)} %slice.312), channel_id=1, source_target_pairs={{1,0},{2,1},{3,2},{4,3},{5,4},{6,5},{7,6},{8,7},{9,8},{10,9},{11,1... | collective-permute-start | bytes 786440 | tf_op jit(solution)/shard_map/ppermute | solution.py:13

commit v2 on v1

--- a/solution.py
+++ b/solution.py
@@ -13,39 +13,34 @@
     return lax.ppermute(block, AXIS, [((i - distance) % n, i) for i in range(n)])
 
 
-def partner_block(block):
+def from_all(block):
     n = lax.axis_size(AXIS)
-    return lax.ppermute(block, AXIS, [(i, i ^ 1) for i in range(n)])
+    return lax.all_to_all(jnp.broadcast_to(block[None], (n,) + block.shape), AXIS, 0, 0)
 
 
-def gather_relative(block):
-    n = lax.axis_size(AXIS)
-    if n % 2:
-        return jnp.concatenate([block] + [shifted(block, k) for k in range(1, n)], axis=0)
-    same = jnp.concatenate([block] + [shifted(block, 2 * k) for k in range(1, n // 2)], axis=0)
-    return jnp.concatenate([same, partner_block(same)], axis=0)
+def exact_parts(x):
+    high = lax.reduce_precision(x, 8, 7)
+    middle = lax.reduce_precision(x - high, 8, 7)
+    return [part.astype(BF16) for part in (high, middle, x - high - middle)]
 
 
-def relative_columns(rows):
-    n = lax.axis_size(AXIS)
-    me = lax.axis_index(AXIS)
-    count, width = rows.shape[0], rows.shape[1] // n
-    group = 1 if n % 2 else 2
-    pairs = rows.reshape(count, n // group, group, width)[:, ::-1]
-    first = n // group - 1 - me // group
-    doubled = jnp.concatenate([pairs, pairs], axis=1)
-    turned = lax.dynamic_slice_in_dim(doubled, first, n // group, axis=1)
-    if group == 2:
-        turned = jnp.where(me % 2 == 0, turned, turned[:, :, ::-1])
-    return turned.transpose(0, 2, 1, 3).reshape(count, n * width)
-
-
-def sum_all(block):
-    n = lax.axis_size(AXIS)
-    total = block
-    for k in range(1, n):
-        total = total + shifted(block, k)
-    return total
+def halo(load, weight, rows, inverse):
+    columns = load.shape[1]
+    pieces = [load]
+    for array in [rows, inverse] + exact_parts(weight):
+        pieces += [array[:, k : k + columns] for k in range(0, array.shape[1], columns)]
+    heights = [piece.shape[0] for piece in pieces]
+    got = shifted(jnp.concatenate(pieces, axis=0), 1)
+    parts, at = [], 0
+    for height in heights:
+        parts.append(got[at : at + height])
+        at += height
+    results, at = [], 1
+    for array in [rows, inverse, weight, weight, weight]:
+        count = array.shape[1] // columns
+        results.append(jnp.concatenate(parts[at : at + count], axis=1))
+        at += count
+    return parts[0], results[0], results[1], sum(part.astype(F32) for part in results[2:])
 
 
 def dot(a, b):
@@ -82,12 +77,14 @@
     own_rows = [constraint[j * ncf : (j + 1) * ncf] for j in range(subs)]
 
     coarse = jnp.concatenate([dot(own_rows[j], load[j].astype(BF16)) for j in range(subs)], axis=0).astype(BF16)
+    coarse_all = from_all(coarse).reshape(-1, columns)
     weight = [face_weight[j].reshape(nf, 1) for j in range(subs)]
-    halo_source = shifted(((1.0 - weight[-1]) * load[-1]).astype(BF16), 1)
-    coarse_all = gather_relative(coarse)
-    weight = [shifted(face_weight[-1:], 1).reshape(nf, 1)] + weight
-    rows = [shifted(own_rows[-1], 1)] + own_rows
-    inverse = relative_columns(jnp.concatenate([shifted(coarse_inverse[-ncf:], 1), coarse_inverse], axis=0))
+    halo_source, halo_rows, halo_inverse, halo_weight = halo(
+        ((1.0 - weight[-1]) * load[-1]).astype(BF16), face_weight[-1:], own_rows[-1], coarse_inverse[-ncf:]
+    )
+    weight = [halo_weight.reshape(nf, 1)] + weight
+    rows = [halo_rows] + own_rows
+    inverse = jnp.concatenate([halo_inverse, coarse_inverse], axis=0)
 
     def neumann_halves(left, right):
         first, second = [], []
@@ -126,14 +123,14 @@
     coarse_back = shifted(split_dot(rows[0], first[0]), -1)
     parts = [split_dot(rows[j], second[j - 1] + first[j]) for j in range(1, subs)]
     parts.append(split_dot(rows[subs], second[-1]) + coarse_back)
-    coarse_all = gather_relative(jnp.concatenate(parts, axis=0).astype(BF16))
+    coarse_all = from_all(jnp.concatenate(parts, axis=0).astype(BF16)).reshape(-1, columns)
     image = exchange(first, second)
     left = [((1.0 - weight[j]) * image[j]).astype(BF16) for j in range(subs)]
     right = [(weight[j + 1] * image[j + 1]).astype(BF16) for j in range(subs)]
     y = add_coarse(exchange(*neumann_halves(left, right)), coarse_all)
     first, second = schur_halves(y)
     image_y, y_image = inner(image[1:], y[1:]), energy(y, first, second)
-    a, b, c, d = sum_all(jnp.stack([load_z, z_image, image_y, y_image], axis=0))
+    a, b, c, d = jnp.sum(from_all(jnp.stack([load_z, z_image, image_y, y_image], axis=0)), axis=0)
     image_y_faces = exchange(first, second)[1:]
 
     step = a / b

time: 117 us -> 119 us (1.017)
  starting transfers between devices: 48.2 us -> 26.3 us
  waiting for transfers between devices: 33.8 us -> 41.9 us
  other arithmetic: 4.14 us -> 10.6 us
  matrix products: 18.7 us -> 24.9 us
  local copies, waits for them, and re-layouts: 10.3 us -> 12.8 us
    ppermute x41 -> x9, starting transfers between devices: 47.3 us -> 9.38 us  [shifted(): lax.ppermute(block, AXIS, [((i - distance) % n, i) for i in range(n)])]
    all_to_all x0 -> x3, starting transfers between devices: none -> 16.9 us  [from_all(): lax.all_to_all(jnp.broadcast_to(block[None], (n,) + block.shape), AXIS, 0...]
    dot_general x34, matrix products: 18.7 us -> 24.9 us  [dot(): return jnp.dot(a, b, preferred_element_type=F32)]
    all_to_all x0 -> x3, waiting for transfers between devices: none -> 4.83 us  [from_all(): lax.all_to_all(jnp.broadcast_to(block[None], (n,) + block.shape), AXIS, 0...]
    ppermute x41 -> x9, waiting for transfers between devices: 33 us -> 37.1 us  [shifted(): lax.ppermute(block, AXIS, [((i - distance) % n, i) for i in range(n)])]
    add x1, other arithmetic: 0.49 us -> 3.34 us  [shards(): load[j] - s * image[j + 1] + t * image_y_faces[j]]
    broadcast_in_dim x0 -> x3, local copies, waits for them, and re-layouts: none -> 2.35 us  [from_all(): jnp.broadcast_to(block[None], (n,) + block.shape)]
    slice x2, local copies, waits for them, and re-layouts: 0.07 us -> 1.8 us  [schur_halves(): first.append(product[:nf])]
  transfers between devices with their start and end apart: 43 -> 12, of which waited for: 15 -> 8; matrix products, arithmetic and copies ran while one was open for 18% -> 23% of each run, Pallas kernels for 0% -> 0%
where the time goes in v2:
time: 119 us; the launch traced here: 118 us
  waiting for transfers between devices  41.9 us (35%)
  starting transfers between devices  26.3 us (22%)
  matrix products  24.9 us (21%)
  local copies, waits for them, and re-layouts  12.8 us (11%)
  other arithmetic  10.6 us (9%)
  between operations  1.45 us (1%)
    ppermute x9, waiting for transfers between devices, shifted(): lax.ppermute(block, AXIS, [((i - distance) % n, i) for i in range(n)])  37.1 us
    dot_general x34, matrix products, dot(): return jnp.dot(a, b, preferred_element_type=F32)  24.9 us
    all_to_all x3, starting transfers between devices, from_all(): lax.all_to_all(jnp.broadcast_to(block[None], (n,) + block.shape), AXIS, 0...  16.9 us
    ppermute x9, starting transfers between devices, shifted(): lax.ppermute(block, AXIS, [((i - distance) % n, i) for i in range(n)])  9.38 us
    unnamed x65, local copies, waits for them, and re-layouts  5.79 us
    all_to_all x3, waiting for transfers between devices, from_all(): lax.all_to_all(jnp.broadcast_to(block[None], (n,) + block.shape), AXIS, 0...  4.83 us
    add x1, other arithmetic, shards(): load[j] - s * image[j + 1] + t * image_y_faces[j]  3.34 us
  transfers between devices with their start and end apart: 12, of which 8 were waited for; matrix products, arithmetic and copies ran while one was open for 23% of the time, Pallas kernels for 0%

profile of v2, /device:TPU:0, one launch (start us, length us, event | category | flops | bytes accessed | tf_op | source)
XLA Modules:
  0.0 118.0 jit_solution(14643359293834026267)
XLA Ops:
  0.7 1.3 %fusion.134 = (f32[512,256]{1,0:T(8,128)S(1)}, f32[512,256]{1,0:T(8,128)S(1)}) fusion(f32[1024,256]{1,0:T(8,128)} %param.6), kind=kLoop, calls=%fused_computation.224 | loop fusion | bytes 2097152 | tf_op jit(solution)/shard_map/slice | solution.py:76
  2.8 0.8 broadcast_in_dim.6
  3.6 7.4 %all-to-all-start = ((bf16[16,64,256]{2,1,0:T(8,128)(2,1)}), bf16[16,64,256]{2,1,0:T(8,128)(2,1)S(1)}, u32[]{:S(2)}, u32[]{:S(2)}) async-start(bf16[16,64,256]{2,1,0:T(8,128)(2,1)} %broadcast_in_dim.6), calls=%async_computation | async-start | bytes 1048576 | tf_op jit(solution)/shard_map/all_to_all | solution.py:18
  12.2 0.5 concatenate.100
  12.7 0.5 collective-permute-start
  13.1 0.8 multiply_convert_fusion.6
  13.9 3.3 %fusion.14 = f32[1024,256]{0,1:T(8,128)} fusion(bf16[2048,1024]{1,0:T(8,128)(2,1)} %param.9, bf16[512,256]{0,1:T(8,128)(2,1)S(1)} %get-tuple-element.55, bf16[512,256]{0,1:T(8,128)(2,1)S(1)} %get-tuple-element.54), kind=kOutput, calls=%fused_computation.18 | convolution fusion | flops 537919488 | bytes 3670016 | tf_op jit(solution)/shard_map/dot_general | solution.py:47
  17.2 12.5 %collective-permute-done = bf16[710,256]{0,1:T(8,128)(2,1)S(1)} collective-permute-done((bf16[710,256]{0,1:T(8,128)(2,1)S(1)}, bf16[710,256]{0,1:T(8,128)(2,1)S(1)}, u32[]{:S(2)}, u32[]{:S(2)}) %collective-permute-start) | collective-permute-done | bytes 363552 | tf_op jit(solution)/shard_map/ppermute | solution.py:13
  30.2 0.3 slice_reduce_fusion.1
  30.6 2.4 %fusion.8 = f32[1024,256]{0,1:T(8,128)S(1)} fusion(bf16[2048,1024]{1,0:T(8,128)(2,1)} %param.9, bf16[512,256]{0,1:T(8,128)(2,1)} %get-tuple-element.53, bf16[512,256]{0,1:T(8,128)(2,1)S(1)} %slice.242), kind=kOutput, calls=%fused_computation.16 | convolution fusion | flops 537919488 | bytes 3670016 | tf_op jit(solution)/shard_map/dot_general | solution.py:47
  33.0 0.8 fusion.73
  34.6 1.6 %fusion.40 = f32[512,256]{0,1:T(8,128)S(1)} fusion(f32[256,512]{1,0:T(8,128)S(1)} %fusion.99, f32[1024,256]{0,1:T(8,128)} %fusion.14, f32[1024,256]{0,1:T(8,128)S(1)} %fusion.8, f32[512]{0:T(512)S(1)} %broadcast_subtract_fusion, f32[512]{0:T(512)S(1)} %bitcast.56, f32[96,256]{1,0:T(8,128)S(1)} %fusion.132, bf16[64,512]{1,0:T(8,128)(2,1)S(1)} %copy-done.7), kind=kOutput, calls=%fused_computation.50 | convolution fusion | flops 9068544 | bytes 2166784 | tf_op jit(solution)/shard_map/dot_general | solution.py:47
  36.7 1.4 %collective-permute-done.1 = bf16[512,256]{0,1:T(8,128)(2,1)} collective-permute-done((bf16[512,256]{0,1:T(8,128)(2,1)}, bf16[512,256]{0,1:T(8,128)(2,1)}, u32[]{:S(2)}, u32[]{:S(2)}) %collective-permute-start.1) | collective-permute-done | bytes 262176 | tf_op jit(solution)/shard_map/ppermute | solution.py:13
  38.1 1.3 %add_add_fusion.3 = (f32[512,256]{0,1:T(8,128)S(1)}, bf16[512,256]{0,1:T(8,128)(2,1)S(1)}) fusion(f32[512,256]{0,1:T(8,128)S(1)} %fusion.38, bf16[512,256]{0,1:T(8,128)(2,1)} %collective-permute-done.1, f32[1024,256]{0,1:T(8,128)} %fusion.14, f32[512]{0:T(512)S(1)} %bitcast.51), kind=kLoop, calls=%fused_computation.126 | loop fusion | flops 655360 | bytes 2099200 | tf_op jit(solution)/shard_map/add | solution.py:99
  39.4 0.8 fusion.28
  40.2 0.8 fusion.22
  41.4 6.8 %collective-permute-done.2 = bf16[512,256]{0,1:T(8,128)(2,1)S(1)} collective-permute-done((bf16[512,256]{0,1:T(8,128)(2,1)S(1)}, bf16[512,256]{0,1:T(8,128)(2,1)S(1)}, u32[]{:S(2)}, u32[]{:S(2)}) %collective-permute-start.2) | collective-permute-done | bytes 262176 | tf_op jit(solution)/shard_map/ppermute | solution.py:13
  48.5 0.8 fusion.34
  49.3 0.8 fusion.23
  50.7 3.8 %collective-permute-done.5 = f32[32,256]{1,0:T(8,128)S(1)} collective-permute-done((f32[32,256]{1,0:T(8,128)S(1)}, f32[32,256]{1,0:T(8,128)S(1)}, u32[]{:S(2)}, u32[]{:S(2)}) %collective-permute-start.5) | collective-permute-done | bytes 32800 | tf_op jit(solution)/shard_map/ppermute | solution.py:13
  54.8 1.1 multiply_convert_fusion.1
  56.2 0.9 broadcast_in_dim.7
  57.1 6.0 %all-to-all-start.1 = ((bf16[16,64,256]{2,1,0:T(8,128)(2,1)}), bf16[16,64,256]{2,1,0:T(8,128)(2,1)}, u32[]{:S(2)}, u32[]{:S(2)}) async-start(bf16[16,64,256]{2,1,0:T(8,128)(2,1)} %broadcast_in_dim.7), calls=%async_computation.1 | async-start | bytes 1048576 | tf_op jit(solution)/shard_map/all_to_all | solution.py:18
  63.2 2.6 %fusion.11 = f32[1024,256]{0,1:T(8,128)S(1)} fusion(bf16[2048,1024]{1,0:T(8,128)(2,1)} %param.9, bf16[512,256]{0,1:T(8,128)(2,1)S(1)} %multiply_convert_fusion.2, bf16[512,256]{0,1:T(8,128)(2,1)} %get-tuple-element.50), kind=kOutput, calls=%fused_computation.17 | convolution fusion | flops 537919488 | bytes 3670016 | tf_op jit(solution)/shard_map/dot_general | solution.py:47
  65.8 1.0 copy-done.9
  66.8 0.8 fusion.75
  67.5 4.3 %collective-permute-start.6 = (bf16[512,256]{0,1:T(8,128)(2,1)}, bf16[512,256]{0,1:T(8,128)(2,1)}, u32[]{:S(2)}, u32[]{:S(2)}) collective-permute-start(bf16[512,256]{0,1:T(8,128)(2,1)} %fusion.75), channel_id=1, source_target_pairs={{1,0},{2,1},{3,2},{4,3},{5,4},{6,5},{7,6},{8,7},{9,8},{10,9},{11,1... | collective-permute-start | bytes 786440 | tf_op jit(solution)/shard_map/ppermute | solution.py:13
  71.9 1.7 %fusion.17 = f32[1024,256]{0,1:T(8,128)} fusion(bf16[2048,1024]{1,0:T(8,128)(2,1)S(1)} %copy-done.24, bf16[512,256]{0,1:T(8,128)(2,1)S(1)} %copy-done.19, bf16[512,256]{0,1:T(8,128)(2,1)S(1)} %copy-done.18), kind=kOutput, calls=%fused_computation.19 | convolution fusion | flops 537919488 | bytes 3670016 | tf_op jit(solution)/shard_map/dot_general | solution.py:47
  73.6 4.1 %all-to-all-done.1 = bf16[16,64,256]{2,1,0:T(8,128)(2,1)} async-done(((bf16[16,64,256]{2,1,0:T(8,128)(2,1)}), bf16[16,64,256]{2,1,0:T(8,128)(2,1)}, u32[]{:S(2)}, u32[]{:S(2)}) %all-to-all-start.1) | async-done | bytes 524320 | tf_op jit(solution)/shard_map/all_to_all | solution.py:18
  77.6 1.5 %fusion.131 = f32[96,256]{1,0:T(8,128)S(1)} fusion(bf16[1024,256]{1,0:T(8,128)(2,1)} %bitcast.14, bf16[64,1024]{1,0:T(8,128)(2,1)} %param.11, bf16[32,256]{1,0:T(8,128)(2,1)S(1)} %copy.94, bf16[32,256]{1,0:T(8,128)(2,1)S(1)} %copy.93, bf16[32,256]{1,0:T(8,128)(2,1)} %copy-done.21, bf16[32,256]{1,0:T(8,128)(2,1)} %copy-done.22), kind=kOutput, calls=%fused_computation.222 | convolution fusion | flops 51314688 | bytes 819200 | tf_op jit(solution)/shard_map/dot_general | solution.py:47
  79.4 1.5 %fusion.41 = f32[512,256]{0,1:T(8,128)S(1)} fusion(f32[256,512]{1,0:T(8,128)S(1)} %fusion.101, f32[1024,256]{0,1:T(8,128)} %fusion.17, f32[1024,256]{0,1:T(8,128)} %copy-done.9, f32[512]{0:T(512)S(1)} %broadcast_subtract_fusion, f32[512]{0:T(512)S(1)} %bitcast.58, f32[96,256]{1,0:T(8,128)S(1)} %fusion.131, bf16[64,512]{1,0:T(8,128)(2,1)S(1)} %copy-done.7), kind=kOutput, calls=%fused_computation.51 | convolution fusion | flops 9068544 | bytes 2166784 | tf_op jit(solution)/shard_map/dot_general | solution.py:47
  81.5 1.7 %multiply_reduce_fusion.8 = (f32[256]{0:T(256)S(1)}, f32[256]{0:T(256)S(1)}, f32[256]{0:T(256)S(1)}, f32[256]{0:T(256)S(1)}, f32[256]{0:T(256)S(1)}, /*index=5*/...) fusion(f32[512,256]{0,1:T(8,128)S(1)} %copy-done.3, ...), kind=kLoop, calls=%fused_computation.122 | loop fusion | flops 2750720 | bytes 7087104 | tf_op jit(solution)/shard_map/reduce_sum | solution.py:112
  83.4 0.7 fusion.25
  84.2 0.8 fusion.20
  85.3 9.2 %collective-permute-done.7 = bf16[512,256]{0,1:T(8,128)(2,1)S(1)} collective-permute-done((bf16[512,256]{0,1:T(8,128)(2,1)S(1)}, bf16[512,256]{0,1:T(8,128)(2,1)S(1)}, u32[]{:S(2)}, u32[]{:S(2)}) %collective-permute-start.7) | collective-permute-done | bytes 262176 | tf_op jit(solution)/shard_map/ppermute | solution.py:13
  94.8 0.8 fusion.31
  95.6 0.8 fusion.21
  96.4 0.4 multiply_reduce_fusion.2
  96.7 0.6 copy-done.8
  97.4 0.6 broadcast_in_dim.8
  98.0 3.5 %all-to-all-start.2 = ((f32[16,4,256]{2,1,0:T(4,128)}), f32[16,4,256]{2,1,0:T(4,128)S(1)}, u32[]{:S(2)}, u32[]{:S(2)}) async-start(f32[16,4,256]{2,1,0:T(4,128)} %broadcast_in_dim.8), calls=%async_computation.2 | async-start | bytes 131072 | tf_op jit(solution)/shard_map/all_to_all | solution.py:18
  101.5 1.8 %slice.439 = bf16[512,256]{0,1:T(8,128)(2,1)} slice(f32[1024,256]{0,1:T(8,128)} %copy-done.8), slice={[0:512], [0:256]} | slice | bytes 524288 | tf_op jit(solution)/shard_map/slice | solution.py:105
  103.3 4.3 %collective-permute-start.8 = (bf16[512,256]{0,1:T(8,128)(2,1)}, bf16[512,256]{0,1:T(8,128)(2,1)}, u32[]{:S(2)}, u32[]{:S(2)}) collective-permute-start(bf16[512,256]{0,1:T(8,128)(2,1)} %slice.439), channel_id=1, source_target_pairs={{1,0},{2,1},{3,2},{4,3},{5,4},{6,5},{7,6},{8,7},{9,8},{10,9},{11,1... | collective-permute-start | bytes 786440 | tf_op jit(solution)/shard_map/ppermute | solution.py:13
  107.6 0.8 all-to-all-done.2
  108.4 3.4 %collective-permute-done.8 = bf16[512,256]{0,1:T(8,128)(2,1)} collective-permute-done((bf16[512,256]{0,1:T(8,128)(2,1)}, bf16[512,256]{0,1:T(8,128)(2,1)}, u32[]{:S(2)}, u32[]{:S(2)}) %collective-permute-start.8) | collective-permute-done | bytes 262176 | tf_op jit(solution)/shard_map/ppermute | solution.py:13
  111.8 3.3 %multiply_add_fusion.1 = (f32[512,256]{0,1:T(8,128)}, f32[512,256]{0,1:T(8,128)}, f32[512,256]{0,1:T(8,128)S(1)}, f32[512,256]{0,1:T(8,128)S(1)}) fusion(f32[512,256]{0,1:T(8,128)S(1)} %copy.109, f32[512,256]{0,1:T(8,128)S(1)} %get-tuple-element.43, f32[1024,256]{0,1:T(8,128)} %copy-done.6, f32[1024,256]{0,1:T(8,128)} %copy-done.8, f32[256]{0:T(256)S(1)} %bitcast.60, ...), kind=kLoop, calls=%fused_computation.104 | loop fusion | flops 2490368 | bytes 8390656 | tf_op jit(solution)/shard_map/add | solution.py:142
  115.2 1.3 %copy.102 = f32[1024,256]{1,0:T(8,128)} copy(f32[1024,256]{0,1:T(8,128)S(1)} %pad_maximum_fusion.4) | data formatting | bytes 2097152
  116.7 1.3 %copy.103 = f32[1024,256]{1,0:T(8,128)} copy(f32[1024,256]{0,1:T(8,128)S(1)} %pad_maximum_fusion.5) | data formatting | bytes 2097152
  (123 shorter events, 7.4 us)
Async XLA Ops:
  0.6 1.8 %copy-start.7 = (bf16[64,512]{1,0:T(8,128)(2,1)S(1)}, bf16[64,512]{1,0:T(8,128)(2,1)}, u32[]{:S(2)}) copy-start(bf16[64,512]{1,0:T(8,128)(2,1)} %param.10) | copy-start | bytes 196612
  0.6 10.4 %copy-start.23 = (f32[2,512]{1,0:T(2,128)S(1)}, f32[2,512]{1,0:T(2,128)}, u32[]{:S(2)}) copy-start(f32[2,512]{1,0:T(2,128)} %param.7) | copy-start | bytes 12292
  0.6 10.9 %copy-start.20 = (bf16[64,1024]{1,0:T(8,128)(2,1)S(1)}, bf16[64,1024]{1,0:T(8,128)(2,1)}, u32[]{:S(2)}) copy-start(bf16[64,1024]{1,0:T(8,128)(2,1)} %param.11) | copy-start | bytes 393220
  3.6 30.4 %all-to-all-start = ((bf16[16,64,256]{2,1,0:T(8,128)(2,1)}), bf16[16,64,256]{2,1,0:T(8,128)(2,1)S(1)}, u32[]{:S(2)}, u32[]{:S(2)}) async-start(bf16[16,64,256]{2,1,0:T(8,128)(2,1)} %broadcast_in_dim.6), calls=%async_computation | async-start | bytes 1048576 | tf_op jit(solution)/shard_map/all_to_all | solution.py:18
  12.7 17.0 %collective-permute-start = (bf16[710,256]{0,1:T(8,128)(2,1)S(1)}, bf16[710,256]{0,1:T(8,128)(2,1)S(1)}, u32[]{:S(2)}, u32[]{:S(2)}) collective-permute-start(bf16[710,256]{0,1:T(8,128)(2,1)S(1)} %concatenate.100), channel_id=1, source_target_pairs={{15,0},{0,1},{1,2},{2,3},{3,4},{4,5},{5,6},{6,7},{7,8},{8,9},{9,10... | collective-permute-start | bytes 1090568 | tf_op jit(solution)/shard_map/ppermute | solution.py:13
  30.1 4.5 %copy-start.21 = (bf16[32,256]{1,0:T(8,128)(2,1)}, bf16[32,256]{1,0:T(8,128)(2,1)S(1)}, u32[]{:S(2)}) copy-start(bf16[32,256]{1,0:T(8,128)(2,1)S(1)} %copy.92) | copy-start | bytes 49156
  30.2 4.4 %copy-start.22 = (bf16[32,256]{1,0:T(8,128)(2,1)}, bf16[32,256]{1,0:T(8,128)(2,1)S(1)}, u32[]{:S(2)}) copy-start(bf16[32,256]{1,0:T(8,128)(2,1)S(1)} %copy.91) | copy-start | bytes 49156
  33.0 3.6 %copy-start.11 = (f32[1024,256]{0,1:T(8,128)}, f32[1024,256]{0,1:T(8,128)S(1)}, u32[]{:S(2)}) copy-start(f32[1024,256]{0,1:T(8,128)S(1)} %fusion.8) | copy-start | bytes 3145732
  33.9 4.2 %collective-permute-start.1 = (bf16[512,256]{0,1:T(8,128)(2,1)}, bf16[512,256]{0,1:T(8,128)(2,1)}, u32[]{:S(2)}, u32[]{:S(2)}) collective-permute-start(bf16[512,256]{0,1:T(8,128)(2,1)} %fusion.73), channel_id=1, source_target_pairs={{1,0},{2,1},{3,2},{4,3},{5,4},{6,5},{7,6},{8,7},{9,8},{10,9},{11,1... | collective-permute-start | bytes 786440 | tf_op jit(solution)/shard_map/ppermute | solution.py:13
  34.0 5.4 %copy-start.25 = (bf16[2048,1024]{1,0:T(8,128)(2,1)S(1)}, bf16[2048,1024]{1,0:T(8,128)(2,1)}, u32[]{:S(2)}) copy-start(bf16[2048,1024]{1,0:T(8,128)(2,1)} %param.8) | copy-start | bytes 12582916
  36.1 13.1 %copy-start.2 = (f32[512,256]{0,1:T(8,128)}, f32[512,256]{0,1:T(8,128)S(1)}, u32[]{:S(2)}) copy-start(f32[512,256]{0,1:T(8,128)S(1)} %fusion.40) | copy-start | bytes 1572868
  39.3 8.9 %collective-permute-start.2 = (bf16[512,256]{0,1:T(8,128)(2,1)S(1)}, bf16[512,256]{0,1:T(8,128)(2,1)S(1)}, u32[]{:S(2)}, u32[]{:S(2)}) collective-permute-start(bf16[512,256]{0,1:T(8,128)(2,1)S(1)} %get-tuple-element.48), channel_id=1, source_target_pairs={{15,0},{0,1},{1,2},{2,3},{3,4},{4,5},{5,6},{6,7},{7,8},{8,9},{9,10... | collective-permute-start | bytes 786440 | tf_op jit(solution)/shard_map/ppermute | solution.py:13
  40.2 8.0 %copy-start.12 = (f32[1024,256]{0,1:T(8,128)S(1)}, f32[1024,256]{0,1:T(8,128)}, u32[]{:S(2)}) copy-start(f32[1024,256]{0,1:T(8,128)} %copy-done.11) | copy-start | bytes 3145732
  41.0 13.7 %collective-permute-start.3 = (bf16[512,256]{0,1:T(8,128)(2,1)S(1)}, bf16[512,256]{0,1:T(8,128)(2,1)S(1)}, u32[]{:S(2)}, u32[]{:S(2)}) collective-permute-start(bf16[512,256]{0,1:T(8,128)(2,1)S(1)} %slice.440), channel_id=1, source_target_pairs={{15,0},{0,1},{1,2},{2,3},{3,4},{4,5},{5,6},{6,7},{7,8},{8,9},{9,10... | collective-permute-start | bytes 786440 | tf_op jit(solution)/shard_map/ppermute | solution.py:13
  48.5 1.5 %copy-start.13 = (f32[512,256]{0,1:T(8,128)}, f32[512,256]{0,1:T(8,128)S(1)}, u32[]{:S(2)}) copy-start(f32[512,256]{0,1:T(8,128)S(1)} %add_add_fusion.2) | copy-start | bytes 1572868
  50.0 4.7 %copy-start = (f32[1024,256]{0,1:T(8,128)}, f32[1024,256]{0,1:T(8,128)S(1)}, u32[]{:S(2)}) copy-start(f32[1024,256]{0,1:T(8,128)S(1)} %fusion.23) | copy-start | bytes 3145732
  50.3 4.5 %collective-permute-start.4 = (bf16[512,256]{0,1:T(8,128)(2,1)S(1)}, bf16[512,256]{0,1:T(8,128)(2,1)S(1)}, u32[]{:S(2)}, u32[]{:S(2)}) collective-permute-start(bf16[512,256]{0,1:T(8,128)(2,1)S(1)} %slice.441), channel_id=1, source_target_pairs={{1,0},{2,1},{3,2},{4,3},{5,4},{6,5},{7,6},{8,7},{9,8},{10,9},{11,1... | collective-permute-start | bytes 786440 | tf_op jit(solution)/shard_map/ppermute | solution.py:13
  50.5 4.0 %collective-permute-start.5 = (f32[32,256]{1,0:T(8,128)S(1)}, f32[32,256]{1,0:T(8,128)S(1)}, u32[]{:S(2)}, u32[]{:S(2)}) collective-permute-start(f32[32,256]{1,0:T(8,128)S(1)} %convolution_add_fusion.10), channel_id=1, source_target_pairs={{1,0},{2,1},{3,2},{4,3},{5,4},{6,5},{7,6},{8,7},{9,8},{10,9},{11,1... | collective-permute-start | bytes 98312 | tf_op jit(solution)/shard_map/ppermute | solution.py:13
  57.1 20.6 %all-to-all-start.1 = ((bf16[16,64,256]{2,1,0:T(8,128)(2,1)}), bf16[16,64,256]{2,1,0:T(8,128)(2,1)}, u32[]{:S(2)}, u32[]{:S(2)}) async-start(bf16[16,64,256]{2,1,0:T(8,128)(2,1)} %broadcast_in_dim.7), calls=%async_computation.1 | async-start | bytes 1048576 | tf_op jit(solution)/shard_map/all_to_all | solution.py:18
  63.1 8.8 %copy-start.18 = (bf16[512,256]{0,1:T(8,128)(2,1)S(1)}, bf16[512,256]{0,1:T(8,128)(2,1)}, u32[]{:S(2)}) copy-start(bf16[512,256]{0,1:T(8,128)(2,1)} %get-tuple-element.42) | copy-start | bytes 786436
  63.1 8.7 %copy-start.19 = (bf16[512,256]{0,1:T(8,128)(2,1)S(1)}, bf16[512,256]{0,1:T(8,128)(2,1)}, u32[]{:S(2)}) copy-start(bf16[512,256]{0,1:T(8,128)(2,1)} %get-tuple-element.49) | copy-start | bytes 786436
  63.1 8.7 %copy-start.24 = (bf16[2048,1024]{1,0:T(8,128)(2,1)S(1)}, bf16[2048,1024]{1,0:T(8,128)(2,1)}, u32[]{:S(2)}) copy-start(bf16[2048,1024]{1,0:T(8,128)(2,1)} %param.9) | copy-start | bytes 12582916
  65.8 1.0 copy-start.9
  67.5 13.9 %collective-permute-start.6 = (bf16[512,256]{0,1:T(8,128)(2,1)}, bf16[512,256]{0,1:T(8,128)(2,1)}, u32[]{:S(2)}, u32[]{:S(2)}) collective-permute-start(bf16[512,256]{0,1:T(8,128)(2,1)} %fusion.75), channel_id=1, source_target_pairs={{1,0},{2,1},{3,2},{4,3},{5,4},{6,5},{7,6},{8,7},{9,8},{10,9},{11,1... | collective-permute-start | bytes 786440 | tf_op jit(solution)/shard_map/ppermute | solution.py:13
  77.6 3.8 %copy-start.1 = (f32[1024,256]{0,1:T(8,128)S(1)}, f32[1024,256]{0,1:T(8,128)}, u32[]{:S(2)}) copy-start(f32[1024,256]{0,1:T(8,128)} %copy-done) | copy-start | bytes 3145732
  77.6 3.8 %copy-start.3 = (f32[512,256]{0,1:T(8,128)S(1)}, f32[512,256]{0,1:T(8,128)}, u32[]{:S(2)}) copy-start(f32[512,256]{0,1:T(8,128)} %copy-done.2) | copy-start | bytes 1572868
  77.6 3.8 %copy-start.14 = (f32[512,256]{0,1:T(8,128)S(1)}, f32[512,256]{0,1:T(8,128)}, u32[]{:S(2)}) copy-start(f32[512,256]{0,1:T(8,128)} %copy-done.13) | copy-start | bytes 1572868
  77.6 3.8 %copy-start.17 = (f32[1024,256]{0,1:T(8,128)S(1)}, f32[1024,256]{0,1:T(8,128)}, u32[]{:S(2)}) copy-start(f32[1024,256]{0,1:T(8,128)} %fusion.17) | copy-start | bytes 3145732
  80.9 15.4 %copy-start.5 = (f32[512,256]{0,1:T(8,128)}, f32[512,256]{0,1:T(8,128)S(1)}, u32[]{:S(2)}) copy-start(f32[512,256]{0,1:T(8,128)S(1)} %fusion.41) | copy-start | bytes 1572868
  81.2 2.3 %copy-start.26 = (bf16[2048,1024]{1,0:T(8,128)(2,1)S(1)}, bf16[2048,1024]{1,0:T(8,128)(2,1)}, u32[]{:S(2)}) copy-start(bf16[2048,1024]{1,0:T(8,128)(2,1)} %param.8) | copy-start | bytes 12582916
  83.2 13.2 %copy-start.4 = (f32[512,256]{0,1:T(8,128)}, f32[512,256]{0,1:T(8,128)S(1)}, u32[]{:S(2)}) copy-start(f32[512,256]{0,1:T(8,128)S(1)} %get-tuple-element.41) | copy-start | bytes 1572868
  83.4 11.1 %copy-start.10 = (f32[1024,256]{0,1:T(8,128)S(1)}, f32[1024,256]{0,1:T(8,128)}, u32[]{:S(2)}) copy-start(f32[1024,256]{0,1:T(8,128)} %copy-done.9) | copy-start | bytes 3145732
  85.0 11.4 %copy-start.6 = (f32[1024,256]{0,1:T(8,128)}, f32[1024,256]{0,1:T(8,128)S(1)}, u32[]{:S(2)}) copy-start(f32[1024,256]{0,1:T(8,128)S(1)} %fusion.20) | copy-start | bytes 3145732
  85.0 9.5 %collective-permute-start.7 = (bf16[512,256]{0,1:T(8,128)(2,1)S(1)}, bf16[512,256]{0,1:T(8,128)(2,1)S(1)}, u32[]{:S(2)}, u32[]{:S(2)}) collective-permute-start(bf16[512,256]{0,1:T(8,128)(2,1)S(1)} %get-tuple-element.46), channel_id=1, source_target_pairs={{15,0},{0,1},{1,2},{2,3},{3,4},{4,5},{5,6},{6,7},{7,8},{8,9},{9,10... | collective-permute-start | bytes 786440 | tf_op jit(solution)/shard_map/ppermute | solution.py:13
  96.4 1.0 copy-start.8
  98.0 10.4 %all-to-all-start.2 = ((f32[16,4,256]{2,1,0:T(4,128)}), f32[16,4,256]{2,1,0:T(4,128)S(1)}, u32[]{:S(2)}, u32[]{:S(2)}) async-start(f32[16,4,256]{2,1,0:T(4,128)} %broadcast_in_dim.8), calls=%async_computation.2 | async-start | bytes 131072 | tf_op jit(solution)/shard_map/all_to_all | solution.py:18
  103.3 8.6 %collective-permute-start.8 = (bf16[512,256]{0,1:T(8,128)(2,1)}, bf16[512,256]{0,1:T(8,128)(2,1)}, u32[]{:S(2)}, u32[]{:S(2)}) collective-permute-start(bf16[512,256]{0,1:T(8,128)(2,1)} %slice.439), channel_id=1, source_target_pairs={{1,0},{2,1},{3,2},{4,3},{5,4},{6,5},{7,6},{8,7},{9,8},{10,9},{11,1... | collective-permute-start | bytes 786440 | tf_op jit(solution)/shard_map/ppermute | solution.py:13
  115.2 1.4 %copy-start.15 = (f32[512,256]{0,1:T(8,128)S(1)}, f32[512,256]{0,1:T(8,128)}, u32[]{:S(2)}) copy-start(f32[512,256]{0,1:T(8,128)} %get-tuple-element.44) | copy-start | bytes 1572868
  115.2 1.4 %copy-start.16 = (f32[512,256]{0,1:T(8,128)S(1)}, f32[512,256]{0,1:T(8,128)}, u32[]{:S(2)}) copy-start(f32[512,256]{0,1:T(8,128)} %get-tuple-element.45) | copy-start | bytes 1572868

commit v3 on v2

v3 whole, which is shorter than its diff:
```python
import functools

import jax
import jax.numpy as jnp
from jax import lax
from jax.experimental import pallas as pl
from jax.experimental.pallas import tpu as pltpu
from jax.sharding import PartitionSpec as P

AXIS = "sub"
BF16 = jnp.bfloat16
F32 = jnp.float32
LANES = 128
VMEM_BYTES = 48 * 2**20


def shifted(block, distance):
    n = lax.axis_size(AXIS)
    return lax.ppermute(block, AXIS, [((i - distance) % n, i) for i in range(n)])


def from_all(copies):
    return lax.all_to_all(copies, AXIS, 0, 0)


def dot(a, b):
    return jnp.dot(a, b, preferred_element_type=F32)


def dot_nt(a, b):
    return lax.dot_general(a, b, (((1,), (1,)), ((), ())), preferred_element_type=F32)


def dot_tn(a, b):
    return lax.dot_general(a, b, (((0,), (0,)), ((), ())), preferred_element_type=F32)


def split(x):
    high = x.astype(BF16)
    return high, (x - high.astype(F32)).astype(BF16)


def split_dot(a, b, contract=dot):
    high, low = split(b)
    if isinstance(a, tuple):
        return contract(a[0], high) + contract(a[0], low) + contract(a[1], high)
    return contract(a, high) + contract(a, low)


def column_sum(x):
    return jnp.sum(x, axis=0, keepdims=True)


def rows_of(ref, index, count):
    return ref[index * count : (index + 1) * count]


def stage(kernel, shapes, *operands):
    out = [jax.ShapeDtypeStruct(shape, dtype) for shape, dtype in shapes]
    params = pltpu.CompilerParams(vmem_limit_bytes=VMEM_BYTES)
    return pl.pallas_call(kernel, out_shape=out, compiler_params=params, name=kernel.func.__name__)(*operands)


def prepare(subs, load, weight, weight_rows, rows, inverse, copies, coarse, message):
    nf, columns = load.shape[0] // subs, load.shape[1]
    ncf = rows.shape[0] // subs
    for j in range(subs):
        coarse[j * ncf : (j + 1) * ncf] = dot(rows_of(rows, j, ncf), rows_of(load, j, nf).astype(BF16))
    rounded = coarse[...].astype(BF16)
    for k in range(copies.shape[0]):
        copies[k] = rounded
    last = slice((subs - 1) * nf, subs * nf)
    message[:nf] = ((1.0 - weight[last]) * load[last]).astype(BF16)
    at = nf
    for array in (rows, inverse):
        for k in range(0, array.shape[1], columns):
            message[at : at + ncf] = array[(subs - 1) * ncf :, k : k + columns]
            at += ncf
    message[at:] = weight_rows[...]


def neumann_products(subs, nf, left, right, weight, neumann, part, back, forward):
    previous = None
    for j in range(subs):
        product = dot(rows_of(neumann, j, 2 * nf), jnp.concatenate([left[j], right[j]], axis=0))
        first, second = product[:nf], product[nf:]
        if j == 0:
            part[:nf] = first
            back[...] = first.astype(BF16)
        else:
            own = weight(j)
            part[j * nf : (j + 1) * nf] = own * previous + (1.0 - own) * first
        previous = second
    part[subs * nf :] = previous
    forward[...] = previous.astype(BF16)


def neumann_load(subs, load, weight, halo_left, neumann, part, back, forward):
    nf = load.shape[0] // subs
    own = lambda e: rows_of(weight, e - 1, nf)
    left = [halo_left[...]] + [((1.0 - own(j)) * rows_of(load, j - 1, nf)).astype(BF16) for j in range(1, subs)]
    right = [(own(j + 1) * rows_of(load, j, nf)).astype(BF16) for j in range(subs)]
    neumann_products(subs, nf, left, right, own, neumann, part, back, forward)


def neumann_image(subs, part_in, from_next, from_previous, weight, neumann, image, part, back, forward):
    nf = part_in.shape[0] // (subs + 1)
    faces = [rows_of(part_in, e, nf) for e in range(subs + 1)]
    faces[0] = faces[0] + from_previous[...].astype(F32)
    faces[subs] = faces[subs] + from_next[...].astype(F32)
    for e in range(1, subs + 1):
        image[(e - 1) * nf : e * nf] = faces[e]
    own = lambda e: rows_of(weight, e, nf)
    left = [((1.0 - own(j)) * faces[j]).astype(BF16) for j in range(subs)]
    right = [(own(j + 1) * faces[j + 1]).astype(BF16) for j in range(subs)]
    neumann_products(subs, nf, left, right, own, neumann, part, back, forward)


def schur_products(subs, nf, other, part, from_next, from_previous, weight, schur, local, product, quadratic):
    own = lambda e: rows_of(weight, e, nf)
    local[:nf] = (1.0 - own(0)) * part[:nf] + own(0) * from_previous[...].astype(F32)
    for e in range(1, subs):
        local[e * nf : (e + 1) * nf] = rows_of(part, e, nf)
    local[subs * nf :] = own(subs) * part[subs * nf :] + (1.0 - own(subs)) * from_next[...].astype(F32)
    columns = local.shape[1]
    energy, previous = 0.0, None
    for j in range(subs):
        vector = local[j * nf : (j + 2) * nf]
        both = dot(rows_of(schur, j, 2 * nf), jnp.concatenate(split(vector), axis=1))
        result = both[:, :columns] + both[:, columns:]
        energy = energy + column_sum(vector * result)
        first = result[:nf]
        product[j * nf : (j + 1) * nf] = first if j == 0 else previous + first
        previous = result[nf:]
    product[subs * nf :] = previous
    quadratic[0:1] = energy
    quadratic[1:2] = column_sum(other[...] * local[nf:])


def schur_load(
    subs, load, part, from_next, from_previous, weight, schur, rows,
    local, product, quadratic, basis_high, basis_low, base, gram, message,
):
    nf = part.shape[0] // (subs + 1)
    ncf = rows.shape[0] // (subs + 1)
    schur_products(subs, nf, load, part, from_next, from_previous, weight, schur, local, product, quadratic)
    gram[...] = jnp.zeros_like(gram)
    for j in range(subs):
        matrix = rows_of(schur, j, 2 * nf)
        left, right = rows_of(rows, j, ncf), rows_of(rows, j + 1, ncf)
        basis = jnp.concatenate([dot(left, matrix[:nf]), dot(right, matrix[nf:])], axis=0)
        pair = split(basis)
        here = slice(2 * j * ncf, 2 * (j + 1) * ncf)
        basis_high[here], basis_low[here] = pair
        base[here] = split_dot(pair, local[j * nf : (j + 2) * nf])
        for side, block in ((0, left), (1, right)):
            half = slice(side * nf, (side + 1) * nf)
            gram[here, side * ncf : (side + 1) * ncf] = dot_nt(pair[0][:, half], block) + dot_nt(pair[1][:, half], block)
    message[:, : base.shape[1]] = base[:ncf]
    message[:, base.shape[1] :] = gram[:ncf]


def coarse_products(subs, ncf, x, base, gram):
    results, energy = [], 0.0
    for j in range(subs):
        here = slice(2 * j * ncf, 2 * (j + 1) * ncf)
        pair = jnp.concatenate([x[j], x[j + 1]], axis=0)
        change = split_dot(split(gram[here, : 2 * ncf]), pair)
        energy = energy + column_sum(pair * (2.0 * base[here] + change))
        results.append(base[here] + change)
    return results, energy


def add_basis(subs, nf, ncf, x, basis_high, basis_low, product):
    faces = [rows_of(product, e, nf) for e in range(subs + 1)]
    for j in range(subs):
        here = slice(2 * j * ncf, 2 * (j + 1) * ncf)
        pair = jnp.concatenate([x[j], x[j + 1]], axis=0)
        change = split_dot((basis_high[here], basis_low[here]), pair, dot_tn)
        faces[j] = faces[j] + change[:nf]
        faces[j + 1] = faces[j + 1] + change[nf:]
    return faces


def coarse_load(
    subs, coarse_all, inverse, halo_inverse, next_inverse, from_next, coarse, base, gram, quadratic, basis_high, basis_low, product,
    copies, image_coarse, solution, part, back, forward, sums,
):
    ncf = inverse.shape[0] // subs
    nf = product.shape[0] // (subs + 1)
    columns = coarse.shape[1]
    everything = coarse_all[...]
    own = dot(inverse[...], everything)
    x = [dot(halo_inverse[...], everything)] + [own[j * ncf : (j + 1) * ncf] for j in range(subs)]
    beyond = dot(next_inverse[...], everything)
    results, energy = coarse_products(subs, ncf, x, base, gram)
    for e in range(1, subs):
        image_coarse[(e - 1) * ncf : e * ncf] = results[e - 1][ncf:] + results[e][:ncf]
    share = from_next[:, :columns] + split_dot(
        split(from_next[:, columns : columns + 2 * ncf]), jnp.concatenate([x[subs], beyond], axis=0)
    )
    image_coarse[(subs - 1) * ncf :] = results[subs - 1][ncf:] + share
    rounded = image_coarse[...].astype(BF16)
    for k in range(copies.shape[0]):
        copies[k] = rounded
    for e in range(subs + 1):
        solution[e * ncf : (e + 1) * ncf] = x[e]
    sums[0:1] = quadratic[1:2] + column_sum(coarse[...] * own)
    sums[1:2] = quadratic[0:1] + energy
    faces = add_basis(subs, nf, ncf, x, basis_high, basis_low, product)
    for e in range(subs + 1):
        part[e * nf : (e + 1) * nf] = faces[e]
    back[...] = faces[0].astype(BF16)
    forward[...] = faces[subs].astype(BF16)


def schur_image(
    subs, image, part, from_next, from_previous, weight, schur, basis_high, basis_low, local, product, quadratic, base
):
    nf = part.shape[0] // (subs + 1)
    ncf = basis_high.shape[0] // (2 * subs)
    schur_products(subs, nf, image, part, from_next, from_previous, weight, schur, local, product, quadratic)
    for j in range(subs):
        here = slice(2 * j * ncf, 2 * (j + 1) * ncf)
        base[here] = split_dot((basis_high[here], basis_low[here]), local[j * nf : (j + 2) * nf])


def coarse_image(
    subs, coarse_all, inverse, halo_inverse, coarse, base, gram, quadratic, basis_high, basis_low, product, sums,
    copies, solution, part, back,
):
    ncf = inverse.shape[0] // subs
    nf = product.shape[0] // (subs + 1)
    everything = coarse_all[...]
    own = dot(inverse[...], everything)
    x = [dot(halo_inverse[...], everything)] + [own[j * ncf : (j + 1) * ncf] for j in range(subs)]
    _, energy = coarse_products(subs, ncf, x, base, gram)
    third = quadratic[1:2] + column_sum(coarse[...] * own)
    fourth = quadratic[0:1] + energy
    for k in range(copies.shape[0]):
        copies[k, 0:2] = sums[0:2]
        copies[k, 2:3] = third
        copies[k, 3:4] = fourth
    solution[...] = own
    faces = add_basis(subs, nf, ncf, x, basis_high, basis_low, product)
    for e in range(1, subs + 1):
        part[(e - 1) * nf : e * nf] = faces[e]
    back[...] = faces[0].astype(BF16)


def combine(subs, sums, load, z_local, z_coarse, y_local, y_coarse, rows, image, part, from_next, solution, residual):
    nf = load.shape[0] // subs
    ncf = rows.shape[0] // (subs + 1)
    total = sums[0]
    for k in range(1, sums.shape[0]):
        total = total + sums[k]
    a, b, c, d = (total[k : k + 1] for k in range(4))
    step = a / b
    grow = step * (c / b)
    next_step = (grow - 1.0) / ((d - c * (c / b)) * (step / b))
    s = step + next_step * grow
    t = step * next_step
    for j in range(subs):
        here, beside = slice(j * nf, (j + 1) * nf), slice((j + 1) * nf, (j + 2) * nf)
        block = rows_of(rows, j + 1, ncf)
        x = s * rows_of(z_coarse, j + 1, ncf) - t * rows_of(y_coarse, j, ncf)
        solution[here] = s * z_local[beside] - t * y_local[beside] + split_dot(block, x, dot_tn)
        last = part[here]
        if j == subs - 1:
            last = last + from_next[...].astype(F32)
        residual[here] = load[here] - s * image[here] + t * last


def exact_parts(x):
    high = lax.reduce_precision(x, 8, 7)
    middle = lax.reduce_precision(x - high, 8, 7)
    return [part.astype(BF16) for part in (high, middle, x - high - middle)]


def shards(right_side, face_weight, schur, neumann, constraint, coarse_inverse):
    subs, nf = face_weight.shape
    ncf = constraint.shape[0] // subs
    nco = coarse_inverse.shape[1]
    columns = right_side.shape[1]
    n = lax.axis_size(AXIS)
    bind = lambda kernel: functools.partial(kernel, subs)
    face, faces, own = (nf, columns), ((subs + 1) * nf, columns), (subs * nf, columns)
    coarse_own, basis = (subs * ncf, columns), (2 * subs * ncf, 2 * nf)
    copies = ((n,) + coarse_own, BF16)

    weight = face_weight.reshape(subs * nf, 1)
    pieces = jnp.concatenate([part.reshape(-1, columns) for part in exact_parts(face_weight[-1:])], axis=0)
    count = pieces.shape[0]
    padded = -(-count // 16) * 16
    weight_rows = jnp.pad(pieces, ((0, padded - count), (0, 0)))
    row_count, inverse_count = ncf * nf // columns, ncf * nco // columns
    message_rows = nf + row_count + inverse_count + padded
    coarse_copies, coarse, message = stage(
        bind(prepare), [copies, (coarse_own, F32), ((message_rows, columns), BF16)],
        right_side, weight, weight_rows, constraint, coarse_inverse,
    )
    got = shifted(message, 1)
    coarse_all = from_all(coarse_copies).reshape(nco, columns)
    next_inverse = shifted(coarse_inverse[:ncf], -1)

    def unfolded(start, stop):
        return jnp.concatenate([got[k : k + ncf] for k in range(start, stop, ncf)], axis=1)

    halo_left = got[:nf]
    rows = jnp.concatenate([unfolded(nf, nf + row_count), constraint], axis=0)
    halo_inverse = unfolded(nf + row_count, nf + row_count + inverse_count)
    third = count // 3
    got_weight = got[nf + row_count + inverse_count :].astype(F32)
    halo_weight = sum(got_weight[k * third : (k + 1) * third] for k in range(3)).reshape(nf, 1)
    weight_all = jnp.concatenate([halo_weight, weight], axis=0)

    halves = [(face, BF16), (face, BF16)]
    part, back, forward = stage(bind(neumann_load), [(faces, F32)] + halves, right_side, weight, halo_left, neumann)
    back, forward = shifted(back, -1), shifted(forward, 1)
    local, product, quadratic, basis_high, basis_low, base, gram, message = stage(
        bind(schur_load),
        [(faces, F32), (faces, F32), ((8, columns), F32), (basis, BF16), (basis, BF16), ((basis[0], columns), F32),
         ((basis[0], LANES), F32), ((ncf, columns + LANES), F32)],
        right_side, part, back, forward, weight_all, schur, rows,
    )
    from_next = shifted(message, -1)
    coarse_copies, coarse, z_coarse, part, back, forward, sums = stage(
        bind(coarse_load),
        [copies, (coarse_own, F32), (((subs + 1) * ncf, columns), F32), (faces, F32)] + halves + [((8, columns), F32)],
        coarse_all, coarse_inverse, halo_inverse, next_inverse, from_next, coarse, base, gram, quadratic,
        basis_high, basis_low, product,
    )
    back, forward = shifted(back, -1), shifted(forward, 1)
    coarse_all = from_all(coarse_copies).reshape(nco, columns)
    image, part, back, forward = stage(
        bind(neumann_image), [(own, F32), (faces, F32)] + halves, part, back, forward, weight_all, neumann
    )
    back, forward = shifted(back, -1), shifted(forward, 1)
    y_local, product, quadratic, base = stage(
        bind(schur_image), [(faces, F32), (faces, F32), ((8, columns), F32), ((basis[0], columns), F32)],
        image, part, back, forward, weight_all, schur, basis_high, basis_low,
    )
    sum_copies, y_coarse, part, back = stage(
        bind(coarse_image), [((n, 4, columns), F32), (coarse_own, F32), (own, F32), (face, BF16)],
        coarse_all, coarse_inverse, halo_inverse, coarse, base, gram, quadratic, basis_high, basis_low, product, sums,
    )
    sums = from_all(sum_copies)
    back = shifted(back, -1)
    return stage(
        bind(combine), [(own, F32), (own, F32)],
        sums, right_side, local, z_coarse, y_local, y_coarse, rows, image, part, back,
    )


def solution(mesh):
    specs = P(("parts", AXIS), None)
    return jax.shard_map(shards, mesh=mesh, in_specs=(specs,) * 6, out_specs=(specs, specs), check_vma=False)
```

time: 119 us -> 121 us (1.017)
  Pallas kernels: 0 us -> 28.6 us
  matrix products: 24.9 us -> 0 us
  local copies, waits for them, and re-layouts: 12.8 us -> 24.8 us
  blocking collectives: 0 us -> 9.9 us
  waiting for transfers between devices: 41.9 us -> 32 us
  other arithmetic: 10.6 us -> 1.46 us
  starting transfers between devices: 26.3 us -> 22.9 us
    pallas_call x0 -> x8, Pallas kernels: none -> 28.6 us  [stage(): pl.pallas_call(kernel, out_shape=out, compiler_params=params, name=kernel...]
    dot_general x34 -> x0, matrix products: 24.9 us -> none  [dot(): return jnp.dot(a, b, preferred_element_type=F32)]
    unnamed x65 -> x64, local copies, waits for them, and re-layouts: 5.79 us -> 22.4 us
    all_to_all x0 -> x1, blocking collectives: none -> 9.9 us  [from_all(): return lax.all_to_all(copies, AXIS, 0, 0)]
    all_to_all x3 -> x2, starting transfers between devices: 16.9 us -> 9.53 us  [from_all(): return lax.all_to_all(copies, AXIS, 0, 0)]
    ppermute x9 -> x10, waiting for transfers between devices: 37.1 us -> 32 us  [shifted(): lax.ppermute(block, AXIS, [((i - distance) % n, i) for i in range(n)])]
    all_to_all x3 -> x2, waiting for transfers between devices: 4.83 us -> 0.01 us  [from_all(): return lax.all_to_all(copies, AXIS, 0, 0)]
    add x7 -> x0, other arithmetic: 4.63 us -> none  [the longest x1 3.34 us: shards(): load[j] - s * image[j + 1] + t * image_y_faces[j]]
  transfers between devices with their start and end apart: 12 -> 12, of which waited for: 8 -> 8; matrix products, arithmetic and copies ran while one was open for 23% -> 2% of each run, Pallas kernels for 0% -> 17%
where the time goes in v3:
time: 121 us; the launch traced here: 120 us
  waiting for transfers between devices  32 us (26%)
  Pallas kernels  28.6 us (24%)
  local copies, waits for them, and re-layouts  24.8 us (20%)
  starting transfers between devices  22.9 us (19%)
  blocking collectives  9.9 us (8%)
  other arithmetic  1.46 us (1%)
    ppermute x10, waiting for transfers between devices, shifted(): lax.ppermute(block, AXIS, [((i - distance) % n, i) for i in range(n)])  32 us
    pallas_call x8, Pallas kernels, stage(): pl.pallas_call(kernel, out_shape=out, compiler_params=params, name=kernel...  28.6 us
    unnamed x64, local copies, waits for them, and re-layouts  22.4 us
    ppermute x10, starting transfers between devices, shifted(): lax.ppermute(block, AXIS, [((i - distance) % n, i) for i in range(n)])  13.4 us
    all_to_all x1, blocking collectives, from_all(): return lax.all_to_all(copies, AXIS, 0, 0)  9.9 us
    all_to_all x2, starting transfers between devices, from_all(): return lax.all_to_all(copies, AXIS, 0, 0)  9.53 us
  transfers between devices with their start and end apart: 12, of which 8 were waited for; matrix products, arithmetic and copies ran while one was open for 2% of the time, Pallas kernels for 17%

profile of v3, /device:TPU:0, one launch (start us, length us, event | category | flops | bytes accessed | tf_op | source)
XLA Modules:
  0.0 120.5 jit_solution(10678281608991479067)
XLA Ops:
  0.6 0.7 fusion.5
  1.4 0.7 copy.18
  2.3 1.2 %copy-done = f32[1024,256]{1,0:T(8,128)S(1)} copy-done((f32[1024,256]{1,0:T(8,128)S(1)}, f32[1024,256]{1,0:T(8,128)}, u32[]{:S(2)}) %copy-start) | copy-done | bytes 1048600
  3.6 0.9 copy-done.2
  4.5 0.8 copy-done.19
  5.3 1.0 prepare.1
  6.8 5.0 %collective-permute-start.1 = (bf16[32,1024]{1,0:T(8,128)(2,1)S(1)}, bf16[32,1024]{1,0:T(8,128)(2,1)S(1)}, u32[]{:S(2)}, u32[]{:S(2)}) collective-permute-start(bf16[32,1024]{1,0:T(8,128)(2,1)S(1)} %slice.44), channel_id=1, source_target_pairs={{1,0},{2,1},{3,2},{4,3},{5,4},{6,5},{7,6},{8,7},{9,8},{10,9},{11,1... | collective-permute-start | bytes 196616 | tf_op jit(solution)/shard_map/ppermute | solution.py:19
  11.9 3.6 %all-to-all-start = ((bf16[16,64,256]{2,1,0:T(8,128)(2,1)}), bf16[16,64,256]{2,1,0:T(8,128)(2,1)S(1)}, u32[]{:S(2)}, u32[]{:S(2)}) async-start(bf16[16,64,256]{2,1,0:T(8,128)(2,1)} %get-tuple-element.35), calls=%async_computation | async-start | bytes 1048576 | tf_op jit(solution)/shard_map/all_to_all | solution.py:23
  15.5 1.7 %collective-permute-done = bf16[720,256]{1,0:T(8,128)(2,1)} collective-permute-done((bf16[720,256]{1,0:T(8,128)(2,1)S(1)}, bf16[720,256]{1,0:T(8,128)(2,1)}, u32[]{:S(2)}, u32[]{:S(2)}) %collective-permute-start) | collective-permute-done | bytes 368672 | tf_op jit(solution)/shard_map/ppermute | solution.py:19
  17.2 0.7 slice_convert_fusion
  18.2 1.0 slice.56.halo_left
  19.2 3.5 %neumann_load.1 = (f32[1536,256]{1,0:T(8,128)S(1)}, bf16[512,256]{1,0:T(8,128)(2,1)S(1)}, bf16[512,256]{1,0:T(8,128)(2,1)S(1)}) custom-call(f32[1024,256]{1,0:T(8,128)S(1)} %copy-done.1, f32[1024,1]{1,0:T(8,128)S(1)} %copy.13.weight, bf16[512,256]{1,0:T(8,128)(2,1)S(1)} %slice.56.halo_left, bf16[2048,1024]{1,0:T(8,128)(2,1)} %neumann.3), custom_call_target="tpu_custom_call" | custom-call | tf_op jit(solution)/shard_map/neumann_load/pallas_call | solution.py:61
  22.8 1.2 copy-done.12
  23.9 2.7 %collective-permute-start.2 = (bf16[512,256]{1,0:T(8,128)(2,1)S(1)}, bf16[512,256]{1,0:T(8,128)(2,1)S(1)}, u32[]{:S(2)}, u32[]{:S(2)}) collective-permute-start(bf16[512,256]{1,0:T(8,128)(2,1)S(1)} %get-tuple-element.38), channel_id=1, source_target_pairs={{1,0},{2,1},{3,2},{4,3},{5,4},{6,5},{7,6},{8,7},{9,8},{10,9},{11,1... | collective-permute-start | bytes 786440 | tf_op jit(solution)/shard_map/ppermute | solution.py:19
  26.6 0.8 fusion.10
  27.5 3.1 %collective-permute-done.2.from_next = bf16[512,256]{1,0:T(8,128)(2,1)S(1)} collective-permute-done((bf16[512,256]{1,0:T(8,128)(2,1)S(1)}, bf16[512,256]{1,0:T(8,128)(2,1)S(1)}, u32[]{:S(2)}, u32[]{:S(2)}) %collective-permute-start.2) | collective-permute-done | bytes 262176 | tf_op jit(solution)/shard_map/ppermute | solution.py:19
  30.6 4.6 %collective-permute-done.3.from_previous = bf16[512,256]{1,0:T(8,128)(2,1)S(1)} collective-permute-done((bf16[512,256]{1,0:T(8,128)(2,1)S(1)}, bf16[512,256]{1,0:T(8,128)(2,1)S(1)}, u32[]{:S(2)}, u32[]{:S(2)}) %collective-permute-start.3) | collective-permute-done | bytes 262176 | tf_op jit(solution)/shard_map/ppermute | solution.py:19
  35.1 7.6 %schur_load.1 = (f32[1536,256]{1,0:T(8,128)S(1)}, f32[1536,256]{1,0:T(8,128)}, f32[8,256]{1,0:T(8,128)S(1)}, bf16[128,1024]{1,0:T(8,128)(2,1)S(1)}, bf16[128,102...) custom-call(f32[1024,256]{1,0:T(8,128)S(1)} %copy-done.1, ...), custom_call_target="tpu_custom_call" | custom-call | tf_op jit(solution)/shard_map/schur_load/pallas_call | solution.py:61
  42.7 1.2 copy-done.9
  44.1 1.7 %collective-permute-done.4.from_next = f32[32,384]{1,0:T(8,128)S(1)} collective-permute-done((f32[32,384]{1,0:T(8,128)S(1)}, f32[32,384]{1,0:T(8,128)S(1)}, u32[]{:S(2)}, u32[]{:S(2)}) %collective-permute-start.4) | collective-permute-done | bytes 49184 | tf_op jit(solution)/shard_map/ppermute | solution.py:19
  45.8 1.4 %copy-done.6 = f32[1536,256]{1,0:T(8,128)S(1)} copy-done((f32[1536,256]{1,0:T(8,128)S(1)}, f32[1536,256]{1,0:T(8,128)}, u32[]{:S(2)}) %copy-start.6) | copy-done | bytes 1572888
  47.2 1.4 %coarse_load.1 = (bf16[16,64,256]{2,1,0:T(8,128)(2,1)S(1)}, f32[64,256]{1,0:T(8,128)S(1)}, f32[96,256]{1,0:T(8,128)S(1)}, f32[1536,256]{1,0:T(8,128)S(1)}, bf16[...) custom-call(bf16[1024,256]{1,0:T(8,128)(2,1)S(1)} %bitcast.11, ...), custom_call_target="tpu_custom_call" | custom-call | tf_op jit(solution)/shard_map/coarse_load/pallas_call | solution.py:61
  48.7 1.2 copy-done.4
  49.9 0.8 copy-done.18
  50.7 0.6 copy-done.25
  51.9 0.7 copy-done.29
  52.6 0.7 copy-done.30
  53.3 5.9 %all-to-all-start.1 = ((bf16[16,64,256]{2,1,0:T(8,128)(2,1)}), bf16[16,64,256]{2,1,0:T(8,128)(2,1)}, u32[]{:S(2)}, u32[]{:S(2)}) async-start(bf16[16,64,256]{2,1,0:T(8,128)(2,1)} %copy-done.18), calls=%async_computation.1 | async-start | bytes 1048576 | tf_op jit(solution)/shard_map/all_to_all | solution.py:23
  59.2 4.3 %collective-permute-start.5 = (bf16[512,256]{1,0:T(8,128)(2,1)}, bf16[512,256]{1,0:T(8,128)(2,1)S(1)}, u32[]{:S(2)}, u32[]{:S(2)}) collective-permute-start(bf16[512,256]{1,0:T(8,128)(2,1)} %copy-done.30), channel_id=1, source_target_pairs={{1,0},{2,1},{3,2},{4,3},{5,4},{6,5},{7,6},{8,7},{9,8},{10,9},{11,1... | collective-permute-start | bytes 786440 | tf_op jit(solution)/shard_map/ppermute | solution.py:19
  63.6 8.0 %collective-permute-done.5.from_next = bf16[512,256]{1,0:T(8,128)(2,1)S(1)} collective-permute-done((bf16[512,256]{1,0:T(8,128)(2,1)}, bf16[512,256]{1,0:T(8,128)(2,1)S(1)}, u32[]{:S(2)}, u32[]{:S(2)}) %collective-permute-start.5) | collective-permute-done | bytes 262176 | tf_op jit(solution)/shard_map/ppermute | solution.py:19
  71.6 4.8 %collective-permute-done.6.from_previous = bf16[512,256]{1,0:T(8,128)(2,1)S(1)} collective-permute-done((bf16[512,256]{1,0:T(8,128)(2,1)}, bf16[512,256]{1,0:T(8,128)(2,1)S(1)}, u32[]{:S(2)}, u32[]{:S(2)}) %collective-permute-start.6) | collective-permute-done | bytes 262176 | tf_op jit(solution)/shard_map/ppermute | solution.py:19
  76.5 1.4 %copy-done.5 = f32[1536,256]{1,0:T(8,128)S(1)} copy-done((f32[1536,256]{1,0:T(8,128)S(1)}, f32[1536,256]{1,0:T(8,128)}, u32[]{:S(2)}) %copy-start.5) | copy-done | bytes 1572888
  77.9 3.6 %neumann_image.1 = (f32[1024,256]{1,0:T(8,128)S(1)}, f32[1536,256]{1,0:T(8,128)S(1)}, bf16[512,256]{1,0:T(8,128)(2,1)S(1)}, bf16[512,256]{1,0:T(8,128)(2,1)S(1)}) custom-call(f32[1536,256]{1,0:T(8,128)S(1)} %copy-done.5, bf16[512,256]{1,0:T(8,128)(2,1)S(1)} %collective-permute-done.5.from_next, bf16[512,256]{1,0:T(8,128)(2,1)S(1)} %collective-permute-done.6.from_previous, ...), custom_call_target="tpu_custom_call" | custom-call | tf_op jit(solution)/shard_map/neumann_image/pallas_call | solution.py:61
  81.4 1.2 copy-done.13
  83.1 3.4 %collective-permute-done.7.from_next = bf16[512,256]{1,0:T(8,128)(2,1)S(1)} collective-permute-done((bf16[512,256]{1,0:T(8,128)(2,1)S(1)}, bf16[512,256]{1,0:T(8,128)(2,1)S(1)}, u32[]{:S(2)}, u32[]{:S(2)}) %collective-permute-start.7) | collective-permute-done | bytes 262176 | tf_op jit(solution)/shard_map/ppermute | solution.py:19
  86.5 4.6 %collective-permute-done.8.from_previous = bf16[512,256]{1,0:T(8,128)(2,1)S(1)} collective-permute-done((bf16[512,256]{1,0:T(8,128)(2,1)S(1)}, bf16[512,256]{1,0:T(8,128)(2,1)S(1)}, u32[]{:S(2)}, u32[]{:S(2)}) %collective-permute-start.8) | collective-permute-done | bytes 262176 | tf_op jit(solution)/shard_map/ppermute | solution.py:19
  91.1 5.6 %schur_image.1 = (f32[1536,256]{1,0:T(8,128)S(1)}, f32[1536,256]{1,0:T(8,128)S(1)}, f32[8,256]{1,0:T(8,128)S(1)}, f32[128,256]{1,0:T(8,128)S(1)}) custom-call(f32[1024,256]{1,0:T(8,128)S(1)} %get-tuple-element.53.image, f32[1536,256]{1,0:T(8,128)} %copy-done.13, bf16[512,256]{1,0:T(8,128)(2,1)S(1)} %collective-permute-done.7.from_next, ...), custom_call_target="tpu_custom_call" | custom-call | tf_op jit(solution)/shard_map/schur_image/pallas_call | solution.py:61
  96.8 1.1 copy-done.7
  97.9 1.2 copy-done.11
  99.1 0.7 copy-done.23
  99.7 1.4 %copy-done.8 = f32[1536,256]{1,0:T(8,128)S(1)} copy-done((f32[1536,256]{1,0:T(8,128)S(1)}, f32[1536,256]{1,0:T(8,128)}, u32[]{:S(2)}) %copy-start.8) | copy-done | bytes 1572888
  101.1 0.8 copy-done.17
  102.0 0.8 copy-done.22
  102.8 0.9 copy-done.24
  103.7 0.8 copy-done.28
  104.6 2.5 %coarse_image.1 = (f32[16,4,256]{2,1,0:T(4,128)S(1)}, f32[64,256]{1,0:T(8,128)S(1)}, f32[1024,256]{1,0:T(8,128)S(1)}, bf16[512,256]{1,0:T(8,128)(2,1)S(1)}) custom-call(bf16[1024,256]{1,0:T(8,128)(2,1)} %bitcast.1.coarse_all, bf16[64,1024]{1,0:T(8,128)(2,1)S(1)} %copy-done.3, bf16[32,1024]{1,0:T(8,128)(2,1)S(1)} %copy-done.17, f32[64,256]{1,0:T(8,128)S(1)} %copy-done.28, ...), custom_call_target="tpu_custom_call" | custom-call | tf_op jit(solution)/shard_map/coarse_image/pallas_call | solution.py:61
  107.2 9.9 %all_to_all.15.sums = f32[16,4,256]{2,1,0:T(4,128)S(1)} all-to-all(f32[16,4,256]{2,1,0:T(4,128)S(1)} %get-tuple-element.61), channel_id=1, replica_groups=mesh['parts'=2,'sub'=16] {'sub'}, dimensions={0} | all-to-all | bytes 131072 | tf_op jit(solution)/shard_map/all_to_all | solution.py:23
  117.1 3.3 %combine.1 = (f32[1024,256]{1,0:T(8,128)}, f32[1024,256]{1,0:T(8,128)}) custom-call(f32[16,4,256]{2,1,0:T(4,128)S(1)} %all_to_all.15.sums, f32[1024,256]{1,0:T(8,128)S(1)} %copy-done.1, f32[1536,256]{1,0:T(8,128)S(1)} %copy-done.10, f32[96,256]{1,0:T(8,128)S(1)} %copy-done.26, f32[1536,256]{1,0:T(8,128)} %copy-done.11, ...), custom_call_target="tpu_custom_call" | custom-call | tf_op jit(solution)/shard_map/combine/pallas_call | solution.py:61
  (64 shorter events, 2.7 us)
Async XLA Ops:
  2.3 1.2 %copy-start = (f32[1024,256]{1,0:T(8,128)S(1)}, f32[1024,256]{1,0:T(8,128)}, u32[]{:S(2)}) copy-start(f32[1024,256]{1,0:T(8,128)} %load.7) | copy-start | bytes 3145732
  3.6 0.9 copy-start.2
  4.5 0.8 copy-start.19
  6.4 12.9 %copy-start.1 = (f32[1024,256]{1,0:T(8,128)S(1)}, f32[1024,256]{1,0:T(8,128)}, u32[]{:S(2)}) copy-start(f32[1024,256]{1,0:T(8,128)} %load.7) | copy-start | bytes 3145732
  6.4 10.8 %collective-permute-start = (bf16[720,256]{1,0:T(8,128)(2,1)S(1)}, bf16[720,256]{1,0:T(8,128)(2,1)}, u32[]{:S(2)}, u32[]{:S(2)}) collective-permute-start(bf16[720,256]{1,0:T(8,128)(2,1)S(1)} %get-tuple-element.36), channel_id=1, source_target_pairs={{15,0},{0,1},{1,2},{2,3},{3,4},{4,5},{5,6},{6,7},{7,8},{8,9},{9,10... | collective-permute-start | bytes 1105928 | tf_op jit(solution)/shard_map/ppermute | solution.py:19
  6.8 37.3 %collective-permute-start.1 = (bf16[32,1024]{1,0:T(8,128)(2,1)S(1)}, bf16[32,1024]{1,0:T(8,128)(2,1)S(1)}, u32[]{:S(2)}, u32[]{:S(2)}) collective-permute-start(bf16[32,1024]{1,0:T(8,128)(2,1)S(1)} %slice.44), channel_id=1, source_target_pairs={{1,0},{2,1},{3,2},{4,3},{5,4},{6,5},{7,6},{8,7},{9,8},{10,9},{11,1... | collective-permute-start | bytes 196616 | tf_op jit(solution)/shard_map/ppermute | solution.py:19
  11.9 34.0 %all-to-all-start = ((bf16[16,64,256]{2,1,0:T(8,128)(2,1)}), bf16[16,64,256]{2,1,0:T(8,128)(2,1)S(1)}, u32[]{:S(2)}, u32[]{:S(2)}) async-start(bf16[16,64,256]{2,1,0:T(8,128)(2,1)} %get-tuple-element.35), calls=%async_computation | async-start | bytes 1048576 | tf_op jit(solution)/shard_map/all_to_all | solution.py:23
  19.2 8.2 %copy-start.20 = (bf16[64,512]{1,0:T(8,128)(2,1)S(1)}, bf16[64,512]{1,0:T(8,128)(2,1)}, u32[]{:S(2)}) copy-start(bf16[64,512]{1,0:T(8,128)(2,1)} %rows.1) | copy-start | bytes 196612
  22.8 1.2 copy-start.12
  23.9 6.6 %collective-permute-start.2 = (bf16[512,256]{1,0:T(8,128)(2,1)S(1)}, bf16[512,256]{1,0:T(8,128)(2,1)S(1)}, u32[]{:S(2)}, u32[]{:S(2)}) collective-permute-start(bf16[512,256]{1,0:T(8,128)(2,1)S(1)} %get-tuple-element.38), channel_id=1, source_target_pairs={{1,0},{2,1},{3,2},{4,3},{5,4},{6,5},{7,6},{8,7},{9,8},{10,9},{11,1... | collective-permute-start | bytes 786440 | tf_op jit(solution)/shard_map/ppermute | solution.py:19
  26.6 8.5 %collective-permute-start.3 = (bf16[512,256]{1,0:T(8,128)(2,1)S(1)}, bf16[512,256]{1,0:T(8,128)(2,1)S(1)}, u32[]{:S(2)}, u32[]{:S(2)}) collective-permute-start(bf16[512,256]{1,0:T(8,128)(2,1)S(1)} %get-tuple-element.39), channel_id=1, source_target_pairs={{15,0},{0,1},{1,2},{2,3},{3,4},{4,5},{5,6},{6,7},{7,8},{8,9},{9,10... | collective-permute-start | bytes 786440 | tf_op jit(solution)/shard_map/ppermute | solution.py:19
  27.5 15.2 %copy-start.14 = (bf16[96,512]{1,0:T(8,128)(2,1)}, bf16[96,512]{1,0:T(8,128)(2,1)S(1)}, u32[]{:S(2)}) copy-start(bf16[96,512]{1,0:T(8,128)(2,1)S(1)} %pad_maximum_fusion.rows) | copy-start | bytes 294916
  35.1 10.7 %copy-start.3 = (bf16[64,1024]{1,0:T(8,128)(2,1)S(1)}, bf16[64,1024]{1,0:T(8,128)(2,1)}, u32[]{:S(2)}) copy-start(bf16[64,1024]{1,0:T(8,128)(2,1)} %inverse.5) | copy-start | bytes 393220
  42.7 1.2 copy-start.9
  43.9 4.8 %copy-start.21 = (f32[128,128]{1,0:T(8,128)}, f32[128,128]{1,0:T(8,128)S(1)}, u32[]{:S(2)}) copy-start(f32[128,128]{1,0:T(8,128)S(1)} %get-tuple-element.43.gram) | copy-start | bytes 196612
  43.9 2.0 %collective-permute-start.4 = (f32[32,384]{1,0:T(8,128)S(1)}, f32[32,384]{1,0:T(8,128)S(1)}, u32[]{:S(2)}, u32[]{:S(2)}) collective-permute-start(f32[32,384]{1,0:T(8,128)S(1)} %get-tuple-element.40), channel_id=1, source_target_pairs={{1,0},{2,1},{3,2},{4,3},{5,4},{6,5},{7,6},{8,7},{9,8},{10,9},{11,1... | collective-permute-start | bytes 147464 | tf_op jit(solution)/shard_map/ppermute | solution.py:19
  44.1 4.6 %copy-start.16 = (bf16[32,1024]{1,0:T(8,128)(2,1)}, bf16[32,1024]{1,0:T(8,128)(2,1)S(1)}, u32[]{:S(2)}) copy-start(bf16[32,1024]{1,0:T(8,128)(2,1)S(1)} %pad_maximum_fusion.1.halo_inverse) | copy-start | bytes 196612
  45.8 1.4 %copy-start.6 = (f32[1536,256]{1,0:T(8,128)S(1)}, f32[1536,256]{1,0:T(8,128)}, u32[]{:S(2)}) copy-start(f32[1536,256]{1,0:T(8,128)} %get-tuple-element.47.product) | copy-start | bytes 4718596
  48.7 1.2 copy-start.4
  49.9 0.8 copy-start.18
  50.7 0.6 copy-start.25
  51.3 0.6 copy-start.27
  51.9 0.7 copy-start.29
  52.6 0.7 copy-start.30
  53.3 46.4 %all-to-all-start.1 = ((bf16[16,64,256]{2,1,0:T(8,128)(2,1)}), bf16[16,64,256]{2,1,0:T(8,128)(2,1)}, u32[]{:S(2)}, u32[]{:S(2)}) async-start(bf16[16,64,256]{2,1,0:T(8,128)(2,1)} %copy-done.18), calls=%async_computation.1 | async-start | bytes 1048576 | tf_op jit(solution)/shard_map/all_to_all | solution.py:23
  59.2 12.4 %collective-permute-start.5 = (bf16[512,256]{1,0:T(8,128)(2,1)}, bf16[512,256]{1,0:T(8,128)(2,1)S(1)}, u32[]{:S(2)}, u32[]{:S(2)}) collective-permute-start(bf16[512,256]{1,0:T(8,128)(2,1)} %copy-done.30), channel_id=1, source_target_pairs={{1,0},{2,1},{3,2},{4,3},{5,4},{6,5},{7,6},{8,7},{9,8},{10,9},{11,1... | collective-permute-start | bytes 786440 | tf_op jit(solution)/shard_map/ppermute | solution.py:19
  63.6 12.9 %collective-permute-start.6 = (bf16[512,256]{1,0:T(8,128)(2,1)}, bf16[512,256]{1,0:T(8,128)(2,1)S(1)}, u32[]{:S(2)}, u32[]{:S(2)}) collective-permute-start(bf16[512,256]{1,0:T(8,128)(2,1)} %copy-done.29), channel_id=1, source_target_pairs={{15,0},{0,1},{1,2},{2,3},{3,4},{4,5},{5,6},{6,7},{7,8},{8,9},{9,10... | collective-permute-start | bytes 786440 | tf_op jit(solution)/shard_map/ppermute | solution.py:19
  76.5 1.4 %copy-start.5 = (f32[1536,256]{1,0:T(8,128)S(1)}, f32[1536,256]{1,0:T(8,128)}, u32[]{:S(2)}) copy-start(f32[1536,256]{1,0:T(8,128)} %copy-done.4) | copy-start | bytes 4718596
  81.4 1.2 copy-start.13
  82.6 3.9 %collective-permute-start.7 = (bf16[512,256]{1,0:T(8,128)(2,1)S(1)}, bf16[512,256]{1,0:T(8,128)(2,1)S(1)}, u32[]{:S(2)}, u32[]{:S(2)}) collective-permute-start(bf16[512,256]{1,0:T(8,128)(2,1)S(1)} %get-tuple-element.55), channel_id=1, source_target_pairs={{1,0},{2,1},{3,2},{4,3},{5,4},{6,5},{7,6},{8,7},{9,8},{10,9},{11,1... | collective-permute-start | bytes 786440 | tf_op jit(solution)/shard_map/ppermute | solution.py:19
  82.6 8.5 %collective-permute-start.8 = (bf16[512,256]{1,0:T(8,128)(2,1)S(1)}, bf16[512,256]{1,0:T(8,128)(2,1)S(1)}, u32[]{:S(2)}, u32[]{:S(2)}) collective-permute-start(bf16[512,256]{1,0:T(8,128)(2,1)S(1)} %get-tuple-element.56), channel_id=1, source_target_pairs={{15,0},{0,1},{1,2},{2,3},{3,4},{4,5},{5,6},{6,7},{7,8},{8,9},{9,10... | collective-permute-start | bytes 786440 | tf_op jit(solution)/shard_map/ppermute | solution.py:19
  96.8 1.2 copy-start.7
  97.9 1.2 copy-start.11
  99.1 0.7 copy-start.23
  99.7 1.4 %copy-start.8 = (f32[1536,256]{1,0:T(8,128)S(1)}, f32[1536,256]{1,0:T(8,128)}, u32[]{:S(2)}) copy-start(f32[1536,256]{1,0:T(8,128)} %copy-done.7) | copy-start | bytes 4718596
  101.1 0.8 copy-start.17
  102.0 0.8 copy-start.22
  102.8 0.9 copy-start.24
  103.7 0.8 copy-start.28
  104.6 12.6 %copy-start.10 = (f32[1536,256]{1,0:T(8,128)S(1)}, f32[1536,256]{1,0:T(8,128)}, u32[]{:S(2)}) copy-start(f32[1536,256]{1,0:T(8,128)} %copy-done.9) | copy-start | bytes 4718596
  104.6 12.6 %copy-start.15 = (bf16[96,512]{1,0:T(8,128)(2,1)S(1)}, bf16[96,512]{1,0:T(8,128)(2,1)}, u32[]{:S(2)}) copy-start(bf16[96,512]{1,0:T(8,128)(2,1)} %copy-done.14) | copy-start | bytes 294916
  104.6 12.6 %copy-start.26 = (f32[96,256]{1,0:T(8,128)S(1)}, f32[96,256]{1,0:T(8,128)}, u32[]{:S(2)}) copy-start(f32[96,256]{1,0:T(8,128)} %copy-done.25) | copy-start | bytes 294916
  107.1 10.1 %collective-permute-start.9 = (bf16[512,256]{1,0:T(8,128)(2,1)S(1)}, bf16[512,256]{1,0:T(8,128)(2,1)S(1)}, u32[]{:S(2)}, u32[]{:S(2)}) collective-permute-start(bf16[512,256]{1,0:T(8,128)(2,1)S(1)} %get-tuple-element.67), channel_id=1, source_target_pairs={{1,0},{2,1},{3,2},{4,3},{5,4},{6,5},{7,6},{8,7},{9,8},{10,9},{11,1... | collective-permute-start | bytes 786440 | tf_op jit(solution)/shard_map/ppermute | solution.py:19

commit v4 on v3

v4 whole, which is shorter than its diff:
```python
import functools

import jax
import jax.numpy as jnp
from jax import lax
from jax.experimental import pallas as pl
from jax.experimental.pallas import tpu as pltpu
from jax.sharding import PartitionSpec as P

AXIS = "sub"
BF16 = jnp.bfloat16
F32 = jnp.float32
LANES = 128
VMEM_BYTES = 20 * 2**20


def shifted(block, distance):
    n = lax.axis_size(AXIS)
    return lax.ppermute(block, AXIS, [((i - distance) % n, i) for i in range(n)])


def crossed(block, bit):
    return lax.ppermute(block, AXIS, [(i, i ^ bit) for i in range(lax.axis_size(AXIS))])


def bits():
    return [1 << k for k in reversed(range(lax.axis_size(AXIS).bit_length() - 1))]


def gather_halves(block):
    for bit in bits()[:-1]:
        block = jnp.concatenate([block, crossed(block, bit)], axis=0)
    return block, crossed(block, 1)


def half_order():
    order = [0]
    for bit in bits()[:-1]:
        order += [place ^ bit for place in order]
    return order


def sum_all(block):
    for bit in bits():
        block = block + crossed(block, bit)
    return block


def dot(a, b):
    return jnp.dot(a, b, preferred_element_type=F32)


def dot_nt(a, b):
    return lax.dot_general(a, b, (((1,), (1,)), ((), ())), preferred_element_type=F32)


def dot_tn(a, b):
    return lax.dot_general(a, b, (((0,), (0,)), ((), ())), preferred_element_type=F32)


def split(x):
    high = x.astype(BF16)
    return high, (x - high.astype(F32)).astype(BF16)


def split_dot(a, b, contract=dot):
    high, low = split(b)
    if isinstance(a, tuple):
        return contract(a[0], high) + contract(a[0], low) + contract(a[1], high)
    return contract(a, high) + contract(a, low)


def column_sum(x):
    return jnp.sum(x, axis=0, keepdims=True)


def rows_of(ref, index, count):
    return ref[index * count : (index + 1) * count]


def column_of(row):
    return jnp.broadcast_to(row, (8, row.shape[1])).T[:, :1]


def parts_of(row):
    high = row.astype(BF16).astype(F32)
    middle = (row - high).astype(BF16).astype(F32)
    return high, middle, row - high - middle


class Halo:
    def __init__(self, nf, ncf, nco, columns):
        self.nf, self.ncf, self.columns = nf, ncf, columns
        self.folds = nf // columns
        self.at_rows = nf
        self.at_inverse = nf + ncf * self.folds
        self.at_weight = self.at_inverse + ncf * (nco // columns)
        self.weight_count = -(-3 * self.folds // 16) * 16
        self.height = self.at_weight + self.weight_count

    def load(self, message):
        return message[: self.nf]

    def pieces(self, message, start, stop):
        return [message[k : k + self.ncf] for k in range(start, stop, self.ncf)]

    def rows(self, message):
        return jnp.concatenate(self.pieces(message, self.at_rows, self.at_inverse), axis=1)

    def inverse(self, message):
        return jnp.concatenate(self.pieces(message, self.at_inverse, self.at_weight), axis=1)

    def weight(self, message):
        got = message[self.at_weight : self.height].astype(F32)
        f = self.folds
        row = [sum(got[k * f + i : k * f + i + 1] for k in range(3)) for i in range(f)]
        return jnp.concatenate([column_of(piece) for piece in row], axis=0)


def all_rows(halo, message, rows):
    ncf = halo.ncf
    return [halo.rows(message)] + [rows_of(rows, j, ncf) for j in range(rows.shape[0] // ncf)]


def all_weights(halo, message, weight):
    return [halo.weight(message)] + [column_of(weight[j : j + 1]) for j in range(weight.shape[0])]


def stage(kernel, shapes, *operands, scratch=()):
    out = [jax.ShapeDtypeStruct(shape, dtype) for shape, dtype in shapes]
    params = pltpu.CompilerParams(vmem_limit_bytes=VMEM_BYTES)
    call = pl.pallas_call(
        kernel, out_shape=out, scratch_shapes=list(scratch), compiler_params=params, name=kernel.func.__name__
    )
    return call(*operands)


def prepare(halo, load, weight, rows, inverse, coarse_rounded, coarse, message, pieces):
    subs, nf = weight.shape
    ncf, columns, folds = halo.ncf, halo.columns, halo.folds
    for j in range(subs):
        coarse[j * ncf : (j + 1) * ncf] = dot(rows_of(rows, j, ncf), rows_of(load, j, nf).astype(BF16))
    coarse_rounded[...] = coarse[...].astype(BF16)
    last = weight[subs - 1 : subs]
    message[:nf] = ((1.0 - column_of(last)) * load[(subs - 1) * nf :]).astype(BF16)
    for array, at in ((rows, halo.at_rows), (inverse, halo.at_inverse)):
        for k in range(array.shape[1] // columns):
            message[at + k * ncf : at + (k + 1) * ncf] = array[(subs - 1) * ncf :, k * columns : (k + 1) * columns]
    pieces[...] = jnp.zeros_like(pieces)
    for k, part in enumerate(parts_of(last)):
        for i in range(folds):
            pieces[k * folds + i : k * folds + i + 1] = part[:, i * columns : (i + 1) * columns]
    message[halo.at_weight :] = pieces[...].astype(BF16)


def neumann_products(left, right, weights, neumann, part, back, forward):
    subs, nf = len(left), left[0].shape[0]
    previous = None
    for j in range(subs):
        product = dot(rows_of(neumann, j, 2 * nf), jnp.concatenate([left[j], right[j]], axis=0))
        first, second = product[:nf], product[nf:]
        if j == 0:
            part[:nf] = first
            back[...] = first.astype(BF16)
        else:
            part[j * nf : (j + 1) * nf] = weights[j] * previous + (1.0 - weights[j]) * first
        previous = second
    part[subs * nf :] = previous
    forward[...] = previous.astype(BF16)


def neumann_load(halo, load, weight, message, neumann, part, back, forward):
    subs, nf = weight.shape
    weights = [None] + [column_of(weight[j : j + 1]) for j in range(subs)]
    left = [halo.load(message)]
    left += [((1.0 - weights[j]) * rows_of(load, j - 1, nf)).astype(BF16) for j in range(1, subs)]
    right = [(weights[j + 1] * rows_of(load, j, nf)).astype(BF16) for j in range(subs)]
    neumann_products(left, right, weights, neumann, part, back, forward)


def neumann_image(halo, part_in, from_next, from_previous, weight, message, neumann, image, part, back, forward):
    subs, nf = weight.shape
    weights = all_weights(halo, message, weight)
    faces = [rows_of(part_in, e, nf) for e in range(subs + 1)]
    faces[0] = faces[0] + from_previous[...].astype(F32)
    faces[subs] = faces[subs] + from_next[...].astype(F32)
    for e in range(1, subs + 1):
        image[(e - 1) * nf : e * nf] = faces[e]
    left = [((1.0 - weights[j]) * faces[j]).astype(BF16) for j in range(subs)]
    right = [(weights[j + 1] * faces[j + 1]).astype(BF16) for j in range(subs)]
    neumann_products(left, right, weights, neumann, part, back, forward)


def static_basis(halo, schur, message, rows, basis_high, basis_low, turned_high, turned_low, gram):
    ncf, nf = halo.ncf, halo.nf
    blocks = all_rows(halo, message, rows)
    gram[...] = jnp.zeros_like(gram)
    for j in range(len(blocks) - 1):
        matrix, pair = rows_of(schur, j, 2 * nf), blocks[j : j + 2]
        basis = jnp.concatenate([dot_nt(matrix[:, k * nf : (k + 1) * nf], pair[k]) for k in range(2)], axis=1)
        long, wide = slice(2 * j * nf, 2 * (j + 1) * nf), slice(2 * j * ncf, 2 * (j + 1) * ncf)
        basis_high[long], basis_low[long] = split(basis)
        turned = split(basis.T)
        turned_high[wide], turned_low[wide] = turned
        for k in range(2):
            half = slice(k * nf, (k + 1) * nf)
            gram[wide, k * ncf : (k + 1) * ncf] = dot_nt(turned[0][:, half], pair[k]) + dot_nt(turned[1][:, half], pair[k])


def schur_products(
    halo, other, part, from_next, from_previous, weight, message, schur, turned_high, turned_low,
    local, product, quadratic, base,
):
    subs, nf = weight.shape
    ncf, columns = halo.ncf, halo.columns
    weights = all_weights(halo, message, weight)
    local[:nf] = (1.0 - weights[0]) * part[:nf] + weights[0] * from_previous[...].astype(F32)
    for e in range(1, subs):
        local[e * nf : (e + 1) * nf] = rows_of(part, e, nf)
    local[subs * nf :] = weights[subs] * part[subs * nf :] + (1.0 - weights[subs]) * from_next[...].astype(F32)
    energy, previous = 0.0, None
    for j in range(subs):
        vector = local[j * nf : (j + 2) * nf]
        high, low = split(vector)
        both = dot(rows_of(schur, j, 2 * nf), jnp.concatenate([high, low], axis=1))
        result = both[:, :columns] + both[:, columns:]
        energy = energy + column_sum(vector * result)
        first = result[:nf]
        product[j * nf : (j + 1) * nf] = first if j == 0 else previous + first
        previous = result[nf:]
        here = slice(2 * j * ncf, 2 * (j + 1) * ncf)
        base[here] = dot(turned_high[here], high) + dot(turned_high[here], low) + dot(turned_low[here], high)
    product[subs * nf :] = previous
    quadratic[0:1] = energy
    quadratic[1:2] = column_sum(other[...] * local[nf:])


def schur_load(*refs):
    *refs, gram, local, product, quadratic, base, share = refs
    schur_products(*refs, local, product, quadratic, base)
    ncf, columns = share.shape[0], base.shape[1]
    share[:, :columns] = base[:ncf]
    share[:, columns:] = gram[:ncf]


def schur_image(*refs):
    schur_products(*refs)


def coarse_solve(halo, half, crossed_half, inverses, gathered):
    me = lax.axis_index(AXIS)
    order = half_order()
    count = half.shape[0] // len(order)
    for flip, blocks in ((0, half), (1, crossed_half)):
        for k, place in enumerate(order):
            start = pl.multiple_of((me ^ (place ^ flip)) * count, count)
            gathered[pl.ds(start, count)] = rows_of(blocks, k, count)
    everything = gathered[...]
    return [dot(inverse, everything) for inverse in inverses]


def coarse_products(ncf, x, base, gram):
    results, energy = [], 0.0
    for j in range(len(x) - 1):
        here = slice(2 * j * ncf, 2 * (j + 1) * ncf)
        pair = jnp.concatenate([x[j], x[j + 1]], axis=0)
        change = split_dot(split(gram[here, : 2 * ncf]), pair)
        energy = energy + column_sum(pair * (2.0 * base[here] + change))
        results.append(base[here] + change)
    return results, energy


def add_basis(nf, x, basis_high, basis_low, product):
    faces = [rows_of(product, e, nf) for e in range(len(x))]
    for j in range(len(x) - 1):
        here = slice(2 * j * nf, 2 * (j + 1) * nf)
        pair = jnp.concatenate([x[j], x[j + 1]], axis=0)
        change = split_dot((basis_high[here], basis_low[here]), pair)
        faces[j] = faces[j] + change[:nf]
        faces[j + 1] = faces[j + 1] + change[nf:]
    return faces


def coarse_load(
    halo, half, crossed_half, inverse, message, next_inverse, share, coarse, base, gram, quadratic, basis_high, basis_low, product,
    coarse_rounded, image_coarse, solution, part, back, forward, sums, gathered,
):
    ncf, nf, columns = halo.ncf, halo.nf, halo.columns
    subs = inverse.shape[0] // ncf
    first, own, beyond = coarse_solve(
        halo, half, crossed_half, (halo.inverse(message), inverse[...], next_inverse[...]), gathered
    )
    x = [first] + [own[j * ncf : (j + 1) * ncf] for j in range(subs)]
    results, energy = coarse_products(ncf, x, base, gram)
    for e in range(1, subs):
        image_coarse[(e - 1) * ncf : e * ncf] = results[e - 1][ncf:] + results[e][:ncf]
    change = split_dot(split(share[:, columns : columns + 2 * ncf]), jnp.concatenate([x[subs], beyond], axis=0))
    image_coarse[(subs - 1) * ncf :] = results[subs - 1][ncf:] + share[:, :columns] + change
    coarse_rounded[...] = image_coarse[...].astype(BF16)
    solution[...] = own
    sums[0:1] = quadratic[1:2] + column_sum(coarse[...] * own)
    sums[1:2] = quadratic[0:1] + energy
    faces = add_basis(nf, x, basis_high, basis_low, product)
    for e in range(subs + 1):
        part[e * nf : (e + 1) * nf] = faces[e]
    back[...] = faces[0].astype(BF16)
    forward[...] = faces[subs].astype(BF16)


def coarse_image(
    halo, half, crossed_half, inverse, message, coarse, base, gram, quadratic, basis_high, basis_low, product, sums_in,
    sums, solution, part, back, gathered,
):
    ncf, nf = halo.ncf, halo.nf
    subs = inverse.shape[0] // ncf
    first, own = coarse_solve(halo, half, crossed_half, (halo.inverse(message), inverse[...]), gathered)
    x = [first] + [own[j * ncf : (j + 1) * ncf] for j in range(subs)]
    _, energy = coarse_products(ncf, x, base, gram)
    sums[0:2] = sums_in[0:2]
    sums[2:3] = quadratic[1:2] + column_sum(coarse[...] * own)
    sums[3:4] = quadratic[0:1] + energy
    solution[...] = own
    faces = add_basis(nf, x, basis_high, basis_low, product)
    for e in range(1, subs + 1):
        part[(e - 1) * nf : e * nf] = faces[e]
    back[...] = faces[0].astype(BF16)


def combine(halo, sums, load, z_local, z_coarse, y_local, y_coarse, rows, image, part, from_next, solution, residual):
    ncf, nf = halo.ncf, halo.nf
    subs = rows.shape[0] // ncf
    a, b, c, d = (sums[k : k + 1] for k in range(4))
    step = a / b
    grow = step * (c / b)
    next_step = (grow - 1.0) / ((d - c * (c / b)) * (step / b))
    s = step + next_step * grow
    t = step * next_step
    for j in range(subs):
        here, beside = slice(j * nf, (j + 1) * nf), slice((j + 1) * nf, (j + 2) * nf)
        x = s * rows_of(z_coarse, j, ncf) - t * rows_of(y_coarse, j, ncf)
        solution[here] = s * z_local[beside] - t * y_local[beside] + split_dot(rows_of(rows, j, ncf), x, dot_tn)
        last = part[here]
        if j == subs - 1:
            last = last + from_next[...].astype(F32)
        residual[here] = load[here] - s * image[here] + t * last


def shards(right_side, face_weight, schur, neumann, constraint, coarse_inverse):
    subs, nf = face_weight.shape
    ncf = constraint.shape[0] // subs
    nco = coarse_inverse.shape[1]
    columns = right_side.shape[1]
    halo = Halo(nf, ncf, nco, columns)
    bind = lambda kernel: functools.partial(kernel, halo)
    faces, own = ((subs + 1) * nf, columns), (subs * nf, columns)
    coarse_own, local_rows = (subs * ncf, columns), 2 * subs * ncf
    halves = [((nf, columns), BF16)] * 2
    products = [(faces, F32), (faces, F32), ((8, columns), F32), ((local_rows, columns), F32)]
    gathered = [pltpu.VMEM((nco, columns), BF16)]

    coarse_rounded, coarse, message = stage(
        bind(prepare), [(coarse_own, BF16), (coarse_own, F32), ((halo.height, columns), BF16)],
        right_side, face_weight, constraint, coarse_inverse, scratch=[pltpu.VMEM((halo.weight_count, columns), F32)],
    )
    message = shifted(message, 1)
    coarse_halves = gather_halves(coarse_rounded)
    next_inverse = shifted(coarse_inverse[:ncf], -1)

    part, back, forward = stage(
        bind(neumann_load), [(faces, F32)] + halves, right_side, face_weight, message, neumann
    )
    back, forward = shifted(back, -1), shifted(forward, 1)
    long, wide = ((2 * subs * nf, 2 * ncf), BF16), ((local_rows, 2 * nf), BF16)
    basis_high, basis_low, turned_high, turned_low, gram = stage(
        bind(static_basis), [long, long, wide, wide, ((local_rows, LANES), F32)], schur, message, constraint
    )
    local, product, quadratic, base, share = stage(
        bind(schur_load), products + [((ncf, columns + LANES), F32)],
        right_side, part, back, forward, face_weight, message, schur, turned_high, turned_low, gram,
    )
    share = shifted(share, -1)
    coarse_rounded, coarse, z_coarse, part, back, forward, sums = stage(
        bind(coarse_load),
        [(coarse_own, BF16), (coarse_own, F32), (coarse_own, F32), (faces, F32)] + halves + [((8, columns), F32)],
        *coarse_halves, coarse_inverse, message, next_inverse, share, coarse, base, gram, quadratic,
        basis_high, basis_low, product, scratch=gathered,
    )
    coarse_halves = gather_halves(coarse_rounded)
    back, forward = shifted(back, -1), shifted(forward, 1)
    image, part, back, forward = stage(
        bind(neumann_image), [(own, F32), (faces, F32)] + halves, part, back, forward, face_weight, message, neumann
    )
    back, forward = shifted(back, -1), shifted(forward, 1)
    y_local, product, quadratic, base = stage(
        bind(schur_image), products,
        image, part, back, forward, face_weight, message, schur, turned_high, turned_low,
    )
    sums, y_coarse, part, back = stage(
        bind(coarse_image), [((4, columns), F32), (coarse_own, F32), (own, F32), ((nf, columns), BF16)],
        *coarse_halves, coarse_inverse, message, coarse, base, gram, quadratic, basis_high, basis_low, product, sums,
        scratch=gathered,
    )
    sums = sum_all(sums)
    back = shifted(back, -1)
    return stage(
        bind(combine), [(own, F32), (own, F32)],
        sums, right_side, local, z_coarse, y_local, y_coarse, constraint, image, part, back,
    )


def solution(mesh):
    specs = P(("parts", AXIS), None)
    return jax.shard_map(shards, mesh=mesh, in_specs=(specs,) * 6, out_specs=(specs, specs), check_vma=False)
```

time: 121 us -> 82.8 us (0.68)
  local copies, waits for them, and re-layouts: 24.8 us -> 5.91 us
  Pallas kernels: 28.6 us -> 16.6 us
  blocking collectives: 9.9 us -> 0 us
  waiting for transfers between devices: 32 us -> 36.5 us
  other arithmetic: 1.46 us -> 0.04 us
    ppermute x0 -> x12, waiting for transfers between devices: none -> 23 us  [crossed(): lax.ppermute(block, AXIS, [(i, i ^ bit) for i in range(lax.axis_size(AXIS...]
    ppermute x10, waiting for transfers between devices: 32 us -> 13.5 us  [shifted(): lax.ppermute(block, AXIS, [((i - distance) % n, i) for i in range(n)])]
    unnamed x64 -> x28, local copies, waits for them, and re-layouts: 22.4 us -> 5.88 us
    ppermute x0 -> x12, starting transfers between devices: none -> 13 us  [crossed(): lax.ppermute(block, AXIS, [(i, i ^ bit) for i in range(lax.axis_size(AXIS...]
    pallas_call x8 -> x9, Pallas kernels: 28.6 us -> 16.6 us  [stage(): return call(*operands)]
    all_to_all x1 -> x0, blocking collectives: 9.9 us -> none  [from_all(): return lax.all_to_all(copies, AXIS, 0, 0)]
    all_to_all x2 -> x0, starting transfers between devices: 9.53 us -> none  [from_all(): return lax.all_to_all(copies, AXIS, 0, 0)]
    ppermute x10, starting transfers between devices: 13.4 us -> 9.64 us  [shifted(): lax.ppermute(block, AXIS, [((i - distance) % n, i) for i in range(n)])]
  transfers between devices with their start and end apart: 12 -> 22, of which waited for: 8 -> 14; matrix products, arithmetic and copies ran while one was open for 2% -> 0% of each run, Pallas kernels for 17% -> 14%
where the time goes in v4:
time: 82.8 us; the launch traced here: 82.5 us
  waiting for transfers between devices  36.5 us (44%)
  starting transfers between devices  22.6 us (27%)
  Pallas kernels  16.6 us (20%)
  local copies, waits for them, and re-layouts  5.91 us (7%)
  between operations  0.83 us (1%)
    ppermute x12, waiting for transfers between devices, crossed(): lax.ppermute(block, AXIS, [(i, i ^ bit) for i in range(lax.axis_size(AXIS...  23 us
    pallas_call x9, Pallas kernels, stage(): return call(*operands)  16.6 us
    ppermute x10, waiting for transfers between devices, shifted(): lax.ppermute(block, AXIS, [((i - distance) % n, i) for i in range(n)])  13.5 us
    ppermute x12, starting transfers between devices, crossed(): lax.ppermute(block, AXIS, [(i, i ^ bit) for i in range(lax.axis_size(AXIS...  13 us
    ppermute x10, starting transfers between devices, shifted(): lax.ppermute(block, AXIS, [((i - distance) % n, i) for i in range(n)])  9.64 us
    unnamed x28, local copies, waits for them, and re-layouts  5.88 us
  transfers between devices with their start and end apart: 22, of which 14 were waited for; matrix products, arithmetic and copies ran while one was open for 0% of the time, Pallas kernels for 14%

profile of v4, /device:TPU:0, one launch (start us, length us, event | category | flops | bytes accessed | tf_op | source)
XLA Modules:
  0.0 82.5 jit_solution(5186617064016415758)
XLA Ops:
  0.6 0.0 copy-start.1
  0.6 1.2 %copy-done.1 = f32[1024,256]{1,0:T(8,128)S(1)} copy-done((f32[1024,256]{1,0:T(8,128)S(1)}, f32[1024,256]{1,0:T(8,128)}, u32[]{:S(2)}) %copy-start.1) | copy-done | bytes 1048600
  1.9 0.9 %copy-done.5 = bf16[64,1024]{1,0:T(8,128)(2,1)S(1)} copy-done((bf16[64,1024]{1,0:T(8,128)(2,1)S(1)}, bf16[64,1024]{1,0:T(8,128)(2,1)}, u32[]{:S(2)}) %copy-start.5) | copy-done | bytes 131096
  2.8 0.8 %copy-done.7 = bf16[64,512]{1,0:T(8,128)(2,1)S(1)} copy-done((bf16[64,512]{1,0:T(8,128)(2,1)S(1)}, bf16[64,512]{1,0:T(8,128)(2,1)}, u32[]{:S(2)}) %copy-start.7) | copy-done | bytes 65560
  3.6 0.7 copy-done.9
  4.3 0.3 prepare.1
  4.6 4.1 %collective-permute-start = (bf16[64,256]{1,0:T(8,128)(2,1)S(1)}, bf16[64,256]{1,0:T(8,128)(2,1)S(1)}, u32[]{:S(2)}, u32[]{:S(2)}) collective-permute-start(bf16[64,256]{1,0:T(8,128)(2,1)S(1)} %get-tuple-element.37), channel_id=1, source_target_pairs={{0,8},{1,9},{2,10},{3,11},{4,12},{5,13},{6,14},{7,15},{8,0},{9,1},... | collective-permute-start | bytes 98312 | tf_op jit(solution)/shard_map/ppermute | solution.py:23
  8.7 2.2 %collective-permute-done = bf16[64,256]{1,0:T(8,128)(2,1)S(1)} collective-permute-done((bf16[64,256]{1,0:T(8,128)(2,1)S(1)}, bf16[64,256]{1,0:T(8,128)(2,1)S(1)}, u32[]{:S(2)}, u32[]{:S(2)}) %collective-permute-start) | collective-permute-done | bytes 32800 | tf_op jit(solution)/shard_map/ppermute | solution.py:23
  10.9 1.6 %collective-permute-start.1 = (bf16[128,256]{1,0:T(8,128)(2,1)S(1)}, bf16[128,256]{1,0:T(8,128)(2,1)S(1)}, u32[]{:S(2)}, u32[]{:S(2)}) collective-permute-start(bf16[128,256]{1,0:T(8,128)(2,1)S(1)} %pad_maximum_fusion.2), channel_id=1, source_target_pairs={{0,4},{1,5},{2,6},{3,7},{4,0},{5,1},{6,2},{7,3},{8,12},{9,13},{10,... | collective-permute-start | bytes 196616 | tf_op jit(solution)/shard_map/ppermute | solution.py:23
  12.5 2.7 %collective-permute-done.1 = bf16[128,256]{1,0:T(8,128)(2,1)S(1)} collective-permute-done((bf16[128,256]{1,0:T(8,128)(2,1)S(1)}, bf16[128,256]{1,0:T(8,128)(2,1)S(1)}, u32[]{:S(2)}, u32[]{:S(2)}) %collective-permute-start.1) | collective-permute-done | bytes 65568 | tf_op jit(solution)/shard_map/ppermute | solution.py:23
  15.2 4.7 %collective-permute-start.2 = (bf16[256,256]{1,0:T(8,128)(2,1)S(1)}, bf16[256,256]{1,0:T(8,128)(2,1)S(1)}, u32[]{:S(2)}, u32[]{:S(2)}) collective-permute-start(bf16[256,256]{1,0:T(8,128)(2,1)S(1)} %pad_maximum_fusion), channel_id=1, source_target_pairs={{0,2},{1,3},{2,0},{3,1},{4,6},{5,7},{6,4},{7,5},{8,10},{9,11},{10,... | collective-permute-start | bytes 393224 | tf_op jit(solution)/shard_map/ppermute | solution.py:23
  20.0 0.0 copy-start.3
  20.0 2.2 %copy-done.3 = bf16[2048,1024]{1,0:T(8,128)(2,1)S(1)} copy-done((bf16[2048,1024]{1,0:T(8,128)(2,1)S(1)}, bf16[2048,1024]{1,0:T(8,128)(2,1)}, u32[]{:S(2)}) %copy-start.3) | copy-done | bytes 4194328
  22.2 1.5 %neumann_load.1 = (f32[1536,256]{1,0:T(8,128)S(1)}, bf16[512,256]{1,0:T(8,128)(2,1)S(1)}, bf16[512,256]{1,0:T(8,128)(2,1)S(1)}) custom-call(f32[1024,256]{1,0:T(8,128)S(1)} %copy-done.1, f32[2,512]{1,0:T(2,128)S(1)} %copy-done.9, bf16[720,256]{1,0:T(8,128)(2,1)S(1)} %collective-permute-done.4.message.refs_5_, bf16[2048,1024]{1,0:T(8,128)(2,1)S(1)} %copy-done.3), custom_call_target="tpu_custom_call" | custom-call | tf_op jit(solution)/shard_map/neumann_load/pallas_call | solution.py:135
  23.7 0.1 collective-permute-start.6
  23.7 0.5 collective-permute-start.7
  24.3 0.4 collective-permute-start.3
  24.7 0.0 copy-start.2
  24.7 3.8 %collective-permute-start.5 = (bf16[32,1024]{1,0:T(8,128)(2,1)S(1)}, bf16[32,1024]{1,0:T(8,128)(2,1)S(1)}, u32[]{:S(2)}, u32[]{:S(2)}) collective-permute-start(bf16[32,1024]{1,0:T(8,128)(2,1)S(1)} %slice.3), channel_id=1, source_target_pairs={{1,0},{2,1},{3,2},{4,3},{5,4},{6,5},{7,6},{8,7},{9,8},{10,9},{11,1... | collective-permute-start | bytes 196616 | tf_op jit(solution)/shard_map/ppermute | solution.py:19
  28.4 1.9 %static_basis.1 = (bf16[2048,64]{1,0:T(8,128)(2,1)S(1)}, bf16[2048,64]{1,0:T(8,128)(2,1)S(1)}, bf16[128,1024]{1,0:T(8,128)(2,1)S(1)}, bf16[128,1024]{1,0:T(8,128)(2,1)S(1)}, f32[128,128]{1,0:T(8,128)S(1)}) custom-call(bf16[2048,1024]{1,0:T(8,128)(2,1)S(1)} %copy-done, bf16[720,256]{1,0:T(8,128)(2,1)S(1)} %collective-permute-done.4.message.refs_5_, ...), custom_call_target="tpu_custom_call" | custom-call | tf_op jit(solution)/shard_map/static_basis/pallas_call | solution.py:135
  30.3 0.0 collective-permute-done.6.refs_2_
  30.4 1.9 %collective-permute-done.7.refs_3_ = bf16[512,256]{1,0:T(8,128)(2,1)S(1)} collective-permute-done((bf16[512,256]{1,0:T(8,128)(2,1)S(1)}, bf16[512,256]{1,0:T(8,128)(2,1)S(1)}, u32[]{:S(2)}, u32[]{:S(2)}) %collective-permute-start.7) | collective-permute-done | bytes 262176 | tf_op jit(solution)/shard_map/ppermute | solution.py:19
  32.3 3.3 %schur_load.1 = (f32[1536,256]{1,0:T(8,128)S(1)}, f32[1536,256]{1,0:T(8,128)S(1)}, f32[8,256]{1,0:T(8,128)S(1)}, f32[128,256]{1,0:T(8,128)S(1)}, f32[32,384]{1,0:T(8,128)S(1)}) custom-call(f32[1024,256]{1,0:T(8,128)S(1)} %copy-done.2, f32[1536,256]{1,0:T(8,128)S(1)} %get-tuple-element.39.refs_1_, bf16[512,256]{1,0:T(8,128)(2,1)S(1)} %collective-permute-done.6.refs_2_, ...), custom_call_target="tpu_custom_call" | custom-call | tf_op jit(solution)/shard_map/schur_load/pallas_call | solution.py:135
  35.6 0.1 collective-permute-start.8
  35.7 1.7 %collective-permute-done.8.share = f32[32,384]{1,0:T(8,128)S(1)} collective-permute-done((f32[32,384]{1,0:T(8,128)S(1)}, f32[32,384]{1,0:T(8,128)S(1)}, u32[]{:S(2)}, u32[]{:S(2)}) %collective-permute-start.8) | collective-permute-done | bytes 49184 | tf_op jit(solution)/shard_map/ppermute | solution.py:19
  37.5 1.4 %coarse_load.1 = (bf16[64,256]{1,0:T(8,128)(2,1)S(1)}, f32[64,256]{1,0:T(8,128)S(1)}, f32[64,256]{1,0:T(8,128)S(1)}, f32[1536,256]{1,0:T(8,128)S(1)}, bf16[512,2...) custom-call(bf16[512,256]{1,0:T(8,128)(2,1)S(1)} %constant_dynamic-update-slice_fusion.half, ...), custom_call_target="tpu_custom_call" | custom-call | tf_op jit(solution)/shard_map/coarse_load/pallas_call | solution.py:135
  38.9 0.1 collective-permute-start.9
  39.0 4.5 %collective-permute-start.13 = (bf16[512,256]{1,0:T(8,128)(2,1)S(1)}, bf16[512,256]{1,0:T(8,128)(2,1)S(1)}, u32[]{:S(2)}, u32[]{:S(2)}) collective-permute-start(bf16[512,256]{1,0:T(8,128)(2,1)S(1)} %get-tuple-element.55), channel_id=1, source_target_pairs={{1,0},{2,1},{3,2},{4,3},{5,4},{6,5},{7,6},{8,7},{9,8},{10,9},{11,1... | collective-permute-start | bytes 786440 | tf_op jit(solution)/shard_map/ppermute | solution.py:19
  43.5 0.3 collective-permute-done.9
  43.8 5.0 %collective-permute-done.10 = bf16[128,256]{1,0:T(8,128)(2,1)S(1)} collective-permute-done((bf16[128,256]{1,0:T(8,128)(2,1)S(1)}, bf16[128,256]{1,0:T(8,128)(2,1)S(1)}, u32[]{:S(2)}, u32[]{:S(2)}) %collective-permute-start.10) | collective-permute-done | bytes 65568 | tf_op jit(solution)/shard_map/ppermute | solution.py:23
  48.8 1.4 %collective-permute-start.11 = (bf16[256,256]{1,0:T(8,128)(2,1)S(1)}, bf16[256,256]{1,0:T(8,128)(2,1)S(1)}, u32[]{:S(2)}, u32[]{:S(2)}) collective-permute-start(bf16[256,256]{1,0:T(8,128)(2,1)S(1)} %pad_maximum_fusion.1), channel_id=1, source_target_pairs={{0,2},{1,3},{2,0},{3,1},{4,6},{5,7},{6,4},{7,5},{8,10},{9,11},{10,... | collective-permute-start | bytes 393224 | tf_op jit(solution)/shard_map/ppermute | solution.py:23
  50.2 2.2 %collective-permute-done.14.from_previous = bf16[512,256]{1,0:T(8,128)(2,1)S(1)} collective-permute-done((bf16[512,256]{1,0:T(8,128)(2,1)S(1)}, bf16[512,256]{1,0:T(8,128)(2,1)S(1)}, u32[]{:S(2)}, u32[]{:S(2)}) %collective-permute-start.14) | collective-permute-done | bytes 262176 | tf_op jit(solution)/shard_map/ppermute | solution.py:19
  52.5 1.5 %neumann_image.1 = (f32[1024,256]{1,0:T(8,128)S(1)}, f32[1536,256]{1,0:T(8,128)S(1)}, bf16[512,256]{1,0:T(8,128)(2,1)S(1)}, bf16[512,256]{1,0:T(8,128)(2,1)S(1)}) custom-call(f32[1536,256]{1,0:T(8,128)S(1)} %get-tuple-element.54.part_in, bf16[512,256]{1,0:T(8,128)(2,1)S(1)} %collective-permute-done.13.from_next, ...), custom_call_target="tpu_custom_call" | custom-call | tf_op jit(solution)/shard_map/neumann_image/pallas_call | solution.py:135
  54.0 0.3 collective-permute-start.15
  54.3 0.3 collective-permute-start.16
  54.6 0.6 collective-permute-done.11
  55.2 0.1 collective-permute-start.12
  55.3 2.9 %collective-permute-done.15.refs_2_ = bf16[512,256]{1,0:T(8,128)(2,1)S(1)} collective-permute-done((bf16[512,256]{1,0:T(8,128)(2,1)S(1)}, bf16[512,256]{1,0:T(8,128)(2,1)S(1)}, u32[]{:S(2)}, u32[]{:S(2)}) %collective-permute-start.15) | collective-permute-done | bytes 262176 | tf_op jit(solution)/shard_map/ppermute | solution.py:19
  58.2 4.6 %collective-permute-done.16.refs_3_ = bf16[512,256]{1,0:T(8,128)(2,1)S(1)} collective-permute-done((bf16[512,256]{1,0:T(8,128)(2,1)S(1)}, bf16[512,256]{1,0:T(8,128)(2,1)S(1)}, u32[]{:S(2)}, u32[]{:S(2)}) %collective-permute-start.16) | collective-permute-done | bytes 262176 | tf_op jit(solution)/shard_map/ppermute | solution.py:19
  62.8 3.3 %schur_image.1 = (f32[1536,256]{1,0:T(8,128)S(1)}, f32[1536,256]{1,0:T(8,128)S(1)}, f32[8,256]{1,0:T(8,128)S(1)}, f32[128,256]{1,0:T(8,128)S(1)}) custom-call(f32[1024,256]{1,0:T(8,128)S(1)} %get-tuple-element.57.refs_0_.image, f32[1536,256]{1,0:T(8,128)S(1)} %get-tuple-element.58.refs_1_, bf16[512,256]{1,0:T(8,128)(2,1)S(1)} %collective-permute-done.15.refs_2_, ...), custom_call_target="tpu_custom_call" | custom-call | tf_op jit(solution)/shard_map/schur_image/pallas_call | solution.py:135
  66.1 1.4 %coarse_image.1 = (f32[4,256]{1,0:T(4,128)S(1)}, f32[64,256]{1,0:T(8,128)S(1)}, f32[1024,256]{1,0:T(8,128)S(1)}, bf16[512,256]{1,0:T(8,128)(2,1)S(1)}) custom-call(bf16[512,256]{1,0:T(8,128)(2,1)S(1)} %constant_dynamic-update-slice_fusion.4.half, bf16[512,256]{1,0:T(8,128)(2,1)S(1)} %collective-permute-done.12.crossed_half, bf16[64,1024]{1,0:T(8,128)(2,1)S(1)} %copy-done.6, ...), custom_call_target="tpu_custom_call" | custom-call | tf_op jit(solution)/shard_map/coarse_image/pallas_call | solution.py:135
  67.5 0.2 collective-permute-start.21
  67.7 4.5 %collective-permute-done.17 = f32[4,256]{1,0:T(4,128)S(1)} collective-permute-done((f32[4,256]{1,0:T(4,128)S(1)}, f32[4,256]{1,0:T(4,128)S(1)}, u32[]{:S(2)}, u32[]{:S(2)}) %collective-permute-start.17) | collective-permute-done | bytes 4128 | tf_op jit(solution)/shard_map/ppermute | solution.py:23
  72.2 0.7 collective-permute-start.18
  72.8 3.0 %collective-permute-done.18 = f32[4,256]{1,0:T(4,128)S(1)} collective-permute-done((f32[4,256]{1,0:T(4,128)S(1)}, f32[4,256]{1,0:T(4,128)S(1)}, u32[]{:S(2)}, u32[]{:S(2)}) %collective-permute-start.18) | collective-permute-done | bytes 4128 | tf_op jit(solution)/shard_map/ppermute | solution.py:23
  75.8 3.6 %collective-permute-done.19 = f32[4,256]{1,0:T(4,128)S(1)} collective-permute-done((f32[4,256]{1,0:T(4,128)S(1)}, f32[4,256]{1,0:T(4,128)S(1)}, u32[]{:S(2)}, u32[]{:S(2)}) %collective-permute-start.19) | collective-permute-done | bytes 4128 | tf_op jit(solution)/shard_map/ppermute | solution.py:23
  79.4 1.2 %collective-permute-done.20 = f32[4,256]{1,0:T(4,128)S(1)} collective-permute-done((f32[4,256]{1,0:T(4,128)S(1)}, f32[4,256]{1,0:T(4,128)S(1)}, u32[]{:S(2)}, u32[]{:S(2)}) %collective-permute-start.20) | collective-permute-done | bytes 4128 | tf_op jit(solution)/shard_map/ppermute | solution.py:23
  80.6 1.9 %combine.1 = (f32[1024,256]{1,0:T(8,128)}, f32[1024,256]{1,0:T(8,128)}) custom-call(f32[4,256]{1,0:T(4,128)S(1)} %add.15.sums, f32[1024,256]{1,0:T(8,128)S(1)} %copy-done.2, f32[1536,256]{1,0:T(8,128)S(1)} %get-tuple-element.66.z_local, f32[64,256]{1,0:T(8,128)S(1)} %get-tuple-element.67.z_coarse, f32[1536,256]{1,0:T(8,128)S(1)} %get-tuple-element.68.y_local, ...), custom_call_target="tpu_custom_call" | custom-call | tf_op jit(solution)/shard_map/combine/pallas_call | solution.py:135
  (44 shorter events, 0.1 us)
Async XLA Ops:
  0.6 1.2 %copy-start.1 = (f32[1024,256]{1,0:T(8,128)S(1)}, f32[1024,256]{1,0:T(8,128)}, u32[]{:S(2)}) copy-start(f32[1024,256]{1,0:T(8,128)} %load.5) | copy-start | bytes 3145732
  1.9 0.9 %copy-start.5 = (bf16[64,1024]{1,0:T(8,128)(2,1)S(1)}, bf16[64,1024]{1,0:T(8,128)(2,1)}, u32[]{:S(2)}) copy-start(bf16[64,1024]{1,0:T(8,128)(2,1)} %inverse.5) | copy-start | bytes 393220
  2.8 0.8 %copy-start.7 = (bf16[64,512]{1,0:T(8,128)(2,1)S(1)}, bf16[64,512]{1,0:T(8,128)(2,1)}, u32[]{:S(2)}) copy-start(bf16[64,512]{1,0:T(8,128)(2,1)} %rows.5) | copy-start | bytes 196612
  3.6 0.7 copy-start.9
  4.6 6.3 %collective-permute-start = (bf16[64,256]{1,0:T(8,128)(2,1)S(1)}, bf16[64,256]{1,0:T(8,128)(2,1)S(1)}, u32[]{:S(2)}, u32[]{:S(2)}) collective-permute-start(bf16[64,256]{1,0:T(8,128)(2,1)S(1)} %get-tuple-element.37), channel_id=1, source_target_pairs={{0,8},{1,9},{2,10},{3,11},{4,12},{5,13},{6,14},{7,15},{8,0},{9,1},... | collective-permute-start | bytes 98312 | tf_op jit(solution)/shard_map/ppermute | solution.py:23
  8.7 11.3 %collective-permute-start.4 = (bf16[720,256]{1,0:T(8,128)(2,1)S(1)}, bf16[720,256]{1,0:T(8,128)(2,1)S(1)}, u32[]{:S(2)}, u32[]{:S(2)}) collective-permute-start(bf16[720,256]{1,0:T(8,128)(2,1)S(1)} %get-tuple-element.38), channel_id=1, source_target_pairs={{15,0},{0,1},{1,2},{2,3},{3,4},{4,5},{5,6},{6,7},{7,8},{8,9},{9,10... | collective-permute-start | bytes 1105928 | tf_op jit(solution)/shard_map/ppermute | solution.py:19
  10.9 4.3 %collective-permute-start.1 = (bf16[128,256]{1,0:T(8,128)(2,1)S(1)}, bf16[128,256]{1,0:T(8,128)(2,1)S(1)}, u32[]{:S(2)}, u32[]{:S(2)}) collective-permute-start(bf16[128,256]{1,0:T(8,128)(2,1)S(1)} %pad_maximum_fusion.2), channel_id=1, source_target_pairs={{0,4},{1,5},{2,6},{3,7},{4,0},{5,1},{6,2},{7,3},{8,12},{9,13},{10,... | collective-permute-start | bytes 196616 | tf_op jit(solution)/shard_map/ppermute | solution.py:23
  15.2 9.0 %collective-permute-start.2 = (bf16[256,256]{1,0:T(8,128)(2,1)S(1)}, bf16[256,256]{1,0:T(8,128)(2,1)S(1)}, u32[]{:S(2)}, u32[]{:S(2)}) collective-permute-start(bf16[256,256]{1,0:T(8,128)(2,1)S(1)} %pad_maximum_fusion), channel_id=1, source_target_pairs={{0,2},{1,3},{2,0},{3,1},{4,6},{5,7},{6,4},{7,5},{8,10},{9,11},{10,... | collective-permute-start | bytes 393224 | tf_op jit(solution)/shard_map/ppermute | solution.py:23
  20.0 2.2 %copy-start.3 = (bf16[2048,1024]{1,0:T(8,128)(2,1)S(1)}, bf16[2048,1024]{1,0:T(8,128)(2,1)}, u32[]{:S(2)}) copy-start(bf16[2048,1024]{1,0:T(8,128)(2,1)} %neumann.3) | copy-start | bytes 12582916
  22.2 2.5 %copy-start.6 = (bf16[64,1024]{1,0:T(8,128)(2,1)S(1)}, bf16[64,1024]{1,0:T(8,128)(2,1)}, u32[]{:S(2)}) copy-start(bf16[64,1024]{1,0:T(8,128)(2,1)} %inverse.5) | copy-start | bytes 393220
  22.2 6.3 %copy-start = (bf16[2048,1024]{1,0:T(8,128)(2,1)S(1)}, bf16[2048,1024]{1,0:T(8,128)(2,1)}, u32[]{:S(2)}) copy-start(bf16[2048,1024]{1,0:T(8,128)(2,1)} %refs_6_.3) | copy-start | bytes 12582916
  22.2 6.3 %copy-start.8 = (bf16[64,512]{1,0:T(8,128)(2,1)S(1)}, bf16[64,512]{1,0:T(8,128)(2,1)}, u32[]{:S(2)}) copy-start(bf16[64,512]{1,0:T(8,128)(2,1)} %rows.5) | copy-start | bytes 196612
  23.7 6.7 %collective-permute-start.6 = (bf16[512,256]{1,0:T(8,128)(2,1)S(1)}, bf16[512,256]{1,0:T(8,128)(2,1)S(1)}, u32[]{:S(2)}, u32[]{:S(2)}) collective-permute-start(bf16[512,256]{1,0:T(8,128)(2,1)S(1)} %get-tuple-element.40), channel_id=1, source_target_pairs={{1,0},{2,1},{3,2},{4,3},{5,4},{6,5},{7,6},{8,7},{9,8},{10,9},{11,1... | collective-permute-start | bytes 786440 | tf_op jit(solution)/shard_map/ppermute | solution.py:19
  23.7 8.6 %collective-permute-start.7 = (bf16[512,256]{1,0:T(8,128)(2,1)S(1)}, bf16[512,256]{1,0:T(8,128)(2,1)S(1)}, u32[]{:S(2)}, u32[]{:S(2)}) collective-permute-start(bf16[512,256]{1,0:T(8,128)(2,1)S(1)} %get-tuple-element.41), channel_id=1, source_target_pairs={{15,0},{0,1},{1,2},{2,3},{3,4},{4,5},{5,6},{6,7},{7,8},{8,9},{9,10... | collective-permute-start | bytes 786440 | tf_op jit(solution)/shard_map/ppermute | solution.py:19
  24.3 11.5 %collective-permute-start.3 = (bf16[512,256]{1,0:T(8,128)(2,1)S(1)}, bf16[512,256]{1,0:T(8,128)(2,1)S(1)}, u32[]{:S(2)}, u32[]{:S(2)}) collective-permute-start(bf16[512,256]{1,0:T(8,128)(2,1)S(1)} %constant_dynamic-update-slice_fusion.half), channel_id=1, source_target_pairs={{0,1},{1,0},{2,3},{3,2},{4,5},{5,4},{6,7},{7,6},{8,9},{9,8},{10,11... | collective-permute-start | bytes 786440 | tf_op jit(solution)/shard_map/ppermute | solution.py:23
  24.7 7.7 %copy-start.2 = (f32[1024,256]{1,0:T(8,128)S(1)}, f32[1024,256]{1,0:T(8,128)}, u32[]{:S(2)}) copy-start(f32[1024,256]{1,0:T(8,128)} %load.5) | copy-start | bytes 3145732
  24.7 11.0 %collective-permute-start.5 = (bf16[32,1024]{1,0:T(8,128)(2,1)S(1)}, bf16[32,1024]{1,0:T(8,128)(2,1)S(1)}, u32[]{:S(2)}, u32[]{:S(2)}) collective-permute-start(bf16[32,1024]{1,0:T(8,128)(2,1)S(1)} %slice.3), channel_id=1, source_target_pairs={{1,0},{2,1},{3,2},{4,3},{5,4},{6,5},{7,6},{8,7},{9,8},{10,9},{11,1... | collective-permute-start | bytes 196616 | tf_op jit(solution)/shard_map/ppermute | solution.py:19
  35.6 1.8 %collective-permute-start.8 = (f32[32,384]{1,0:T(8,128)S(1)}, f32[32,384]{1,0:T(8,128)S(1)}, u32[]{:S(2)}, u32[]{:S(2)}) collective-permute-start(f32[32,384]{1,0:T(8,128)S(1)} %get-tuple-element.45), channel_id=1, source_target_pairs={{1,0},{2,1},{3,2},{4,3},{5,4},{6,5},{7,6},{8,7},{9,8},{10,9},{11,1... | collective-permute-start | bytes 147464 | tf_op jit(solution)/shard_map/ppermute | solution.py:19
  37.5 15.0 %copy-start.4 = (bf16[2048,1024]{1,0:T(8,128)(2,1)S(1)}, bf16[2048,1024]{1,0:T(8,128)(2,1)}, u32[]{:S(2)}) copy-start(bf16[2048,1024]{1,0:T(8,128)(2,1)} %neumann.3) | copy-start | bytes 12582916
  37.5 15.0 %copy-start.10 = (f32[2,512]{1,0:T(2,128)S(1)}, f32[2,512]{1,0:T(2,128)}, u32[]{:S(2)}) copy-start(f32[2,512]{1,0:T(2,128)} %refs_4_.3) | copy-start | bytes 12292
  38.9 4.9 %collective-permute-start.9 = (bf16[64,256]{1,0:T(8,128)(2,1)S(1)}, bf16[64,256]{1,0:T(8,128)(2,1)S(1)}, u32[]{:S(2)}, u32[]{:S(2)}) collective-permute-start(bf16[64,256]{1,0:T(8,128)(2,1)S(1)} %get-tuple-element.52), channel_id=1, source_target_pairs={{0,8},{1,9},{2,10},{3,11},{4,12},{5,13},{6,14},{7,15},{8,0},{9,1},... | collective-permute-start | bytes 98312 | tf_op jit(solution)/shard_map/ppermute | solution.py:23
  39.0 11.2 %collective-permute-start.13 = (bf16[512,256]{1,0:T(8,128)(2,1)S(1)}, bf16[512,256]{1,0:T(8,128)(2,1)S(1)}, u32[]{:S(2)}, u32[]{:S(2)}) collective-permute-start(bf16[512,256]{1,0:T(8,128)(2,1)S(1)} %get-tuple-element.55), channel_id=1, source_target_pairs={{1,0},{2,1},{3,2},{4,3},{5,4},{6,5},{7,6},{8,7},{9,8},{10,9},{11,1... | collective-permute-start | bytes 786440 | tf_op jit(solution)/shard_map/ppermute | solution.py:19
  43.5 9.0 %collective-permute-start.14 = (bf16[512,256]{1,0:T(8,128)(2,1)S(1)}, bf16[512,256]{1,0:T(8,128)(2,1)S(1)}, u32[]{:S(2)}, u32[]{:S(2)}) collective-permute-start(bf16[512,256]{1,0:T(8,128)(2,1)S(1)} %get-tuple-element.56), channel_id=1, source_target_pairs={{15,0},{0,1},{1,2},{2,3},{3,4},{4,5},{5,6},{6,7},{7,8},{8,9},{9,10... | collective-permute-start | bytes 786440 | tf_op jit(solution)/shard_map/ppermute | solution.py:19
  43.8 5.0 %collective-permute-start.10 = (bf16[128,256]{1,0:T(8,128)(2,1)S(1)}, bf16[128,256]{1,0:T(8,128)(2,1)S(1)}, u32[]{:S(2)}, u32[]{:S(2)}) collective-permute-start(bf16[128,256]{1,0:T(8,128)(2,1)S(1)} %pad_maximum_fusion.3), channel_id=1, source_target_pairs={{0,4},{1,5},{2,6},{3,7},{4,0},{5,1},{6,2},{7,3},{8,12},{9,13},{10,... | collective-permute-start | bytes 196616 | tf_op jit(solution)/shard_map/ppermute | solution.py:23
  48.8 6.4 %collective-permute-start.11 = (bf16[256,256]{1,0:T(8,128)(2,1)S(1)}, bf16[256,256]{1,0:T(8,128)(2,1)S(1)}, u32[]{:S(2)}, u32[]{:S(2)}) collective-permute-start(bf16[256,256]{1,0:T(8,128)(2,1)S(1)} %pad_maximum_fusion.1), channel_id=1, source_target_pairs={{0,2},{1,3},{2,0},{3,1},{4,6},{5,7},{6,4},{7,5},{8,10},{9,11},{10,... | collective-permute-start | bytes 393224 | tf_op jit(solution)/shard_map/ppermute | solution.py:23
  54.0 4.2 %collective-permute-start.15 = (bf16[512,256]{1,0:T(8,128)(2,1)S(1)}, bf16[512,256]{1,0:T(8,128)(2,1)S(1)}, u32[]{:S(2)}, u32[]{:S(2)}) collective-permute-start(bf16[512,256]{1,0:T(8,128)(2,1)S(1)} %get-tuple-element.59), channel_id=1, source_target_pairs={{1,0},{2,1},{3,2},{4,3},{5,4},{6,5},{7,6},{8,7},{9,8},{10,9},{11,1... | collective-permute-start | bytes 786440 | tf_op jit(solution)/shard_map/ppermute | solution.py:19
  54.3 8.5 %collective-permute-start.16 = (bf16[512,256]{1,0:T(8,128)(2,1)S(1)}, bf16[512,256]{1,0:T(8,128)(2,1)S(1)}, u32[]{:S(2)}, u32[]{:S(2)}) collective-permute-start(bf16[512,256]{1,0:T(8,128)(2,1)S(1)} %get-tuple-element.60), channel_id=1, source_target_pairs={{15,0},{0,1},{1,2},{2,3},{3,4},{4,5},{5,6},{6,7},{7,8},{8,9},{9,10... | collective-permute-start | bytes 786440 | tf_op jit(solution)/shard_map/ppermute | solution.py:19
  55.2 10.9 %collective-permute-start.12 = (bf16[512,256]{1,0:T(8,128)(2,1)S(1)}, bf16[512,256]{1,0:T(8,128)(2,1)S(1)}, u32[]{:S(2)}, u32[]{:S(2)}) collective-permute-start(bf16[512,256]{1,0:T(8,128)(2,1)S(1)} %constant_dynamic-update-slice_fusion.4.half), channel_id=1, source_target_pairs={{0,1},{1,0},{2,3},{3,2},{4,5},{5,4},{6,7},{7,6},{8,9},{9,8},{10,11... | collective-permute-start | bytes 786440 | tf_op jit(solution)/shard_map/ppermute | solution.py:23
  67.5 13.1 %collective-permute-start.21 = (bf16[512,256]{1,0:T(8,128)(2,1)S(1)}, bf16[512,256]{1,0:T(8,128)(2,1)S(1)}, u32[]{:S(2)}, u32[]{:S(2)}) collective-permute-start(bf16[512,256]{1,0:T(8,128)(2,1)S(1)} %get-tuple-element.71), channel_id=1, source_target_pairs={{1,0},{2,1},{3,2},{4,3},{5,4},{6,5},{7,6},{8,7},{9,8},{10,9},{11,1... | collective-permute-start | bytes 786440 | tf_op jit(solution)/shard_map/ppermute | solution.py:19
  67.7 4.5 %collective-permute-start.17 = (f32[4,256]{1,0:T(4,128)S(1)}, f32[4,256]{1,0:T(4,128)S(1)}, u32[]{:S(2)}, u32[]{:S(2)}) collective-permute-start(f32[4,256]{1,0:T(4,128)S(1)} %get-tuple-element.65), channel_id=1, source_target_pairs={{0,8},{1,9},{2,10},{3,11},{4,12},{5,13},{6,14},{7,15},{8,0},{9,1},... | collective-permute-start | bytes 12296 | tf_op jit(solution)/shard_map/ppermute | solution.py:23
  72.2 3.6 %collective-permute-start.18 = (f32[4,256]{1,0:T(4,128)S(1)}, f32[4,256]{1,0:T(4,128)S(1)}, u32[]{:S(2)}, u32[]{:S(2)}) collective-permute-start(f32[4,256]{1,0:T(4,128)S(1)} %add.12), channel_id=1, source_target_pairs={{0,4},{1,5},{2,6},{3,7},{4,0},{5,1},{6,2},{7,3},{8,12},{9,13},{10,... | collective-permute-start | bytes 12296 | tf_op jit(solution)/shard_map/ppermute | solution.py:23
  75.8 3.6 %collective-permute-start.19 = (f32[4,256]{1,0:T(4,128)S(1)}, f32[4,256]{1,0:T(4,128)S(1)}, u32[]{:S(2)}, u32[]{:S(2)}) collective-permute-start(f32[4,256]{1,0:T(4,128)S(1)} %add.13), channel_id=1, source_target_pairs={{0,2},{1,3},{2,0},{3,1},{4,6},{5,7},{6,4},{7,5},{8,10},{9,11},{10,... | collective-permute-start | bytes 12296 | tf_op jit(solution)/shard_map/ppermute | solution.py:23
  79.4 1.2 %collective-permute-start.20 = (f32[4,256]{1,0:T(4,128)S(1)}, f32[4,256]{1,0:T(4,128)S(1)}, u32[]{:S(2)}, u32[]{:S(2)}) collective-permute-start(f32[4,256]{1,0:T(4,128)S(1)} %add.14), channel_id=1, source_target_pairs={{0,1},{1,0},{2,3},{3,2},{4,5},{5,4},{6,7},{7,6},{8,9},{9,8},{10,11... | collective-permute-start | bytes 12296 | tf_op jit(solution)/shard_map/ppermute | solution.py:23

commit v5 on v4

v5 whole, which is shorter than its diff:
```python
import functools

import jax
import jax.numpy as jnp
from jax import lax
from jax.experimental import pallas as pl
from jax.experimental.pallas import tpu as pltpu
from jax.sharding import PartitionSpec as P

AXIS = "sub"
BF16 = jnp.bfloat16
F32 = jnp.float32
LANES = 128
VMEM_BYTES = 20 * 2**20


def shifted(block, distance):
    n = lax.axis_size(AXIS)
    return lax.ppermute(block, AXIS, [((i - distance) % n, i) for i in range(n)])


def crossed(block, bit):
    return lax.ppermute(block, AXIS, [(i, i ^ bit) for i in range(lax.axis_size(AXIS))])


def bits():
    return [1 << k for k in reversed(range(lax.axis_size(AXIS).bit_length() - 1))]


def gather_halves(block):
    for bit in bits()[:-1]:
        block = jnp.concatenate([block, crossed(block, bit)], axis=0)
    return block, crossed(block, 1)


def half_order():
    order = [0]
    for bit in bits()[:-1]:
        order += [place ^ bit for place in order]
    return order


def dot(a, b):
    return jnp.dot(a, b, preferred_element_type=F32)


def dot_nt(a, b):
    return lax.dot_general(a, b, (((1,), (1,)), ((), ())), preferred_element_type=F32)


def dot_tn(a, b):
    return lax.dot_general(a, b, (((0,), (0,)), ((), ())), preferred_element_type=F32)


def split(x):
    high = x.astype(BF16)
    return high, (x - high.astype(F32)).astype(BF16)


def split_dot(a, b, contract=dot):
    high, low = split(b)
    if isinstance(a, tuple):
        return contract(a[0], high) + contract(a[0], low) + contract(a[1], high)
    return contract(a, high) + contract(a, low)


def column_sum(x):
    return jnp.sum(x, axis=0, keepdims=True)


def rows_of(ref, index, count):
    return ref[index * count : (index + 1) * count]


def column_of(row):
    return jnp.broadcast_to(row, (8, row.shape[1])).T[:, :1]


def parts_of(row):
    high = row.astype(BF16).astype(F32)
    middle = (row - high).astype(BF16).astype(F32)
    return high, middle, row - high - middle


class Halo:
    def __init__(self, nf, ncf, nco, columns):
        self.nf, self.ncf, self.columns = nf, ncf, columns
        self.folds = nf // columns
        self.inverse_folds = nco // columns
        self.first_height = nf + ncf * self.folds
        self.at_weight = nf + ncf * self.inverse_folds
        self.weight_count = -(-3 * self.folds // 16) * 16
        self.second_height = self.at_weight + self.weight_count

    def unfolded(self, message, folds):
        start, ncf = self.nf, self.ncf
        return jnp.concatenate([message[start + k * ncf : start + (k + 1) * ncf] for k in range(folds)], axis=1)

    def fold(self, message, block, folds):
        start, ncf, columns = self.nf, self.ncf, self.columns
        for k in range(folds):
            message[start + k * ncf : start + (k + 1) * ncf] = block[:, k * columns : (k + 1) * columns]

    def product(self, message):
        return message[: self.nf].astype(F32)

    def rows(self, message):
        return self.unfolded(message, self.folds)

    def inverse(self, message):
        return self.unfolded(message, self.inverse_folds)

    def weight(self, message):
        got = message[self.at_weight : self.second_height].astype(F32)
        f = self.folds
        row = [sum(got[k * f + i : k * f + i + 1] for k in range(3)) for i in range(f)]
        return jnp.concatenate([column_of(piece) for piece in row], axis=0)


def all_rows(halo, message, rows):
    ncf = halo.ncf
    return [halo.rows(message)] + [rows_of(rows, j, ncf) for j in range(rows.shape[0] // ncf)]


def all_weights(halo, message, weight):
    return [halo.weight(message)] + [column_of(weight[j : j + 1]) for j in range(weight.shape[0])]


def stage(kernel, shapes, *operands, scratch=(), fetched=0):
    out = [jax.ShapeDtypeStruct(shape, dtype) for shape, dtype in shapes]
    params = pltpu.CompilerParams(vmem_limit_bytes=VMEM_BYTES)
    spaces = [pltpu.HBM] * fetched + [pltpu.VMEM] * (len(operands) - fetched)
    call = pl.pallas_call(
        kernel,
        out_shape=out,
        in_specs=[pl.BlockSpec(memory_space=space) for space in spaces],
        scratch_shapes=list(scratch),
        compiler_params=params,
        name=kernel.func.__name__,
    )
    return call(*operands)


def prepare(halo, load, rows, weight, load_here, rows_here, weight_here, coarse_rounded, coarse, done):
    ncf, nf = halo.ncf, halo.nf
    subs = load.shape[0] // nf
    copies = [pltpu.make_async_copy(rows, rows_here, done.at[subs])]
    copies += [
        pltpu.make_async_copy(rows_of(load.at, j, nf), rows_of(load_here.at, j, nf), done.at[j]) for j in range(subs)
    ]
    copies.append(pltpu.make_async_copy(weight, weight_here, done.at[subs + 1]))
    for copy in copies:
        copy.start()
    copies[0].wait()
    for j in range(subs):
        copies[1 + j].wait()
        coarse[j * ncf : (j + 1) * ncf] = dot(rows_of(rows_here, j, ncf), rows_of(load_here, j, nf).astype(BF16))
    coarse_rounded[...] = coarse[...].astype(BF16)
    copies[-1].wait()


def first_message(halo, load, weight, rows, message):
    ncf, nf = halo.ncf, halo.nf
    message[:nf] = ((1.0 - column_of(weight[weight.shape[0] - 1 :])) * load[load.shape[0] - nf :]).astype(BF16)
    halo.fold(message, rows[rows.shape[0] - ncf :], halo.folds)


def fetch(halo, neumann, schur, inverse, neumann_here, schur_here, inverse_here, done):
    pairs = ((neumann, neumann_here), (schur, schur_here), (inverse, inverse_here))
    copies = [pltpu.make_async_copy(source, here, done.at[k]) for k, (source, here) in enumerate(pairs)]
    for copy in copies:
        copy.start()
    for copy in copies:
        copy.wait()


def neumann_products(left, right, weights, neumann, part, back, forward):
    subs, nf = len(left), left[0].shape[0]
    previous = None
    for j in range(subs):
        product = dot(rows_of(neumann, j, 2 * nf), jnp.concatenate([left[j], right[j]], axis=0))
        first, second = product[:nf], product[nf:]
        if j == 0:
            part[:nf] = first
            back[...] = first.astype(BF16)
        else:
            part[j * nf : (j + 1) * nf] = weights[j] * previous + (1.0 - weights[j]) * first
        previous = second
    part[subs * nf :] = previous
    forward[:nf] = previous.astype(BF16)


def neumann_load(halo, load, weight, message, neumann, inverse, part, back, forward, pieces):
    subs, nf = weight.shape
    ncf, columns, folds = halo.ncf, halo.columns, halo.folds
    halo.fold(forward, inverse[inverse.shape[0] - ncf :], halo.inverse_folds)
    pieces[...] = jnp.zeros_like(pieces)
    for k, values in enumerate(parts_of(weight[subs - 1 : subs])):
        for i in range(folds):
            pieces[k * folds + i : k * folds + i + 1] = values[:, i * columns : (i + 1) * columns]
    forward[halo.at_weight :] = pieces[...].astype(BF16)
    weights = [None] + [column_of(weight[j : j + 1]) for j in range(subs)]
    left = [message[:nf]]
    left += [((1.0 - weights[j]) * rows_of(load, j - 1, nf)).astype(BF16) for j in range(1, subs)]
    right = [(weights[j + 1] * rows_of(load, j, nf)).astype(BF16) for j in range(subs)]
    neumann_products(left, right, weights, neumann, part, back, forward)


def neumann_image(halo, part_in, from_next, from_previous, weight, message, neumann, image, part, back, forward):
    subs, nf = weight.shape
    weights = all_weights(halo, message, weight)
    faces = [rows_of(part_in, e, nf) for e in range(subs + 1)]
    faces[0] = faces[0] + from_previous[...].astype(F32)
    faces[subs] = faces[subs] + from_next[...].astype(F32)
    for e in range(1, subs + 1):
        image[(e - 1) * nf : e * nf] = faces[e]
    left = [((1.0 - weights[j]) * faces[j]).astype(BF16) for j in range(subs)]
    right = [(weights[j + 1] * faces[j + 1]).astype(BF16) for j in range(subs)]
    neumann_products(left, right, weights, neumann, part, back, forward)


def static_basis(halo, schur, message, rows, basis_high, basis_low, turned_high, turned_low, gram):
    ncf, nf = halo.ncf, halo.nf
    blocks = all_rows(halo, message, rows)
    gram[...] = jnp.zeros_like(gram)
    for j in range(len(blocks) - 1):
        matrix, pair = rows_of(schur, j, 2 * nf), blocks[j : j + 2]
        basis = jnp.concatenate([dot_nt(matrix[:, k * nf : (k + 1) * nf], pair[k]) for k in range(2)], axis=1)
        long, wide = slice(2 * j * nf, 2 * (j + 1) * nf), slice(2 * j * ncf, 2 * (j + 1) * ncf)
        basis_high[long], basis_low[long] = split(basis)
        turned = split(basis.T)
        turned_high[wide], turned_low[wide] = turned
        for k in range(2):
            half = slice(k * nf, (k + 1) * nf)
            gram[wide, k * ncf : (k + 1) * ncf] = dot_nt(turned[0][:, half], pair[k]) + dot_nt(turned[1][:, half], pair[k])


def schur_products(
    halo, other, part, from_next, from_previous, weight, message, schur, turned_high, turned_low,
    local, product, quadratic, base,
):
    subs, nf = weight.shape
    ncf, columns = halo.ncf, halo.columns
    weights = all_weights(halo, message, weight)
    local[:nf] = (1.0 - weights[0]) * part[:nf] + weights[0] * halo.product(from_previous)
    for e in range(1, subs):
        local[e * nf : (e + 1) * nf] = rows_of(part, e, nf)
    local[subs * nf :] = weights[subs] * part[subs * nf :] + (1.0 - weights[subs]) * from_next[...].astype(F32)
    energy, previous = 0.0, None
    for j in range(subs):
        vector = local[j * nf : (j + 2) * nf]
        high, low = split(vector)
        both = dot(rows_of(schur, j, 2 * nf), jnp.concatenate([high, low], axis=1))
        result = both[:, :columns] + both[:, columns:]
        energy = energy + column_sum(vector * result)
        first = result[:nf]
        product[j * nf : (j + 1) * nf] = first if j == 0 else previous + first
        previous = result[nf:]
        here = slice(2 * j * ncf, 2 * (j + 1) * ncf)
        base[here] = dot(turned_high[here], high) + dot(turned_high[here], low) + dot(turned_low[here], high)
    product[subs * nf :] = previous
    quadratic[0:1] = energy
    quadratic[1:2] = column_sum(other[...] * local[nf:])


def schur_load(halo, load, part, from_next, from_previous, weight, schur, turned_high, turned_low, *outs):
    schur_products(
        halo, load, part, from_next, from_previous, weight, from_previous, schur, turned_high, turned_low, *outs
    )


def schur_image(halo, *refs):
    schur_products(halo, *refs)


def placed(half, crossed_half):
    me = lax.axis_index(AXIS)
    order = half_order()
    count = half.shape[0] // len(order)
    for flip, blocks in ((0, half), (1, crossed_half)):
        for k, place in enumerate(order):
            yield me ^ (place ^ flip), blocks, k * count, (k + 1) * count


def coarse_shares(ncf, results):
    shares = [results[0][:ncf]]
    for before, after in zip(results[:-1], results[1:]):
        shares.append(before[ncf:] + after[:ncf])
    return shares + [results[-1][ncf:]]


def coarse_products(ncf, x, base, gram):
    results, energy = [], 0.0
    for j in range(len(x) - 1):
        here = slice(2 * j * ncf, 2 * (j + 1) * ncf)
        pair = jnp.concatenate([x[j], x[j + 1]], axis=0)
        change = split_dot(split(gram[here, : 2 * ncf]), pair)
        energy = energy + column_sum(pair * (2.0 * base[here] + change))
        results.append(base[here] + change)
    return results, energy


def add_basis(nf, x, basis_high, basis_low, product):
    faces = [rows_of(product, e, nf) for e in range(len(x))]
    for j in range(len(x) - 1):
        here = slice(2 * j * nf, 2 * (j + 1) * nf)
        pair = jnp.concatenate([x[j], x[j + 1]], axis=0)
        change = split_dot((basis_high[here], basis_low[here]), pair)
        faces[j] = faces[j] + change[:nf]
        faces[j + 1] = faces[j + 1] + change[nf:]
    return faces


def coarse_load(
    halo, half, crossed_half, inverse, message, coarse, base, gram, quadratic, basis_high, basis_low, product,
    shares_rounded, shares, solution, part, back, forward, sums, gathered,
):
    ncf, nf = halo.ncf, halo.nf
    subs = inverse.shape[0] // ncf
    for place, blocks, start, stop in placed(half, crossed_half):
        gathered[pl.ds(pl.multiple_of(place * subs * ncf, subs * ncf), subs * ncf)] = blocks[start:stop]
    everything = gathered[...]
    own = dot(inverse[...], everything)
    x = [dot(halo.inverse(message), everything)] + [own[j * ncf : (j + 1) * ncf] for j in range(subs)]
    results, energy = coarse_products(ncf, x, base, gram)
    for e, share in enumerate(coarse_shares(ncf, results)):
        shares[e * ncf : (e + 1) * ncf] = share
    shares_rounded[...] = shares[...].astype(BF16)
    solution[...] = own
    sums[0:1] = quadratic[1:2] + column_sum(coarse[...] * own)
    sums[1:2] = quadratic[0:1] + energy
    faces = add_basis(nf, x, basis_high, basis_low, product)
    for e in range(subs + 1):
        part[e * nf : (e + 1) * nf] = faces[e]
    back[...] = faces[0].astype(BF16)
    forward[...] = faces[subs].astype(BF16)


def coarse_image(
    halo, half, crossed_half, inverse, message, shares, base, gram, quadratic, basis_high, basis_low, product, sums_in,
    sums, solution, part, back, gathered,
):
    ncf, nf = halo.ncf, halo.nf
    subs = inverse.shape[0] // ncf
    total = gathered.shape[0]
    for place, blocks, start, stop in placed(half, crossed_half):
        gathered[pl.ds(pl.multiple_of(place * subs * ncf, subs * ncf), subs * ncf)] = blocks[start + ncf : stop].astype(F32)
    for place, blocks, start, stop in placed(half, crossed_half):
        before = pl.multiple_of(lax.rem(place * subs * ncf + (total - ncf), total), ncf)
        gathered[pl.ds(before, ncf)] += blocks[start : start + ncf].astype(F32)
    everything = gathered[...]
    own = split_dot(inverse[...], everything)
    x = [split_dot(halo.inverse(message), everything)] + [own[j * ncf : (j + 1) * ncf] for j in range(subs)]
    _, energy = coarse_products(ncf, x, base, gram)
    sums[0:2] = sums_in[0:2]
    sums[2:3] = quadratic[1:2] + sum(column_sum(rows_of(shares, e, ncf) * x[e]) for e in range(subs + 1))
    sums[3:4] = quadratic[0:1] + energy
    solution[...] = own
    faces = add_basis(nf, x, basis_high, basis_low, product)
    for e in range(1, subs + 1):
        part[(e - 1) * nf : e * nf] = faces[e]
    back[...] = faces[0].astype(BF16)


def complete(halo, z_local, z_coarse, y_local, y_coarse, rows, z, y):
    ncf, nf = halo.ncf, halo.nf
    for j in range(rows.shape[0] // ncf):
        here, beside = slice(j * nf, (j + 1) * nf), slice((j + 1) * nf, (j + 2) * nf)
        for local, coarse, whole in ((z_local, z_coarse, z), (y_local, y_coarse, y)):
            whole[here] = local[beside] + split_dot(rows_of(rows, j, ncf), rows_of(coarse, j, ncf), dot_tn)


def combine(halo, sums, load, z, y, image, part, from_next, solution, residual):
    nf = halo.nf
    a, b, c, d = (sums[k : k + 1] for k in range(4))
    step = a / b
    grow = step * (c / b)
    next_step = (grow - 1.0) / ((d - c * (c / b)) * (step / b))
    s = step + next_step * grow
    t = step * next_step
    solution[...] = s * z[...] - t * y[...]
    last = load.shape[0] - nf
    residual[:last] = load[:last] - s * image[:last] + t * part[:last]
    residual[last:] = load[last:] - s * image[last:] + t * (part[last:] + from_next[...].astype(F32))


def shards(right_side, face_weight, schur, neumann, constraint, coarse_inverse):
    subs, nf = face_weight.shape
    ncf = constraint.shape[0] // subs
    nco = coarse_inverse.shape[1]
    columns = right_side.shape[1]
    halo = Halo(nf, ncf, nco, columns)
    bind = lambda kernel: functools.partial(kernel, halo)
    faces, own = ((subs + 1) * nf, columns), (subs * nf, columns)
    coarse_own, local_rows = (subs * ncf, columns), 2 * subs * ncf
    halves = [((nf, columns), BF16)] * 2
    products = [(faces, F32), (faces, F32), ((8, columns), F32), ((local_rows, columns), F32)]
    semaphores = lambda count: [pltpu.SemaphoreType.DMA((count,))]
    described = lambda array: (array.shape, array.dtype)

    load, rows, weight, coarse_rounded, coarse = stage(
        bind(prepare),
        [described(right_side), described(constraint), described(face_weight), (coarse_own, BF16), (coarse_own, F32)],
        right_side, constraint, face_weight, scratch=semaphores(subs + 2), fetched=3,
    )
    (first,) = stage(bind(first_message), [((halo.first_height, columns), BF16)], load, weight, rows)
    coarse_halves = gather_halves(coarse_rounded)
    tied, _ = lax.optimization_barrier(((neumann, schur, coarse_inverse), first))
    neumann, schur, inverse = stage(
        bind(fetch), [described(array) for array in tied], *tied, scratch=semaphores(3), fetched=3
    )
    first = shifted(first, 1)
    part, back, forward = stage(
        bind(neumann_load), [(faces, F32), ((nf, columns), BF16), ((halo.second_height, columns), BF16)],
        load, weight, first, neumann, inverse, scratch=[pltpu.VMEM((halo.weight_count, columns), F32)],
    )
    back, second = shifted(back, -1), shifted(forward, 1)
    long, wide = ((2 * subs * nf, 2 * ncf), BF16), ((local_rows, 2 * nf), BF16)
    basis_high, basis_low, turned_high, turned_low, gram = stage(
        bind(static_basis), [long, long, wide, wide, ((local_rows, LANES), F32)], schur, first, rows
    )
    z_local, product, quadratic, base = stage(
        bind(schur_load), products, load, part, back, second, weight, schur, turned_high, turned_low
    )
    share_rows = ((subs + 1) * ncf, columns)
    shares_rounded, shares, z_coarse, part, back, forward, sums = stage(
        bind(coarse_load),
        [(share_rows, BF16), (share_rows, F32), (coarse_own, F32), (faces, F32)] + halves + [((8, columns), F32)],
        *coarse_halves, inverse, second, coarse, base, gram, quadratic, basis_high, basis_low, product,
        scratch=[pltpu.VMEM((nco, columns), BF16)],
    )
    coarse_halves = gather_halves(shares_rounded)
    back, forward = shifted(back, -1), shifted(forward, 1)
    image, part, back, forward = stage(
        bind(neumann_image), [(own, F32), (faces, F32)] + halves, part, back, forward, weight, second, neumann
    )
    back, forward = shifted(back, -1), shifted(forward, 1)
    y_local, product, quadratic, base = stage(
        bind(schur_image), products, image, part, back, forward, weight, second, schur, turned_high, turned_low
    )
    sums, y_coarse, part, back = stage(
        bind(coarse_image), [((4, columns), F32), (coarse_own, F32), (own, F32), ((nf, columns), BF16)],
        *coarse_halves, inverse, second, shares, base, gram, quadratic, basis_high, basis_low, product, sums,
        scratch=[pltpu.VMEM((nco, columns), F32)],
    )
    steps = bits()
    for k, bit in enumerate(steps):
        sums = sums + crossed(sums, bit)
        if k + 1 == len(steps) // 2:
            sums, back = lax.optimization_barrier((sums, back))
            back = shifted(back, -1)
    z, y = stage(bind(complete), [(own, F32), (own, F32)], z_local, z_coarse, y_local, y_coarse, rows)
    return stage(bind(combine), [(own, F32), (own, F32)], sums, load, z, y, image, part, back)


def solution(mesh):
    specs = P(("parts", AXIS), None)
    return jax.shard_map(shards, mesh=mesh, in_specs=(specs,) * 6, out_specs=(specs, specs), check_vma=False)
```

time: 82.8 us -> 86.1 us (1.040)
  Pallas kernels: 16.6 us -> 18.3 us
  local copies, waits for them, and re-layouts: 5.91 us -> 7.17 us
    ppermute x12, waiting for transfers between devices: 23 us -> 25.4 us  [crossed(): lax.ppermute(block, AXIS, [(i, i ^ bit) for i in range(lax.axis_size(AXIS...]
    ppermute x10 -> x8, waiting for transfers between devices: 13.5 us -> 11.4 us  [shifted(): lax.ppermute(block, AXIS, [((i - distance) % n, i) for i in range(n)])]
    pallas_call x9 -> x12, Pallas kernels: 16.6 us -> 18.3 us  [stage(): return call(*operands)]
    ppermute x12, starting transfers between devices: 13 us -> 11.7 us  [crossed(): lax.ppermute(block, AXIS, [(i, i ^ bit) for i in range(lax.axis_size(AXIS...]
    unnamed x28 -> x18, local copies, waits for them, and re-layouts: 5.88 us -> 7.15 us
    ppermute x10 -> x8, starting transfers between devices: 9.64 us -> 10.9 us  [shifted(): lax.ppermute(block, AXIS, [((i - distance) % n, i) for i in range(n)])]
  transfers between devices with their start and end apart: 22 -> 20, of which waited for: 14 -> 12; matrix products, arithmetic and copies ran while one was open for 0% -> 0% of each run, Pallas kernels for 14% -> 15%
where the time goes in v5:
time: 86.1 us; the launch traced here: 85.8 us
  waiting for transfers between devices  36.8 us (43%)
  starting transfers between devices  22.6 us (26%)
  Pallas kernels  18.3 us (21%)
  local copies, waits for them, and re-layouts  7.17 us (8%)
  between operations  0.89 us (1%)
    ppermute x12, waiting for transfers between devices, crossed(): lax.ppermute(block, AXIS, [(i, i ^ bit) for i in range(lax.axis_size(AXIS...  25.4 us
    pallas_call x12, Pallas kernels, stage(): return call(*operands)  18.3 us
    ppermute x12, starting transfers between devices, crossed(): lax.ppermute(block, AXIS, [(i, i ^ bit) for i in range(lax.axis_size(AXIS...  11.7 us
    ppermute x8, waiting for transfers between devices, shifted(): lax.ppermute(block, AXIS, [((i - distance) % n, i) for i in range(n)])  11.4 us
    ppermute x8, starting transfers between devices, shifted(): lax.ppermute(block, AXIS, [((i - distance) % n, i) for i in range(n)])  10.9 us
    unnamed x18, local copies, waits for them, and re-layouts  7.15 us
  transfers between devices with their start and end apart: 20, of which 12 were waited for; matrix products, arithmetic and copies ran while one was open for 0% of the time, Pallas kernels for 15%

profile of v5, /device:TPU:0, one launch (start us, length us, event | category | flops | bytes accessed | tf_op | source)
XLA Modules:
  0.0 85.8 jit_solution(1006241860085775632)
XLA Ops:
  0.6 1.2 %copy-done.2 = f32[1024,256]{1,0:T(8,128)S(1)} copy-done((f32[1024,256]{1,0:T(8,128)S(1)}, f32[1024,256]{1,0:T(8,128)}, u32[]{:S(2)}) %copy-start.2) | copy-done | bytes 1048600
  1.9 0.8 copy-done.4
  2.7 0.7 copy-done.5
  3.4 0.6 prepare.1
  4.0 4.1 %collective-permute-start = (bf16[64,256]{1,0:T(8,128)(2,1)S(1)}, bf16[64,256]{1,0:T(8,128)(2,1)S(1)}, u32[]{:S(2)}, u32[]{:S(2)}) collective-permute-start(bf16[64,256]{1,0:T(8,128)(2,1)S(1)} %get-tuple-element.48), channel_id=1, source_target_pairs={{0,8},{1,9},{2,10},{3,11},{4,12},{5,13},{6,14},{7,15},{8,0},{9,1},... | collective-permute-start | bytes 98312 | tf_op jit(solution)/shard_map/ppermute | solution.py:23
  8.1 0.3 first_message.1
  8.3 0.1 collective-permute-start.4
  8.4 0.0 copy-start
  8.4 2.2 %copy-done = bf16[2048,1024]{1,0:T(8,128)(2,1)S(1)} copy-done((bf16[2048,1024]{1,0:T(8,128)(2,1)S(1)}, bf16[2048,1024]{1,0:T(8,128)(2,1)}, u32[]{:S(2)}) %copy-start) | copy-done | bytes 4194328
  10.6 2.2 %copy-done.1 = bf16[2048,1024]{1,0:T(8,128)(2,1)S(1)} copy-done((bf16[2048,1024]{1,0:T(8,128)(2,1)S(1)}, bf16[2048,1024]{1,0:T(8,128)(2,1)}, u32[]{:S(2)}) %copy-start.1) | copy-done | bytes 4194328
  12.8 0.8 fetch.1
  13.5 0.0 collective-permute-done
  13.6 1.6 %collective-permute-start.1 = (bf16[128,256]{1,0:T(8,128)(2,1)S(1)}, bf16[128,256]{1,0:T(8,128)(2,1)S(1)}, u32[]{:S(2)}, u32[]{:S(2)}) collective-permute-start(bf16[128,256]{1,0:T(8,128)(2,1)S(1)} %pad_maximum_fusion.3), channel_id=1, source_target_pairs={{0,4},{1,5},{2,6},{3,7},{4,0},{5,1},{6,2},{7,3},{8,12},{9,13},{10,... | collective-permute-start | bytes 196616 | tf_op jit(solution)/shard_map/ppermute | solution.py:23
  15.2 2.8 %collective-permute-done.1 = bf16[128,256]{1,0:T(8,128)(2,1)S(1)} collective-permute-done((bf16[128,256]{1,0:T(8,128)(2,1)S(1)}, bf16[128,256]{1,0:T(8,128)(2,1)S(1)}, u32[]{:S(2)}, u32[]{:S(2)}) %collective-permute-start.1) | collective-permute-done | bytes 65568 | tf_op jit(solution)/shard_map/ppermute | solution.py:23
  18.0 1.6 %collective-permute-start.2 = (bf16[256,256]{1,0:T(8,128)(2,1)S(1)}, bf16[256,256]{1,0:T(8,128)(2,1)S(1)}, u32[]{:S(2)}, u32[]{:S(2)}) collective-permute-start(bf16[256,256]{1,0:T(8,128)(2,1)S(1)} %pad_maximum_fusion.1), channel_id=1, source_target_pairs={{0,2},{1,3},{2,0},{3,1},{4,6},{5,7},{6,4},{7,5},{8,10},{9,11},{10,... | collective-permute-start | bytes 393224 | tf_op jit(solution)/shard_map/ppermute | solution.py:23
  19.6 0.0 collective-permute-done.4.message
  19.6 1.5 %neumann_load.1 = (f32[1536,256]{1,0:T(8,128)S(1)}, bf16[512,256]{1,0:T(8,128)(2,1)S(1)}, bf16[656,256]{1,0:T(8,128)(2,1)S(1)}) custom-call(f32[1024,256]{1,0:T(8,128)S(1)} %get-tuple-element.49.load, f32[2,512]{1,0:T(2,128)S(1)} %get-tuple-element.50.weight.refs_4_, bf16[576,256]{1,0:T(8,128)(2,1)S(1)} %collective-permute-done.4.message, ...), custom_call_target="tpu_custom_call" | custom-call | tf_op jit(solution)/shard_map/neumann_load/pallas_call | solution.py:141
  21.1 0.2 collective-permute-start.5
  21.3 4.3 %collective-permute-start.6 = (bf16[512,256]{1,0:T(8,128)(2,1)S(1)}, bf16[512,256]{1,0:T(8,128)(2,1)S(1)}, u32[]{:S(2)}, u32[]{:S(2)}) collective-permute-start(bf16[512,256]{1,0:T(8,128)(2,1)S(1)} %get-tuple-element.60), channel_id=1, source_target_pairs={{1,0},{2,1},{3,2},{4,3},{5,4},{6,5},{7,6},{8,7},{9,8},{10,9},{11,1... | collective-permute-start | bytes 786440 | tf_op jit(solution)/shard_map/ppermute | solution.py:19
  25.6 0.0 collective-permute-done.2
  25.6 0.1 collective-permute-start.3
  25.7 1.9 %static_basis.1 = (bf16[2048,64]{1,0:T(8,128)(2,1)S(1)}, bf16[2048,64]{1,0:T(8,128)(2,1)S(1)}, bf16[128,1024]{1,0:T(8,128)(2,1)S(1)}, bf16[128,1024]{1,0:T(8,128)(2,1)S(1)}, f32[128,128]{1,0:T(8,128)S(1)}) custom-call(bf16[2048,1024]{1,0:T(8,128)(2,1)S(1)} %get-tuple-element.61.schur.refs_6_, bf16[576,256]{1,0:T(8,128)(2,1)S(1)} %collective-permute-done.4.message, ...), custom_call_target="tpu_custom_call" | custom-call | tf_op jit(solution)/shard_map/static_basis/pallas_call | solution.py:141
  27.6 1.9 %collective-permute-done.6.from_next = bf16[512,256]{1,0:T(8,128)(2,1)S(1)} collective-permute-done((bf16[512,256]{1,0:T(8,128)(2,1)S(1)}, bf16[512,256]{1,0:T(8,128)(2,1)S(1)}, u32[]{:S(2)}, u32[]{:S(2)}) %collective-permute-start.6) | collective-permute-done | bytes 262176 | tf_op jit(solution)/shard_map/ppermute | solution.py:19
  29.5 1.1 %collective-permute-done.5.from_previous.message.refs_5_ = bf16[656,256]{1,0:T(8,128)(2,1)S(1)} collective-permute-done((bf16[656,256]{1,0:T(8,128)(2,1)S(1)}, bf16[656,256]{1,0:T(8,128)(2,1)S(1)}, u32[]{:S(2)}, u32[]{:S(2)}) %collective-permute-start.5) | collective-permute-done | bytes 335904 | tf_op jit(solution)/shard_map/ppermute | solution.py:19
  30.6 3.2 %schur_load.1 = (f32[1536,256]{1,0:T(8,128)S(1)}, f32[1536,256]{1,0:T(8,128)S(1)}, f32[8,256]{1,0:T(8,128)S(1)}, f32[128,256]{1,0:T(8,128)S(1)}) custom-call(f32[1024,256]{1,0:T(8,128)S(1)} %get-tuple-element.49.load, f32[1536,256]{1,0:T(8,128)S(1)} %get-tuple-element.59.part, bf16[512,256]{1,0:T(8,128)(2,1)S(1)} %collective-permute-done.6.from_next, ...), custom_call_target="tpu_custom_call" | custom-call | tf_op jit(solution)/shard_map/schur_load/pallas_call | solution.py:141
  33.8 1.4 %coarse_load.1 = (bf16[96,256]{1,0:T(8,128)(2,1)S(1)}, f32[96,256]{1,0:T(8,128)S(1)}, f32[64,256]{1,0:T(8,128)S(1)}, f32[1536,256]{1,0:T(8,128)S(1)}, bf16[512,2...) custom-call(bf16[512,256]{1,0:T(8,128)(2,1)S(1)} %constant_dynamic-update-slice_fusion.half, ...), custom_call_target="tpu_custom_call" | custom-call | tf_op jit(solution)/shard_map/coarse_load/pallas_call | solution.py:141
  35.2 0.1 collective-permute-start.7
  35.3 3.6 %collective-permute-start.11 = (bf16[512,256]{1,0:T(8,128)(2,1)S(1)}, bf16[512,256]{1,0:T(8,128)(2,1)S(1)}, u32[]{:S(2)}, u32[]{:S(2)}) collective-permute-start(bf16[512,256]{1,0:T(8,128)(2,1)S(1)} %get-tuple-element.73), channel_id=1, source_target_pairs={{1,0},{2,1},{3,2},{4,3},{5,4},{6,5},{7,6},{8,7},{9,8},{10,9},{11,1... | collective-permute-start | bytes 786440 | tf_op jit(solution)/shard_map/ppermute | solution.py:19
  38.9 1.7 %collective-permute-done.7 = bf16[96,256]{1,0:T(8,128)(2,1)S(1)} collective-permute-done((bf16[96,256]{1,0:T(8,128)(2,1)S(1)}, bf16[96,256]{1,0:T(8,128)(2,1)S(1)}, u32[]{:S(2)}, u32[]{:S(2)}) %collective-permute-start.7) | collective-permute-done | bytes 49184 | tf_op jit(solution)/shard_map/ppermute | solution.py:23
  40.5 0.1 collective-permute-start.8
  40.6 4.6 %collective-permute-done.8 = bf16[192,256]{1,0:T(8,128)(2,1)S(1)} collective-permute-done((bf16[192,256]{1,0:T(8,128)(2,1)S(1)}, bf16[192,256]{1,0:T(8,128)(2,1)S(1)}, u32[]{:S(2)}, u32[]{:S(2)}) %collective-permute-start.8) | collective-permute-done | bytes 98336 | tf_op jit(solution)/shard_map/ppermute | solution.py:23
  45.2 4.0 %collective-permute-start.9 = (bf16[384,256]{1,0:T(8,128)(2,1)S(1)}, bf16[384,256]{1,0:T(8,128)(2,1)S(1)}, u32[]{:S(2)}, u32[]{:S(2)}) collective-permute-start(bf16[384,256]{1,0:T(8,128)(2,1)S(1)} %pad_maximum_fusion), channel_id=1, source_target_pairs={{0,2},{1,3},{2,0},{3,1},{4,6},{5,7},{6,4},{7,5},{8,10},{9,11},{10,... | collective-permute-start | bytes 589832 | tf_op jit(solution)/shard_map/ppermute | solution.py:23
  49.3 3.6 %collective-permute-done.9 = bf16[384,256]{1,0:T(8,128)(2,1)S(1)} collective-permute-done((bf16[384,256]{1,0:T(8,128)(2,1)S(1)}, bf16[384,256]{1,0:T(8,128)(2,1)S(1)}, u32[]{:S(2)}, u32[]{:S(2)}) %collective-permute-start.9) | collective-permute-done | bytes 196640 | tf_op jit(solution)/shard_map/ppermute | solution.py:23
  52.9 0.1 collective-permute-start.10
  53.0 1.5 %neumann_image.1 = (f32[1024,256]{1,0:T(8,128)S(1)}, f32[1536,256]{1,0:T(8,128)S(1)}, bf16[512,256]{1,0:T(8,128)(2,1)S(1)}, bf16[512,256]{1,0:T(8,128)(2,1)S(1)}) custom-call(f32[1536,256]{1,0:T(8,128)S(1)} %get-tuple-element.72.part_in, bf16[512,256]{1,0:T(8,128)(2,1)S(1)} %collective-permute-done.11.from_next, ...), custom_call_target="tpu_custom_call" | custom-call | tf_op jit(solution)/shard_map/neumann_image/pallas_call | solution.py:141
  54.5 2.7 %collective-permute-start.13 = (bf16[512,256]{1,0:T(8,128)(2,1)S(1)}, bf16[512,256]{1,0:T(8,128)(2,1)S(1)}, u32[]{:S(2)}, u32[]{:S(2)}) collective-permute-start(bf16[512,256]{1,0:T(8,128)(2,1)S(1)} %get-tuple-element.77), channel_id=1, source_target_pairs={{1,0},{2,1},{3,2},{4,3},{5,4},{6,5},{7,6},{8,7},{9,8},{10,9},{11,1... | collective-permute-start | bytes 786440 | tf_op jit(solution)/shard_map/ppermute | solution.py:19
  57.3 0.0 collective-permute-start.14
  57.3 3.9 %collective-permute-done.13.refs_2_ = bf16[512,256]{1,0:T(8,128)(2,1)S(1)} collective-permute-done((bf16[512,256]{1,0:T(8,128)(2,1)S(1)}, bf16[512,256]{1,0:T(8,128)(2,1)S(1)}, u32[]{:S(2)}, u32[]{:S(2)}) %collective-permute-start.13) | collective-permute-done | bytes 262176 | tf_op jit(solution)/shard_map/ppermute | solution.py:19
  61.2 4.6 %collective-permute-done.14.refs_3_ = bf16[512,256]{1,0:T(8,128)(2,1)S(1)} collective-permute-done((bf16[512,256]{1,0:T(8,128)(2,1)S(1)}, bf16[512,256]{1,0:T(8,128)(2,1)S(1)}, u32[]{:S(2)}, u32[]{:S(2)}) %collective-permute-start.14) | collective-permute-done | bytes 262176 | tf_op jit(solution)/shard_map/ppermute | solution.py:19
  65.8 3.3 %schur_image.1 = (f32[1536,256]{1,0:T(8,128)S(1)}, f32[1536,256]{1,0:T(8,128)S(1)}, f32[8,256]{1,0:T(8,128)S(1)}, f32[128,256]{1,0:T(8,128)S(1)}) custom-call(f32[1024,256]{1,0:T(8,128)S(1)} %get-tuple-element.75.refs_0_.image, f32[1536,256]{1,0:T(8,128)S(1)} %get-tuple-element.76.refs_1_, bf16[512,256]{1,0:T(8,128)(2,1)S(1)} %collective-permute-done.13.refs_2_, ...), custom_call_target="tpu_custom_call" | custom-call | tf_op jit(solution)/shard_map/schur_image/pallas_call | solution.py:141
  69.1 1.7 %coarse_image.1 = (f32[4,256]{1,0:T(4,128)S(1)}, f32[64,256]{1,0:T(8,128)S(1)}, f32[1024,256]{1,0:T(8,128)S(1)}, bf16[512,256]{1,0:T(8,128)(2,1)S(1)}) custom-call(bf16[768,256]{1,0:T(8,128)(2,1)S(1)} %constant_dynamic-update-slice_fusion.4.half, bf16[768,256]{1,0:T(8,128)(2,1)S(1)} %collective-permute-done.10.crossed_half, ...), custom_call_target="tpu_custom_call" | custom-call | tf_op jit(solution)/shard_map/coarse_image/pallas_call | solution.py:141
  70.7 0.1 collective-permute-start.15
  70.8 4.5 %collective-permute-done.15 = f32[4,256]{1,0:T(4,128)S(1)} collective-permute-done((f32[4,256]{1,0:T(4,128)S(1)}, f32[4,256]{1,0:T(4,128)S(1)}, u32[]{:S(2)}, u32[]{:S(2)}) %collective-permute-start.15) | collective-permute-done | bytes 4128 | tf_op jit(solution)/shard_map/ppermute | solution.py:23
  75.3 3.6 %collective-permute-done.16 = f32[4,256]{1,0:T(4,128)S(1)} collective-permute-done((f32[4,256]{1,0:T(4,128)S(1)}, f32[4,256]{1,0:T(4,128)S(1)}, u32[]{:S(2)}, u32[]{:S(2)}) %collective-permute-start.16) | collective-permute-done | bytes 4128 | tf_op jit(solution)/shard_map/ppermute | solution.py:23
  78.9 4.1 %collective-permute-done.17 = f32[4,256]{1,0:T(4,128)S(1)} collective-permute-done((f32[4,256]{1,0:T(4,128)S(1)}, f32[4,256]{1,0:T(4,128)S(1)}, u32[]{:S(2)}, u32[]{:S(2)}) %collective-permute-start.17) | collective-permute-done | bytes 4128 | tf_op jit(solution)/shard_map/ppermute | solution.py:23
  83.1 0.7 complete.1
  83.8 0.4 collective-permute-done.18
  84.2 1.6 %combine.1 = (f32[1024,256]{1,0:T(8,128)}, f32[1024,256]{1,0:T(8,128)}) custom-call(f32[4,256]{1,0:T(4,128)S(1)} %add.15.sums, f32[1024,256]{1,0:T(8,128)S(1)} %get-tuple-element.49.load, f32[1024,256]{1,0:T(8,128)S(1)} %get-tuple-element.90.z, f32[1024,256]{1,0:T(8,128)S(1)} %get-tuple-element.91.y, f32[1024,256]{1,0:T(8,128)S(1)} %get-tuple-element.75.refs_0_.image, ...), custom_call_target="tpu_custom_call" | custom-call | tf_op jit(solution)/shard_map/combine/pallas_call | solution.py:141
  (32 shorter events, 0.1 us)
Async XLA Ops:
  0.6 1.2 %copy-start.2 = (f32[1024,256]{1,0:T(8,128)S(1)}, f32[1024,256]{1,0:T(8,128)}, u32[]{:S(2)}) copy-start(f32[1024,256]{1,0:T(8,128)} %load.1) | copy-start | bytes 3145732
  1.9 0.8 copy-start.4
  2.7 0.7 copy-start.5
  3.4 5.0 %copy-start.3 = (bf16[64,1024]{1,0:T(8,128)(2,1)S(1)}, bf16[64,1024]{1,0:T(8,128)(2,1)}, u32[]{:S(2)}) copy-start(bf16[64,1024]{1,0:T(8,128)(2,1)} %inverse) | copy-start | bytes 393220
  4.0 9.6 %collective-permute-start = (bf16[64,256]{1,0:T(8,128)(2,1)S(1)}, bf16[64,256]{1,0:T(8,128)(2,1)S(1)}, u32[]{:S(2)}, u32[]{:S(2)}) collective-permute-start(bf16[64,256]{1,0:T(8,128)(2,1)S(1)} %get-tuple-element.48), channel_id=1, source_target_pairs={{0,8},{1,9},{2,10},{3,11},{4,12},{5,13},{6,14},{7,15},{8,0},{9,1},... | collective-permute-start | bytes 98312 | tf_op jit(solution)/shard_map/ppermute | solution.py:23
  8.3 11.3 %collective-permute-start.4 = (bf16[576,256]{1,0:T(8,128)(2,1)S(1)}, bf16[576,256]{1,0:T(8,128)(2,1)S(1)}, u32[]{:S(2)}, u32[]{:S(2)}) collective-permute-start(bf16[576,256]{1,0:T(8,128)(2,1)S(1)} %first_message.1), channel_id=1, source_target_pairs={{15,0},{0,1},{1,2},{2,3},{3,4},{4,5},{5,6},{6,7},{7,8},{8,9},{9,10... | collective-permute-start | bytes 884744 | tf_op jit(solution)/shard_map/ppermute | solution.py:19
  8.4 2.2 %copy-start = (bf16[2048,1024]{1,0:T(8,128)(2,1)S(1)}, bf16[2048,1024]{1,0:T(8,128)(2,1)}, u32[]{:S(2)}) copy-start(bf16[2048,1024]{1,0:T(8,128)(2,1)} %neumann) | copy-start | bytes 12582916
  10.6 2.2 %copy-start.1 = (bf16[2048,1024]{1,0:T(8,128)(2,1)S(1)}, bf16[2048,1024]{1,0:T(8,128)(2,1)}, u32[]{:S(2)}) copy-start(bf16[2048,1024]{1,0:T(8,128)(2,1)} %schur) | copy-start | bytes 12582916
  13.6 4.4 %collective-permute-start.1 = (bf16[128,256]{1,0:T(8,128)(2,1)S(1)}, bf16[128,256]{1,0:T(8,128)(2,1)S(1)}, u32[]{:S(2)}, u32[]{:S(2)}) collective-permute-start(bf16[128,256]{1,0:T(8,128)(2,1)S(1)} %pad_maximum_fusion.3), channel_id=1, source_target_pairs={{0,4},{1,5},{2,6},{3,7},{4,0},{5,1},{6,2},{7,3},{8,12},{9,13},{10,... | collective-permute-start | bytes 196616 | tf_op jit(solution)/shard_map/ppermute | solution.py:23
  18.0 7.6 %collective-permute-start.2 = (bf16[256,256]{1,0:T(8,128)(2,1)S(1)}, bf16[256,256]{1,0:T(8,128)(2,1)S(1)}, u32[]{:S(2)}, u32[]{:S(2)}) collective-permute-start(bf16[256,256]{1,0:T(8,128)(2,1)S(1)} %pad_maximum_fusion.1), channel_id=1, source_target_pairs={{0,2},{1,3},{2,0},{3,1},{4,6},{5,7},{6,4},{7,5},{8,10},{9,11},{10,... | collective-permute-start | bytes 393224 | tf_op jit(solution)/shard_map/ppermute | solution.py:23
  21.1 9.4 %collective-permute-start.5 = (bf16[656,256]{1,0:T(8,128)(2,1)S(1)}, bf16[656,256]{1,0:T(8,128)(2,1)S(1)}, u32[]{:S(2)}, u32[]{:S(2)}) collective-permute-start(bf16[656,256]{1,0:T(8,128)(2,1)S(1)} %get-tuple-element.57), channel_id=1, source_target_pairs={{15,0},{0,1},{1,2},{2,3},{3,4},{4,5},{5,6},{6,7},{7,8},{8,9},{9,10... | collective-permute-start | bytes 1007624 | tf_op jit(solution)/shard_map/ppermute | solution.py:19
  21.3 8.2 %collective-permute-start.6 = (bf16[512,256]{1,0:T(8,128)(2,1)S(1)}, bf16[512,256]{1,0:T(8,128)(2,1)S(1)}, u32[]{:S(2)}, u32[]{:S(2)}) collective-permute-start(bf16[512,256]{1,0:T(8,128)(2,1)S(1)} %get-tuple-element.60), channel_id=1, source_target_pairs={{1,0},{2,1},{3,2},{4,3},{5,4},{6,5},{7,6},{8,7},{9,8},{10,9},{11,1... | collective-permute-start | bytes 786440 | tf_op jit(solution)/shard_map/ppermute | solution.py:19
  25.6 8.2 %collective-permute-start.3 = (bf16[512,256]{1,0:T(8,128)(2,1)S(1)}, bf16[512,256]{1,0:T(8,128)(2,1)S(1)}, u32[]{:S(2)}, u32[]{:S(2)}) collective-permute-start(bf16[512,256]{1,0:T(8,128)(2,1)S(1)} %constant_dynamic-update-slice_fusion.half), channel_id=1, source_target_pairs={{0,1},{1,0},{2,3},{3,2},{4,5},{5,4},{6,7},{7,6},{8,9},{9,8},{10,11... | collective-permute-start | bytes 786440 | tf_op jit(solution)/shard_map/ppermute | solution.py:23
  35.2 5.4 %collective-permute-start.7 = (bf16[96,256]{1,0:T(8,128)(2,1)S(1)}, bf16[96,256]{1,0:T(8,128)(2,1)S(1)}, u32[]{:S(2)}, u32[]{:S(2)}) collective-permute-start(bf16[96,256]{1,0:T(8,128)(2,1)S(1)} %get-tuple-element.70), channel_id=1, source_target_pairs={{0,8},{1,9},{2,10},{3,11},{4,12},{5,13},{6,14},{7,15},{8,0},{9,1},... | collective-permute-start | bytes 147464 | tf_op jit(solution)/shard_map/ppermute | solution.py:23
  35.3 17.8 %collective-permute-start.11 = (bf16[512,256]{1,0:T(8,128)(2,1)S(1)}, bf16[512,256]{1,0:T(8,128)(2,1)S(1)}, u32[]{:S(2)}, u32[]{:S(2)}) collective-permute-start(bf16[512,256]{1,0:T(8,128)(2,1)S(1)} %get-tuple-element.73), channel_id=1, source_target_pairs={{1,0},{2,1},{3,2},{4,3},{5,4},{6,5},{7,6},{8,7},{9,8},{10,9},{11,1... | collective-permute-start | bytes 786440 | tf_op jit(solution)/shard_map/ppermute | solution.py:19
  38.9 14.2 %collective-permute-start.12 = (bf16[512,256]{1,0:T(8,128)(2,1)S(1)}, bf16[512,256]{1,0:T(8,128)(2,1)S(1)}, u32[]{:S(2)}, u32[]{:S(2)}) collective-permute-start(bf16[512,256]{1,0:T(8,128)(2,1)S(1)} %get-tuple-element.74), channel_id=1, source_target_pairs={{15,0},{0,1},{1,2},{2,3},{3,4},{4,5},{5,6},{6,7},{7,8},{8,9},{9,10... | collective-permute-start | bytes 786440 | tf_op jit(solution)/shard_map/ppermute | solution.py:19
  40.5 4.7 %collective-permute-start.8 = (bf16[192,256]{1,0:T(8,128)(2,1)S(1)}, bf16[192,256]{1,0:T(8,128)(2,1)S(1)}, u32[]{:S(2)}, u32[]{:S(2)}) collective-permute-start(bf16[192,256]{1,0:T(8,128)(2,1)S(1)} %pad_maximum_fusion.2), channel_id=1, source_target_pairs={{0,4},{1,5},{2,6},{3,7},{4,0},{5,1},{6,2},{7,3},{8,12},{9,13},{10,... | collective-permute-start | bytes 294920 | tf_op jit(solution)/shard_map/ppermute | solution.py:23
  45.2 7.7 %collective-permute-start.9 = (bf16[384,256]{1,0:T(8,128)(2,1)S(1)}, bf16[384,256]{1,0:T(8,128)(2,1)S(1)}, u32[]{:S(2)}, u32[]{:S(2)}) collective-permute-start(bf16[384,256]{1,0:T(8,128)(2,1)S(1)} %pad_maximum_fusion), channel_id=1, source_target_pairs={{0,2},{1,3},{2,0},{3,1},{4,6},{5,7},{6,4},{7,5},{8,10},{9,11},{10,... | collective-permute-start | bytes 589832 | tf_op jit(solution)/shard_map/ppermute | solution.py:23
  52.9 16.1 %collective-permute-start.10 = (bf16[768,256]{1,0:T(8,128)(2,1)S(1)}, bf16[768,256]{1,0:T(8,128)(2,1)S(1)}, u32[]{:S(2)}, u32[]{:S(2)}) collective-permute-start(bf16[768,256]{1,0:T(8,128)(2,1)S(1)} %constant_dynamic-update-slice_fusion.4.half), channel_id=1, source_target_pairs={{0,1},{1,0},{2,3},{3,2},{4,5},{5,4},{6,7},{7,6},{8,9},{9,8},{10,11... | collective-permute-start | bytes 1179656 | tf_op jit(solution)/shard_map/ppermute | solution.py:23
  54.5 6.6 %collective-permute-start.13 = (bf16[512,256]{1,0:T(8,128)(2,1)S(1)}, bf16[512,256]{1,0:T(8,128)(2,1)S(1)}, u32[]{:S(2)}, u32[]{:S(2)}) collective-permute-start(bf16[512,256]{1,0:T(8,128)(2,1)S(1)} %get-tuple-element.77), channel_id=1, source_target_pairs={{1,0},{2,1},{3,2},{4,3},{5,4},{6,5},{7,6},{8,7},{9,8},{10,9},{11,1... | collective-permute-start | bytes 786440 | tf_op jit(solution)/shard_map/ppermute | solution.py:19
  57.3 8.5 %collective-permute-start.14 = (bf16[512,256]{1,0:T(8,128)(2,1)S(1)}, bf16[512,256]{1,0:T(8,128)(2,1)S(1)}, u32[]{:S(2)}, u32[]{:S(2)}) collective-permute-start(bf16[512,256]{1,0:T(8,128)(2,1)S(1)} %get-tuple-element.78), channel_id=1, source_target_pairs={{15,0},{0,1},{1,2},{2,3},{3,4},{4,5},{5,6},{6,7},{7,8},{8,9},{9,10... | collective-permute-start | bytes 786440 | tf_op jit(solution)/shard_map/ppermute | solution.py:19
  70.7 4.6 %collective-permute-start.15 = (f32[4,256]{1,0:T(4,128)S(1)}, f32[4,256]{1,0:T(4,128)S(1)}, u32[]{:S(2)}, u32[]{:S(2)}) collective-permute-start(f32[4,256]{1,0:T(4,128)S(1)} %get-tuple-element.83), channel_id=1, source_target_pairs={{0,8},{1,9},{2,10},{3,11},{4,12},{5,13},{6,14},{7,15},{8,0},{9,1},... | collective-permute-start | bytes 12296 | tf_op jit(solution)/shard_map/ppermute | solution.py:23
  75.3 3.6 %collective-permute-start.16 = (f32[4,256]{1,0:T(4,128)S(1)}, f32[4,256]{1,0:T(4,128)S(1)}, u32[]{:S(2)}, u32[]{:S(2)}) collective-permute-start(f32[4,256]{1,0:T(4,128)S(1)} %add.12), channel_id=1, source_target_pairs={{0,4},{1,5},{2,6},{3,7},{4,0},{5,1},{6,2},{7,3},{8,12},{9,13},{10,... | collective-permute-start | bytes 12296 | tf_op jit(solution)/shard_map/ppermute | solution.py:23
  78.9 5.3 %collective-permute-start.19 = (bf16[512,256]{1,0:T(8,128)(2,1)S(1)}, bf16[512,256]{1,0:T(8,128)(2,1)S(1)}, u32[]{:S(2)}, u32[]{:S(2)}) collective-permute-start(bf16[512,256]{1,0:T(8,128)(2,1)S(1)} %get-tuple-element.93), channel_id=1, source_target_pairs={{1,0},{2,1},{3,2},{4,3},{5,4},{6,5},{7,6},{8,7},{9,8},{10,9},{11,1... | collective-permute-start | bytes 786440 | tf_op jit(solution)/shard_map/ppermute | solution.py:19
  78.9 4.1 %collective-permute-start.17 = (f32[4,256]{1,0:T(4,128)S(1)}, f32[4,256]{1,0:T(4,128)S(1)}, u32[]{:S(2)}, u32[]{:S(2)}) collective-permute-start(f32[4,256]{1,0:T(4,128)S(1)} %add.13), channel_id=1, source_target_pairs={{0,2},{1,3},{2,0},{3,1},{4,6},{5,7},{6,4},{7,5},{8,10},{9,11},{10,... | collective-permute-start | bytes 12296 | tf_op jit(solution)/shard_map/ppermute | solution.py:23
  83.1 1.2 %collective-permute-start.18 = (f32[4,256]{1,0:T(4,128)S(1)}, f32[4,256]{1,0:T(4,128)S(1)}, u32[]{:S(2)}, u32[]{:S(2)}) collective-permute-start(f32[4,256]{1,0:T(4,128)S(1)} %add.14), channel_id=1, source_target_pairs={{0,1},{1,0},{2,3},{3,2},{4,5},{5,4},{6,7},{7,6},{8,9},{9,8},{10,11... | collective-permute-start | bytes 12296 | tf_op jit(solution)/shard_map/ppermute | solution.py:23

commit v6 on v5

--- a/solution.py
+++ b/solution.py
@@ -23,21 +23,12 @@
     return lax.ppermute(block, AXIS, [(i, i ^ bit) for i in range(lax.axis_size(AXIS))])
 
 
-def bits():
-    return [1 << k for k in reversed(range(lax.axis_size(AXIS).bit_length() - 1))]
-
-
-def gather_halves(block):
-    for bit in bits()[:-1]:
-        block = jnp.concatenate([block, crossed(block, bit)], axis=0)
-    return block, crossed(block, 1)
-
-
-def half_order():
-    order = [0]
-    for bit in bits()[:-1]:
-        order += [place ^ bit for place in order]
-    return order
+def groups():
+    return [list(range(k, lax.axis_size(AXIS), 2)) for k in range(2)]
+
+
+def from_group(copies):
+    return lax.all_to_all(copies, AXIS, 0, 0, axis_index_groups=groups())
 
 
 def dot(a, b):
@@ -141,7 +132,7 @@
     return call(*operands)
 
 
-def prepare(halo, load, rows, weight, load_here, rows_here, weight_here, coarse_rounded, coarse, done):
+def prepare(halo, load, rows, weight, load_here, rows_here, weight_here, coarse, done):
     ncf, nf = halo.ncf, halo.nf
     subs = load.shape[0] // nf
     copies = [pltpu.make_async_copy(rows, rows_here, done.at[subs])]
@@ -155,7 +146,6 @@
     for j in range(subs):
         copies[1 + j].wait()
         coarse[j * ncf : (j + 1) * ncf] = dot(rows_of(rows_here, j, ncf), rows_of(load_here, j, nf).astype(BF16))
-    coarse_rounded[...] = coarse[...].astype(BF16)
     copies[-1].wait()
 
 
@@ -274,12 +264,16 @@
 
 
 def placed(half, crossed_half):
-    me = lax.axis_index(AXIS)
-    order = half_order()
-    count = half.shape[0] // len(order)
+    parity = lax.rem(lax.axis_index(AXIS), 2)
     for flip, blocks in ((0, half), (1, crossed_half)):
-        for k, place in enumerate(order):
-            yield me ^ (place ^ flip), blocks, k * count, (k + 1) * count
+        for k in range(blocks.shape[0]):
+            yield 2 * k + (parity ^ flip), blocks, k
+
+
+def copy_out(halo, block, copies):
+    rounded = block[...].astype(copies.dtype)
+    for k in range(copies.shape[0]):
+        copies[k] = rounded
 
 
 def coarse_shares(ncf, results):
@@ -313,19 +307,18 @@
 
 def coarse_load(
     halo, half, crossed_half, inverse, message, coarse, base, gram, quadratic, basis_high, basis_low, product,
-    shares_rounded, shares, solution, part, back, forward, sums, gathered,
+    shares, solution, part, back, forward, sums, gathered,
 ):
     ncf, nf = halo.ncf, halo.nf
     subs = inverse.shape[0] // ncf
-    for place, blocks, start, stop in placed(half, crossed_half):
-        gathered[pl.ds(pl.multiple_of(place * subs * ncf, subs * ncf), subs * ncf)] = blocks[start:stop]
+    for place, blocks, k in placed(half, crossed_half):
+        gathered[pl.ds(pl.multiple_of(place * subs * ncf, subs * ncf), subs * ncf)] = blocks[k]
     everything = gathered[...]
     own = dot(inverse[...], everything)
     x = [dot(halo.inverse(message), everything)] + [own[j * ncf : (j + 1) * ncf] for j in range(subs)]
     results, energy = coarse_products(ncf, x, base, gram)
     for e, share in enumerate(coarse_shares(ncf, results)):
         shares[e * ncf : (e + 1) * ncf] = share
-    shares_rounded[...] = shares[...].astype(BF16)
     solution[...] = own
     sums[0:1] = quadratic[1:2] + column_sum(coarse[...] * own)
     sums[1:2] = quadratic[0:1] + energy
@@ -343,18 +336,21 @@
     ncf, nf = halo.ncf, halo.nf
     subs = inverse.shape[0] // ncf
     total = gathered.shape[0]
-    for place, blocks, start, stop in placed(half, crossed_half):
-        gathered[pl.ds(pl.multiple_of(place * subs * ncf, subs * ncf), subs * ncf)] = blocks[start + ncf : stop].astype(F32)
-    for place, blocks, start, stop in placed(half, crossed_half):
+    for place, blocks, k in placed(half, crossed_half):
+        gathered[pl.ds(pl.multiple_of(place * subs * ncf, subs * ncf), subs * ncf)] = blocks[k, ncf:].astype(F32)
+    for place, blocks, k in placed(half, crossed_half):
         before = pl.multiple_of(lax.rem(place * subs * ncf + (total - ncf), total), ncf)
-        gathered[pl.ds(before, ncf)] += blocks[start : start + ncf].astype(F32)
+        gathered[pl.ds(before, ncf)] += blocks[k, :ncf].astype(F32)
     everything = gathered[...]
     own = split_dot(inverse[...], everything)
     x = [split_dot(halo.inverse(message), everything)] + [own[j * ncf : (j + 1) * ncf] for j in range(subs)]
     _, energy = coarse_products(ncf, x, base, gram)
-    sums[0:2] = sums_in[0:2]
-    sums[2:3] = quadratic[1:2] + sum(column_sum(rows_of(shares, e, ncf) * x[e]) for e in range(subs + 1))
-    sums[3:4] = quadratic[0:1] + energy
+    third = quadratic[1:2] + sum(column_sum(rows_of(shares, e, ncf) * x[e]) for e in range(subs + 1))
+    fourth = quadratic[0:1] + energy
+    for k in range(sums.shape[0]):
+        sums[k, 0:2] = sums_in[0:2]
+        sums[k, 2:3] = third
+        sums[k, 3:4] = fourth
     solution[...] = own
     faces = add_basis(nf, x, basis_high, basis_low, product)
     for e in range(1, subs + 1):
@@ -370,9 +366,10 @@
             whole[here] = local[beside] + split_dot(rows_of(rows, j, ncf), rows_of(coarse, j, ncf), dot_tn)
 
 
-def combine(halo, sums, load, z, y, image, part, from_next, solution, residual):
+def combine(halo, sums, crossed_sums, load, z, y, image, part, from_next, solution, residual):
     nf = halo.nf
-    a, b, c, d = (sums[k : k + 1] for k in range(4))
+    total = sums[...] + crossed_sums[...]
+    a, b, c, d = (total[k : k + 1] for k in range(4))
     step = a / b
     grow = step * (c / b)
     next_step = (grow - 1.0) / ((d - c * (c / b)) * (step / b))
@@ -398,22 +395,33 @@
     semaphores = lambda count: [pltpu.SemaphoreType.DMA((count,))]
     described = lambda array: (array.shape, array.dtype)
 
-    load, rows, weight, coarse_rounded, coarse = stage(
+    group = lax.axis_size(AXIS) // 2
+
+    def gather(block):
+        shape = (group,) + block.shape
+        (copies,) = stage(bind(copy_out), [(shape, BF16)], block)
+        return from_group(copies)
+
+    outside = [pltpu.with_memory_space_constraint(x, pltpu.HBM) for x in (right_side, constraint, face_weight)]
+    load, rows, weight, coarse = stage(
         bind(prepare),
-        [described(right_side), described(constraint), described(face_weight), (coarse_own, BF16), (coarse_own, F32)],
-        right_side, constraint, face_weight, scratch=semaphores(subs + 2), fetched=3,
+        [described(right_side), described(constraint), described(face_weight), (coarse_own, F32)],
+        *outside, scratch=semaphores(subs + 2), fetched=3,
     )
     (first,) = stage(bind(first_message), [((halo.first_height, columns), BF16)], load, weight, rows)
-    coarse_halves = gather_halves(coarse_rounded)
-    tied, _ = lax.optimization_barrier(((neumann, schur, coarse_inverse), first))
+    half = gather(coarse)
+    outside = [pltpu.with_memory_space_constraint(x, pltpu.HBM) for x in (neumann, schur, coarse_inverse)]
+    outside, _ = lax.optimization_barrier((outside, first))
     neumann, schur, inverse = stage(
-        bind(fetch), [described(array) for array in tied], *tied, scratch=semaphores(3), fetched=3
+        bind(fetch), [described(array) for array in outside], *outside, scratch=semaphores(3), fetched=3
     )
     first = shifted(first, 1)
     part, back, forward = stage(
         bind(neumann_load), [(faces, F32), ((nf, columns), BF16), ((halo.second_height, columns), BF16)],
         load, weight, first, neumann, inverse, scratch=[pltpu.VMEM((halo.weight_count, columns), F32)],
     )
+    half, _ = lax.optimization_barrier((half, back))
+    crossed_half = crossed(half, 1)
     back, second = shifted(back, -1), shifted(forward, 1)
     long, wide = ((2 * subs * nf, 2 * ncf), BF16), ((local_rows, 2 * nf), BF16)
     basis_high, basis_low, turned_high, turned_low, gram = stage(
@@ -422,35 +430,33 @@
     z_local, product, quadratic, base = stage(
         bind(schur_load), products, load, part, back, second, weight, schur, turned_high, turned_low
     )
-    share_rows = ((subs + 1) * ncf, columns)
-    shares_rounded, shares, z_coarse, part, back, forward, sums = stage(
+    shares, z_coarse, part, back, forward, sums = stage(
         bind(coarse_load),
-        [(share_rows, BF16), (share_rows, F32), (coarse_own, F32), (faces, F32)] + halves + [((8, columns), F32)],
-        *coarse_halves, inverse, second, coarse, base, gram, quadratic, basis_high, basis_low, product,
+        [(((subs + 1) * ncf, columns), F32), (coarse_own, F32), (faces, F32)] + halves + [((8, columns), F32)],
+        half, crossed_half, inverse, second, coarse, base, gram, quadratic, basis_high, basis_low, product,
         scratch=[pltpu.VMEM((nco, columns), BF16)],
     )
-    coarse_halves = gather_halves(shares_rounded)
     back, forward = shifted(back, -1), shifted(forward, 1)
+    half = gather(shares)
     image, part, back, forward = stage(
         bind(neumann_image), [(own, F32), (faces, F32)] + halves, part, back, forward, weight, second, neumann
     )
+    half, _ = lax.optimization_barrier((half, back))
+    crossed_half = crossed(half, 1)
     back, forward = shifted(back, -1), shifted(forward, 1)
     y_local, product, quadratic, base = stage(
         bind(schur_image), products, image, part, back, forward, weight, second, schur, turned_high, turned_low
     )
     sums, y_coarse, part, back = stage(
-        bind(coarse_image), [((4, columns), F32), (coarse_own, F32), (own, F32), ((nf, columns), BF16)],
-        *coarse_halves, inverse, second, shares, base, gram, quadratic, basis_high, basis_low, product, sums,
+        bind(coarse_image), [((group, 4, columns), F32), (coarse_own, F32), (own, F32), ((nf, columns), BF16)],
+        half, crossed_half, inverse, second, shares, base, gram, quadratic, basis_high, basis_low, product, sums,
         scratch=[pltpu.VMEM((nco, columns), F32)],
     )
-    steps = bits()
-    for k, bit in enumerate(steps):
-        sums = sums + crossed(sums, bit)
-        if k + 1 == len(steps) // 2:
-            sums, back = lax.optimization_barrier((sums, back))
-            back = shifted(back, -1)
+    sums = jnp.sum(from_group(sums), axis=0)
+    crossed_sums = crossed(sums, 1)
+    back = shifted(back, -1)
     z, y = stage(bind(complete), [(own, F32), (own, F32)], z_local, z_coarse, y_local, y_coarse, rows)
-    return stage(bind(combine), [(own, F32), (own, F32)], sums, load, z, y, image, part, back)
+    return stage(bind(combine), [(own, F32), (own, F32)], sums, crossed_sums, load, z, y, image, part, back)
 
 
 def solution(mesh):

time: 86.1 us -> 118 us (1.37)
  local copies, waits for them, and re-layouts: 7.17 us -> 28 us
  waiting for transfers between devices: 36.8 us -> 22.4 us
  blocking collectives: 0 us -> 9.05 us
  Pallas kernels: 18.3 us -> 26.9 us
  starting transfers between devices: 22.6 us -> 29.8 us
    ppermute x12 -> x3, waiting for transfers between devices: 25.4 us -> 0.01 us  [crossed(): lax.ppermute(block, AXIS, [(i, i ^ bit) for i in range(lax.axis_size(AXIS...]
    unnamed x18 -> x72, local copies, waits for them, and re-layouts: 7.15 us -> 28 us
    ppermute x12 -> x3, starting transfers between devices: 11.7 us -> 0.07 us  [crossed(): lax.ppermute(block, AXIS, [(i, i ^ bit) for i in range(lax.axis_size(AXIS...]
    all_to_all x0 -> x2, starting transfers between devices: none -> 11.4 us  [from_group(): return lax.all_to_all(copies, AXIS, 0, 0, axis_index_groups=groups())]
    ppermute x8, waiting for transfers between devices: 11.4 us -> 22.4 us  [shifted(): lax.ppermute(block, AXIS, [((i - distance) % n, i) for i in range(n)])]
    all_to_all x0 -> x1, blocking collectives: none -> 9.05 us  [from_group(): return lax.all_to_all(copies, AXIS, 0, 0, axis_index_groups=groups())]
    pallas_call x12 -> x14, Pallas kernels: 18.3 us -> 26.9 us  [stage(): return call(*operands)]
    ppermute x8, starting transfers between devices: 10.9 us -> 18.4 us  [shifted(): lax.ppermute(block, AXIS, [((i - distance) % n, i) for i in range(n)])]
  transfers between devices with their start and end apart: 20 -> 13, of which waited for: 12 -> 5; matrix products, arithmetic and copies ran while one was open for 0% -> 0% of each run, Pallas kernels for 15% -> 15%
where the time goes in v6:
time: 118 us; the launch traced here: 117 us
  starting transfers between devices  29.8 us (25%)
  local copies, waits for them, and re-layouts  28 us (24%)
  Pallas kernels  26.9 us (23%)
  waiting for transfers between devices  22.4 us (19%)
  blocking collectives  9.05 us (8%)
    unnamed x72, local copies, waits for them, and re-layouts  28 us
    pallas_call x14, Pallas kernels, stage(): return call(*operands)  26.9 us
    ppermute x8, waiting for transfers between devices, shifted(): lax.ppermute(block, AXIS, [((i - distance) % n, i) for i in range(n)])  22.4 us
    ppermute x8, starting transfers between devices, shifted(): lax.ppermute(block, AXIS, [((i - distance) % n, i) for i in range(n)])  18.4 us
    all_to_all x2, starting transfers between devices, from_group(): return lax.all_to_all(copies, AXIS, 0, 0, axis_index_groups=groups())  11.4 us
    all_to_all x1, blocking collectives, from_group(): return lax.all_to_all(copies, AXIS, 0, 0, axis_index_groups=groups())  9.05 us
  transfers between devices with their start and end apart: 13, of which 5 were waited for; matrix products, arithmetic and copies ran while one was open for 0% of the time, Pallas kernels for 15%

profile of v6, /device:TPU:0, one launch (start us, length us, event | category | flops | bytes accessed | tf_op | source)
XLA Modules:
  0.0 117.1 jit_solution(12498693959497886415)
XLA Ops:
  0.6 1.5 %prepare.1 = (f32[1024,256]{1,0:T(8,128)S(1)}, bf16[64,512]{1,0:T(8,128)(2,1)S(1)}, f32[2,512]{1,0:T(2,128)S(1)}, f32[64,256]{1,0:T(8,128)S(1)}) custom-call(f32[1024,256]{1,0:T(8,128)} %load.1, bf16[64,512]{1,0:T(8,128)(2,1)} %rows.1, f32[2,512]{1,0:T(2,128)} %weight.1), custom_call_target="tpu_custom_call" | custom-call | tf_op jit(solution)/shard_map/prepare/pallas_call | solution.py:132
  2.1 0.7 copy_out.2
  2.9 7.3 %all-to-all-start = ((bf16[8,64,256]{2,1,0:T(8,128)(2,1)}), bf16[8,64,256]{2,1,0:T(8,128)(2,1)S(1)}, u32[]{:S(2)}, u32[]{:S(2)}) async-start(bf16[8,64,256]{2,1,0:T(8,128)(2,1)} %copy_out.2), calls=%async_computation | async-start | bytes 524288 | tf_op jit(solution)/shard_map/all_to_all | solution.py:31
  10.5 3.5 %fetch.1 = (bf16[2048,1024]{1,0:T(8,128)(2,1)S(1)}, bf16[2048,1024]{1,0:T(8,128)(2,1)S(1)}, bf16[64,1024]{1,0:T(8,128)(2,1)S(1)}) custom-call(bf16[2048,1024]{1,0:T(8,128)(2,1)} %neumann, bf16[2048,1024]{1,0:T(8,128)(2,1)} %schur, bf16[64,1024]{1,0:T(8,128)(2,1)} %inverse), custom_call_target="tpu_custom_call" | custom-call | tf_op jit(solution)/shard_map/fetch/pallas_call | solution.py:132
  14.0 2.0 %copy-done = bf16[2048,1024]{1,0:T(8,128)(2,1)} copy-done((bf16[2048,1024]{1,0:T(8,128)(2,1)}, bf16[2048,1024]{1,0:T(8,128)(2,1)S(1)}, u32[]{:S(2)}) %copy-start) | copy-done | bytes 4194328
  16.0 6.6 %collective-permute-done.message = bf16[576,256]{1,0:T(8,128)(2,1)S(1)} collective-permute-done((bf16[576,256]{1,0:T(8,128)(2,1)S(1)}, bf16[576,256]{1,0:T(8,128)(2,1)S(1)}, u32[]{:S(2)}, u32[]{:S(2)}) %collective-permute-start) | collective-permute-done | bytes 294944 | tf_op jit(solution)/shard_map/ppermute | solution.py:19
  22.6 2.2 %neumann_load.1 = (f32[1536,256]{1,0:T(8,128)S(1)}, bf16[512,256]{1,0:T(8,128)(2,1)}, bf16[656,256]{1,0:T(8,128)(2,1)}) custom-call(f32[1024,256]{1,0:T(8,128)S(1)} %get-tuple-element.47.load, f32[2,512]{1,0:T(2,128)S(1)} %get-tuple-element.48.weight.refs_4_, bf16[576,256]{1,0:T(8,128)(2,1)S(1)} %collective-permute-done.message, ...), custom_call_target="tpu_custom_call" | custom-call | tf_op jit(solution)/shard_map/neumann_load/pallas_call | solution.py:132
  24.8 1.2 copy-done.12
  26.0 4.4 %collective-permute-start.3 = (bf16[512,256]{1,0:T(8,128)(2,1)}, bf16[512,256]{1,0:T(8,128)(2,1)}, u32[]{:S(2)}, u32[]{:S(2)}) collective-permute-start(bf16[512,256]{1,0:T(8,128)(2,1)} %get-tuple-element.55), channel_id=1, source_target_pairs={{1,0},{2,1},{3,2},{4,3},{5,4},{6,5},{7,6},{8,7},{9,8},{10,9},{11,1... | collective-permute-start | bytes 786440 | tf_op jit(solution)/shard_map/ppermute | solution.py:19
  30.4 2.2 %copy-done.1 = bf16[2048,1024]{1,0:T(8,128)(2,1)S(1)} copy-done((bf16[2048,1024]{1,0:T(8,128)(2,1)S(1)}, bf16[2048,1024]{1,0:T(8,128)(2,1)}, u32[]{:S(2)}) %copy-start.1) | copy-done | bytes 4194328
  32.6 1.9 %static_basis.1 = (bf16[2048,64]{1,0:T(8,128)(2,1)S(1)}, bf16[2048,64]{1,0:T(8,128)(2,1)S(1)}, bf16[128,1024]{1,0:T(8,128)(2,1)S(1)}, bf16[128,1024]{1,0:T(8,128)(2,1)S(1)}, f32[128,128]{1,0:T(8,128)S(1)}) custom-call(bf16[2048,1024]{1,0:T(8,128)(2,1)S(1)} %copy-done.1, bf16[576,256]{1,0:T(8,128)(2,1)S(1)} %collective-permute-done.message, ...), custom_call_target="tpu_custom_call" | custom-call | tf_op jit(solution)/shard_map/static_basis/pallas_call | solution.py:132
  34.6 0.8 collective-permute-done.2.from_previous.message.refs_5_
  35.5 1.4 %copy-done.13 = f32[1536,256]{1,0:T(8,128)S(1)} copy-done((f32[1536,256]{1,0:T(8,128)S(1)}, f32[1536,256]{1,0:T(8,128)}, u32[]{:S(2)}) %copy-start.13) | copy-done | bytes 1572888
  36.9 4.2 %schur_load.1 = (f32[1536,256]{1,0:T(8,128)S(1)}, f32[1536,256]{1,0:T(8,128)S(1)}, f32[8,256]{1,0:T(8,128)S(1)}, f32[128,256]{1,0:T(8,128)S(1)}) custom-call(f32[1024,256]{1,0:T(8,128)S(1)} %get-tuple-element.47.load, f32[1536,256]{1,0:T(8,128)S(1)} %copy-done.13, bf16[512,256]{1,0:T(8,128)(2,1)} %collective-permute-done.3.from_next, ...), custom_call_target="tpu_custom_call" | custom-call | tf_op jit(solution)/shard_map/schur_load/pallas_call | solution.py:132
  41.2 1.4 %coarse_load.1 = (f32[96,256]{1,0:T(8,128)S(1)}, f32[64,256]{1,0:T(8,128)S(1)}, f32[1536,256]{1,0:T(8,128)S(1)}, bf16[512,256]{1,0:T(8,128)(2,1)S(1)}, bf16[512,...) custom-call(bf16[8,64,256]{2,1,0:T(8,128)(2,1)S(1)} %all-to-all-done.half, ...), custom_call_target="tpu_custom_call" | custom-call | tf_op jit(solution)/shard_map/coarse_load/pallas_call | solution.py:132
  42.6 1.1 copy-done.14
  43.7 0.6 copy-done.28
  44.3 0.6 copy-done.32
  44.9 0.8 copy_out.3
  45.7 0.6 copy-done.24
  46.3 4.1 %all-to-all-start.1 = ((bf16[8,96,256]{2,1,0:T(8,128)(2,1)}), bf16[8,96,256]{2,1,0:T(8,128)(2,1)}, u32[]{:S(2)}, u32[]{:S(2)}) async-start(bf16[8,96,256]{2,1,0:T(8,128)(2,1)} %copy_out.3), calls=%async_computation.1 | async-start | bytes 786432 | tf_op jit(solution)/shard_map/all_to_all | solution.py:31
  50.4 5.1 %collective-permute-start.4 = (bf16[512,256]{1,0:T(8,128)(2,1)S(1)}, bf16[512,256]{1,0:T(8,128)(2,1)S(1)}, u32[]{:S(2)}, u32[]{:S(2)}) collective-permute-start(bf16[512,256]{1,0:T(8,128)(2,1)S(1)} %get-tuple-element.70), channel_id=1, source_target_pairs={{1,0},{2,1},{3,2},{4,3},{5,4},{6,5},{7,6},{8,7},{9,8},{10,9},{11,1... | collective-permute-start | bytes 786440 | tf_op jit(solution)/shard_map/ppermute | solution.py:19
  55.5 5.3 %collective-permute-done.4.from_next = bf16[512,256]{1,0:T(8,128)(2,1)S(1)} collective-permute-done((bf16[512,256]{1,0:T(8,128)(2,1)S(1)}, bf16[512,256]{1,0:T(8,128)(2,1)S(1)}, u32[]{:S(2)}, u32[]{:S(2)}) %collective-permute-start.4) | collective-permute-done | bytes 262176 | tf_op jit(solution)/shard_map/ppermute | solution.py:19
  60.8 5.3 %collective-permute-done.5.from_previous = bf16[512,256]{1,0:T(8,128)(2,1)S(1)} collective-permute-done((bf16[512,256]{1,0:T(8,128)(2,1)S(1)}, bf16[512,256]{1,0:T(8,128)(2,1)S(1)}, u32[]{:S(2)}, u32[]{:S(2)}) %collective-permute-start.5) | collective-permute-done | bytes 262176 | tf_op jit(solution)/shard_map/ppermute | solution.py:19
  66.1 2.2 %copy-done.5 = bf16[2048,1024]{1,0:T(8,128)(2,1)S(1)} copy-done((bf16[2048,1024]{1,0:T(8,128)(2,1)S(1)}, bf16[2048,1024]{1,0:T(8,128)(2,1)}, u32[]{:S(2)}) %copy-start.5) | copy-done | bytes 4194328
  68.2 1.4 %copy-done.15 = f32[1536,256]{1,0:T(8,128)S(1)} copy-done((f32[1536,256]{1,0:T(8,128)S(1)}, f32[1536,256]{1,0:T(8,128)}, u32[]{:S(2)}) %copy-start.15) | copy-done | bytes 1572888
  69.6 1.5 %neumann_image.1 = (f32[1024,256]{1,0:T(8,128)S(1)}, f32[1536,256]{1,0:T(8,128)S(1)}, bf16[512,256]{1,0:T(8,128)(2,1)S(1)}, bf16[512,256]{1,0:T(8,128)(2,1)S(1)}) custom-call(f32[1536,256]{1,0:T(8,128)S(1)} %copy-done.15, bf16[512,256]{1,0:T(8,128)(2,1)S(1)} %collective-permute-done.4.from_next, bf16[512,256]{1,0:T(8,128)(2,1)S(1)} %collective-permute-done.5.from_previous, ...), custom_call_target="tpu_custom_call" | custom-call | tf_op jit(solution)/shard_map/neumann_image/pallas_call | solution.py:132
  71.2 1.2 %copy-done.6 = f32[1536,256]{1,0:T(8,128)} copy-done((f32[1536,256]{1,0:T(8,128)}, f32[1536,256]{1,0:T(8,128)S(1)}, u32[]{:S(2)}) %copy-start.6) | copy-done | bytes 1572888
  72.4 0.7 copy-done.34
  73.1 0.7 copy-done.35
  74.3 3.9 %collective-permute-start.7 = (bf16[512,256]{1,0:T(8,128)(2,1)}, bf16[512,256]{1,0:T(8,128)(2,1)S(1)}, u32[]{:S(2)}, u32[]{:S(2)}) collective-permute-start(bf16[512,256]{1,0:T(8,128)(2,1)} %copy-done.34), channel_id=1, source_target_pairs={{1,0},{2,1},{3,2},{4,3},{5,4},{6,5},{7,6},{8,7},{9,8},{10,9},{11,1... | collective-permute-start | bytes 786440 | tf_op jit(solution)/shard_map/ppermute | solution.py:19
  78.2 4.4 %collective-permute-done.8.refs_3_ = bf16[512,256]{1,0:T(8,128)(2,1)S(1)} collective-permute-done((bf16[512,256]{1,0:T(8,128)(2,1)}, bf16[512,256]{1,0:T(8,128)(2,1)S(1)}, u32[]{:S(2)}, u32[]{:S(2)}) %collective-permute-start.8) | collective-permute-done | bytes 262176 | tf_op jit(solution)/shard_map/ppermute | solution.py:19
  82.6 2.2 %copy-done.3 = bf16[2048,1024]{1,0:T(8,128)(2,1)S(1)} copy-done((bf16[2048,1024]{1,0:T(8,128)(2,1)S(1)}, bf16[2048,1024]{1,0:T(8,128)(2,1)}, u32[]{:S(2)}) %copy-start.3) | copy-done | bytes 4194328
  84.8 1.4 %copy-done.7 = f32[1536,256]{1,0:T(8,128)S(1)} copy-done((f32[1536,256]{1,0:T(8,128)S(1)}, f32[1536,256]{1,0:T(8,128)}, u32[]{:S(2)}) %copy-start.7) | copy-done | bytes 1572888
  86.2 0.9 copy-done.19
  87.1 0.9 copy-done.21
  88.1 3.3 %schur_image.1 = (f32[1536,256]{1,0:T(8,128)S(1)}, f32[1536,256]{1,0:T(8,128)S(1)}, f32[8,256]{1,0:T(8,128)S(1)}, f32[128,256]{1,0:T(8,128)S(1)}) custom-call(f32[1024,256]{1,0:T(8,128)S(1)} %get-tuple-element.74.refs_0_.image, f32[1536,256]{1,0:T(8,128)S(1)} %copy-done.7, bf16[512,256]{1,0:T(8,128)(2,1)S(1)} %collective-permute-done.7.refs_2_, ...), custom_call_target="tpu_custom_call" | custom-call | tf_op jit(solution)/shard_map/schur_image/pallas_call | solution.py:132
  91.4 3.3 %coarse_image.1 = (f32[8,4,256]{2,1,0:T(4,128)S(1)}, f32[64,256]{1,0:T(8,128)S(1)}, f32[1024,256]{1,0:T(8,128)S(1)}, bf16[512,256]{1,0:T(8,128)(2,1)}) custom-call(bf16[8,96,256]{2,1,0:T(8,128)(2,1)} %all-to-all-done.1.half, bf16[8,96,256]{2,1,0:T(8,128)(2,1)S(1)} %collective-permute-done.6.crossed_half, bf16[64,1024]{1,0:T(8,128)(2,1)S(1)} %copy-done.17, ...), custom_call_target="tpu_custom_call" | custom-call | tf_op jit(solution)/shard_map/coarse_image/pallas_call | solution.py:132
  94.7 1.0 copy-done.22
  95.7 0.6 copy-done.30
  96.3 4.3 %collective-permute-start.10 = (bf16[512,256]{1,0:T(8,128)(2,1)}, bf16[512,256]{1,0:T(8,128)(2,1)S(1)}, u32[]{:S(2)}, u32[]{:S(2)}) collective-permute-start(bf16[512,256]{1,0:T(8,128)(2,1)} %get-tuple-element.89), channel_id=1, source_target_pairs={{1,0},{2,1},{3,2},{4,3},{5,4},{6,5},{7,6},{8,7},{9,8},{10,9},{11,1... | collective-permute-start | bytes 786440 | tf_op jit(solution)/shard_map/ppermute | solution.py:19
  100.6 9.0 %all_to_all.15 = f32[8,4,256]{2,1,0:T(4,128)S(1)} all-to-all(f32[8,4,256]{2,1,0:T(4,128)S(1)} %get-tuple-element.81), channel_id=1, replica_groups={{0,2,4,6,8,10,12,14},{1,3,5,7,9,11,13,15},{16,18,20,22,24,26,28,30},{17..., dimensions={0} | all-to-all | bytes 65536 | tf_op jit(solution)/shard_map/all_to_all | solution.py:31
  109.8 1.4 %copy-done.9 = f32[1536,256]{1,0:T(8,128)S(1)} copy-done((f32[1536,256]{1,0:T(8,128)S(1)}, f32[1536,256]{1,0:T(8,128)}, u32[]{:S(2)}) %copy-start.9) | copy-done | bytes 1572888
  111.2 1.4 %copy-done.11 = f32[1536,256]{1,0:T(8,128)S(1)} copy-done((f32[1536,256]{1,0:T(8,128)S(1)}, f32[1536,256]{1,0:T(8,128)}, u32[]{:S(2)}) %copy-start.11) | copy-done | bytes 1572888
  112.6 0.8 copy-done.29
  113.4 0.8 copy-done.31
  114.3 0.7 complete.1
  115.5 1.6 %combine.1 = (f32[1024,256]{1,0:T(8,128)}, f32[1024,256]{1,0:T(8,128)}) custom-call(f32[4,256]{1,0:T(4,128)S(1)} %reduce_sum.9.sums, f32[4,256]{1,0:T(4,128)S(1)} %collective-permute-done.9.crossed_sums, f32[1024,256]{1,0:T(8,128)S(1)} %get-tuple-element.47.load, f32[1024,256]{1,0:T(8,128)S(1)} %get-tuple-element.86.z, f32[1024,256]{1,0:T(8,128)S(1)} %get-tuple-element.87.y, ...), custom_call_target="tpu_custom_call" | custom-call | tf_op jit(solution)/shard_map/combine/pallas_call | solution.py:132
  (66 shorter events, 1.5 us)
Async XLA Ops:
  2.9 27.6 %all-to-all-start = ((bf16[8,64,256]{2,1,0:T(8,128)(2,1)}), bf16[8,64,256]{2,1,0:T(8,128)(2,1)S(1)}, u32[]{:S(2)}, u32[]{:S(2)}) async-start(bf16[8,64,256]{2,1,0:T(8,128)(2,1)} %copy_out.2), calls=%async_computation | async-start | bytes 524288 | tf_op jit(solution)/shard_map/all_to_all | solution.py:31
  10.4 12.2 %collective-permute-start = (bf16[576,256]{1,0:T(8,128)(2,1)S(1)}, bf16[576,256]{1,0:T(8,128)(2,1)S(1)}, u32[]{:S(2)}, u32[]{:S(2)}) collective-permute-start(bf16[576,256]{1,0:T(8,128)(2,1)S(1)} %first_message.1), channel_id=1, source_target_pairs={{15,0},{0,1},{1,2},{2,3},{3,4},{4,5},{5,6},{6,7},{7,8},{8,9},{9,10... | collective-permute-start | bytes 884744 | tf_op jit(solution)/shard_map/ppermute | solution.py:19
  14.0 2.0 %copy-start = (bf16[2048,1024]{1,0:T(8,128)(2,1)}, bf16[2048,1024]{1,0:T(8,128)(2,1)S(1)}, u32[]{:S(2)}) copy-start(bf16[2048,1024]{1,0:T(8,128)(2,1)S(1)} %get-tuple-element.59.schur.refs_6_) | copy-start | bytes 12582916
  16.0 8.9 %copy-start.4 = (bf16[2048,1024]{1,0:T(8,128)(2,1)}, bf16[2048,1024]{1,0:T(8,128)(2,1)S(1)}, u32[]{:S(2)}) copy-start(bf16[2048,1024]{1,0:T(8,128)(2,1)S(1)} %get-tuple-element.53.neumann) | copy-start | bytes 12582916
  16.0 25.2 %copy-start.16 = (bf16[64,1024]{1,0:T(8,128)(2,1)}, bf16[64,1024]{1,0:T(8,128)(2,1)S(1)}, u32[]{:S(2)}) copy-start(bf16[64,1024]{1,0:T(8,128)(2,1)S(1)} %get-tuple-element.54.inverse) | copy-start | bytes 393220
  24.8 1.2 copy-start.12
  26.0 9.5 %collective-permute-start.2 = (bf16[656,256]{1,0:T(8,128)(2,1)}, bf16[656,256]{1,0:T(8,128)(2,1)S(1)}, u32[]{:S(2)}, u32[]{:S(2)}) collective-permute-start(bf16[656,256]{1,0:T(8,128)(2,1)} %get-tuple-element.57), channel_id=1, source_target_pairs={{15,0},{0,1},{1,2},{2,3},{3,4},{4,5},{5,6},{6,7},{7,8},{8,9},{9,10... | collective-permute-start | bytes 1007624 | tf_op jit(solution)/shard_map/ppermute | solution.py:19
  26.0 8.6 %collective-permute-start.3 = (bf16[512,256]{1,0:T(8,128)(2,1)}, bf16[512,256]{1,0:T(8,128)(2,1)}, u32[]{:S(2)}, u32[]{:S(2)}) collective-permute-start(bf16[512,256]{1,0:T(8,128)(2,1)} %get-tuple-element.55), channel_id=1, source_target_pairs={{1,0},{2,1},{3,2},{4,3},{5,4},{6,5},{7,6},{8,7},{9,8},{10,9},{11,1... | collective-permute-start | bytes 786440 | tf_op jit(solution)/shard_map/ppermute | solution.py:19
  30.4 10.7 %collective-permute-start.1 = (bf16[8,64,256]{2,1,0:T(8,128)(2,1)S(1)}, bf16[8,64,256]{2,1,0:T(8,128)(2,1)S(1)}, u32[]{:S(2)}, u32[]{:S(2)}) collective-permute-start(bf16[8,64,256]{2,1,0:T(8,128)(2,1)S(1)} %all-to-all-done.half), channel_id=1, source_target_pairs={{0,1},{1,0},{2,3},{3,2},{4,5},{5,4},{6,7},{7,6},{8,9},{9,8},{10,11... | collective-permute-start | bytes 786440 | tf_op jit(solution)/shard_map/ppermute | solution.py:23
  30.4 2.2 %copy-start.1 = (bf16[2048,1024]{1,0:T(8,128)(2,1)S(1)}, bf16[2048,1024]{1,0:T(8,128)(2,1)}, u32[]{:S(2)}) copy-start(bf16[2048,1024]{1,0:T(8,128)(2,1)} %copy-done) | copy-start | bytes 12582916
  32.6 2.9 %copy-start.2 = (bf16[2048,1024]{1,0:T(8,128)(2,1)S(1)}, bf16[2048,1024]{1,0:T(8,128)(2,1)}, u32[]{:S(2)}) copy-start(bf16[2048,1024]{1,0:T(8,128)(2,1)} %copy-done) | copy-start | bytes 12582916
  34.5 6.6 %copy-start.18 = (bf16[128,1024]{1,0:T(8,128)(2,1)}, bf16[128,1024]{1,0:T(8,128)(2,1)S(1)}, u32[]{:S(2)}) copy-start(bf16[128,1024]{1,0:T(8,128)(2,1)S(1)} %get-tuple-element.60.turned_high.refs_7_) | copy-start | bytes 786436
  34.6 6.6 %copy-start.20 = (bf16[128,1024]{1,0:T(8,128)(2,1)}, bf16[128,1024]{1,0:T(8,128)(2,1)S(1)}, u32[]{:S(2)}) copy-start(bf16[128,1024]{1,0:T(8,128)(2,1)S(1)} %get-tuple-element.61.turned_low.refs_8_) | copy-start | bytes 786436
  34.6 6.6 %copy-start.26 = (f32[128,128]{1,0:T(8,128)}, f32[128,128]{1,0:T(8,128)S(1)}, u32[]{:S(2)}) copy-start(f32[128,128]{1,0:T(8,128)S(1)} %get-tuple-element.63.gram) | copy-start | bytes 196612
  35.5 1.4 %copy-start.13 = (f32[1536,256]{1,0:T(8,128)S(1)}, f32[1536,256]{1,0:T(8,128)}, u32[]{:S(2)}) copy-start(f32[1536,256]{1,0:T(8,128)} %copy-done.12) | copy-start | bytes 4718596
  41.1 1.4 %copy-start.8 = (f32[1536,256]{1,0:T(8,128)}, f32[1536,256]{1,0:T(8,128)S(1)}, u32[]{:S(2)}) copy-start(f32[1536,256]{1,0:T(8,128)S(1)} %get-tuple-element.82.z_local) | copy-start | bytes 4718596
  42.6 1.1 copy-start.14
  43.7 0.6 copy-start.28
  45.7 0.6 copy-start.24
  46.3 27.4 %all-to-all-start.1 = ((bf16[8,96,256]{2,1,0:T(8,128)(2,1)}), bf16[8,96,256]{2,1,0:T(8,128)(2,1)}, u32[]{:S(2)}, u32[]{:S(2)}) async-start(bf16[8,96,256]{2,1,0:T(8,128)(2,1)} %copy_out.3), calls=%async_computation.1 | async-start | bytes 786432 | tf_op jit(solution)/shard_map/all_to_all | solution.py:31
  50.4 10.3 %collective-permute-start.4 = (bf16[512,256]{1,0:T(8,128)(2,1)S(1)}, bf16[512,256]{1,0:T(8,128)(2,1)S(1)}, u32[]{:S(2)}, u32[]{:S(2)}) collective-permute-start(bf16[512,256]{1,0:T(8,128)(2,1)S(1)} %get-tuple-element.70), channel_id=1, source_target_pairs={{1,0},{2,1},{3,2},{4,3},{5,4},{6,5},{7,6},{8,7},{9,8},{10,9},{11,1... | collective-permute-start | bytes 786440 | tf_op jit(solution)/shard_map/ppermute | solution.py:19
  55.5 10.5 %collective-permute-start.5 = (bf16[512,256]{1,0:T(8,128)(2,1)S(1)}, bf16[512,256]{1,0:T(8,128)(2,1)S(1)}, u32[]{:S(2)}, u32[]{:S(2)}) collective-permute-start(bf16[512,256]{1,0:T(8,128)(2,1)S(1)} %get-tuple-element.71), channel_id=1, source_target_pairs={{15,0},{0,1},{1,2},{2,3},{3,4},{4,5},{5,6},{6,7},{7,8},{8,9},{9,10... | collective-permute-start | bytes 786440 | tf_op jit(solution)/shard_map/ppermute | solution.py:19
  66.1 2.2 %copy-start.5 = (bf16[2048,1024]{1,0:T(8,128)(2,1)S(1)}, bf16[2048,1024]{1,0:T(8,128)(2,1)}, u32[]{:S(2)}) copy-start(bf16[2048,1024]{1,0:T(8,128)(2,1)} %copy-done.4) | copy-start | bytes 12582916
  68.2 1.4 %copy-start.15 = (f32[1536,256]{1,0:T(8,128)S(1)}, f32[1536,256]{1,0:T(8,128)}, u32[]{:S(2)}) copy-start(f32[1536,256]{1,0:T(8,128)} %copy-done.14) | copy-start | bytes 4718596
  71.2 1.2 %copy-start.6 = (f32[1536,256]{1,0:T(8,128)}, f32[1536,256]{1,0:T(8,128)S(1)}, u32[]{:S(2)}) copy-start(f32[1536,256]{1,0:T(8,128)S(1)} %get-tuple-element.75.refs_1_) | copy-start | bytes 4718596
  72.4 0.7 copy-start.34
  73.1 0.7 copy-start.35
  73.8 17.6 %collective-permute-start.6 = (bf16[8,96,256]{2,1,0:T(8,128)(2,1)}, bf16[8,96,256]{2,1,0:T(8,128)(2,1)S(1)}, u32[]{:S(2)}, u32[]{:S(2)}) collective-permute-start(bf16[8,96,256]{2,1,0:T(8,128)(2,1)} %all-to-all-done.1.half), channel_id=1, source_target_pairs={{0,1},{1,0},{2,3},{3,2},{4,5},{5,4},{6,7},{7,6},{8,9},{9,8},{10,11... | collective-permute-start | bytes 1179656 | tf_op jit(solution)/shard_map/ppermute | solution.py:23
  73.8 8.8 %collective-permute-start.8 = (bf16[512,256]{1,0:T(8,128)(2,1)}, bf16[512,256]{1,0:T(8,128)(2,1)S(1)}, u32[]{:S(2)}, u32[]{:S(2)}) collective-permute-start(bf16[512,256]{1,0:T(8,128)(2,1)} %copy-done.35), channel_id=1, source_target_pairs={{15,0},{0,1},{1,2},{2,3},{3,4},{4,5},{5,6},{6,7},{7,8},{8,9},{9,10... | collective-permute-start | bytes 786440 | tf_op jit(solution)/shard_map/ppermute | solution.py:19
  74.3 8.3 %collective-permute-start.7 = (bf16[512,256]{1,0:T(8,128)(2,1)}, bf16[512,256]{1,0:T(8,128)(2,1)S(1)}, u32[]{:S(2)}, u32[]{:S(2)}) collective-permute-start(bf16[512,256]{1,0:T(8,128)(2,1)} %copy-done.34), channel_id=1, source_target_pairs={{1,0},{2,1},{3,2},{4,3},{5,4},{6,5},{7,6},{8,7},{9,8},{10,9},{11,1... | collective-permute-start | bytes 786440 | tf_op jit(solution)/shard_map/ppermute | solution.py:19
  82.6 2.2 %copy-start.3 = (bf16[2048,1024]{1,0:T(8,128)(2,1)S(1)}, bf16[2048,1024]{1,0:T(8,128)(2,1)}, u32[]{:S(2)}) copy-start(bf16[2048,1024]{1,0:T(8,128)(2,1)} %copy-done) | copy-start | bytes 12582916
  84.8 1.4 %copy-start.7 = (f32[1536,256]{1,0:T(8,128)S(1)}, f32[1536,256]{1,0:T(8,128)}, u32[]{:S(2)}) copy-start(f32[1536,256]{1,0:T(8,128)} %copy-done.6) | copy-start | bytes 4718596
  86.2 0.9 copy-start.19
  87.1 0.9 copy-start.21
  88.1 3.3 %copy-start.17 = (bf16[64,1024]{1,0:T(8,128)(2,1)S(1)}, bf16[64,1024]{1,0:T(8,128)(2,1)}, u32[]{:S(2)}) copy-start(bf16[64,1024]{1,0:T(8,128)(2,1)} %copy-done.16) | copy-start | bytes 393220
  88.1 3.3 %copy-start.25 = (f32[96,256]{1,0:T(8,128)S(1)}, f32[96,256]{1,0:T(8,128)}, u32[]{:S(2)}) copy-start(f32[96,256]{1,0:T(8,128)} %copy-done.24) | copy-start | bytes 294916
  88.1 3.3 %copy-start.27 = (f32[128,128]{1,0:T(8,128)S(1)}, f32[128,128]{1,0:T(8,128)}, u32[]{:S(2)}) copy-start(f32[128,128]{1,0:T(8,128)} %copy-done.26) | copy-start | bytes 196612
  88.1 3.3 %copy-start.33 = (f32[8,256]{1,0:T(8,128)S(1)}, f32[8,256]{1,0:T(8,128)}, u32[]{:S(2)}) copy-start(f32[8,256]{1,0:T(8,128)} %copy-done.32) | copy-start | bytes 24580
  91.4 3.3 %copy-start.10 = (f32[1536,256]{1,0:T(8,128)}, f32[1536,256]{1,0:T(8,128)S(1)}, u32[]{:S(2)}) copy-start(f32[1536,256]{1,0:T(8,128)S(1)} %get-tuple-element.84.y_local) | copy-start | bytes 4718596
  94.7 1.0 copy-start.22
  95.7 0.6 copy-start.30
  96.3 18.7 %collective-permute-start.10 = (bf16[512,256]{1,0:T(8,128)(2,1)}, bf16[512,256]{1,0:T(8,128)(2,1)S(1)}, u32[]{:S(2)}, u32[]{:S(2)}) collective-permute-start(bf16[512,256]{1,0:T(8,128)(2,1)} %get-tuple-element.89), channel_id=1, source_target_pairs={{1,0},{2,1},{3,2},{4,3},{5,4},{6,5},{7,6},{8,7},{9,8},{10,9},{11,1... | collective-permute-start | bytes 786440 | tf_op jit(solution)/shard_map/ppermute | solution.py:19
  109.7 5.3 %collective-permute-start.9 = (f32[4,256]{1,0:T(4,128)S(1)}, f32[4,256]{1,0:T(4,128)S(1)}, u32[]{:S(2)}, u32[]{:S(2)}) collective-permute-start(f32[4,256]{1,0:T(4,128)S(1)} %reduce_sum.9.sums), channel_id=1, source_target_pairs={{0,1},{1,0},{2,3},{3,2},{4,5},{5,4},{6,7},{7,6},{8,9},{9,8},{10,11... | collective-permute-start | bytes 12296 | tf_op jit(solution)/shard_map/ppermute | solution.py:23
  109.8 1.4 %copy-start.9 = (f32[1536,256]{1,0:T(8,128)S(1)}, f32[1536,256]{1,0:T(8,128)}, u32[]{:S(2)}) copy-start(f32[1536,256]{1,0:T(8,128)} %copy-done.8) | copy-start | bytes 4718596
  111.2 1.4 %copy-start.11 = (f32[1536,256]{1,0:T(8,128)S(1)}, f32[1536,256]{1,0:T(8,128)}, u32[]{:S(2)}) copy-start(f32[1536,256]{1,0:T(8,128)} %copy-done.10) | copy-start | bytes 4718596
  112.6 0.8 copy-start.29
  113.4 0.8 copy-start.31
  114.3 1.2 %copy-start.23 = (f32[1024,256]{1,0:T(8,128)S(1)}, f32[1024,256]{1,0:T(8,128)}, u32[]{:S(2)}) copy-start(f32[1024,256]{1,0:T(8,128)} %copy-done.22) | copy-start | bytes 3145732
  (1 other events, 0.6 us)

commit v7 on v5

--- a/solution.py
+++ b/solution.py
@@ -27,10 +27,14 @@
     return [1 << k for k in reversed(range(lax.axis_size(AXIS).bit_length() - 1))]
 
 
-def gather_halves(block):
-    for bit in bits()[:-1]:
-        block = jnp.concatenate([block, crossed(block, bit)], axis=0)
-    return block, crossed(block, 1)
+def after(value, *others):
+    return lax.optimization_barrier((value, others))[0]
+
+
+def gather_half(block, steps, *others):
+    for bit in steps:
+        block = jnp.concatenate([block, after(crossed(block, bit), *others)], axis=0)
+    return block
 
 
 def half_order():
@@ -397,28 +401,35 @@
     products = [(faces, F32), (faces, F32), ((8, columns), F32), ((local_rows, columns), F32)]
     semaphores = lambda count: [pltpu.SemaphoreType.DMA((count,))]
     described = lambda array: (array.shape, array.dtype)
+    outside = lambda array: pltpu.with_memory_space_constraint(array, pltpu.HBM)
+    steps = bits()
+    early, late = steps[:-2], steps[-2:-1]
 
     load, rows, weight, coarse_rounded, coarse = stage(
         bind(prepare),
         [described(right_side), described(constraint), described(face_weight), (coarse_own, BF16), (coarse_own, F32)],
-        right_side, constraint, face_weight, scratch=semaphores(subs + 2), fetched=3,
+        *map(outside, (right_side, constraint, face_weight)), scratch=semaphores(subs + 2), fetched=3,
     )
     (first,) = stage(bind(first_message), [((halo.first_height, columns), BF16)], load, weight, rows)
-    coarse_halves = gather_halves(coarse_rounded)
-    tied, _ = lax.optimization_barrier(((neumann, schur, coarse_inverse), first))
+    half = gather_half(coarse_rounded, early[:1])
+    tied = after(tuple(map(outside, (neumann, schur, coarse_inverse))), first)
     neumann, schur, inverse = stage(
         bind(fetch), [described(array) for array in tied], *tied, scratch=semaphores(3), fetched=3
     )
-    first = shifted(first, 1)
+    first = after(shifted(first, 1), half)
     part, back, forward = stage(
         bind(neumann_load), [(faces, F32), ((nf, columns), BF16), ((halo.second_height, columns), BF16)],
         load, weight, first, neumann, inverse, scratch=[pltpu.VMEM((halo.weight_count, columns), F32)],
     )
+    half = gather_half(half, early[1:], back)
     back, second = shifted(back, -1), shifted(forward, 1)
     long, wide = ((2 * subs * nf, 2 * ncf), BF16), ((local_rows, 2 * nf), BF16)
     basis_high, basis_low, turned_high, turned_low, gram = stage(
         bind(static_basis), [long, long, wide, wide, ((local_rows, LANES), F32)], schur, first, rows
     )
+    half = gather_half(half, late, back, second, gram)
+    crossed_half = crossed(half, 1)
+    part = after(part, half)
     z_local, product, quadratic, base = stage(
         bind(schur_load), products, load, part, back, second, weight, schur, turned_high, turned_low
     )
@@ -426,30 +437,33 @@
     shares_rounded, shares, z_coarse, part, back, forward, sums = stage(
         bind(coarse_load),
         [(share_rows, BF16), (share_rows, F32), (coarse_own, F32), (faces, F32)] + halves + [((8, columns), F32)],
-        *coarse_halves, inverse, second, coarse, base, gram, quadratic, basis_high, basis_low, product,
+        half, crossed_half, inverse, second, coarse, base, gram, quadratic, basis_high, basis_low, product,
         scratch=[pltpu.VMEM((nco, columns), BF16)],
     )
-    coarse_halves = gather_halves(shares_rounded)
+    half = gather_half(shares_rounded, early[:1])
     back, forward = shifted(back, -1), shifted(forward, 1)
     image, part, back, forward = stage(
         bind(neumann_image), [(own, F32), (faces, F32)] + halves, part, back, forward, weight, second, neumann
     )
+    half = gather_half(half, early[1:], back)
     back, forward = shifted(back, -1), shifted(forward, 1)
+    half = gather_half(half, late, back, forward)
+    crossed_half = crossed(half, 1)
+    part = after(part, half)
     y_local, product, quadratic, base = stage(
         bind(schur_image), products, image, part, back, forward, weight, second, schur, turned_high, turned_low
     )
     sums, y_coarse, part, back = stage(
         bind(coarse_image), [((4, columns), F32), (coarse_own, F32), (own, F32), ((nf, columns), BF16)],
-        *coarse_halves, inverse, second, shares, base, gram, quadratic, basis_high, basis_low, product, sums,
+        half, crossed_half, inverse, second, shares, base, gram, quadratic, basis_high, basis_low, product, sums,
         scratch=[pltpu.VMEM((nco, columns), F32)],
     )
-    steps = bits()
-    for k, bit in enumerate(steps):
+    for bit in early:
         sums = sums + crossed(sums, bit)
-        if k + 1 == len(steps) // 2:
-            sums, back = lax.optimization_barrier((sums, back))
-            back = shifted(back, -1)
-    z, y = stage(bind(complete), [(own, F32), (own, F32)], z_local, z_coarse, y_local, y_coarse, rows)
+    z, y = stage(bind(complete), [(own, F32), (own, F32)], z_local, z_coarse, after(y_local, sums), y_coarse, rows)
+    for bit in steps[-2:]:
+        sums = sums + crossed(sums, bit)
+    back = shifted(after(back, y), -1)
     return stage(bind(combine), [(own, F32), (own, F32)], sums, load, z, y, image, part, back)
 
 

time: 86.1 us -> 80.8 us (0.938)
  local copies, waits for them, and re-layouts: 7.17 us -> 0 us
  Pallas kernels: 18.3 us -> 22.3 us
  waiting for transfers between devices: 36.8 us -> 33.9 us
  starting transfers between devices: 22.6 us -> 23.5 us
    ppermute x8, waiting for transfers between devices: 11.4 us -> 2.68 us  [shifted(): lax.ppermute(block, AXIS, [((i - distance) % n, i) for i in range(n)])]
    unnamed x18 -> x0, local copies, waits for them, and re-layouts: 7.15 us -> none
    ppermute x12, waiting for transfers between devices: 25.4 us -> 31.3 us  [crossed(): lax.ppermute(block, AXIS, [(i, i ^ bit) for i in range(lax.axis_size(AXIS...]
    pallas_call x12, Pallas kernels: 18.3 us -> 22.3 us  [stage(): return call(*operands)]
    ppermute x8, starting transfers between devices: 10.9 us -> 14.6 us  [shifted(): lax.ppermute(block, AXIS, [((i - distance) % n, i) for i in range(n)])]
    ppermute x12, starting transfers between devices: 11.7 us -> 8.89 us  [crossed(): lax.ppermute(block, AXIS, [(i, i ^ bit) for i in range(lax.axis_size(AXIS...]
  transfers between devices with their start and end apart: 20 -> 20, of which waited for: 12 -> 9; matrix products, arithmetic and copies ran while one was open for 0% -> 0% of each run, Pallas kernels for 15% -> 17%
where the time goes in v7:
time: 80.8 us; the launch traced here: 80.7 us
  waiting for transfers between devices  33.9 us (42%)
  starting transfers between devices  23.5 us (29%)
  Pallas kernels  22.3 us (28%)
  between operations  0.82 us (1%)
    ppermute x12, waiting for transfers between devices, crossed(): lax.ppermute(block, AXIS, [(i, i ^ bit) for i in range(lax.axis_size(AXIS...  31.3 us
    pallas_call x12, Pallas kernels, stage(): return call(*operands)  22.3 us
    ppermute x8, starting transfers between devices, shifted(): lax.ppermute(block, AXIS, [((i - distance) % n, i) for i in range(n)])  14.6 us
    ppermute x12, starting transfers between devices, crossed(): lax.ppermute(block, AXIS, [(i, i ^ bit) for i in range(lax.axis_size(AXIS...  8.89 us
    ppermute x8, waiting for transfers between devices, shifted(): lax.ppermute(block, AXIS, [((i - distance) % n, i) for i in range(n)])  2.68 us
  transfers between devices with their start and end apart: 20, of which 9 were waited for; matrix products, arithmetic and copies ran while one was open for 0% of the time, Pallas kernels for 17%

profile of v7, /device:TPU:0, one launch (start us, length us, event | category | flops | bytes accessed | tf_op | source)
XLA Modules:
  0.0 80.7 jit_solution(15972715949413807493)
XLA Ops:
  0.6 1.5 %prepare.1 = (f32[1024,256]{1,0:T(8,128)S(1)}, bf16[64,512]{1,0:T(8,128)(2,1)S(1)}, f32[2,512]{1,0:T(2,128)S(1)}, bf16[64,256]{1,0:T(8,128)(2,1)S(1)}, f32[64,256]{1,0:T(8,128)S(1)}) custom-call(f32[1024,256]{1,0:T(8,128)} %load.1, bf16[64,512]{1,0:T(8,128)(2,1)} %rows.1, f32[2,512]{1,0:T(2,128)} %weight.1), custom_call_target="tpu_custom_call" | custom-call | tf_op jit(solution)/shard_map/prepare/pallas_call | solution.py:145
  2.1 0.3 first_message.1
  2.4 0.5 collective-permute-start.2
  2.9 3.7 %collective-permute-start = (bf16[64,256]{1,0:T(8,128)(2,1)S(1)}, bf16[64,256]{1,0:T(8,128)(2,1)S(1)}, u32[]{:S(2)}, u32[]{:S(2)}) collective-permute-start(bf16[64,256]{1,0:T(8,128)(2,1)S(1)} %get-tuple-element.55), channel_id=1, source_target_pairs={{0,8},{1,9},{2,10},{3,11},{4,12},{5,13},{6,14},{7,15},{8,0},{9,1},... | collective-permute-start | bytes 98312 | tf_op jit(solution)/shard_map/ppermute | solution.py:23
  6.6 3.5 %fetch.1 = (bf16[2048,1024]{1,0:T(8,128)(2,1)S(1)}, bf16[2048,1024]{1,0:T(8,128)(2,1)S(1)}, bf16[64,1024]{1,0:T(8,128)(2,1)S(1)}) custom-call(bf16[2048,1024]{1,0:T(8,128)(2,1)} %neumann, bf16[2048,1024]{1,0:T(8,128)(2,1)} %schur, bf16[64,1024]{1,0:T(8,128)(2,1)} %inverse), custom_call_target="tpu_custom_call" | custom-call | tf_op jit(solution)/shard_map/fetch/pallas_call | solution.py:145
  10.1 0.0 collective-permute-done
  10.1 2.7 %collective-permute-done.2.message = bf16[576,256]{1,0:T(8,128)(2,1)S(1)} collective-permute-done((bf16[576,256]{1,0:T(8,128)(2,1)S(1)}, bf16[576,256]{1,0:T(8,128)(2,1)S(1)}, u32[]{:S(2)}, u32[]{:S(2)}) %collective-permute-start.2) | collective-permute-done | bytes 294944 | tf_op jit(solution)/shard_map/ppermute | solution.py:19
  12.8 1.5 %neumann_load.1 = (f32[1536,256]{1,0:T(8,128)S(1)}, bf16[512,256]{1,0:T(8,128)(2,1)S(1)}, bf16[656,256]{1,0:T(8,128)(2,1)S(1)}) custom-call(f32[1024,256]{1,0:T(8,128)S(1)} %get-tuple-element.56.load, f32[2,512]{1,0:T(2,128)S(1)} %get-tuple-element.57.weight.refs_4_, bf16[576,256]{1,0:T(8,128)(2,1)S(1)} %collective-permute-done.2.message, ...), custom_call_target="tpu_custom_call" | custom-call | tf_op jit(solution)/shard_map/neumann_load/pallas_call | solution.py:145
  14.2 0.1 collective-permute-start.5
  14.3 0.2 collective-permute-start.1
  14.5 4.3 %collective-permute-start.4 = (bf16[512,256]{1,0:T(8,128)(2,1)S(1)}, bf16[512,256]{1,0:T(8,128)(2,1)S(1)}, u32[]{:S(2)}, u32[]{:S(2)}) collective-permute-start(bf16[512,256]{1,0:T(8,128)(2,1)S(1)} %get-tuple-element.65), channel_id=1, source_target_pairs={{1,0},{2,1},{3,2},{4,3},{5,4},{6,5},{7,6},{8,7},{9,8},{10,9},{11,1... | collective-permute-start | bytes 786440 | tf_op jit(solution)/shard_map/ppermute | solution.py:19
  18.8 0.1 collective-permute-done.1
  18.9 1.7 %collective-permute-start.3 = (bf16[256,256]{1,0:T(8,128)(2,1)S(1)}, bf16[256,256]{1,0:T(8,128)(2,1)S(1)}, u32[]{:S(2)}, u32[]{:S(2)}) collective-permute-start(bf16[256,256]{1,0:T(8,128)(2,1)S(1)} %pad_maximum_fusion.3), channel_id=1, source_target_pairs={{0,2},{1,3},{2,0},{3,1},{4,6},{5,7},{6,4},{7,5},{8,10},{9,11},{10,... | collective-permute-start | bytes 393224 | tf_op jit(solution)/shard_map/ppermute | solution.py:23
  20.6 1.9 %static_basis.1 = (bf16[2048,64]{1,0:T(8,128)(2,1)S(1)}, bf16[2048,64]{1,0:T(8,128)(2,1)S(1)}, bf16[128,1024]{1,0:T(8,128)(2,1)S(1)}, bf16[128,1024]{1,0:T(8,128)(2,1)S(1)}, f32[128,128]{1,0:T(8,128)S(1)}) custom-call(bf16[2048,1024]{1,0:T(8,128)(2,1)S(1)} %get-tuple-element.68.schur.refs_6_, bf16[576,256]{1,0:T(8,128)(2,1)S(1)} %collective-permute-done.2.message, ...), custom_call_target="tpu_custom_call" | custom-call | tf_op jit(solution)/shard_map/static_basis/pallas_call | solution.py:145
  22.5 5.7 %collective-permute-done.3 = bf16[256,256]{1,0:T(8,128)(2,1)S(1)} collective-permute-done((bf16[256,256]{1,0:T(8,128)(2,1)S(1)}, bf16[256,256]{1,0:T(8,128)(2,1)S(1)}, u32[]{:S(2)}, u32[]{:S(2)}) %collective-permute-start.3) | collective-permute-done | bytes 131104 | tf_op jit(solution)/shard_map/ppermute | solution.py:23
  28.3 0.0 collective-permute-done.4.from_next
  28.3 0.0 collective-permute-done.5.from_previous.message.refs_5_
  28.3 0.1 collective-permute-start.6
  28.4 3.3 %schur_load.1 = (f32[1536,256]{1,0:T(8,128)S(1)}, f32[1536,256]{1,0:T(8,128)S(1)}, f32[8,256]{1,0:T(8,128)S(1)}, f32[128,256]{1,0:T(8,128)S(1)}) custom-call(f32[1024,256]{1,0:T(8,128)S(1)} %get-tuple-element.56.load, f32[1536,256]{1,0:T(8,128)S(1)} %get-tuple-element.73.part, bf16[512,256]{1,0:T(8,128)(2,1)S(1)} %collective-permute-done.4.from_next, ...), custom_call_target="tpu_custom_call" | custom-call | tf_op jit(solution)/shard_map/schur_load/pallas_call | solution.py:145
  31.7 0.0 collective-permute-done.6.crossed_half
  31.7 1.4 %coarse_load.1 = (bf16[96,256]{1,0:T(8,128)(2,1)S(1)}, f32[96,256]{1,0:T(8,128)S(1)}, f32[64,256]{1,0:T(8,128)S(1)}, f32[1536,256]{1,0:T(8,128)S(1)}, bf16[512,2...) custom-call(bf16[512,256]{1,0:T(8,128)(2,1)S(1)} %pad_maximum_fusion.1.half, ...), custom_call_target="tpu_custom_call" | custom-call | tf_op jit(solution)/shard_map/coarse_load/pallas_call | solution.py:145
  33.1 0.5 collective-permute-start.10
  33.7 3.9 %collective-permute-start.9 = (bf16[512,256]{1,0:T(8,128)(2,1)S(1)}, bf16[512,256]{1,0:T(8,128)(2,1)S(1)}, u32[]{:S(2)}, u32[]{:S(2)}) collective-permute-start(bf16[512,256]{1,0:T(8,128)(2,1)S(1)} %get-tuple-element.83), channel_id=1, source_target_pairs={{1,0},{2,1},{3,2},{4,3},{5,4},{6,5},{7,6},{8,7},{9,8},{10,9},{11,1... | collective-permute-start | bytes 786440 | tf_op jit(solution)/shard_map/ppermute | solution.py:19
  37.6 0.0 collective-permute-start.7
  37.6 5.4 %collective-permute-done.7 = bf16[96,256]{1,0:T(8,128)(2,1)S(1)} collective-permute-done((bf16[96,256]{1,0:T(8,128)(2,1)S(1)}, bf16[96,256]{1,0:T(8,128)(2,1)S(1)}, u32[]{:S(2)}, u32[]{:S(2)}) %collective-permute-start.7) | collective-permute-done | bytes 49184 | tf_op jit(solution)/shard_map/ppermute | solution.py:23
  43.0 0.0 collective-permute-start.8
  43.0 0.0 collective-permute-done.10.from_previous
  43.0 0.0 collective-permute-done.9.from_next
  43.0 1.5 %neumann_image.1 = (f32[1024,256]{1,0:T(8,128)S(1)}, f32[1536,256]{1,0:T(8,128)S(1)}, bf16[512,256]{1,0:T(8,128)(2,1)S(1)}, bf16[512,256]{1,0:T(8,128)(2,1)S(1)}) custom-call(f32[1536,256]{1,0:T(8,128)S(1)} %get-tuple-element.82.part_in, bf16[512,256]{1,0:T(8,128)(2,1)S(1)} %collective-permute-done.9.from_next, ...), custom_call_target="tpu_custom_call" | custom-call | tf_op jit(solution)/shard_map/neumann_image/pallas_call | solution.py:145
  44.6 4.2 %collective-permute-start.12 = (bf16[512,256]{1,0:T(8,128)(2,1)S(1)}, bf16[512,256]{1,0:T(8,128)(2,1)S(1)}, u32[]{:S(2)}, u32[]{:S(2)}) collective-permute-start(bf16[512,256]{1,0:T(8,128)(2,1)S(1)} %get-tuple-element.85), channel_id=1, source_target_pairs={{1,0},{2,1},{3,2},{4,3},{5,4},{6,5},{7,6},{8,7},{9,8},{10,9},{11,1... | collective-permute-start | bytes 786440 | tf_op jit(solution)/shard_map/ppermute | solution.py:19
  48.8 0.0 collective-permute-done.8
  48.8 0.0 collective-permute-start.13
  48.8 0.1 collective-permute-start.11
  48.9 9.4 %collective-permute-done.11 = bf16[384,256]{1,0:T(8,128)(2,1)S(1)} collective-permute-done((bf16[384,256]{1,0:T(8,128)(2,1)S(1)}, bf16[384,256]{1,0:T(8,128)(2,1)S(1)}, u32[]{:S(2)}, u32[]{:S(2)}) %collective-permute-start.11) | collective-permute-done | bytes 196640 | tf_op jit(solution)/shard_map/ppermute | solution.py:23
  58.3 0.0 collective-permute-done.12.refs_2_
  58.4 0.1 collective-permute-start.14
  58.4 3.3 %schur_image.1 = (f32[1536,256]{1,0:T(8,128)S(1)}, f32[1536,256]{1,0:T(8,128)S(1)}, f32[8,256]{1,0:T(8,128)S(1)}, f32[128,256]{1,0:T(8,128)S(1)}) custom-call(f32[1024,256]{1,0:T(8,128)S(1)} %get-tuple-element.90.refs_0_.image, f32[1536,256]{1,0:T(8,128)S(1)} %get-tuple-element.92.refs_1_, bf16[512,256]{1,0:T(8,128)(2,1)S(1)} %collective-permute-done.12.refs_2_, ...), custom_call_target="tpu_custom_call" | custom-call | tf_op jit(solution)/shard_map/schur_image/pallas_call | solution.py:145
  61.8 1.7 %coarse_image.1 = (f32[4,256]{1,0:T(4,128)S(1)}, f32[64,256]{1,0:T(8,128)S(1)}, f32[1024,256]{1,0:T(8,128)S(1)}, bf16[512,256]{1,0:T(8,128)(2,1)S(1)}) custom-call(bf16[768,256]{1,0:T(8,128)(2,1)S(1)} %pad_maximum_fusion.half, bf16[768,256]{1,0:T(8,128)(2,1)S(1)} %collective-permute-done.14.crossed_half, bf16[64,1024]{1,0:T(8,128)(2,1)S(1)} %get-tuple-element.64.inverse, ...), custom_call_target="tpu_custom_call" | custom-call | tf_op jit(solution)/shard_map/coarse_image/pallas_call | solution.py:145
  63.4 2.4 %collective-permute-start.15 = (f32[4,256]{1,0:T(4,128)S(1)}, f32[4,256]{1,0:T(4,128)S(1)}, u32[]{:S(2)}, u32[]{:S(2)}) collective-permute-start(f32[4,256]{1,0:T(4,128)S(1)} %get-tuple-element.97), channel_id=1, source_target_pairs={{0,8},{1,9},{2,10},{3,11},{4,12},{5,13},{6,14},{7,15},{8,0},{9,1},... | collective-permute-start | bytes 12296 | tf_op jit(solution)/shard_map/ppermute | solution.py:23
  65.8 2.2 %collective-permute-done.15 = f32[4,256]{1,0:T(4,128)S(1)} collective-permute-done((f32[4,256]{1,0:T(4,128)S(1)}, f32[4,256]{1,0:T(4,128)S(1)}, u32[]{:S(2)}, u32[]{:S(2)}) %collective-permute-start.15) | collective-permute-done | bytes 4128 | tf_op jit(solution)/shard_map/ppermute | solution.py:23
  68.0 0.7 collective-permute-start.16
  68.7 2.9 %collective-permute-done.16 = f32[4,256]{1,0:T(4,128)S(1)} collective-permute-done((f32[4,256]{1,0:T(4,128)S(1)}, f32[4,256]{1,0:T(4,128)S(1)}, u32[]{:S(2)}, u32[]{:S(2)}) %collective-permute-start.16) | collective-permute-done | bytes 4128 | tf_op jit(solution)/shard_map/ppermute | solution.py:23
  71.6 0.7 complete.1
  72.4 1.1 %collective-permute-start.19 = (bf16[512,256]{1,0:T(8,128)(2,1)S(1)}, bf16[512,256]{1,0:T(8,128)(2,1)S(1)}, u32[]{:S(2)}, u32[]{:S(2)}) collective-permute-start(bf16[512,256]{1,0:T(8,128)(2,1)S(1)} %get-tuple-element.107), channel_id=1, source_target_pairs={{1,0},{2,1},{3,2},{4,3},{5,4},{6,5},{7,6},{8,7},{9,8},{10,9},{11,1... | collective-permute-start | bytes 786440 | tf_op jit(solution)/shard_map/ppermute | solution.py:19
  73.4 0.0 collective-permute-start.17
  73.4 4.4 %collective-permute-done.17 = f32[4,256]{1,0:T(4,128)S(1)} collective-permute-done((f32[4,256]{1,0:T(4,128)S(1)}, f32[4,256]{1,0:T(4,128)S(1)}, u32[]{:S(2)}, u32[]{:S(2)}) %collective-permute-start.17) | collective-permute-done | bytes 4128 | tf_op jit(solution)/shard_map/ppermute | solution.py:23
  77.8 1.2 %collective-permute-done.18 = f32[4,256]{1,0:T(4,128)S(1)} collective-permute-done((f32[4,256]{1,0:T(4,128)S(1)}, f32[4,256]{1,0:T(4,128)S(1)}, u32[]{:S(2)}, u32[]{:S(2)}) %collective-permute-start.18) | collective-permute-done | bytes 4128 | tf_op jit(solution)/shard_map/ppermute | solution.py:23
  79.0 1.7 %combine.1 = (f32[1024,256]{1,0:T(8,128)}, f32[1024,256]{1,0:T(8,128)}) custom-call(f32[4,256]{1,0:T(4,128)S(1)} %add.15.sums, f32[1024,256]{1,0:T(8,128)S(1)} %get-tuple-element.56.load, f32[1024,256]{1,0:T(8,128)S(1)} %get-tuple-element.103.z, f32[1024,256]{1,0:T(8,128)S(1)} %get-tuple-element.104.y, f32[1024,256]{1,0:T(8,128)S(1)} %get-tuple-element.90.refs_0_.image, ...), custom_call_target="tpu_custom_call" | custom-call | tf_op jit(solution)/shard_map/combine/pallas_call | solution.py:145
  (14 shorter events, 0.1 us)
Async XLA Ops:
  2.4 10.4 %collective-permute-start.2 = (bf16[576,256]{1,0:T(8,128)(2,1)S(1)}, bf16[576,256]{1,0:T(8,128)(2,1)S(1)}, u32[]{:S(2)}, u32[]{:S(2)}) collective-permute-start(bf16[576,256]{1,0:T(8,128)(2,1)S(1)} %first_message.1), channel_id=1, source_target_pairs={{15,0},{0,1},{1,2},{2,3},{3,4},{4,5},{5,6},{6,7},{7,8},{8,9},{9,10... | collective-permute-start | bytes 884744 | tf_op jit(solution)/shard_map/ppermute | solution.py:19
  2.9 7.2 %collective-permute-start = (bf16[64,256]{1,0:T(8,128)(2,1)S(1)}, bf16[64,256]{1,0:T(8,128)(2,1)S(1)}, u32[]{:S(2)}, u32[]{:S(2)}) collective-permute-start(bf16[64,256]{1,0:T(8,128)(2,1)S(1)} %get-tuple-element.55), channel_id=1, source_target_pairs={{0,8},{1,9},{2,10},{3,11},{4,12},{5,13},{6,14},{7,15},{8,0},{9,1},... | collective-permute-start | bytes 98312 | tf_op jit(solution)/shard_map/ppermute | solution.py:23
  14.2 14.0 %collective-permute-start.5 = (bf16[656,256]{1,0:T(8,128)(2,1)S(1)}, bf16[656,256]{1,0:T(8,128)(2,1)S(1)}, u32[]{:S(2)}, u32[]{:S(2)}) collective-permute-start(bf16[656,256]{1,0:T(8,128)(2,1)S(1)} %get-tuple-element.67), channel_id=1, source_target_pairs={{15,0},{0,1},{1,2},{2,3},{3,4},{4,5},{5,6},{6,7},{7,8},{8,9},{9,10... | collective-permute-start | bytes 1007624 | tf_op jit(solution)/shard_map/ppermute | solution.py:19
  14.3 4.6 %collective-permute-start.1 = (bf16[128,256]{1,0:T(8,128)(2,1)S(1)}, bf16[128,256]{1,0:T(8,128)(2,1)S(1)}, u32[]{:S(2)}, u32[]{:S(2)}) collective-permute-start(bf16[128,256]{1,0:T(8,128)(2,1)S(1)} %pad_maximum_fusion.5), channel_id=1, source_target_pairs={{0,4},{1,5},{2,6},{3,7},{4,0},{5,1},{6,2},{7,3},{8,12},{9,13},{10,... | collective-permute-start | bytes 196616 | tf_op jit(solution)/shard_map/ppermute | solution.py:23
  14.5 13.8 %collective-permute-start.4 = (bf16[512,256]{1,0:T(8,128)(2,1)S(1)}, bf16[512,256]{1,0:T(8,128)(2,1)S(1)}, u32[]{:S(2)}, u32[]{:S(2)}) collective-permute-start(bf16[512,256]{1,0:T(8,128)(2,1)S(1)} %get-tuple-element.65), channel_id=1, source_target_pairs={{1,0},{2,1},{3,2},{4,3},{5,4},{6,5},{7,6},{8,7},{9,8},{10,9},{11,1... | collective-permute-start | bytes 786440 | tf_op jit(solution)/shard_map/ppermute | solution.py:19
  18.9 9.4 %collective-permute-start.3 = (bf16[256,256]{1,0:T(8,128)(2,1)S(1)}, bf16[256,256]{1,0:T(8,128)(2,1)S(1)}, u32[]{:S(2)}, u32[]{:S(2)}) collective-permute-start(bf16[256,256]{1,0:T(8,128)(2,1)S(1)} %pad_maximum_fusion.3), channel_id=1, source_target_pairs={{0,2},{1,3},{2,0},{3,1},{4,6},{5,7},{6,4},{7,5},{8,10},{9,11},{10,... | collective-permute-start | bytes 393224 | tf_op jit(solution)/shard_map/ppermute | solution.py:23
  28.3 3.4 %collective-permute-start.6 = (bf16[512,256]{1,0:T(8,128)(2,1)S(1)}, bf16[512,256]{1,0:T(8,128)(2,1)S(1)}, u32[]{:S(2)}, u32[]{:S(2)}) collective-permute-start(bf16[512,256]{1,0:T(8,128)(2,1)S(1)} %pad_maximum_fusion.1.half), channel_id=1, source_target_pairs={{0,1},{1,0},{2,3},{3,2},{4,5},{5,4},{6,7},{7,6},{8,9},{9,8},{10,11... | collective-permute-start | bytes 786440 | tf_op jit(solution)/shard_map/ppermute | solution.py:23
  33.1 9.9 %collective-permute-start.10 = (bf16[512,256]{1,0:T(8,128)(2,1)S(1)}, bf16[512,256]{1,0:T(8,128)(2,1)S(1)}, u32[]{:S(2)}, u32[]{:S(2)}) collective-permute-start(bf16[512,256]{1,0:T(8,128)(2,1)S(1)} %get-tuple-element.84), channel_id=1, source_target_pairs={{15,0},{0,1},{1,2},{2,3},{3,4},{4,5},{5,6},{6,7},{7,8},{8,9},{9,10... | collective-permute-start | bytes 786440 | tf_op jit(solution)/shard_map/ppermute | solution.py:19
  33.7 9.3 %collective-permute-start.9 = (bf16[512,256]{1,0:T(8,128)(2,1)S(1)}, bf16[512,256]{1,0:T(8,128)(2,1)S(1)}, u32[]{:S(2)}, u32[]{:S(2)}) collective-permute-start(bf16[512,256]{1,0:T(8,128)(2,1)S(1)} %get-tuple-element.83), channel_id=1, source_target_pairs={{1,0},{2,1},{3,2},{4,3},{5,4},{6,5},{7,6},{8,7},{9,8},{10,9},{11,1... | collective-permute-start | bytes 786440 | tf_op jit(solution)/shard_map/ppermute | solution.py:19
  37.6 5.4 %collective-permute-start.7 = (bf16[96,256]{1,0:T(8,128)(2,1)S(1)}, bf16[96,256]{1,0:T(8,128)(2,1)S(1)}, u32[]{:S(2)}, u32[]{:S(2)}) collective-permute-start(bf16[96,256]{1,0:T(8,128)(2,1)S(1)} %get-tuple-element.81), channel_id=1, source_target_pairs={{0,8},{1,9},{2,10},{3,11},{4,12},{5,13},{6,14},{7,15},{8,0},{9,1},... | collective-permute-start | bytes 147464 | tf_op jit(solution)/shard_map/ppermute | solution.py:23
  43.0 5.8 %collective-permute-start.8 = (bf16[192,256]{1,0:T(8,128)(2,1)S(1)}, bf16[192,256]{1,0:T(8,128)(2,1)S(1)}, u32[]{:S(2)}, u32[]{:S(2)}) collective-permute-start(bf16[192,256]{1,0:T(8,128)(2,1)S(1)} %pad_maximum_fusion.4), channel_id=1, source_target_pairs={{0,4},{1,5},{2,6},{3,7},{4,0},{5,1},{6,2},{7,3},{8,12},{9,13},{10,... | collective-permute-start | bytes 294920 | tf_op jit(solution)/shard_map/ppermute | solution.py:23
  44.6 13.8 %collective-permute-start.12 = (bf16[512,256]{1,0:T(8,128)(2,1)S(1)}, bf16[512,256]{1,0:T(8,128)(2,1)S(1)}, u32[]{:S(2)}, u32[]{:S(2)}) collective-permute-start(bf16[512,256]{1,0:T(8,128)(2,1)S(1)} %get-tuple-element.85), channel_id=1, source_target_pairs={{1,0},{2,1},{3,2},{4,3},{5,4},{6,5},{7,6},{8,7},{9,8},{10,9},{11,1... | collective-permute-start | bytes 786440 | tf_op jit(solution)/shard_map/ppermute | solution.py:19
  48.8 9.6 %collective-permute-start.13 = (bf16[512,256]{1,0:T(8,128)(2,1)S(1)}, bf16[512,256]{1,0:T(8,128)(2,1)S(1)}, u32[]{:S(2)}, u32[]{:S(2)}) collective-permute-start(bf16[512,256]{1,0:T(8,128)(2,1)S(1)} %get-tuple-element.87), channel_id=1, source_target_pairs={{15,0},{0,1},{1,2},{2,3},{3,4},{4,5},{5,6},{6,7},{7,8},{8,9},{9,10... | collective-permute-start | bytes 786440 | tf_op jit(solution)/shard_map/ppermute | solution.py:19
  48.8 9.5 %collective-permute-start.11 = (bf16[384,256]{1,0:T(8,128)(2,1)S(1)}, bf16[384,256]{1,0:T(8,128)(2,1)S(1)}, u32[]{:S(2)}, u32[]{:S(2)}) collective-permute-start(bf16[384,256]{1,0:T(8,128)(2,1)S(1)} %pad_maximum_fusion.2), channel_id=1, source_target_pairs={{0,2},{1,3},{2,0},{3,1},{4,6},{5,7},{6,4},{7,5},{8,10},{9,11},{10,... | collective-permute-start | bytes 589832 | tf_op jit(solution)/shard_map/ppermute | solution.py:23
  58.4 3.4 %collective-permute-start.14 = (bf16[768,256]{1,0:T(8,128)(2,1)S(1)}, bf16[768,256]{1,0:T(8,128)(2,1)S(1)}, u32[]{:S(2)}, u32[]{:S(2)}) collective-permute-start(bf16[768,256]{1,0:T(8,128)(2,1)S(1)} %pad_maximum_fusion.half), channel_id=1, source_target_pairs={{0,1},{1,0},{2,3},{3,2},{4,5},{5,4},{6,7},{7,6},{8,9},{9,8},{10,11... | collective-permute-start | bytes 1179656 | tf_op jit(solution)/shard_map/ppermute | solution.py:23
  63.4 4.6 %collective-permute-start.15 = (f32[4,256]{1,0:T(4,128)S(1)}, f32[4,256]{1,0:T(4,128)S(1)}, u32[]{:S(2)}, u32[]{:S(2)}) collective-permute-start(f32[4,256]{1,0:T(4,128)S(1)} %get-tuple-element.97), channel_id=1, source_target_pairs={{0,8},{1,9},{2,10},{3,11},{4,12},{5,13},{6,14},{7,15},{8,0},{9,1},... | collective-permute-start | bytes 12296 | tf_op jit(solution)/shard_map/ppermute | solution.py:23
  68.0 3.6 %collective-permute-start.16 = (f32[4,256]{1,0:T(4,128)S(1)}, f32[4,256]{1,0:T(4,128)S(1)}, u32[]{:S(2)}, u32[]{:S(2)}) collective-permute-start(f32[4,256]{1,0:T(4,128)S(1)} %add.12), channel_id=1, source_target_pairs={{0,4},{1,5},{2,6},{3,7},{4,0},{5,1},{6,2},{7,3},{8,12},{9,13},{10,... | collective-permute-start | bytes 12296 | tf_op jit(solution)/shard_map/ppermute | solution.py:23
  72.4 6.6 %collective-permute-start.19 = (bf16[512,256]{1,0:T(8,128)(2,1)S(1)}, bf16[512,256]{1,0:T(8,128)(2,1)S(1)}, u32[]{:S(2)}, u32[]{:S(2)}) collective-permute-start(bf16[512,256]{1,0:T(8,128)(2,1)S(1)} %get-tuple-element.107), channel_id=1, source_target_pairs={{1,0},{2,1},{3,2},{4,3},{5,4},{6,5},{7,6},{8,7},{9,8},{10,9},{11,1... | collective-permute-start | bytes 786440 | tf_op jit(solution)/shard_map/ppermute | solution.py:19
  73.4 4.4 %collective-permute-start.17 = (f32[4,256]{1,0:T(4,128)S(1)}, f32[4,256]{1,0:T(4,128)S(1)}, u32[]{:S(2)}, u32[]{:S(2)}) collective-permute-start(f32[4,256]{1,0:T(4,128)S(1)} %add.13), channel_id=1, source_target_pairs={{0,2},{1,3},{2,0},{3,1},{4,6},{5,7},{6,4},{7,5},{8,10},{9,11},{10,... | collective-permute-start | bytes 12296 | tf_op jit(solution)/shard_map/ppermute | solution.py:23
  77.8 1.2 %collective-permute-start.18 = (f32[4,256]{1,0:T(4,128)S(1)}, f32[4,256]{1,0:T(4,128)S(1)}, u32[]{:S(2)}, u32[]{:S(2)}) collective-permute-start(f32[4,256]{1,0:T(4,128)S(1)} %add.14), channel_id=1, source_target_pairs={{0,1},{1,0},{2,3},{3,2},{4,5},{5,4},{6,7},{7,6},{8,9},{9,8},{10,11... | collective-permute-start | bytes 12296 | tf_op jit(solution)/shard_map/ppermute | solution.py:23

commit v8 on v7

--- a/solution.py
+++ b/solution.py
@@ -23,8 +23,14 @@
     return lax.ppermute(block, AXIS, [(i, i ^ bit) for i in range(lax.axis_size(AXIS))])
 
 
+def far_block(block):
+    n = lax.axis_size(AXIS)
+    return lax.ppermute(block, AXIS, [(i, (i + (1 if i % 2 else -1)) % n) for i in range(n)])
+
+
 def bits():
-    return [1 << k for k in reversed(range(lax.axis_size(AXIS).bit_length() - 1))]
+    order = [1 << k for k in reversed(range(lax.axis_size(AXIS).bit_length() - 1))]
+    return order[:-3] + order[-2:-1] + order[-3:-2] + order[-1:]
 
 
 def after(value, *others):
@@ -90,32 +96,27 @@
     def __init__(self, nf, ncf, nco, columns):
         self.nf, self.ncf, self.columns = nf, ncf, columns
         self.folds = nf // columns
-        self.inverse_folds = nco // columns
-        self.first_height = nf + ncf * self.folds
-        self.at_weight = nf + ncf * self.inverse_folds
+        self.at_inverse = nf + ncf * self.folds
+        self.at_weight = self.at_inverse + ncf * (nco // columns)
         self.weight_count = -(-3 * self.folds // 16) * 16
-        self.second_height = self.at_weight + self.weight_count
-
-    def unfolded(self, message, folds):
-        start, ncf = self.nf, self.ncf
-        return jnp.concatenate([message[start + k * ncf : start + (k + 1) * ncf] for k in range(folds)], axis=1)
-
-    def fold(self, message, block, folds):
-        start, ncf, columns = self.nf, self.ncf, self.columns
-        for k in range(folds):
+        self.height = self.at_weight + self.weight_count
+
+    def unfolded(self, message, start, stop):
+        return jnp.concatenate([message[k : k + self.ncf] for k in range(start, stop, self.ncf)], axis=1)
+
+    def fold(self, message, block, start):
+        ncf, columns = self.ncf, self.columns
+        for k in range(block.shape[1] // columns):
             message[start + k * ncf : start + (k + 1) * ncf] = block[:, k * columns : (k + 1) * columns]
 
-    def product(self, message):
-        return message[: self.nf].astype(F32)
-
     def rows(self, message):
-        return self.unfolded(message, self.folds)
+        return self.unfolded(message, self.nf, self.at_inverse)
 
     def inverse(self, message):
-        return self.unfolded(message, self.inverse_folds)
+        return self.unfolded(message, self.at_inverse, self.at_weight)
 
     def weight(self, message):
-        got = message[self.at_weight : self.second_height].astype(F32)
+        got = message[self.at_weight : self.height].astype(F32)
         f = self.folds
         row = [sum(got[k * f + i : k * f + i + 1] for k in range(3)) for i in range(f)]
         return jnp.concatenate([column_of(piece) for piece in row], axis=0)
@@ -124,6 +125,21 @@
 def all_rows(halo, message, rows):
     ncf = halo.ncf
     return [halo.rows(message)] + [rows_of(rows, j, ncf) for j in range(rows.shape[0] // ncf)]
+
+
+def is_odd():
+    return lax.rem(lax.axis_index(AXIS), 2) == 1
+
+
+def send(first, second, near, far):
+    first, second, odd = first.astype(BF16), second.astype(BF16), is_odd()
+    near[...] = jnp.where(odd, first, second)
+    far[...] = jnp.where(odd, second, first)
+
+
+def received(near, far):
+    near, far, odd = near[...].astype(F32), far[...].astype(F32), is_odd()
+    return jnp.where(odd, far, near), jnp.where(odd, near, far)
 
 
 def all_weights(halo, message, weight):
@@ -145,7 +161,9 @@
     return call(*operands)
 
 
-def prepare(halo, load, rows, weight, load_here, rows_here, weight_here, coarse_rounded, coarse, done):
+def prepare(
+    halo, load, rows, weight, inverse, load_here, rows_here, weight_here, inverse_here, coarse_rounded, coarse, done
+):
     ncf, nf = halo.ncf, halo.nf
     subs = load.shape[0] // nf
     copies = [pltpu.make_async_copy(rows, rows_here, done.at[subs])]
@@ -153,6 +171,7 @@
         pltpu.make_async_copy(rows_of(load.at, j, nf), rows_of(load_here.at, j, nf), done.at[j]) for j in range(subs)
     ]
     copies.append(pltpu.make_async_copy(weight, weight_here, done.at[subs + 1]))
+    copies.append(pltpu.make_async_copy(inverse, inverse_here, done.at[subs + 2]))
     for copy in copies:
         copy.start()
     copies[0].wait()
@@ -160,17 +179,25 @@
         copies[1 + j].wait()
         coarse[j * ncf : (j + 1) * ncf] = dot(rows_of(rows_here, j, ncf), rows_of(load_here, j, nf).astype(BF16))
     coarse_rounded[...] = coarse[...].astype(BF16)
+    copies[-2].wait()
     copies[-1].wait()
 
 
-def first_message(halo, load, weight, rows, message):
-    ncf, nf = halo.ncf, halo.nf
-    message[:nf] = ((1.0 - column_of(weight[weight.shape[0] - 1 :])) * load[load.shape[0] - nf :]).astype(BF16)
-    halo.fold(message, rows[rows.shape[0] - ncf :], halo.folds)
-
-
-def fetch(halo, neumann, schur, inverse, neumann_here, schur_here, inverse_here, done):
-    pairs = ((neumann, neumann_here), (schur, schur_here), (inverse, inverse_here))
+def halo_message(halo, load, weight, rows, inverse, message, pieces):
+    ncf, nf, columns, folds = halo.ncf, halo.nf, halo.columns, halo.folds
+    last = weight[weight.shape[0] - 1 :]
+    message[:nf] = ((1.0 - column_of(last)) * load[load.shape[0] - nf :]).astype(BF16)
+    halo.fold(message, rows[rows.shape[0] - ncf :], nf)
+    halo.fold(message, inverse[inverse.shape[0] - ncf :], halo.at_inverse)
+    pieces[...] = jnp.zeros_like(pieces)
+    for k, values in enumerate(parts_of(last)):
+        for i in range(folds):
+            pieces[k * folds + i : k * folds + i + 1] = values[:, i * columns : (i + 1) * columns]
+    message[halo.at_weight :] = pieces[...].astype(BF16)
+
+
+def fetch(halo, neumann, schur, neumann_here, schur_here, done):
+    pairs = ((neumann, neumann_here), (schur, schur_here))
     copies = [pltpu.make_async_copy(source, here, done.at[k]) for k, (source, here) in enumerate(pairs)]
     for copy in copies:
         copy.start()
@@ -178,49 +205,42 @@
         copy.wait()
 
 
-def neumann_products(left, right, weights, neumann, part, back, forward):
+def neumann_products(left, right, weights, neumann, part, near, far):
     subs, nf = len(left), left[0].shape[0]
     previous = None
     for j in range(subs):
         product = dot(rows_of(neumann, j, 2 * nf), jnp.concatenate([left[j], right[j]], axis=0))
         first, second = product[:nf], product[nf:]
         if j == 0:
-            part[:nf] = first
-            back[...] = first.astype(BF16)
+            part[:nf] = outer = first
         else:
             part[j * nf : (j + 1) * nf] = weights[j] * previous + (1.0 - weights[j]) * first
         previous = second
     part[subs * nf :] = previous
-    forward[:nf] = previous.astype(BF16)
-
-
-def neumann_load(halo, load, weight, message, neumann, inverse, part, back, forward, pieces):
+    send(outer, previous, near, far)
+
+
+def neumann_load(halo, load, weight, message, neumann, part, near, far):
     subs, nf = weight.shape
-    ncf, columns, folds = halo.ncf, halo.columns, halo.folds
-    halo.fold(forward, inverse[inverse.shape[0] - ncf :], halo.inverse_folds)
-    pieces[...] = jnp.zeros_like(pieces)
-    for k, values in enumerate(parts_of(weight[subs - 1 : subs])):
-        for i in range(folds):
-            pieces[k * folds + i : k * folds + i + 1] = values[:, i * columns : (i + 1) * columns]
-    forward[halo.at_weight :] = pieces[...].astype(BF16)
     weights = [None] + [column_of(weight[j : j + 1]) for j in range(subs)]
     left = [message[:nf]]
     left += [((1.0 - weights[j]) * rows_of(load, j - 1, nf)).astype(BF16) for j in range(1, subs)]
     right = [(weights[j + 1] * rows_of(load, j, nf)).astype(BF16) for j in range(subs)]
-    neumann_products(left, right, weights, neumann, part, back, forward)
-
-
-def neumann_image(halo, part_in, from_next, from_previous, weight, message, neumann, image, part, back, forward):
+    neumann_products(left, right, weights, neumann, part, near, far)
+
+
+def neumann_image(halo, part_in, near_in, far_in, weight, message, neumann, image, part, near, far):
     subs, nf = weight.shape
     weights = all_weights(halo, message, weight)
     faces = [rows_of(part_in, e, nf) for e in range(subs + 1)]
-    faces[0] = faces[0] + from_previous[...].astype(F32)
-    faces[subs] = faces[subs] + from_next[...].astype(F32)
+    from_next, from_previous = received(near_in, far_in)
+    faces[0] = faces[0] + from_previous
+    faces[subs] = faces[subs] + from_next
     for e in range(1, subs + 1):
         image[(e - 1) * nf : e * nf] = faces[e]
     left = [((1.0 - weights[j]) * faces[j]).astype(BF16) for j in range(subs)]
     right = [(weights[j + 1] * faces[j + 1]).astype(BF16) for j in range(subs)]
-    neumann_products(left, right, weights, neumann, part, back, forward)
+    neumann_products(left, right, weights, neumann, part, near, far)
 
 
 def static_basis(halo, schur, message, rows, basis_high, basis_low, turned_high, turned_low, gram):
@@ -240,16 +260,16 @@
 
 
 def schur_products(
-    halo, other, part, from_next, from_previous, weight, message, schur, turned_high, turned_low,
-    local, product, quadratic, base,
+    halo, other, part, near, far, weight, message, schur, turned_high, turned_low, local, product, quadratic, base
 ):
     subs, nf = weight.shape
     ncf, columns = halo.ncf, halo.columns
     weights = all_weights(halo, message, weight)
-    local[:nf] = (1.0 - weights[0]) * part[:nf] + weights[0] * halo.product(from_previous)
+    from_next, from_previous = received(near, far)
+    local[:nf] = (1.0 - weights[0]) * part[:nf] + weights[0] * from_previous
     for e in range(1, subs):
         local[e * nf : (e + 1) * nf] = rows_of(part, e, nf)
-    local[subs * nf :] = weights[subs] * part[subs * nf :] + (1.0 - weights[subs]) * from_next[...].astype(F32)
+    local[subs * nf :] = weights[subs] * part[subs * nf :] + (1.0 - weights[subs]) * from_next
     energy, previous = 0.0, None
     for j in range(subs):
         vector = local[j * nf : (j + 2) * nf]
@@ -267,16 +287,6 @@
     quadratic[1:2] = column_sum(other[...] * local[nf:])
 
 
-def schur_load(halo, load, part, from_next, from_previous, weight, schur, turned_high, turned_low, *outs):
-    schur_products(
-        halo, load, part, from_next, from_previous, weight, from_previous, schur, turned_high, turned_low, *outs
-    )
-
-
-def schur_image(halo, *refs):
-    schur_products(halo, *refs)
-
-
 def placed(half, crossed_half):
     me = lax.axis_index(AXIS)
     order = half_order()
@@ -317,7 +327,7 @@
 
 def coarse_load(
     halo, half, crossed_half, inverse, message, coarse, base, gram, quadratic, basis_high, basis_low, product,
-    shares_rounded, shares, solution, part, back, forward, sums, gathered,
+    shares_rounded, shares, solution, part, near, far, sums, gathered,
 ):
     ncf, nf = halo.ncf, halo.nf
     subs = inverse.shape[0] // ncf
@@ -336,8 +346,7 @@
     faces = add_basis(nf, x, basis_high, basis_low, product)
     for e in range(subs + 1):
         part[e * nf : (e + 1) * nf] = faces[e]
-    back[...] = faces[0].astype(BF16)
-    forward[...] = faces[subs].astype(BF16)
+    send(faces[0], faces[subs], near, far)
 
 
 def coarse_image(
@@ -405,57 +414,60 @@
     steps = bits()
     early, late = steps[:-2], steps[-2:-1]
 
-    load, rows, weight, coarse_rounded, coarse = stage(
+    load, rows, weight, inverse, coarse_rounded, coarse = stage(
         bind(prepare),
-        [described(right_side), described(constraint), described(face_weight), (coarse_own, BF16), (coarse_own, F32)],
-        *map(outside, (right_side, constraint, face_weight)), scratch=semaphores(subs + 2), fetched=3,
-    )
-    (first,) = stage(bind(first_message), [((halo.first_height, columns), BF16)], load, weight, rows)
+        [described(right_side), described(constraint), described(face_weight), described(coarse_inverse)]
+        + [(coarse_own, BF16), (coarse_own, F32)],
+        *map(outside, (right_side, constraint, face_weight, coarse_inverse)), scratch=semaphores(subs + 3), fetched=4,
+    )
+    (message,) = stage(
+        bind(halo_message), [((halo.height, columns), BF16)], load, weight, rows, inverse,
+        scratch=[pltpu.VMEM((halo.weight_count, columns), F32)],
+    )
     half = gather_half(coarse_rounded, early[:1])
-    tied = after(tuple(map(outside, (neumann, schur, coarse_inverse))), first)
-    neumann, schur, inverse = stage(
-        bind(fetch), [described(array) for array in tied], *tied, scratch=semaphores(3), fetched=3
-    )
-    first = after(shifted(first, 1), half)
-    part, back, forward = stage(
-        bind(neumann_load), [(faces, F32), ((nf, columns), BF16), ((halo.second_height, columns), BF16)],
-        load, weight, first, neumann, inverse, scratch=[pltpu.VMEM((halo.weight_count, columns), F32)],
-    )
-    half = gather_half(half, early[1:], back)
-    back, second = shifted(back, -1), shifted(forward, 1)
+    tied = after(tuple(map(outside, (neumann, schur))), message, half)
+    neumann, schur = stage(
+        bind(fetch), [described(array) for array in tied], *tied, scratch=semaphores(2), fetched=2
+    )
+    half = gather_half(half, early[1:])
+    message = after(shifted(message, 1), half)
+    part, near, far = stage(
+        bind(neumann_load), [(faces, F32)] + halves, load, weight, message, neumann
+    )
+    far, near = far_block(far), crossed(near, 1)
     long, wide = ((2 * subs * nf, 2 * ncf), BF16), ((local_rows, 2 * nf), BF16)
     basis_high, basis_low, turned_high, turned_low, gram = stage(
-        bind(static_basis), [long, long, wide, wide, ((local_rows, LANES), F32)], schur, first, rows
-    )
-    half = gather_half(half, late, back, second, gram)
+        bind(static_basis), [long, long, wide, wide, ((local_rows, LANES), F32)], schur, message, rows
+    )
+    half = gather_half(half, late, near, far, gram)
     crossed_half = crossed(half, 1)
     part = after(part, half)
     z_local, product, quadratic, base = stage(
-        bind(schur_load), products, load, part, back, second, weight, schur, turned_high, turned_low
+        bind(schur_products), products, load, part, near, far, weight, message, schur, turned_high, turned_low
     )
     share_rows = ((subs + 1) * ncf, columns)
-    shares_rounded, shares, z_coarse, part, back, forward, sums = stage(
+    shares_rounded, shares, z_coarse, part, near, far, sums = stage(
         bind(coarse_load),
         [(share_rows, BF16), (share_rows, F32), (coarse_own, F32), (faces, F32)] + halves + [((8, columns), F32)],
-        half, crossed_half, inverse, second, coarse, base, gram, quadratic, basis_high, basis_low, product,
+        half, crossed_half, inverse, message, coarse, base, gram, quadratic, basis_high, basis_low, product,
         scratch=[pltpu.VMEM((nco, columns), BF16)],
     )
+    far, near = far_block(far), crossed(near, 1)
     half = gather_half(shares_rounded, early[:1])
-    back, forward = shifted(back, -1), shifted(forward, 1)
-    image, part, back, forward = stage(
-        bind(neumann_image), [(own, F32), (faces, F32)] + halves, part, back, forward, weight, second, neumann
-    )
-    half = gather_half(half, early[1:], back)
-    back, forward = shifted(back, -1), shifted(forward, 1)
-    half = gather_half(half, late, back, forward)
+    image, part, near, far = stage(
+        bind(neumann_image), [(own, F32), (faces, F32)] + halves, part, near, far, weight, message, neumann
+    )
+    half = gather_half(half, early[1:], far)
+    far, near = far_block(far), crossed(near, 1)
+    half = gather_half(half, late, near, far)
     crossed_half = crossed(half, 1)
     part = after(part, half)
     y_local, product, quadratic, base = stage(
-        bind(schur_image), products, image, part, back, forward, weight, second, schur, turned_high, turned_low
+        bind(schur_products), products, image, part, near, far, weight, message, schur, turned_high, turned_low
     )
     sums, y_coarse, part, back = stage(
         bind(coarse_image), [((4, columns), F32), (coarse_own, F32), (own, F32), ((nf, columns), BF16)],
-        half, crossed_half, inverse, second, shares, base, gram, quadratic, basis_high, basis_low, product, sums,
+        half, crossed_half, inverse, message, shares, base, gram, quadratic, basis_high, basis_low, product, sums,
         scratch=[pltpu.VMEM((nco, columns), F32)],
     )
     for bit in early:

time: 80.8 us -> 81 us (level)
  starting transfers between devices: 23.5 us -> 24.5 us
    ppermute x8 -> x2, starting transfers between devices: 14.6 us -> 0.56 us  [shifted(): lax.ppermute(block, AXIS, [((i - distance) % n, i) for i in range(n)])]
    ppermute x12 -> x15, starting transfers between devices: 8.89 us -> 20.7 us  [crossed(): lax.ppermute(block, AXIS, [(i, i ^ bit) for i in range(lax.axis_size(AXIS...]
    ppermute x0 -> x3, starting transfers between devices: none -> 3.26 us  [far_block(): lax.ppermute(block, AXIS, [(i, (i + (1 if i % 2 else -1)) % n) for i in r...]
    ppermute x8 -> x2, waiting for transfers between devices: 2.68 us -> 0.01 us  [shifted(): lax.ppermute(block, AXIS, [((i - distance) % n, i) for i in range(n)])]
    ppermute x0 -> x3, waiting for transfers between devices: none -> 1.06 us  [far_block(): lax.ppermute(block, AXIS, [(i, (i + (1 if i % 2 else -1)) % n) for i in r...]
    ppermute x12 -> x15, waiting for transfers between devices: 31.3 us -> 32.1 us  [crossed(): lax.ppermute(block, AXIS, [(i, i ^ bit) for i in range(lax.axis_size(AXIS...]
  transfers between devices with their start and end apart: 20 -> 20, of which waited for: 9 -> 10; matrix products, arithmetic and copies ran while one was open for 0% -> 0% of each run, Pallas kernels for 17% -> 17%
where the time goes in v8:
time: 81 us; the launch traced here: 80.8 us
  waiting for transfers between devices  33.2 us (41%)
  starting transfers between devices  24.5 us (30%)
  Pallas kernels  22.2 us (27%)
  between operations  0.81 us (1%)
    ppermute x15, waiting for transfers between devices, crossed(): lax.ppermute(block, AXIS, [(i, i ^ bit) for i in range(lax.axis_size(AXIS...  32.1 us
    pallas_call x12, Pallas kernels, stage(): return call(*operands)  22.2 us
    ppermute x15, starting transfers between devices, crossed(): lax.ppermute(block, AXIS, [(i, i ^ bit) for i in range(lax.axis_size(AXIS...  20.7 us
    ppermute x3, starting transfers between devices, far_block(): lax.ppermute(block, AXIS, [(i, (i + (1 if i % 2 else -1)) % n) for i in r...  3.26 us
  transfers between devices with their start and end apart: 20, of which 10 were waited for; matrix products, arithmetic and copies ran while one was open for 0% of the time, Pallas kernels for 17%

profile of v8, /device:TPU:0, one launch (start us, length us, event | category | flops | bytes accessed | tf_op | source)
XLA Modules:
  0.0 80.8 jit_solution(8489275820889171800)
XLA Ops:
  0.6 1.5 %prepare.1 = (f32[1024,256]{1,0:T(8,128)S(1)}, bf16[64,512]{1,0:T(8,128)(2,1)S(1)}, f32[2,512]{1,0:T(2,128)S(1)}, bf16[64,1024]{1,0:T(8,128)(2,1)S(1)}, bf16[64,...) custom-call(f32[1024,256]{1,0:T(8,128)} %load.1, bf16[64,512]{1,0:T(8,128)(2,1)} %rows.1, f32[2,512]{1,0:T(2,128)} %weight.1, ...), custom_call_target="tpu_custom_call" | custom-call | tf_op jit(solution)/shard_map/prepare/pallas_call | solution.py:161
  2.1 0.3 halo_message.1
  2.4 0.5 collective-permute-start.3
  2.9 3.7 %collective-permute-start = (bf16[64,256]{1,0:T(8,128)(2,1)S(1)}, bf16[64,256]{1,0:T(8,128)(2,1)S(1)}, u32[]{:S(2)}, u32[]{:S(2)}) collective-permute-start(bf16[64,256]{1,0:T(8,128)(2,1)S(1)} %get-tuple-element.53), channel_id=1, source_target_pairs={{0,8},{1,9},{2,10},{3,11},{4,12},{5,13},{6,14},{7,15},{8,0},{9,1},... | collective-permute-start | bytes 98312 | tf_op jit(solution)/shard_map/ppermute | solution.py:23
  6.6 1.9 %collective-permute-done = bf16[64,256]{1,0:T(8,128)(2,1)S(1)} collective-permute-done((bf16[64,256]{1,0:T(8,128)(2,1)S(1)}, bf16[64,256]{1,0:T(8,128)(2,1)S(1)}, u32[]{:S(2)}, u32[]{:S(2)}) %collective-permute-start) | collective-permute-done | bytes 32800 | tf_op jit(solution)/shard_map/ppermute | solution.py:23
  8.5 6.5 %collective-permute-start.1 = (bf16[128,256]{1,0:T(8,128)(2,1)S(1)}, bf16[128,256]{1,0:T(8,128)(2,1)S(1)}, u32[]{:S(2)}, u32[]{:S(2)}) collective-permute-start(bf16[128,256]{1,0:T(8,128)(2,1)S(1)} %pad_maximum_fusion.5), channel_id=1, source_target_pairs={{0,2},{1,3},{2,0},{3,1},{4,6},{5,7},{6,4},{7,5},{8,10},{9,11},{10,... | collective-permute-start | bytes 196616 | tf_op jit(solution)/shard_map/ppermute | solution.py:23
  15.0 3.5 %fetch.1 = (bf16[2048,1024]{1,0:T(8,128)(2,1)S(1)}, bf16[2048,1024]{1,0:T(8,128)(2,1)S(1)}) custom-call(bf16[2048,1024]{1,0:T(8,128)(2,1)} %neumann, bf16[2048,1024]{1,0:T(8,128)(2,1)} %schur), custom_call_target="tpu_custom_call" | custom-call | tf_op jit(solution)/shard_map/fetch/pallas_call | solution.py:161
  18.5 0.0 collective-permute-done.3.message
  18.6 1.5 %neumann_load.1 = (f32[1536,256]{1,0:T(8,128)S(1)}, bf16[512,256]{1,0:T(8,128)(2,1)S(1)}, bf16[512,256]{1,0:T(8,128)(2,1)S(1)}) custom-call(f32[1024,256]{1,0:T(8,128)S(1)} %get-tuple-element.54.load.other, f32[2,512]{1,0:T(2,128)S(1)} %get-tuple-element.55.weight, bf16[720,256]{1,0:T(8,128)(2,1)S(1)} %collective-permute-done.3.message, ...), custom_call_target="tpu_custom_call" | custom-call | tf_op jit(solution)/shard_map/neumann_load/pallas_call | solution.py:161
  20.1 0.1 collective-permute-start.4
  20.1 1.1 %collective-permute-start.5 = (bf16[512,256]{1,0:T(8,128)(2,1)S(1)}, bf16[512,256]{1,0:T(8,128)(2,1)S(1)}, u32[]{:S(2)}, u32[]{:S(2)}) collective-permute-start(bf16[512,256]{1,0:T(8,128)(2,1)S(1)} %get-tuple-element.63), channel_id=1, source_target_pairs={{0,15},{1,2},{2,1},{3,4},{4,3},{5,6},{6,5},{7,8},{8,7},{9,10},{10,... | collective-permute-start | bytes 786440 | tf_op jit(solution)/shard_map/ppermute | solution.py:28
  21.3 1.2 %collective-permute-start.2 = (bf16[256,256]{1,0:T(8,128)(2,1)S(1)}, bf16[256,256]{1,0:T(8,128)(2,1)S(1)}, u32[]{:S(2)}, u32[]{:S(2)}) collective-permute-start(bf16[256,256]{1,0:T(8,128)(2,1)S(1)} %pad_maximum_fusion.3), channel_id=1, source_target_pairs={{0,4},{1,5},{2,6},{3,7},{4,0},{5,1},{6,2},{7,3},{8,12},{9,13},{10,... | collective-permute-start | bytes 393224 | tf_op jit(solution)/shard_map/ppermute | solution.py:23
  22.5 1.9 %static_basis.1 = (bf16[2048,64]{1,0:T(8,128)(2,1)S(1)}, bf16[2048,64]{1,0:T(8,128)(2,1)S(1)}, bf16[128,1024]{1,0:T(8,128)(2,1)S(1)}, bf16[128,1024]{1,0:T(8,128)(2,1)S(1)}, f32[128,128]{1,0:T(8,128)S(1)}) custom-call(bf16[2048,1024]{1,0:T(8,128)(2,1)S(1)} %get-tuple-element.64.schur, bf16[720,256]{1,0:T(8,128)(2,1)S(1)} %collective-permute-done.3.message, ...), custom_call_target="tpu_custom_call" | custom-call | tf_op jit(solution)/shard_map/static_basis/pallas_call | solution.py:161
  24.4 5.0 %collective-permute-done.2 = bf16[256,256]{1,0:T(8,128)(2,1)S(1)} collective-permute-done((bf16[256,256]{1,0:T(8,128)(2,1)S(1)}, bf16[256,256]{1,0:T(8,128)(2,1)S(1)}, u32[]{:S(2)}, u32[]{:S(2)}) %collective-permute-start.2) | collective-permute-done | bytes 131104 | tf_op jit(solution)/shard_map/ppermute | solution.py:23
  29.4 0.2 collective-permute-start.6
  29.5 3.4 %schur_products.2 = (f32[1536,256]{1,0:T(8,128)S(1)}, f32[1536,256]{1,0:T(8,128)S(1)}, f32[8,256]{1,0:T(8,128)S(1)}, f32[128,256]{1,0:T(8,128)S(1)}) custom-call(f32[1024,256]{1,0:T(8,128)S(1)} %get-tuple-element.54.load.other, f32[1536,256]{1,0:T(8,128)S(1)} %get-tuple-element.69.part, bf16[512,256]{1,0:T(8,128)(2,1)S(1)} %collective-permute-done.4.near, ...), custom_call_target="tpu_custom_call" | custom-call | tf_op jit(solution)/shard_map/schur_products/pallas_call | solution.py:161
  32.9 0.0 collective-permute-done.6.crossed_half
  32.9 1.4 %coarse_load.1 = (bf16[96,256]{1,0:T(8,128)(2,1)S(1)}, f32[96,256]{1,0:T(8,128)S(1)}, f32[64,256]{1,0:T(8,128)S(1)}, f32[1536,256]{1,0:T(8,128)S(1)}, bf16[512,2...) custom-call(bf16[512,256]{1,0:T(8,128)(2,1)S(1)} %pad_maximum_fusion.1.half, ...), custom_call_target="tpu_custom_call" | custom-call | tf_op jit(solution)/shard_map/coarse_load/pallas_call | solution.py:161
  34.3 1.4 %collective-permute-start.10 = (bf16[512,256]{1,0:T(8,128)(2,1)S(1)}, bf16[512,256]{1,0:T(8,128)(2,1)S(1)}, u32[]{:S(2)}, u32[]{:S(2)}) collective-permute-start(bf16[512,256]{1,0:T(8,128)(2,1)S(1)} %get-tuple-element.80), channel_id=1, source_target_pairs={{0,15},{1,2},{2,1},{3,4},{4,3},{5,6},{6,5},{7,8},{8,7},{9,10},{10,... | collective-permute-start | bytes 786440 | tf_op jit(solution)/shard_map/ppermute | solution.py:28
  35.7 0.4 collective-permute-start.7
  36.1 5.4 %collective-permute-done.7 = bf16[96,256]{1,0:T(8,128)(2,1)S(1)} collective-permute-done((bf16[96,256]{1,0:T(8,128)(2,1)S(1)}, bf16[96,256]{1,0:T(8,128)(2,1)S(1)}, u32[]{:S(2)}, u32[]{:S(2)}) %collective-permute-start.7) | collective-permute-done | bytes 49184 | tf_op jit(solution)/shard_map/ppermute | solution.py:23
  41.5 3.9 %collective-permute-start.8 = (bf16[192,256]{1,0:T(8,128)(2,1)S(1)}, bf16[192,256]{1,0:T(8,128)(2,1)S(1)}, u32[]{:S(2)}, u32[]{:S(2)}) collective-permute-start(bf16[192,256]{1,0:T(8,128)(2,1)S(1)} %pad_maximum_fusion.4), channel_id=1, source_target_pairs={{0,2},{1,3},{2,0},{3,1},{4,6},{5,7},{6,4},{7,5},{8,10},{9,11},{10,... | collective-permute-start | bytes 294920 | tf_op jit(solution)/shard_map/ppermute | solution.py:23
  45.4 0.0 collective-permute-done.10.far_in
  45.4 0.0 collective-permute-done.9.near_in
  45.4 1.5 %neumann_image.1 = (f32[1024,256]{1,0:T(8,128)S(1)}, f32[1536,256]{1,0:T(8,128)S(1)}, bf16[512,256]{1,0:T(8,128)(2,1)S(1)}, bf16[512,256]{1,0:T(8,128)(2,1)S(1)}) custom-call(f32[1536,256]{1,0:T(8,128)S(1)} %get-tuple-element.78.part_in, bf16[512,256]{1,0:T(8,128)(2,1)S(1)} %collective-permute-done.9.near_in, ...), custom_call_target="tpu_custom_call" | custom-call | tf_op jit(solution)/shard_map/neumann_image/pallas_call | solution.py:161
  46.9 0.7 collective-permute-start.13
  47.6 0.5 collective-permute-done.8
  48.1 0.0 collective-permute-start.12
  48.2 0.1 collective-permute-start.11
  48.2 8.2 %collective-permute-done.11 = bf16[384,256]{1,0:T(8,128)(2,1)S(1)} collective-permute-done((bf16[384,256]{1,0:T(8,128)(2,1)S(1)}, bf16[384,256]{1,0:T(8,128)(2,1)S(1)}, u32[]{:S(2)}, u32[]{:S(2)}) %collective-permute-start.11) | collective-permute-done | bytes 196640 | tf_op jit(solution)/shard_map/ppermute | solution.py:23
  56.5 0.0 collective-permute-done.12.near
  56.5 1.1 %collective-permute-done.13.far = bf16[512,256]{1,0:T(8,128)(2,1)S(1)} collective-permute-done((bf16[512,256]{1,0:T(8,128)(2,1)S(1)}, bf16[512,256]{1,0:T(8,128)(2,1)S(1)}, u32[]{:S(2)}, u32[]{:S(2)}) %collective-permute-start.13) | collective-permute-done | bytes 262176 | tf_op jit(solution)/shard_map/ppermute | solution.py:28
  57.6 0.1 collective-permute-start.14
  57.6 3.3 %schur_products.3 = (f32[1536,256]{1,0:T(8,128)S(1)}, f32[1536,256]{1,0:T(8,128)S(1)}, f32[8,256]{1,0:T(8,128)S(1)}, f32[128,256]{1,0:T(8,128)S(1)}) custom-call(f32[1024,256]{1,0:T(8,128)S(1)} %get-tuple-element.86.other.image, f32[1536,256]{1,0:T(8,128)S(1)} %get-tuple-element.88.part, bf16[512,256]{1,0:T(8,128)(2,1)S(1)} %collective-permute-done.12.near, ...), custom_call_target="tpu_custom_call" | custom-call | tf_op jit(solution)/shard_map/schur_products/pallas_call | solution.py:161
  61.0 0.0 collective-permute-done.14.crossed_half
  61.0 1.7 %coarse_image.1 = (f32[4,256]{1,0:T(4,128)S(1)}, f32[64,256]{1,0:T(8,128)S(1)}, f32[1024,256]{1,0:T(8,128)S(1)}, bf16[512,256]{1,0:T(8,128)(2,1)S(1)}) custom-call(bf16[768,256]{1,0:T(8,128)(2,1)S(1)} %pad_maximum_fusion.half, bf16[768,256]{1,0:T(8,128)(2,1)S(1)} %collective-permute-done.14.crossed_half, bf16[64,1024]{1,0:T(8,128)(2,1)S(1)} %get-tuple-element.57.inverse, ...), custom_call_target="tpu_custom_call" | custom-call | tf_op jit(solution)/shard_map/coarse_image/pallas_call | solution.py:161
  62.7 0.6 collective-permute-start.15
  63.3 3.9 %collective-permute-done.15 = f32[4,256]{1,0:T(4,128)S(1)} collective-permute-done((f32[4,256]{1,0:T(4,128)S(1)}, f32[4,256]{1,0:T(4,128)S(1)}, u32[]{:S(2)}, u32[]{:S(2)}) %collective-permute-start.15) | collective-permute-done | bytes 4128 | tf_op jit(solution)/shard_map/ppermute | solution.py:23
  67.3 2.7 %collective-permute-start.16 = (f32[4,256]{1,0:T(4,128)S(1)}, f32[4,256]{1,0:T(4,128)S(1)}, u32[]{:S(2)}, u32[]{:S(2)}) collective-permute-start(f32[4,256]{1,0:T(4,128)S(1)} %add.12), channel_id=1, source_target_pairs={{0,2},{1,3},{2,0},{3,1},{4,6},{5,7},{6,4},{7,5},{8,10},{9,11},{10,... | collective-permute-start | bytes 12296 | tf_op jit(solution)/shard_map/ppermute | solution.py:23
  69.9 1.6 %collective-permute-done.16 = f32[4,256]{1,0:T(4,128)S(1)} collective-permute-done((f32[4,256]{1,0:T(4,128)S(1)}, f32[4,256]{1,0:T(4,128)S(1)}, u32[]{:S(2)}, u32[]{:S(2)}) %collective-permute-start.16) | collective-permute-done | bytes 4128 | tf_op jit(solution)/shard_map/ppermute | solution.py:23
  71.5 0.7 complete.1
  72.3 0.1 collective-permute-start.19
  72.3 1.3 %collective-permute-start.17 = (f32[4,256]{1,0:T(4,128)S(1)}, f32[4,256]{1,0:T(4,128)S(1)}, u32[]{:S(2)}, u32[]{:S(2)}) collective-permute-start(f32[4,256]{1,0:T(4,128)S(1)} %add.13), channel_id=1, source_target_pairs={{0,4},{1,5},{2,6},{3,7},{4,0},{5,1},{6,2},{7,3},{8,12},{9,13},{10,... | collective-permute-start | bytes 12296 | tf_op jit(solution)/shard_map/ppermute | solution.py:23
  73.6 4.4 %collective-permute-done.17 = f32[4,256]{1,0:T(4,128)S(1)} collective-permute-done((f32[4,256]{1,0:T(4,128)S(1)}, f32[4,256]{1,0:T(4,128)S(1)}, u32[]{:S(2)}, u32[]{:S(2)}) %collective-permute-start.17) | collective-permute-done | bytes 4128 | tf_op jit(solution)/shard_map/ppermute | solution.py:23
  78.0 0.0 collective-permute-start.18
  78.0 1.2 %collective-permute-done.18 = f32[4,256]{1,0:T(4,128)S(1)} collective-permute-done((f32[4,256]{1,0:T(4,128)S(1)}, f32[4,256]{1,0:T(4,128)S(1)}, u32[]{:S(2)}, u32[]{:S(2)}) %collective-permute-start.18) | collective-permute-done | bytes 4128 | tf_op jit(solution)/shard_map/ppermute | solution.py:23
  79.2 0.0 collective-permute-done.19.from_next
  79.2 1.6 %combine.1 = (f32[1024,256]{1,0:T(8,128)}, f32[1024,256]{1,0:T(8,128)}) custom-call(f32[4,256]{1,0:T(4,128)S(1)} %add.15.sums, f32[1024,256]{1,0:T(8,128)S(1)} %get-tuple-element.54.load.other, f32[1024,256]{1,0:T(8,128)S(1)} %get-tuple-element.99.z, f32[1024,256]{1,0:T(8,128)S(1)} %get-tuple-element.100.y, f32[1024,256]{1,0:T(8,128)S(1)} %get-tuple-element.86.other.image, ...), custom_call_target="tpu_custom_call" | custom-call | tf_op jit(solution)/shard_map/combine/pallas_call | solution.py:161
  (14 shorter events, 0.1 us)
Async XLA Ops:
  2.4 16.1 %collective-permute-start.3 = (bf16[720,256]{1,0:T(8,128)(2,1)S(1)}, bf16[720,256]{1,0:T(8,128)(2,1)S(1)}, u32[]{:S(2)}, u32[]{:S(2)}) collective-permute-start(bf16[720,256]{1,0:T(8,128)(2,1)S(1)} %halo_message.1), channel_id=1, source_target_pairs={{15,0},{0,1},{1,2},{2,3},{3,4},{4,5},{5,6},{6,7},{7,8},{8,9},{9,10... | collective-permute-start | bytes 1105928 | tf_op jit(solution)/shard_map/ppermute | solution.py:19
  2.9 5.6 %collective-permute-start = (bf16[64,256]{1,0:T(8,128)(2,1)S(1)}, bf16[64,256]{1,0:T(8,128)(2,1)S(1)}, u32[]{:S(2)}, u32[]{:S(2)}) collective-permute-start(bf16[64,256]{1,0:T(8,128)(2,1)S(1)} %get-tuple-element.53), channel_id=1, source_target_pairs={{0,8},{1,9},{2,10},{3,11},{4,12},{5,13},{6,14},{7,15},{8,0},{9,1},... | collective-permute-start | bytes 98312 | tf_op jit(solution)/shard_map/ppermute | solution.py:23
  8.5 10.0 %collective-permute-start.1 = (bf16[128,256]{1,0:T(8,128)(2,1)S(1)}, bf16[128,256]{1,0:T(8,128)(2,1)S(1)}, u32[]{:S(2)}, u32[]{:S(2)}) collective-permute-start(bf16[128,256]{1,0:T(8,128)(2,1)S(1)} %pad_maximum_fusion.5), channel_id=1, source_target_pairs={{0,2},{1,3},{2,0},{3,1},{4,6},{5,7},{6,4},{7,5},{8,10},{9,11},{10,... | collective-permute-start | bytes 196616 | tf_op jit(solution)/shard_map/ppermute | solution.py:23
  20.1 9.3 %collective-permute-start.4 = (bf16[512,256]{1,0:T(8,128)(2,1)S(1)}, bf16[512,256]{1,0:T(8,128)(2,1)S(1)}, u32[]{:S(2)}, u32[]{:S(2)}) collective-permute-start(bf16[512,256]{1,0:T(8,128)(2,1)S(1)} %get-tuple-element.62), channel_id=1, source_target_pairs={{0,1},{1,0},{2,3},{3,2},{4,5},{5,4},{6,7},{7,6},{8,9},{9,8},{10,11... | collective-permute-start | bytes 786440 | tf_op jit(solution)/shard_map/ppermute | solution.py:23
  20.1 9.2 %collective-permute-start.5 = (bf16[512,256]{1,0:T(8,128)(2,1)S(1)}, bf16[512,256]{1,0:T(8,128)(2,1)S(1)}, u32[]{:S(2)}, u32[]{:S(2)}) collective-permute-start(bf16[512,256]{1,0:T(8,128)(2,1)S(1)} %get-tuple-element.63), channel_id=1, source_target_pairs={{0,15},{1,2},{2,1},{3,4},{4,3},{5,6},{6,5},{7,8},{8,7},{9,10},{10,... | collective-permute-start | bytes 786440 | tf_op jit(solution)/shard_map/ppermute | solution.py:28
  21.3 8.1 %collective-permute-start.2 = (bf16[256,256]{1,0:T(8,128)(2,1)S(1)}, bf16[256,256]{1,0:T(8,128)(2,1)S(1)}, u32[]{:S(2)}, u32[]{:S(2)}) collective-permute-start(bf16[256,256]{1,0:T(8,128)(2,1)S(1)} %pad_maximum_fusion.3), channel_id=1, source_target_pairs={{0,4},{1,5},{2,6},{3,7},{4,0},{5,1},{6,2},{7,3},{8,12},{9,13},{10,... | collective-permute-start | bytes 393224 | tf_op jit(solution)/shard_map/ppermute | solution.py:23
  29.4 3.5 %collective-permute-start.6 = (bf16[512,256]{1,0:T(8,128)(2,1)S(1)}, bf16[512,256]{1,0:T(8,128)(2,1)S(1)}, u32[]{:S(2)}, u32[]{:S(2)}) collective-permute-start(bf16[512,256]{1,0:T(8,128)(2,1)S(1)} %pad_maximum_fusion.1.half), channel_id=1, source_target_pairs={{0,1},{1,0},{2,3},{3,2},{4,5},{5,4},{6,7},{7,6},{8,9},{9,8},{10,11... | collective-permute-start | bytes 786440 | tf_op jit(solution)/shard_map/ppermute | solution.py:23
  34.3 11.1 %collective-permute-start.10 = (bf16[512,256]{1,0:T(8,128)(2,1)S(1)}, bf16[512,256]{1,0:T(8,128)(2,1)S(1)}, u32[]{:S(2)}, u32[]{:S(2)}) collective-permute-start(bf16[512,256]{1,0:T(8,128)(2,1)S(1)} %get-tuple-element.80), channel_id=1, source_target_pairs={{0,15},{1,2},{2,1},{3,4},{4,3},{5,6},{6,5},{7,8},{8,7},{9,10},{10,... | collective-permute-start | bytes 786440 | tf_op jit(solution)/shard_map/ppermute | solution.py:28
  35.7 9.7 %collective-permute-start.9 = (bf16[512,256]{1,0:T(8,128)(2,1)S(1)}, bf16[512,256]{1,0:T(8,128)(2,1)S(1)}, u32[]{:S(2)}, u32[]{:S(2)}) collective-permute-start(bf16[512,256]{1,0:T(8,128)(2,1)S(1)} %get-tuple-element.79), channel_id=1, source_target_pairs={{0,1},{1,0},{2,3},{3,2},{4,5},{5,4},{6,7},{7,6},{8,9},{9,8},{10,11... | collective-permute-start | bytes 786440 | tf_op jit(solution)/shard_map/ppermute | solution.py:23
  35.7 5.8 %collective-permute-start.7 = (bf16[96,256]{1,0:T(8,128)(2,1)S(1)}, bf16[96,256]{1,0:T(8,128)(2,1)S(1)}, u32[]{:S(2)}, u32[]{:S(2)}) collective-permute-start(bf16[96,256]{1,0:T(8,128)(2,1)S(1)} %get-tuple-element.77), channel_id=1, source_target_pairs={{0,8},{1,9},{2,10},{3,11},{4,12},{5,13},{6,14},{7,15},{8,0},{9,1},... | collective-permute-start | bytes 147464 | tf_op jit(solution)/shard_map/ppermute | solution.py:23
  41.5 6.6 %collective-permute-start.8 = (bf16[192,256]{1,0:T(8,128)(2,1)S(1)}, bf16[192,256]{1,0:T(8,128)(2,1)S(1)}, u32[]{:S(2)}, u32[]{:S(2)}) collective-permute-start(bf16[192,256]{1,0:T(8,128)(2,1)S(1)} %pad_maximum_fusion.4), channel_id=1, source_target_pairs={{0,2},{1,3},{2,0},{3,1},{4,6},{5,7},{6,4},{7,5},{8,10},{9,11},{10,... | collective-permute-start | bytes 294920 | tf_op jit(solution)/shard_map/ppermute | solution.py:23
  46.9 10.6 %collective-permute-start.13 = (bf16[512,256]{1,0:T(8,128)(2,1)S(1)}, bf16[512,256]{1,0:T(8,128)(2,1)S(1)}, u32[]{:S(2)}, u32[]{:S(2)}) collective-permute-start(bf16[512,256]{1,0:T(8,128)(2,1)S(1)} %get-tuple-element.81), channel_id=1, source_target_pairs={{0,15},{1,2},{2,1},{3,4},{4,3},{5,6},{6,5},{7,8},{8,7},{9,10},{10,... | collective-permute-start | bytes 786440 | tf_op jit(solution)/shard_map/ppermute | solution.py:28
  48.1 8.3 %collective-permute-start.12 = (bf16[512,256]{1,0:T(8,128)(2,1)S(1)}, bf16[512,256]{1,0:T(8,128)(2,1)S(1)}, u32[]{:S(2)}, u32[]{:S(2)}) collective-permute-start(bf16[512,256]{1,0:T(8,128)(2,1)S(1)} %get-tuple-element.83), channel_id=1, source_target_pairs={{0,1},{1,0},{2,3},{3,2},{4,5},{5,4},{6,7},{7,6},{8,9},{9,8},{10,11... | collective-permute-start | bytes 786440 | tf_op jit(solution)/shard_map/ppermute | solution.py:23
  48.2 8.3 %collective-permute-start.11 = (bf16[384,256]{1,0:T(8,128)(2,1)S(1)}, bf16[384,256]{1,0:T(8,128)(2,1)S(1)}, u32[]{:S(2)}, u32[]{:S(2)}) collective-permute-start(bf16[384,256]{1,0:T(8,128)(2,1)S(1)} %pad_maximum_fusion.2), channel_id=1, source_target_pairs={{0,4},{1,5},{2,6},{3,7},{4,0},{5,1},{6,2},{7,3},{8,12},{9,13},{10,... | collective-permute-start | bytes 589832 | tf_op jit(solution)/shard_map/ppermute | solution.py:23
  57.6 3.4 %collective-permute-start.14 = (bf16[768,256]{1,0:T(8,128)(2,1)S(1)}, bf16[768,256]{1,0:T(8,128)(2,1)S(1)}, u32[]{:S(2)}, u32[]{:S(2)}) collective-permute-start(bf16[768,256]{1,0:T(8,128)(2,1)S(1)} %pad_maximum_fusion.half), channel_id=1, source_target_pairs={{0,1},{1,0},{2,3},{3,2},{4,5},{5,4},{6,7},{7,6},{8,9},{9,8},{10,11... | collective-permute-start | bytes 1179656 | tf_op jit(solution)/shard_map/ppermute | solution.py:23
  62.7 4.6 %collective-permute-start.15 = (f32[4,256]{1,0:T(4,128)S(1)}, f32[4,256]{1,0:T(4,128)S(1)}, u32[]{:S(2)}, u32[]{:S(2)}) collective-permute-start(f32[4,256]{1,0:T(4,128)S(1)} %get-tuple-element.93), channel_id=1, source_target_pairs={{0,8},{1,9},{2,10},{3,11},{4,12},{5,13},{6,14},{7,15},{8,0},{9,1},... | collective-permute-start | bytes 12296 | tf_op jit(solution)/shard_map/ppermute | solution.py:23
  67.3 4.3 %collective-permute-start.16 = (f32[4,256]{1,0:T(4,128)S(1)}, f32[4,256]{1,0:T(4,128)S(1)}, u32[]{:S(2)}, u32[]{:S(2)}) collective-permute-start(f32[4,256]{1,0:T(4,128)S(1)} %add.12), channel_id=1, source_target_pairs={{0,2},{1,3},{2,0},{3,1},{4,6},{5,7},{6,4},{7,5},{8,10},{9,11},{10,... | collective-permute-start | bytes 12296 | tf_op jit(solution)/shard_map/ppermute | solution.py:23
  72.3 6.9 %collective-permute-start.19 = (bf16[512,256]{1,0:T(8,128)(2,1)S(1)}, bf16[512,256]{1,0:T(8,128)(2,1)S(1)}, u32[]{:S(2)}, u32[]{:S(2)}) collective-permute-start(bf16[512,256]{1,0:T(8,128)(2,1)S(1)} %get-tuple-element.103), channel_id=1, source_target_pairs={{1,0},{2,1},{3,2},{4,3},{5,4},{6,5},{7,6},{8,7},{9,8},{10,9},{11,1... | collective-permute-start | bytes 786440 | tf_op jit(solution)/shard_map/ppermute | solution.py:19
  72.3 5.7 %collective-permute-start.17 = (f32[4,256]{1,0:T(4,128)S(1)}, f32[4,256]{1,0:T(4,128)S(1)}, u32[]{:S(2)}, u32[]{:S(2)}) collective-permute-start(f32[4,256]{1,0:T(4,128)S(1)} %add.13), channel_id=1, source_target_pairs={{0,4},{1,5},{2,6},{3,7},{4,0},{5,1},{6,2},{7,3},{8,12},{9,13},{10,... | collective-permute-start | bytes 12296 | tf_op jit(solution)/shard_map/ppermute | solution.py:23
  78.0 1.2 %collective-permute-start.18 = (f32[4,256]{1,0:T(4,128)S(1)}, f32[4,256]{1,0:T(4,128)S(1)}, u32[]{:S(2)}, u32[]{:S(2)}) collective-permute-start(f32[4,256]{1,0:T(4,128)S(1)} %add.14), channel_id=1, source_target_pairs={{0,1},{1,0},{2,3},{3,2},{4,5},{5,4},{6,7},{7,6},{8,9},{9,8},{10,11... | collective-permute-start | bytes 12296 | tf_op jit(solution)/shard_map/ppermute | solution.py:23

commit v9 on v8

--- a/solution.py
+++ b/solution.py
@@ -259,32 +259,58 @@
             gram[wide, k * ncf : (k + 1) * ncf] = dot_nt(turned[0][:, half], pair[k]) + dot_nt(turned[1][:, half], pair[k])
 
 
-def schur_products(
-    halo, other, part, near, far, weight, message, schur, turned_high, turned_low, local, product, quadratic, base
-):
+def complete_local(halo, part, near, far, weight, message, local):
     subs, nf = weight.shape
-    ncf, columns = halo.ncf, halo.columns
     weights = all_weights(halo, message, weight)
     from_next, from_previous = received(near, far)
     local[:nf] = (1.0 - weights[0]) * part[:nf] + weights[0] * from_previous
     for e in range(1, subs):
         local[e * nf : (e + 1) * nf] = rows_of(part, e, nf)
     local[subs * nf :] = weights[subs] * part[subs * nf :] + (1.0 - weights[subs]) * from_next
-    energy, previous = 0.0, None
-    for j in range(subs):
+
+
+def project(halo, local, turned_high, turned_low, base):
+    ncf, nf = halo.ncf, halo.nf
+    for j in range(base.shape[0] // (2 * ncf)):
+        here = slice(2 * j * ncf, 2 * (j + 1) * ncf)
+        base[here] = split_dot((turned_high[here], turned_low[here]), local[j * nf : (j + 2) * nf])
+
+
+def schur_faces(halo, local, schur):
+    nf, columns = halo.nf, halo.columns
+    faces, energy = [], 0.0
+    for j in range(schur.shape[0] // (2 * nf)):
         vector = local[j * nf : (j + 2) * nf]
-        high, low = split(vector)
-        both = dot(rows_of(schur, j, 2 * nf), jnp.concatenate([high, low], axis=1))
+        both = dot(rows_of(schur, j, 2 * nf), jnp.concatenate(split(vector), axis=1))
         result = both[:, :columns] + both[:, columns:]
         energy = energy + column_sum(vector * result)
-        first = result[:nf]
-        product[j * nf : (j + 1) * nf] = first if j == 0 else previous + first
-        previous = result[nf:]
-        here = slice(2 * j * ncf, 2 * (j + 1) * ncf)
-        base[here] = dot(turned_high[here], high) + dot(turned_high[here], low) + dot(turned_low[here], high)
-    product[subs * nf :] = previous
+        faces[j:] = [result[:nf] if j == 0 else faces[j] + result[:nf], result[nf:]]
+    return faces, energy
+
+
+def schur_load(halo, local, schur, basis_high, basis_low, solution, sums_in, part, near, far, sums):
+    ncf, nf = halo.ncf, halo.nf
+    faces, energy = schur_faces(halo, local, schur)
+    x = [rows_of(solution, e, ncf) for e in range(len(faces))]
+    faces = add_basis(nf, x, basis_high, basis_low, faces)
+    for e, face in enumerate(faces):
+        part[e * nf : (e + 1) * nf] = face
+    send(faces[0], faces[-1], near, far)
+    sums[0:1] = sums_in[0:1]
+    sums[1:2] = sums_in[1:2] + energy
+
+
+def schur_image(
+    halo, image, part, near, far, weight, message, schur, turned_high, turned_low, local, product, quadratic, base
+):
+    nf = halo.nf
+    complete_local(halo, part, near, far, weight, message, local)
+    project(halo, local, turned_high, turned_low, base)
+    faces, energy = schur_faces(halo, local, schur)
+    for e, face in enumerate(faces):
+        product[e * nf : (e + 1) * nf] = face
     quadratic[0:1] = energy
-    quadratic[1:2] = column_sum(other[...] * local[nf:])
+    quadratic[1:2] = column_sum(image[...] * local[nf:])
 
 
 def placed(half, crossed_half):
@@ -314,8 +340,8 @@
     return results, energy
 
 
-def add_basis(nf, x, basis_high, basis_low, product):
-    faces = [rows_of(product, e, nf) for e in range(len(x))]
+def add_basis(nf, x, basis_high, basis_low, faces):
+    faces = list(faces)
     for j in range(len(x) - 1):
         here = slice(2 * j * nf, 2 * (j + 1) * nf)
         pair = jnp.concatenate([x[j], x[j + 1]], axis=0)
@@ -326,11 +352,13 @@
 
 
 def coarse_load(
-    halo, half, crossed_half, inverse, message, coarse, base, gram, quadratic, basis_high, basis_low, product,
-    shares_rounded, shares, solution, part, near, far, sums, gathered,
+    halo, load, part, near, far, weight, message, turned_high, turned_low, half, crossed_half, inverse, coarse, gram,
+    local, shares_rounded, shares, solution, sums, base, gathered,
 ):
     ncf, nf = halo.ncf, halo.nf
-    subs = inverse.shape[0] // ncf
+    subs = weight.shape[0]
+    complete_local(halo, part, near, far, weight, message, local)
+    project(halo, local, turned_high, turned_low, base)
     for place, blocks, start, stop in placed(half, crossed_half):
         gathered[pl.ds(pl.multiple_of(place * subs * ncf, subs * ncf), subs * ncf)] = blocks[start:stop]
     everything = gathered[...]
@@ -339,14 +367,10 @@
     results, energy = coarse_products(ncf, x, base, gram)
     for e, share in enumerate(coarse_shares(ncf, results)):
         shares[e * ncf : (e + 1) * ncf] = share
+        solution[e * ncf : (e + 1) * ncf] = x[e]
     shares_rounded[...] = shares[...].astype(BF16)
-    solution[...] = own
-    sums[0:1] = quadratic[1:2] + column_sum(coarse[...] * own)
-    sums[1:2] = quadratic[0:1] + energy
-    faces = add_basis(nf, x, basis_high, basis_low, product)
-    for e in range(subs + 1):
-        part[e * nf : (e + 1) * nf] = faces[e]
-    send(faces[0], faces[subs], near, far)
+    sums[0:1] = column_sum(load[...] * local[nf:]) + column_sum(coarse[...] * own)
+    sums[1:2] = energy
 
 
 def coarse_image(
@@ -369,7 +393,7 @@
     sums[2:3] = quadratic[1:2] + sum(column_sum(rows_of(shares, e, ncf) * x[e]) for e in range(subs + 1))
     sums[3:4] = quadratic[0:1] + energy
     solution[...] = own
-    faces = add_basis(nf, x, basis_high, basis_low, product)
+    faces = add_basis(nf, x, basis_high, basis_low, [rows_of(product, e, nf) for e in range(subs + 1)])
     for e in range(1, subs + 1):
         part[(e - 1) * nf : e * nf] = faces[e]
     back[...] = faces[0].astype(BF16)
@@ -379,7 +403,7 @@
     ncf, nf = halo.ncf, halo.nf
     for j in range(rows.shape[0] // ncf):
         here, beside = slice(j * nf, (j + 1) * nf), slice((j + 1) * nf, (j + 2) * nf)
-        for local, coarse, whole in ((z_local, z_coarse, z), (y_local, y_coarse, y)):
+        for local, coarse, whole in ((z_local, z_coarse[ncf:], z), (y_local, y_coarse[...], y)):
             whole[here] = local[beside] + split_dot(rows_of(rows, j, ncf), rows_of(coarse, j, ncf), dot_tn)
 
 
@@ -425,35 +449,36 @@
         scratch=[pltpu.VMEM((halo.weight_count, columns), F32)],
     )
     half = gather_half(coarse_rounded, early[:1])
-    tied = after(tuple(map(outside, (neumann, schur))), message, half)
+    message = after(message, half)
+    tied = after(tuple(map(outside, (neumann, schur))), message)
     neumann, schur = stage(
         bind(fetch), [described(array) for array in tied], *tied, scratch=semaphores(2), fetched=2
     )
-    half = gather_half(half, early[1:])
-    message = after(shifted(message, 1), half)
+    message = shifted(message, 1)
+    half = gather_half(half, early[1:], neumann)
     part, near, far = stage(
         bind(neumann_load), [(faces, F32)] + halves, load, weight, message, neumann
     )
     far, near = far_block(far), crossed(near, 1)
     long, wide = ((2 * subs * nf, 2 * ncf), BF16), ((local_rows, 2 * nf), BF16)
     basis_high, basis_low, turned_high, turned_low, gram = stage(
-        bind(static_basis), [long, long, wide, wide, ((local_rows, LANES), F32)], schur, message, rows
-    )
-    half = gather_half(half, late, near, far, gram)
+        bind(static_basis), [long, long, wide, wide, ((local_rows, LANES), F32)], schur, after(message, part), rows
+    )
+    half = gather_half(half, late, gram)
     crossed_half = crossed(half, 1)
-    part = after(part, half)
-    z_local, product, quadratic, base = stage(
-        bind(schur_products), products, load, part, near, far, weight, message, schur, turned_high, turned_low
-    )
-    share_rows = ((subs + 1) * ncf, columns)
-    shares_rounded, shares, z_coarse, part, near, far, sums = stage(
-        bind(coarse_load),
-        [(share_rows, BF16), (share_rows, F32), (coarse_own, F32), (faces, F32)] + halves + [((8, columns), F32)],
-        half, crossed_half, inverse, message, coarse, base, gram, quadratic, basis_high, basis_low, product,
-        scratch=[pltpu.VMEM((nco, columns), BF16)],
-    )
+    share_rows, sum_rows = ((subs + 1) * ncf, columns), ((8, columns), F32)
+    z_local, shares_rounded, shares, z_coarse, sums = stage(
+        bind(coarse_load), [(faces, F32), (share_rows, BF16), (share_rows, F32), (share_rows, F32), sum_rows],
+        load, part, near, far, weight, message, turned_high, turned_low, half, crossed_half, inverse, coarse, gram,
+        scratch=[pltpu.VMEM((local_rows, columns), F32), pltpu.VMEM((nco, columns), BF16)],
+    )
+    part, near, far, sums = stage(
+        bind(schur_load), [(faces, F32)] + halves + [sum_rows],
+        z_local, schur, basis_high, basis_low, z_coarse, sums,
+    )
+    half = gather_half(shares_rounded, early[:1])
+    near, far = after((near, far), half)
     far, near = far_block(far), crossed(near, 1)
-    half = gather_half(shares_rounded, early[:1])
     image, part, near, far = stage(
         bind(neumann_image), [(own, F32), (faces, F32)] + halves, part, near, far, weight, message, neumann
     )
@@ -463,19 +488,18 @@
     crossed_half = crossed(half, 1)
     part = after(part, half)
     y_local, product, quadratic, base = stage(
-        bind(schur_products), products, image, part, near, far, weight, message, schur, turned_high, turned_low
+        bind(schur_image), products, image, part, near, far, weight, message, schur, turned_high, turned_low
     )
     sums, y_coarse, part, back = stage(
         bind(coarse_image), [((4, columns), F32), (coarse_own, F32), (own, F32), ((nf, columns), BF16)],
         half, crossed_half, inverse, message, shares, base, gram, quadratic, basis_high, basis_low, product, sums,
         scratch=[pltpu.VMEM((nco, columns), F32)],
     )
-    for bit in early:
-        sums = sums + crossed(sums, bit)
-    z, y = stage(bind(complete), [(own, F32), (own, F32)], z_local, z_coarse, after(y_local, sums), y_coarse, rows)
-    for bit in steps[-2:]:
-        sums = sums + crossed(sums, bit)
-    back = shifted(after(back, y), -1)
+    z, y = stage(bind(complete), [(own, F32), (own, F32)], z_local, z_coarse, y_local, y_coarse, rows)
+    for k, bit in enumerate(steps):
+        sums = sums + after(crossed(sums, bit), y)
+        if k == len(early) - 1:
+            back = shifted(after(back, sums), -1)
     return stage(bind(combine), [(own, F32), (own, F32)], sums, load, z, y, image, part, back)
 
 

time: 81 us -> 80.6 us (level)
  starting transfers between devices: 24.5 us -> 23.3 us
    ppermute x3, waiting for transfers between devices: 1.06 us -> 12.6 us  [far_block(): lax.ppermute(block, AXIS, [(i, (i + (1 if i % 2 else -1)) % n) for i in r...]
    ppermute x15, waiting for transfers between devices: 32.1 us -> 20.9 us  [crossed(): lax.ppermute(block, AXIS, [(i, i ^ bit) for i in range(lax.axis_size(AXIS...]
    ppermute x15, starting transfers between devices: 20.7 us -> 18.9 us  [crossed(): lax.ppermute(block, AXIS, [(i, i ^ bit) for i in range(lax.axis_size(AXIS...]
    ppermute x3, starting transfers between devices: 3.26 us -> 4.39 us  [far_block(): lax.ppermute(block, AXIS, [(i, (i + (1 if i % 2 else -1)) % n) for i in r...]
  transfers between devices with their start and end apart: 20 -> 20, of which waited for: 10 -> 10; matrix products, arithmetic and copies ran while one was open for 0% -> 0% of each run, Pallas kernels for 17% -> 20%
where the time goes in v9:
time: 80.6 us; the launch traced here: 80.4 us
  waiting for transfers between devices  33.5 us (42%)
  starting transfers between devices  23.3 us (29%)
  Pallas kernels  22.7 us (28%)
  between operations  0.82 us (1%)
    pallas_call x12, Pallas kernels, stage(): return call(*operands)  22.7 us
    ppermute x15, waiting for transfers between devices, crossed(): lax.ppermute(block, AXIS, [(i, i ^ bit) for i in range(lax.axis_size(AXIS...  20.9 us
    ppermute x15, starting transfers between devices, crossed(): lax.ppermute(block, AXIS, [(i, i ^ bit) for i in range(lax.axis_size(AXIS...  18.9 us
    ppermute x3, waiting for transfers between devices, far_block(): lax.ppermute(block, AXIS, [(i, (i + (1 if i % 2 else -1)) % n) for i in r...  12.6 us
    ppermute x3, starting transfers between devices, far_block(): lax.ppermute(block, AXIS, [(i, (i + (1 if i % 2 else -1)) % n) for i in r...  4.39 us
  transfers between devices with their start and end apart: 20, of which 10 were waited for; matrix products, arithmetic and copies ran while one was open for 0% of the time, Pallas kernels for 20%

profile of v9, /device:TPU:0, one launch (start us, length us, event | category | flops | bytes accessed | tf_op | source)
XLA Modules:
  0.0 80.4 jit_solution(5004799789391524442)
XLA Ops:
  0.6 1.5 %prepare.1 = (f32[1024,256]{1,0:T(8,128)S(1)}, bf16[64,512]{1,0:T(8,128)(2,1)S(1)}, f32[2,512]{1,0:T(2,128)S(1)}, bf16[64,1024]{1,0:T(8,128)(2,1)S(1)}, bf16[64,...) custom-call(f32[1024,256]{1,0:T(8,128)} %load.1, bf16[64,512]{1,0:T(8,128)(2,1)} %rows.1, f32[2,512]{1,0:T(2,128)} %weight.1, ...), custom_call_target="tpu_custom_call" | custom-call | tf_op jit(solution)/shard_map/prepare/pallas_call | solution.py:161
  2.2 4.1 %collective-permute-start = (bf16[64,256]{1,0:T(8,128)(2,1)S(1)}, bf16[64,256]{1,0:T(8,128)(2,1)S(1)}, u32[]{:S(2)}, u32[]{:S(2)}) collective-permute-start(bf16[64,256]{1,0:T(8,128)(2,1)S(1)} %get-tuple-element.61), channel_id=1, source_target_pairs={{0,8},{1,9},{2,10},{3,11},{4,12},{5,13},{6,14},{7,15},{8,0},{9,1},... | collective-permute-start | bytes 98312 | tf_op jit(solution)/shard_map/ppermute | solution.py:23
  6.3 0.3 halo_message.1
  6.5 2.0 %collective-permute-done = bf16[64,256]{1,0:T(8,128)(2,1)S(1)} collective-permute-done((bf16[64,256]{1,0:T(8,128)(2,1)S(1)}, bf16[64,256]{1,0:T(8,128)(2,1)S(1)}, u32[]{:S(2)}, u32[]{:S(2)}) %collective-permute-start) | collective-permute-done | bytes 32800 | tf_op jit(solution)/shard_map/ppermute | solution.py:23
  8.5 1.8 %collective-permute-start.4 = (bf16[128,256]{1,0:T(8,128)(2,1)S(1)}, bf16[128,256]{1,0:T(8,128)(2,1)S(1)}, u32[]{:S(2)}, u32[]{:S(2)}) collective-permute-start(bf16[128,256]{1,0:T(8,128)(2,1)S(1)} %pad_maximum_fusion.5), channel_id=1, source_target_pairs={{0,2},{1,3},{2,0},{3,1},{4,6},{5,7},{6,4},{7,5},{8,10},{9,11},{10,... | collective-permute-start | bytes 196616 | tf_op jit(solution)/shard_map/ppermute | solution.py:23
  10.3 3.5 %fetch.1 = (bf16[2048,1024]{1,0:T(8,128)(2,1)S(1)}, bf16[2048,1024]{1,0:T(8,128)(2,1)S(1)}) custom-call(bf16[2048,1024]{1,0:T(8,128)(2,1)} %neumann, bf16[2048,1024]{1,0:T(8,128)(2,1)} %schur), custom_call_target="tpu_custom_call" | custom-call | tf_op jit(solution)/shard_map/fetch/pallas_call | solution.py:161
  13.8 0.0 collective-permute-done.4
  13.8 5.0 %collective-permute-start.5 = (bf16[256,256]{1,0:T(8,128)(2,1)S(1)}, bf16[256,256]{1,0:T(8,128)(2,1)S(1)}, u32[]{:S(2)}, u32[]{:S(2)}) collective-permute-start(bf16[256,256]{1,0:T(8,128)(2,1)S(1)} %pad_maximum_fusion.3), channel_id=1, source_target_pairs={{0,4},{1,5},{2,6},{3,7},{4,0},{5,1},{6,2},{7,3},{8,12},{9,13},{10,... | collective-permute-start | bytes 393224 | tf_op jit(solution)/shard_map/ppermute | solution.py:23
  18.8 1.5 %neumann_load.1 = (f32[1536,256]{1,0:T(8,128)S(1)}, bf16[512,256]{1,0:T(8,128)(2,1)S(1)}, bf16[512,256]{1,0:T(8,128)(2,1)S(1)}) custom-call(f32[1024,256]{1,0:T(8,128)S(1)} %get-tuple-element.57.load, f32[2,512]{1,0:T(2,128)S(1)} %get-tuple-element.58.weight, bf16[720,256]{1,0:T(8,128)(2,1)S(1)} %collective-permute-done.1.message, ...), custom_call_target="tpu_custom_call" | custom-call | tf_op jit(solution)/shard_map/neumann_load/pallas_call | solution.py:161
  20.3 0.1 collective-permute-start.2
  20.4 2.4 %collective-permute-start.3 = (bf16[512,256]{1,0:T(8,128)(2,1)S(1)}, bf16[512,256]{1,0:T(8,128)(2,1)S(1)}, u32[]{:S(2)}, u32[]{:S(2)}) collective-permute-start(bf16[512,256]{1,0:T(8,128)(2,1)S(1)} %get-tuple-element.68), channel_id=1, source_target_pairs={{0,15},{1,2},{2,1},{3,4},{4,3},{5,6},{6,5},{7,8},{8,7},{9,10},{10,... | collective-permute-start | bytes 786440 | tf_op jit(solution)/shard_map/ppermute | solution.py:28
  22.8 1.9 %static_basis.1 = (bf16[2048,64]{1,0:T(8,128)(2,1)S(1)}, bf16[2048,64]{1,0:T(8,128)(2,1)S(1)}, bf16[128,1024]{1,0:T(8,128)(2,1)S(1)}, bf16[128,1024]{1,0:T(8,128)(2,1)S(1)}, f32[128,128]{1,0:T(8,128)S(1)}) custom-call(bf16[2048,1024]{1,0:T(8,128)(2,1)S(1)} %get-tuple-element.69.schur, bf16[720,256]{1,0:T(8,128)(2,1)S(1)} %collective-permute-done.1.message, ...), custom_call_target="tpu_custom_call" | custom-call | tf_op jit(solution)/shard_map/static_basis/pallas_call | solution.py:161
  24.7 0.0 collective-permute-done.5
  24.8 0.1 collective-permute-start.6
  24.8 0.0 collective-permute-done.2.near
  24.9 4.2 %collective-permute-done.3.far = bf16[512,256]{1,0:T(8,128)(2,1)S(1)} collective-permute-done((bf16[512,256]{1,0:T(8,128)(2,1)S(1)}, bf16[512,256]{1,0:T(8,128)(2,1)S(1)}, u32[]{:S(2)}, u32[]{:S(2)}) %collective-permute-start.3) | collective-permute-done | bytes 262176 | tf_op jit(solution)/shard_map/ppermute | solution.py:28
  29.1 1.6 %coarse_load.1 = (f32[1536,256]{1,0:T(8,128)S(1)}, bf16[96,256]{1,0:T(8,128)(2,1)S(1)}, f32[96,256]{1,0:T(8,128)S(1)}, f32[96,256]{1,0:T(8,128)S(1)}, f32[8,256]{1,0:T(8,128)S(1)}) custom-call(f32[1024,256]{1,0:T(8,128)S(1)} %get-tuple-element.57.load, f32[1536,256]{1,0:T(8,128)S(1)} %get-tuple-element.66.part, ...), custom_call_target="tpu_custom_call" | custom-call | tf_op jit(solution)/shard_map/coarse_load/pallas_call | solution.py:161
  30.7 1.1 %collective-permute-start.7 = (bf16[96,256]{1,0:T(8,128)(2,1)S(1)}, bf16[96,256]{1,0:T(8,128)(2,1)S(1)}, u32[]{:S(2)}, u32[]{:S(2)}) collective-permute-start(bf16[96,256]{1,0:T(8,128)(2,1)S(1)} %get-tuple-element.77), channel_id=1, source_target_pairs={{0,8},{1,9},{2,10},{3,11},{4,12},{5,13},{6,14},{7,15},{8,0},{9,1},... | collective-permute-start | bytes 147464 | tf_op jit(solution)/shard_map/ppermute | solution.py:23
  31.8 3.3 %schur_load.1 = (f32[1536,256]{1,0:T(8,128)S(1)}, bf16[512,256]{1,0:T(8,128)(2,1)S(1)}, bf16[512,256]{1,0:T(8,128)(2,1)S(1)}, f32[8,256]{1,0:T(8,128)S(1)}) custom-call(f32[1536,256]{1,0:T(8,128)S(1)} %get-tuple-element.78.local.z_local, bf16[2048,1024]{1,0:T(8,128)(2,1)S(1)} %get-tuple-element.69.schur, bf16[2048,64]{1,0:T(8,128)(2,1)S(1)} %get-tuple-element.79.basis_high, ...), custom_call_target="tpu_custom_call" | custom-call | tf_op jit(solution)/shard_map/schur_load/pallas_call | solution.py:161
  35.1 1.1 %collective-permute-done.7 = bf16[96,256]{1,0:T(8,128)(2,1)S(1)} collective-permute-done((bf16[96,256]{1,0:T(8,128)(2,1)S(1)}, bf16[96,256]{1,0:T(8,128)(2,1)S(1)}, u32[]{:S(2)}, u32[]{:S(2)}) %collective-permute-start.7) | collective-permute-done | bytes 49184 | tf_op jit(solution)/shard_map/ppermute | solution.py:23
  36.1 1.0 %collective-permute-start.9 = (bf16[512,256]{1,0:T(8,128)(2,1)S(1)}, bf16[512,256]{1,0:T(8,128)(2,1)S(1)}, u32[]{:S(2)}, u32[]{:S(2)}) collective-permute-start(bf16[512,256]{1,0:T(8,128)(2,1)S(1)} %get-tuple-element.86), channel_id=1, source_target_pairs={{0,1},{1,0},{2,3},{3,2},{4,5},{5,4},{6,7},{7,6},{8,9},{9,8},{10,11... | collective-permute-start | bytes 786440 | tf_op jit(solution)/shard_map/ppermute | solution.py:23
  37.1 1.0 %collective-permute-start.10 = (bf16[512,256]{1,0:T(8,128)(2,1)S(1)}, bf16[512,256]{1,0:T(8,128)(2,1)S(1)}, u32[]{:S(2)}, u32[]{:S(2)}) collective-permute-start(bf16[512,256]{1,0:T(8,128)(2,1)S(1)} %get-tuple-element.87), channel_id=1, source_target_pairs={{0,15},{1,2},{2,1},{3,4},{4,3},{5,6},{6,5},{7,8},{8,7},{9,10},{10,... | collective-permute-start | bytes 786440 | tf_op jit(solution)/shard_map/ppermute | solution.py:28
  38.1 0.7 collective-permute-start.8
  38.8 0.0 collective-permute-done.9.near_in
  38.8 6.9 %collective-permute-done.10.far_in = bf16[512,256]{1,0:T(8,128)(2,1)S(1)} collective-permute-done((bf16[512,256]{1,0:T(8,128)(2,1)S(1)}, bf16[512,256]{1,0:T(8,128)(2,1)S(1)}, u32[]{:S(2)}, u32[]{:S(2)}) %collective-permute-start.10) | collective-permute-done | bytes 262176 | tf_op jit(solution)/shard_map/ppermute | solution.py:28
  45.7 1.6 %neumann_image.1 = (f32[1024,256]{1,0:T(8,128)S(1)}, f32[1536,256]{1,0:T(8,128)S(1)}, bf16[512,256]{1,0:T(8,128)(2,1)S(1)}, bf16[512,256]{1,0:T(8,128)(2,1)S(1)}) custom-call(f32[1536,256]{1,0:T(8,128)S(1)} %get-tuple-element.83.part_in, bf16[512,256]{1,0:T(8,128)(2,1)S(1)} %collective-permute-done.9.near_in, ...), custom_call_target="tpu_custom_call" | custom-call | tf_op jit(solution)/shard_map/neumann_image/pallas_call | solution.py:161
  47.3 1.0 %collective-permute-start.13 = (bf16[512,256]{1,0:T(8,128)(2,1)S(1)}, bf16[512,256]{1,0:T(8,128)(2,1)S(1)}, u32[]{:S(2)}, u32[]{:S(2)}) collective-permute-start(bf16[512,256]{1,0:T(8,128)(2,1)S(1)} %get-tuple-element.88), channel_id=1, source_target_pairs={{0,15},{1,2},{2,1},{3,4},{4,3},{5,6},{6,5},{7,8},{8,7},{9,10},{10,... | collective-permute-start | bytes 786440 | tf_op jit(solution)/shard_map/ppermute | solution.py:28
  48.3 0.0 collective-permute-done.8
  48.3 0.7 collective-permute-start.12
  49.1 0.1 collective-permute-start.11
  49.2 7.3 %collective-permute-done.11 = bf16[384,256]{1,0:T(8,128)(2,1)S(1)} collective-permute-done((bf16[384,256]{1,0:T(8,128)(2,1)S(1)}, bf16[384,256]{1,0:T(8,128)(2,1)S(1)}, u32[]{:S(2)}, u32[]{:S(2)}) %collective-permute-start.11) | collective-permute-done | bytes 196640 | tf_op jit(solution)/shard_map/ppermute | solution.py:23
  56.4 0.0 collective-permute-done.12.near
  56.4 1.5 %collective-permute-done.13.far = bf16[512,256]{1,0:T(8,128)(2,1)S(1)} collective-permute-done((bf16[512,256]{1,0:T(8,128)(2,1)S(1)}, bf16[512,256]{1,0:T(8,128)(2,1)S(1)}, u32[]{:S(2)}, u32[]{:S(2)}) %collective-permute-start.13) | collective-permute-done | bytes 262176 | tf_op jit(solution)/shard_map/ppermute | solution.py:28
  57.9 0.1 collective-permute-start.14
  58.0 3.6 %schur_image.1 = (f32[1536,256]{1,0:T(8,128)S(1)}, f32[1536,256]{1,0:T(8,128)S(1)}, f32[8,256]{1,0:T(8,128)S(1)}, f32[128,256]{1,0:T(8,128)S(1)}) custom-call(f32[1024,256]{1,0:T(8,128)S(1)} %get-tuple-element.93.image, f32[1536,256]{1,0:T(8,128)S(1)} %get-tuple-element.95.part, bf16[512,256]{1,0:T(8,128)(2,1)S(1)} %collective-permute-done.12.near, ...), custom_call_target="tpu_custom_call" | custom-call | tf_op jit(solution)/shard_map/schur_image/pallas_call | solution.py:161
  61.6 0.0 collective-permute-done.14.crossed_half
  61.6 1.7 %coarse_image.1 = (f32[4,256]{1,0:T(4,128)S(1)}, f32[64,256]{1,0:T(8,128)S(1)}, f32[1024,256]{1,0:T(8,128)S(1)}, bf16[512,256]{1,0:T(8,128)(2,1)S(1)}) custom-call(bf16[768,256]{1,0:T(8,128)(2,1)S(1)} %pad_maximum_fusion.half, bf16[768,256]{1,0:T(8,128)(2,1)S(1)} %collective-permute-done.14.crossed_half, bf16[64,1024]{1,0:T(8,128)(2,1)S(1)} %get-tuple-element.60.inverse, ...), custom_call_target="tpu_custom_call" | custom-call | tf_op jit(solution)/shard_map/coarse_image/pallas_call | solution.py:161
  63.3 0.5 collective-permute-start.15
  63.7 0.7 complete.1
  64.5 3.4 %collective-permute-done.15 = f32[4,256]{1,0:T(4,128)S(1)} collective-permute-done((f32[4,256]{1,0:T(4,128)S(1)}, f32[4,256]{1,0:T(4,128)S(1)}, u32[]{:S(2)}, u32[]{:S(2)}) %collective-permute-start.15) | collective-permute-done | bytes 4128 | tf_op jit(solution)/shard_map/ppermute | solution.py:23
  67.9 2.4 %collective-permute-start.16 = (f32[4,256]{1,0:T(4,128)S(1)}, f32[4,256]{1,0:T(4,128)S(1)}, u32[]{:S(2)}, u32[]{:S(2)}) collective-permute-start(f32[4,256]{1,0:T(4,128)S(1)} %add.12), channel_id=1, source_target_pairs={{0,2},{1,3},{2,0},{3,1},{4,6},{5,7},{6,4},{7,5},{8,10},{9,11},{10,... | collective-permute-start | bytes 12296 | tf_op jit(solution)/shard_map/ppermute | solution.py:23
  70.3 1.6 %collective-permute-done.16 = f32[4,256]{1,0:T(4,128)S(1)} collective-permute-done((f32[4,256]{1,0:T(4,128)S(1)}, f32[4,256]{1,0:T(4,128)S(1)}, u32[]{:S(2)}, u32[]{:S(2)}) %collective-permute-start.16) | collective-permute-done | bytes 4128 | tf_op jit(solution)/shard_map/ppermute | solution.py:23
  71.9 1.3 %collective-permute-start.17 = (f32[4,256]{1,0:T(4,128)S(1)}, f32[4,256]{1,0:T(4,128)S(1)}, u32[]{:S(2)}, u32[]{:S(2)}) collective-permute-start(f32[4,256]{1,0:T(4,128)S(1)} %add.13), channel_id=1, source_target_pairs={{0,4},{1,5},{2,6},{3,7},{4,0},{5,1},{6,2},{7,3},{8,12},{9,13},{10,... | collective-permute-start | bytes 12296 | tf_op jit(solution)/shard_map/ppermute | solution.py:23
  73.2 4.4 %collective-permute-done.17 = f32[4,256]{1,0:T(4,128)S(1)} collective-permute-done((f32[4,256]{1,0:T(4,128)S(1)}, f32[4,256]{1,0:T(4,128)S(1)}, u32[]{:S(2)}, u32[]{:S(2)}) %collective-permute-start.17) | collective-permute-done | bytes 4128 | tf_op jit(solution)/shard_map/ppermute | solution.py:23
  77.6 0.0 collective-permute-start.18
  77.6 1.2 %collective-permute-done.18 = f32[4,256]{1,0:T(4,128)S(1)} collective-permute-done((f32[4,256]{1,0:T(4,128)S(1)}, f32[4,256]{1,0:T(4,128)S(1)}, u32[]{:S(2)}, u32[]{:S(2)}) %collective-permute-start.18) | collective-permute-done | bytes 4128 | tf_op jit(solution)/shard_map/ppermute | solution.py:23
  78.8 0.0 collective-permute-done.19.from_next
  78.8 1.7 %combine.1 = (f32[1024,256]{1,0:T(8,128)}, f32[1024,256]{1,0:T(8,128)}) custom-call(f32[4,256]{1,0:T(4,128)S(1)} %add.15.sums, f32[1024,256]{1,0:T(8,128)S(1)} %get-tuple-element.57.load, f32[1024,256]{1,0:T(8,128)S(1)} %get-tuple-element.108.z, f32[1024,256]{1,0:T(8,128)S(1)} %get-tuple-element.103.y, f32[1024,256]{1,0:T(8,128)S(1)} %get-tuple-element.93.image, ...), custom_call_target="tpu_custom_call" | custom-call | tf_op jit(solution)/shard_map/combine/pallas_call | solution.py:161
  (14 shorter events, 0.1 us)
Async XLA Ops:
  2.2 6.3 %collective-permute-start = (bf16[64,256]{1,0:T(8,128)(2,1)S(1)}, bf16[64,256]{1,0:T(8,128)(2,1)S(1)}, u32[]{:S(2)}, u32[]{:S(2)}) collective-permute-start(bf16[64,256]{1,0:T(8,128)(2,1)S(1)} %get-tuple-element.61), channel_id=1, source_target_pairs={{0,8},{1,9},{2,10},{3,11},{4,12},{5,13},{6,14},{7,15},{8,0},{9,1},... | collective-permute-start | bytes 98312 | tf_op jit(solution)/shard_map/ppermute | solution.py:23
  8.5 10.3 %collective-permute-start.1 = (bf16[720,256]{1,0:T(8,128)(2,1)S(1)}, bf16[720,256]{1,0:T(8,128)(2,1)S(1)}, u32[]{:S(2)}, u32[]{:S(2)}) collective-permute-start(bf16[720,256]{1,0:T(8,128)(2,1)S(1)} %halo_message.1), channel_id=1, source_target_pairs={{15,0},{0,1},{1,2},{2,3},{3,4},{4,5},{5,6},{6,7},{7,8},{8,9},{9,10... | collective-permute-start | bytes 1105928 | tf_op jit(solution)/shard_map/ppermute | solution.py:19
  8.5 5.3 %collective-permute-start.4 = (bf16[128,256]{1,0:T(8,128)(2,1)S(1)}, bf16[128,256]{1,0:T(8,128)(2,1)S(1)}, u32[]{:S(2)}, u32[]{:S(2)}) collective-permute-start(bf16[128,256]{1,0:T(8,128)(2,1)S(1)} %pad_maximum_fusion.5), channel_id=1, source_target_pairs={{0,2},{1,3},{2,0},{3,1},{4,6},{5,7},{6,4},{7,5},{8,10},{9,11},{10,... | collective-permute-start | bytes 196616 | tf_op jit(solution)/shard_map/ppermute | solution.py:23
  13.8 10.9 %collective-permute-start.5 = (bf16[256,256]{1,0:T(8,128)(2,1)S(1)}, bf16[256,256]{1,0:T(8,128)(2,1)S(1)}, u32[]{:S(2)}, u32[]{:S(2)}) collective-permute-start(bf16[256,256]{1,0:T(8,128)(2,1)S(1)} %pad_maximum_fusion.3), channel_id=1, source_target_pairs={{0,4},{1,5},{2,6},{3,7},{4,0},{5,1},{6,2},{7,3},{8,12},{9,13},{10,... | collective-permute-start | bytes 393224 | tf_op jit(solution)/shard_map/ppermute | solution.py:23
  20.3 4.5 %collective-permute-start.2 = (bf16[512,256]{1,0:T(8,128)(2,1)S(1)}, bf16[512,256]{1,0:T(8,128)(2,1)S(1)}, u32[]{:S(2)}, u32[]{:S(2)}) collective-permute-start(bf16[512,256]{1,0:T(8,128)(2,1)S(1)} %get-tuple-element.67), channel_id=1, source_target_pairs={{0,1},{1,0},{2,3},{3,2},{4,5},{5,4},{6,7},{7,6},{8,9},{9,8},{10,11... | collective-permute-start | bytes 786440 | tf_op jit(solution)/shard_map/ppermute | solution.py:23
  20.4 8.7 %collective-permute-start.3 = (bf16[512,256]{1,0:T(8,128)(2,1)S(1)}, bf16[512,256]{1,0:T(8,128)(2,1)S(1)}, u32[]{:S(2)}, u32[]{:S(2)}) collective-permute-start(bf16[512,256]{1,0:T(8,128)(2,1)S(1)} %get-tuple-element.68), channel_id=1, source_target_pairs={{0,15},{1,2},{2,1},{3,4},{4,3},{5,6},{6,5},{7,8},{8,7},{9,10},{10,... | collective-permute-start | bytes 786440 | tf_op jit(solution)/shard_map/ppermute | solution.py:28
  24.8 4.3 %collective-permute-start.6 = (bf16[512,256]{1,0:T(8,128)(2,1)S(1)}, bf16[512,256]{1,0:T(8,128)(2,1)S(1)}, u32[]{:S(2)}, u32[]{:S(2)}) collective-permute-start(bf16[512,256]{1,0:T(8,128)(2,1)S(1)} %pad_maximum_fusion.1.half), channel_id=1, source_target_pairs={{0,1},{1,0},{2,3},{3,2},{4,5},{5,4},{6,7},{7,6},{8,9},{9,8},{10,11... | collective-permute-start | bytes 786440 | tf_op jit(solution)/shard_map/ppermute | solution.py:23
  30.7 5.4 %collective-permute-start.7 = (bf16[96,256]{1,0:T(8,128)(2,1)S(1)}, bf16[96,256]{1,0:T(8,128)(2,1)S(1)}, u32[]{:S(2)}, u32[]{:S(2)}) collective-permute-start(bf16[96,256]{1,0:T(8,128)(2,1)S(1)} %get-tuple-element.77), channel_id=1, source_target_pairs={{0,8},{1,9},{2,10},{3,11},{4,12},{5,13},{6,14},{7,15},{8,0},{9,1},... | collective-permute-start | bytes 147464 | tf_op jit(solution)/shard_map/ppermute | solution.py:23
  36.1 2.7 %collective-permute-start.9 = (bf16[512,256]{1,0:T(8,128)(2,1)S(1)}, bf16[512,256]{1,0:T(8,128)(2,1)S(1)}, u32[]{:S(2)}, u32[]{:S(2)}) collective-permute-start(bf16[512,256]{1,0:T(8,128)(2,1)S(1)} %get-tuple-element.86), channel_id=1, source_target_pairs={{0,1},{1,0},{2,3},{3,2},{4,5},{5,4},{6,7},{7,6},{8,9},{9,8},{10,11... | collective-permute-start | bytes 786440 | tf_op jit(solution)/shard_map/ppermute | solution.py:23
  37.1 8.6 %collective-permute-start.10 = (bf16[512,256]{1,0:T(8,128)(2,1)S(1)}, bf16[512,256]{1,0:T(8,128)(2,1)S(1)}, u32[]{:S(2)}, u32[]{:S(2)}) collective-permute-start(bf16[512,256]{1,0:T(8,128)(2,1)S(1)} %get-tuple-element.87), channel_id=1, source_target_pairs={{0,15},{1,2},{2,1},{3,4},{4,3},{5,6},{6,5},{7,8},{8,7},{9,10},{10,... | collective-permute-start | bytes 786440 | tf_op jit(solution)/shard_map/ppermute | solution.py:28
  38.1 10.2 %collective-permute-start.8 = (bf16[192,256]{1,0:T(8,128)(2,1)S(1)}, bf16[192,256]{1,0:T(8,128)(2,1)S(1)}, u32[]{:S(2)}, u32[]{:S(2)}) collective-permute-start(bf16[192,256]{1,0:T(8,128)(2,1)S(1)} %pad_maximum_fusion.4), channel_id=1, source_target_pairs={{0,2},{1,3},{2,0},{3,1},{4,6},{5,7},{6,4},{7,5},{8,10},{9,11},{10,... | collective-permute-start | bytes 294920 | tf_op jit(solution)/shard_map/ppermute | solution.py:23
  47.3 10.6 %collective-permute-start.13 = (bf16[512,256]{1,0:T(8,128)(2,1)S(1)}, bf16[512,256]{1,0:T(8,128)(2,1)S(1)}, u32[]{:S(2)}, u32[]{:S(2)}) collective-permute-start(bf16[512,256]{1,0:T(8,128)(2,1)S(1)} %get-tuple-element.88), channel_id=1, source_target_pairs={{0,15},{1,2},{2,1},{3,4},{4,3},{5,6},{6,5},{7,8},{8,7},{9,10},{10,... | collective-permute-start | bytes 786440 | tf_op jit(solution)/shard_map/ppermute | solution.py:28
  48.3 8.1 %collective-permute-start.12 = (bf16[512,256]{1,0:T(8,128)(2,1)S(1)}, bf16[512,256]{1,0:T(8,128)(2,1)S(1)}, u32[]{:S(2)}, u32[]{:S(2)}) collective-permute-start(bf16[512,256]{1,0:T(8,128)(2,1)S(1)} %get-tuple-element.90), channel_id=1, source_target_pairs={{0,1},{1,0},{2,3},{3,2},{4,5},{5,4},{6,7},{7,6},{8,9},{9,8},{10,11... | collective-permute-start | bytes 786440 | tf_op jit(solution)/shard_map/ppermute | solution.py:23
  49.1 7.3 %collective-permute-start.11 = (bf16[384,256]{1,0:T(8,128)(2,1)S(1)}, bf16[384,256]{1,0:T(8,128)(2,1)S(1)}, u32[]{:S(2)}, u32[]{:S(2)}) collective-permute-start(bf16[384,256]{1,0:T(8,128)(2,1)S(1)} %pad_maximum_fusion.2), channel_id=1, source_target_pairs={{0,4},{1,5},{2,6},{3,7},{4,0},{5,1},{6,2},{7,3},{8,12},{9,13},{10,... | collective-permute-start | bytes 589832 | tf_op jit(solution)/shard_map/ppermute | solution.py:23
  57.9 3.7 %collective-permute-start.14 = (bf16[768,256]{1,0:T(8,128)(2,1)S(1)}, bf16[768,256]{1,0:T(8,128)(2,1)S(1)}, u32[]{:S(2)}, u32[]{:S(2)}) collective-permute-start(bf16[768,256]{1,0:T(8,128)(2,1)S(1)} %pad_maximum_fusion.half), channel_id=1, source_target_pairs={{0,1},{1,0},{2,3},{3,2},{4,5},{5,4},{6,7},{7,6},{8,9},{9,8},{10,11... | collective-permute-start | bytes 1179656 | tf_op jit(solution)/shard_map/ppermute | solution.py:23
  63.3 4.6 %collective-permute-start.15 = (f32[4,256]{1,0:T(4,128)S(1)}, f32[4,256]{1,0:T(4,128)S(1)}, u32[]{:S(2)}, u32[]{:S(2)}) collective-permute-start(f32[4,256]{1,0:T(4,128)S(1)} %get-tuple-element.100), channel_id=1, source_target_pairs={{0,8},{1,9},{2,10},{3,11},{4,12},{5,13},{6,14},{7,15},{8,0},{9,1},... | collective-permute-start | bytes 12296 | tf_op jit(solution)/shard_map/ppermute | solution.py:23
  67.9 4.0 %collective-permute-start.16 = (f32[4,256]{1,0:T(4,128)S(1)}, f32[4,256]{1,0:T(4,128)S(1)}, u32[]{:S(2)}, u32[]{:S(2)}) collective-permute-start(f32[4,256]{1,0:T(4,128)S(1)} %add.12), channel_id=1, source_target_pairs={{0,2},{1,3},{2,0},{3,1},{4,6},{5,7},{6,4},{7,5},{8,10},{9,11},{10,... | collective-permute-start | bytes 12296 | tf_op jit(solution)/shard_map/ppermute | solution.py:23
  71.9 6.9 %collective-permute-start.19 = (bf16[512,256]{1,0:T(8,128)(2,1)S(1)}, bf16[512,256]{1,0:T(8,128)(2,1)S(1)}, u32[]{:S(2)}, u32[]{:S(2)}) collective-permute-start(bf16[512,256]{1,0:T(8,128)(2,1)S(1)} %get-tuple-element.111), channel_id=1, source_target_pairs={{1,0},{2,1},{3,2},{4,3},{5,4},{6,5},{7,6},{8,7},{9,8},{10,9},{11,1... | collective-permute-start | bytes 786440 | tf_op jit(solution)/shard_map/ppermute | solution.py:19
  71.9 5.7 %collective-permute-start.17 = (f32[4,256]{1,0:T(4,128)S(1)}, f32[4,256]{1,0:T(4,128)S(1)}, u32[]{:S(2)}, u32[]{:S(2)}) collective-permute-start(f32[4,256]{1,0:T(4,128)S(1)} %add.13), channel_id=1, source_target_pairs={{0,4},{1,5},{2,6},{3,7},{4,0},{5,1},{6,2},{7,3},{8,12},{9,13},{10,... | collective-permute-start | bytes 12296 | tf_op jit(solution)/shard_map/ppermute | solution.py:23
  77.6 1.2 %collective-permute-start.18 = (f32[4,256]{1,0:T(4,128)S(1)}, f32[4,256]{1,0:T(4,128)S(1)}, u32[]{:S(2)}, u32[]{:S(2)}) collective-permute-start(f32[4,256]{1,0:T(4,128)S(1)} %add.14), channel_id=1, source_target_pairs={{0,1},{1,0},{2,3},{3,2},{4,5},{5,4},{6,7},{7,6},{8,9},{9,8},{10,11... | collective-permute-start | bytes 12296 | tf_op jit(solution)/shard_map/ppermute | solution.py:23

commit v10 on v9

--- a/solution.py
+++ b/solution.py
@@ -476,15 +476,16 @@
         bind(schur_load), [(faces, F32)] + halves + [sum_rows],
         z_local, schur, basis_high, basis_low, z_coarse, sums,
     )
-    half = gather_half(shares_rounded, early[:1])
+    half = gather_half(shares_rounded, early[:1], far)
     near, far = after((near, far), half)
     far, near = far_block(far), crossed(near, 1)
+    half = gather_half(half, early[1:])
+    part = after(part, half)
     image, part, near, far = stage(
         bind(neumann_image), [(own, F32), (faces, F32)] + halves, part, near, far, weight, message, neumann
     )
-    half = gather_half(half, early[1:], far)
     far, near = far_block(far), crossed(near, 1)
-    half = gather_half(half, late, near, far)
+    half = gather_half(half, late, near)
     crossed_half = crossed(half, 1)
     part = after(part, half)
     y_local, product, quadratic, base = stage(
@@ -498,7 +499,7 @@
     z, y = stage(bind(complete), [(own, F32), (own, F32)], z_local, z_coarse, y_local, y_coarse, rows)
     for k, bit in enumerate(steps):
         sums = sums + after(crossed(sums, bit), y)
-        if k == len(early) - 1:
+        if k == len(steps) - 2:
             back = shifted(after(back, sums), -1)
     return stage(bind(combine), [(own, F32), (own, F32)], sums, load, z, y, image, part, back)
 

time: 80.6 us -> 88.8 us (1.10)
  waiting for transfers between devices: 33.5 us -> 45.7 us
  starting transfers between devices: 23.3 us -> 19.1 us
    ppermute x15, waiting for transfers between devices: 20.9 us -> 31 us  [crossed(): lax.ppermute(block, AXIS, [(i, i ^ bit) for i in range(lax.axis_size(AXIS...]
    ppermute x15, starting transfers between devices: 18.9 us -> 15.3 us  [crossed(): lax.ppermute(block, AXIS, [(i, i ^ bit) for i in range(lax.axis_size(AXIS...]
    ppermute x2, waiting for transfers between devices: 0.01 us -> 2.35 us  [shifted(): lax.ppermute(block, AXIS, [((i - distance) % n, i) for i in range(n)])]
  transfers between devices with their start and end apart: 20 -> 20, of which waited for: 10 -> 11; matrix products, arithmetic and copies ran while one was open for 0% -> 0% of each run, Pallas kernels for 20% -> 17%
where the time goes in v10:
time: 88.8 us; the launch traced here: 88.5 us
  waiting for transfers between devices  45.7 us (51%)
  Pallas kernels  22.7 us (26%)
  starting transfers between devices  19.1 us (22%)
    ppermute x15, waiting for transfers between devices, crossed(): lax.ppermute(block, AXIS, [(i, i ^ bit) for i in range(lax.axis_size(AXIS...  31 us
    pallas_call x12, Pallas kernels, stage(): return call(*operands)  22.7 us
    ppermute x15, starting transfers between devices, crossed(): lax.ppermute(block, AXIS, [(i, i ^ bit) for i in range(lax.axis_size(AXIS...  15.3 us
    ppermute x3, waiting for transfers between devices, far_block(): lax.ppermute(block, AXIS, [(i, (i + (1 if i % 2 else -1)) % n) for i in r...  12.4 us
    ppermute x3, starting transfers between devices, far_block(): lax.ppermute(block, AXIS, [(i, (i + (1 if i % 2 else -1)) % n) for i in r...  3.81 us
    ppermute x2, waiting for transfers between devices, shifted(): lax.ppermute(block, AXIS, [((i - distance) % n, i) for i in range(n)])  2.35 us
  transfers between devices with their start and end apart: 20, of which 11 were waited for; matrix products, arithmetic and copies ran while one was open for 0% of the time, Pallas kernels for 17%

profile of v10, /device:TPU:0, one launch (start us, length us, event | category | flops | bytes accessed | tf_op | source)
XLA Modules:
  0.0 88.5 jit_solution(5279314751652811822)
XLA Ops:
  0.6 1.5 %prepare.1 = (f32[1024,256]{1,0:T(8,128)S(1)}, bf16[64,512]{1,0:T(8,128)(2,1)S(1)}, f32[2,512]{1,0:T(2,128)S(1)}, bf16[64,1024]{1,0:T(8,128)(2,1)S(1)}, bf16[64,...) custom-call(f32[1024,256]{1,0:T(8,128)} %load.1, bf16[64,512]{1,0:T(8,128)(2,1)} %rows.1, f32[2,512]{1,0:T(2,128)} %weight.1, ...), custom_call_target="tpu_custom_call" | custom-call | tf_op jit(solution)/shard_map/prepare/pallas_call | solution.py:161
  2.2 4.1 %collective-permute-start = (bf16[64,256]{1,0:T(8,128)(2,1)S(1)}, bf16[64,256]{1,0:T(8,128)(2,1)S(1)}, u32[]{:S(2)}, u32[]{:S(2)}) collective-permute-start(bf16[64,256]{1,0:T(8,128)(2,1)S(1)} %get-tuple-element.62), channel_id=1, source_target_pairs={{0,8},{1,9},{2,10},{3,11},{4,12},{5,13},{6,14},{7,15},{8,0},{9,1},... | collective-permute-start | bytes 98312 | tf_op jit(solution)/shard_map/ppermute | solution.py:23
  6.3 0.3 halo_message.1
  6.5 2.0 %collective-permute-done = bf16[64,256]{1,0:T(8,128)(2,1)S(1)} collective-permute-done((bf16[64,256]{1,0:T(8,128)(2,1)S(1)}, bf16[64,256]{1,0:T(8,128)(2,1)S(1)}, u32[]{:S(2)}, u32[]{:S(2)}) %collective-permute-start) | collective-permute-done | bytes 32800 | tf_op jit(solution)/shard_map/ppermute | solution.py:23
  8.5 0.0 collective-permute-start.1
  8.5 1.8 %collective-permute-start.4 = (bf16[128,256]{1,0:T(8,128)(2,1)S(1)}, bf16[128,256]{1,0:T(8,128)(2,1)S(1)}, u32[]{:S(2)}, u32[]{:S(2)}) collective-permute-start(bf16[128,256]{1,0:T(8,128)(2,1)S(1)} %pad_maximum_fusion.4), channel_id=1, source_target_pairs={{0,2},{1,3},{2,0},{3,1},{4,6},{5,7},{6,4},{7,5},{8,10},{9,11},{10,... | collective-permute-start | bytes 196616 | tf_op jit(solution)/shard_map/ppermute | solution.py:23
  10.3 3.5 %fetch.1 = (bf16[2048,1024]{1,0:T(8,128)(2,1)S(1)}, bf16[2048,1024]{1,0:T(8,128)(2,1)S(1)}) custom-call(bf16[2048,1024]{1,0:T(8,128)(2,1)} %neumann, bf16[2048,1024]{1,0:T(8,128)(2,1)} %schur), custom_call_target="tpu_custom_call" | custom-call | tf_op jit(solution)/shard_map/fetch/pallas_call | solution.py:161
  13.8 0.0 collective-permute-done.4
  13.8 5.0 %collective-permute-start.5 = (bf16[256,256]{1,0:T(8,128)(2,1)S(1)}, bf16[256,256]{1,0:T(8,128)(2,1)S(1)}, u32[]{:S(2)}, u32[]{:S(2)}) collective-permute-start(bf16[256,256]{1,0:T(8,128)(2,1)S(1)} %pad_maximum_fusion.3), channel_id=1, source_target_pairs={{0,4},{1,5},{2,6},{3,7},{4,0},{5,1},{6,2},{7,3},{8,12},{9,13},{10,... | collective-permute-start | bytes 393224 | tf_op jit(solution)/shard_map/ppermute | solution.py:23
  18.8 1.5 %neumann_load.1 = (f32[1536,256]{1,0:T(8,128)S(1)}, bf16[512,256]{1,0:T(8,128)(2,1)S(1)}, bf16[512,256]{1,0:T(8,128)(2,1)S(1)}) custom-call(f32[1024,256]{1,0:T(8,128)S(1)} %get-tuple-element.58.load, f32[2,512]{1,0:T(2,128)S(1)} %get-tuple-element.59.weight, bf16[720,256]{1,0:T(8,128)(2,1)S(1)} %collective-permute-done.1.message, ...), custom_call_target="tpu_custom_call" | custom-call | tf_op jit(solution)/shard_map/neumann_load/pallas_call | solution.py:161
  20.3 0.1 collective-permute-start.2
  20.4 2.4 %collective-permute-start.3 = (bf16[512,256]{1,0:T(8,128)(2,1)S(1)}, bf16[512,256]{1,0:T(8,128)(2,1)S(1)}, u32[]{:S(2)}, u32[]{:S(2)}) collective-permute-start(bf16[512,256]{1,0:T(8,128)(2,1)S(1)} %get-tuple-element.69), channel_id=1, source_target_pairs={{0,15},{1,2},{2,1},{3,4},{4,3},{5,6},{6,5},{7,8},{8,7},{9,10},{10,... | collective-permute-start | bytes 786440 | tf_op jit(solution)/shard_map/ppermute | solution.py:28
  22.8 1.9 %static_basis.1 = (bf16[2048,64]{1,0:T(8,128)(2,1)S(1)}, bf16[2048,64]{1,0:T(8,128)(2,1)S(1)}, bf16[128,1024]{1,0:T(8,128)(2,1)S(1)}, bf16[128,1024]{1,0:T(8,128)(2,1)S(1)}, f32[128,128]{1,0:T(8,128)S(1)}) custom-call(bf16[2048,1024]{1,0:T(8,128)(2,1)S(1)} %get-tuple-element.70.schur, bf16[720,256]{1,0:T(8,128)(2,1)S(1)} %collective-permute-done.1.message, ...), custom_call_target="tpu_custom_call" | custom-call | tf_op jit(solution)/shard_map/static_basis/pallas_call | solution.py:161
  24.7 0.0 collective-permute-done.5
  24.8 0.1 collective-permute-start.6
  24.8 0.0 collective-permute-done.2.near
  24.9 4.2 %collective-permute-done.3.far = bf16[512,256]{1,0:T(8,128)(2,1)S(1)} collective-permute-done((bf16[512,256]{1,0:T(8,128)(2,1)S(1)}, bf16[512,256]{1,0:T(8,128)(2,1)S(1)}, u32[]{:S(2)}, u32[]{:S(2)}) %collective-permute-start.3) | collective-permute-done | bytes 262176 | tf_op jit(solution)/shard_map/ppermute | solution.py:28
  29.1 0.0 collective-permute-done.6.crossed_half
  29.1 1.6 %coarse_load.1 = (f32[1536,256]{1,0:T(8,128)S(1)}, bf16[96,256]{1,0:T(8,128)(2,1)S(1)}, f32[96,256]{1,0:T(8,128)S(1)}, f32[96,256]{1,0:T(8,128)S(1)}, f32[8,256]{1,0:T(8,128)S(1)}) custom-call(f32[1024,256]{1,0:T(8,128)S(1)} %get-tuple-element.58.load, f32[1536,256]{1,0:T(8,128)S(1)} %get-tuple-element.67.part, ...), custom_call_target="tpu_custom_call" | custom-call | tf_op jit(solution)/shard_map/coarse_load/pallas_call | solution.py:161
  30.7 1.1 %collective-permute-start.7 = (bf16[96,256]{1,0:T(8,128)(2,1)S(1)}, bf16[96,256]{1,0:T(8,128)(2,1)S(1)}, u32[]{:S(2)}, u32[]{:S(2)}) collective-permute-start(bf16[96,256]{1,0:T(8,128)(2,1)S(1)} %get-tuple-element.78), channel_id=1, source_target_pairs={{0,8},{1,9},{2,10},{3,11},{4,12},{5,13},{6,14},{7,15},{8,0},{9,1},... | collective-permute-start | bytes 147464 | tf_op jit(solution)/shard_map/ppermute | solution.py:23
  31.8 3.3 %schur_load.1 = (f32[1536,256]{1,0:T(8,128)S(1)}, bf16[512,256]{1,0:T(8,128)(2,1)S(1)}, bf16[512,256]{1,0:T(8,128)(2,1)S(1)}, f32[8,256]{1,0:T(8,128)S(1)}) custom-call(f32[1536,256]{1,0:T(8,128)S(1)} %get-tuple-element.79.local.z_local, bf16[2048,1024]{1,0:T(8,128)(2,1)S(1)} %get-tuple-element.70.schur, bf16[2048,64]{1,0:T(8,128)(2,1)S(1)} %get-tuple-element.80.basis_high, ...), custom_call_target="tpu_custom_call" | custom-call | tf_op jit(solution)/shard_map/schur_load/pallas_call | solution.py:161
  35.1 1.1 %collective-permute-done.7 = bf16[96,256]{1,0:T(8,128)(2,1)S(1)} collective-permute-done((bf16[96,256]{1,0:T(8,128)(2,1)S(1)}, bf16[96,256]{1,0:T(8,128)(2,1)S(1)}, u32[]{:S(2)}, u32[]{:S(2)}) %collective-permute-start.7) | collective-permute-done | bytes 49184 | tf_op jit(solution)/shard_map/ppermute | solution.py:23
  36.1 1.0 %collective-permute-start.10 = (bf16[512,256]{1,0:T(8,128)(2,1)S(1)}, bf16[512,256]{1,0:T(8,128)(2,1)S(1)}, u32[]{:S(2)}, u32[]{:S(2)}) collective-permute-start(bf16[512,256]{1,0:T(8,128)(2,1)S(1)} %get-tuple-element.89), channel_id=1, source_target_pairs={{0,1},{1,0},{2,3},{3,2},{4,5},{5,4},{6,7},{7,6},{8,9},{9,8},{10,11... | collective-permute-start | bytes 786440 | tf_op jit(solution)/shard_map/ppermute | solution.py:23
  37.1 0.9 %collective-permute-start.11 = (bf16[512,256]{1,0:T(8,128)(2,1)S(1)}, bf16[512,256]{1,0:T(8,128)(2,1)S(1)}, u32[]{:S(2)}, u32[]{:S(2)}) collective-permute-start(bf16[512,256]{1,0:T(8,128)(2,1)S(1)} %get-tuple-element.90), channel_id=1, source_target_pairs={{0,15},{1,2},{2,1},{3,4},{4,3},{5,6},{6,5},{7,8},{8,7},{9,10},{10,... | collective-permute-start | bytes 786440 | tf_op jit(solution)/shard_map/ppermute | solution.py:28
  38.0 0.8 collective-permute-start.8
  38.8 9.3 %collective-permute-done.8 = bf16[192,256]{1,0:T(8,128)(2,1)S(1)} collective-permute-done((bf16[192,256]{1,0:T(8,128)(2,1)S(1)}, bf16[192,256]{1,0:T(8,128)(2,1)S(1)}, u32[]{:S(2)}, u32[]{:S(2)}) %collective-permute-start.8) | collective-permute-done | bytes 98336 | tf_op jit(solution)/shard_map/ppermute | solution.py:23
  48.1 0.0 collective-permute-done.10.near_in
  48.1 1.6 %neumann_image.1 = (f32[1024,256]{1,0:T(8,128)S(1)}, f32[1536,256]{1,0:T(8,128)S(1)}, bf16[512,256]{1,0:T(8,128)(2,1)S(1)}, bf16[512,256]{1,0:T(8,128)(2,1)S(1)}) custom-call(f32[1536,256]{1,0:T(8,128)S(1)} %get-tuple-element.87.part_in, bf16[512,256]{1,0:T(8,128)(2,1)S(1)} %collective-permute-done.10.near_in, ...), custom_call_target="tpu_custom_call" | custom-call | tf_op jit(solution)/shard_map/neumann_image/pallas_call | solution.py:161
  49.7 0.1 collective-permute-start.12
  49.8 0.3 collective-permute-start.9
  50.1 7.0 %collective-permute-done.9 = bf16[384,256]{1,0:T(8,128)(2,1)S(1)} collective-permute-done((bf16[384,256]{1,0:T(8,128)(2,1)S(1)}, bf16[384,256]{1,0:T(8,128)(2,1)S(1)}, u32[]{:S(2)}, u32[]{:S(2)}) %collective-permute-start.9) | collective-permute-done | bytes 196640 | tf_op jit(solution)/shard_map/ppermute | solution.py:23
  57.1 0.1 collective-permute-start.13
  57.2 0.5 collective-permute-start.14
  57.7 8.1 %collective-permute-done.14.far = bf16[512,256]{1,0:T(8,128)(2,1)S(1)} collective-permute-done((bf16[512,256]{1,0:T(8,128)(2,1)S(1)}, bf16[512,256]{1,0:T(8,128)(2,1)S(1)}, u32[]{:S(2)}, u32[]{:S(2)}) %collective-permute-start.14) | collective-permute-done | bytes 262176 | tf_op jit(solution)/shard_map/ppermute | solution.py:28
  65.9 3.6 %schur_image.1 = (f32[1536,256]{1,0:T(8,128)S(1)}, f32[1536,256]{1,0:T(8,128)S(1)}, f32[8,256]{1,0:T(8,128)S(1)}, f32[128,256]{1,0:T(8,128)S(1)}) custom-call(f32[1024,256]{1,0:T(8,128)S(1)} %get-tuple-element.94.image, f32[1536,256]{1,0:T(8,128)S(1)} %get-tuple-element.96.part, bf16[512,256]{1,0:T(8,128)(2,1)S(1)} %collective-permute-done.12.near, ...), custom_call_target="tpu_custom_call" | custom-call | tf_op jit(solution)/shard_map/schur_image/pallas_call | solution.py:161
  69.5 1.7 %coarse_image.1 = (f32[4,256]{1,0:T(4,128)S(1)}, f32[64,256]{1,0:T(8,128)S(1)}, f32[1024,256]{1,0:T(8,128)S(1)}, bf16[512,256]{1,0:T(8,128)(2,1)S(1)}) custom-call(bf16[768,256]{1,0:T(8,128)(2,1)S(1)} %pad_maximum_fusion.half, bf16[768,256]{1,0:T(8,128)(2,1)S(1)} %collective-permute-done.13.crossed_half, bf16[64,1024]{1,0:T(8,128)(2,1)S(1)} %get-tuple-element.61.inverse, ...), custom_call_target="tpu_custom_call" | custom-call | tf_op jit(solution)/shard_map/coarse_image/pallas_call | solution.py:161
  71.2 0.1 collective-permute-start.15
  71.2 0.7 complete.1
  72.0 3.8 %collective-permute-done.15 = f32[4,256]{1,0:T(4,128)S(1)} collective-permute-done((f32[4,256]{1,0:T(4,128)S(1)}, f32[4,256]{1,0:T(4,128)S(1)}, u32[]{:S(2)}, u32[]{:S(2)}) %collective-permute-start.15) | collective-permute-done | bytes 4128 | tf_op jit(solution)/shard_map/ppermute | solution.py:23
  75.7 0.3 collective-permute-start.16
  76.1 3.3 %collective-permute-done.16 = f32[4,256]{1,0:T(4,128)S(1)} collective-permute-done((f32[4,256]{1,0:T(4,128)S(1)}, f32[4,256]{1,0:T(4,128)S(1)}, u32[]{:S(2)}, u32[]{:S(2)}) %collective-permute-start.16) | collective-permute-done | bytes 4128 | tf_op jit(solution)/shard_map/ppermute | solution.py:23
  79.3 0.0 collective-permute-start.17
  79.4 3.6 %collective-permute-done.17 = f32[4,256]{1,0:T(4,128)S(1)} collective-permute-done((f32[4,256]{1,0:T(4,128)S(1)}, f32[4,256]{1,0:T(4,128)S(1)}, u32[]{:S(2)}, u32[]{:S(2)}) %collective-permute-start.17) | collective-permute-done | bytes 4128 | tf_op jit(solution)/shard_map/ppermute | solution.py:23
  83.0 0.0 collective-permute-start.19
  83.0 0.5 collective-permute-start.18
  83.5 1.0 %collective-permute-done.18 = f32[4,256]{1,0:T(4,128)S(1)} collective-permute-done((f32[4,256]{1,0:T(4,128)S(1)}, f32[4,256]{1,0:T(4,128)S(1)}, u32[]{:S(2)}, u32[]{:S(2)}) %collective-permute-start.18) | collective-permute-done | bytes 4128 | tf_op jit(solution)/shard_map/ppermute | solution.py:23
  84.5 2.3 %collective-permute-done.19.from_next = bf16[512,256]{1,0:T(8,128)(2,1)S(1)} collective-permute-done((bf16[512,256]{1,0:T(8,128)(2,1)S(1)}, bf16[512,256]{1,0:T(8,128)(2,1)S(1)}, u32[]{:S(2)}, u32[]{:S(2)}) %collective-permute-start.19) | collective-permute-done | bytes 262176 | tf_op jit(solution)/shard_map/ppermute | solution.py:19
  86.9 1.7 %combine.1 = (f32[1024,256]{1,0:T(8,128)}, f32[1024,256]{1,0:T(8,128)}) custom-call(f32[4,256]{1,0:T(4,128)S(1)} %add.15.sums, f32[1024,256]{1,0:T(8,128)S(1)} %get-tuple-element.58.load, f32[1024,256]{1,0:T(8,128)S(1)} %get-tuple-element.110.z, f32[1024,256]{1,0:T(8,128)S(1)} %get-tuple-element.105.y, f32[1024,256]{1,0:T(8,128)S(1)} %get-tuple-element.94.image, ...), custom_call_target="tpu_custom_call" | custom-call | tf_op jit(solution)/shard_map/combine/pallas_call | solution.py:161
  (15 shorter events, 0.1 us)
Async XLA Ops:
  2.2 6.3 %collective-permute-start = (bf16[64,256]{1,0:T(8,128)(2,1)S(1)}, bf16[64,256]{1,0:T(8,128)(2,1)S(1)}, u32[]{:S(2)}, u32[]{:S(2)}) collective-permute-start(bf16[64,256]{1,0:T(8,128)(2,1)S(1)} %get-tuple-element.62), channel_id=1, source_target_pairs={{0,8},{1,9},{2,10},{3,11},{4,12},{5,13},{6,14},{7,15},{8,0},{9,1},... | collective-permute-start | bytes 98312 | tf_op jit(solution)/shard_map/ppermute | solution.py:23
  8.5 10.3 %collective-permute-start.1 = (bf16[720,256]{1,0:T(8,128)(2,1)S(1)}, bf16[720,256]{1,0:T(8,128)(2,1)S(1)}, u32[]{:S(2)}, u32[]{:S(2)}) collective-permute-start(bf16[720,256]{1,0:T(8,128)(2,1)S(1)} %halo_message.1), channel_id=1, source_target_pairs={{15,0},{0,1},{1,2},{2,3},{3,4},{4,5},{5,6},{6,7},{7,8},{8,9},{9,10... | collective-permute-start | bytes 1105928 | tf_op jit(solution)/shard_map/ppermute | solution.py:19
  8.5 5.3 %collective-permute-start.4 = (bf16[128,256]{1,0:T(8,128)(2,1)S(1)}, bf16[128,256]{1,0:T(8,128)(2,1)S(1)}, u32[]{:S(2)}, u32[]{:S(2)}) collective-permute-start(bf16[128,256]{1,0:T(8,128)(2,1)S(1)} %pad_maximum_fusion.4), channel_id=1, source_target_pairs={{0,2},{1,3},{2,0},{3,1},{4,6},{5,7},{6,4},{7,5},{8,10},{9,11},{10,... | collective-permute-start | bytes 196616 | tf_op jit(solution)/shard_map/ppermute | solution.py:23
  13.8 10.9 %collective-permute-start.5 = (bf16[256,256]{1,0:T(8,128)(2,1)S(1)}, bf16[256,256]{1,0:T(8,128)(2,1)S(1)}, u32[]{:S(2)}, u32[]{:S(2)}) collective-permute-start(bf16[256,256]{1,0:T(8,128)(2,1)S(1)} %pad_maximum_fusion.3), channel_id=1, source_target_pairs={{0,4},{1,5},{2,6},{3,7},{4,0},{5,1},{6,2},{7,3},{8,12},{9,13},{10,... | collective-permute-start | bytes 393224 | tf_op jit(solution)/shard_map/ppermute | solution.py:23
  20.3 4.5 %collective-permute-start.2 = (bf16[512,256]{1,0:T(8,128)(2,1)S(1)}, bf16[512,256]{1,0:T(8,128)(2,1)S(1)}, u32[]{:S(2)}, u32[]{:S(2)}) collective-permute-start(bf16[512,256]{1,0:T(8,128)(2,1)S(1)} %get-tuple-element.68), channel_id=1, source_target_pairs={{0,1},{1,0},{2,3},{3,2},{4,5},{5,4},{6,7},{7,6},{8,9},{9,8},{10,11... | collective-permute-start | bytes 786440 | tf_op jit(solution)/shard_map/ppermute | solution.py:23
  20.4 8.7 %collective-permute-start.3 = (bf16[512,256]{1,0:T(8,128)(2,1)S(1)}, bf16[512,256]{1,0:T(8,128)(2,1)S(1)}, u32[]{:S(2)}, u32[]{:S(2)}) collective-permute-start(bf16[512,256]{1,0:T(8,128)(2,1)S(1)} %get-tuple-element.69), channel_id=1, source_target_pairs={{0,15},{1,2},{2,1},{3,4},{4,3},{5,6},{6,5},{7,8},{8,7},{9,10},{10,... | collective-permute-start | bytes 786440 | tf_op jit(solution)/shard_map/ppermute | solution.py:28
  24.8 4.3 %collective-permute-start.6 = (bf16[512,256]{1,0:T(8,128)(2,1)S(1)}, bf16[512,256]{1,0:T(8,128)(2,1)S(1)}, u32[]{:S(2)}, u32[]{:S(2)}) collective-permute-start(bf16[512,256]{1,0:T(8,128)(2,1)S(1)} %pad_maximum_fusion.1.half), channel_id=1, source_target_pairs={{0,1},{1,0},{2,3},{3,2},{4,5},{5,4},{6,7},{7,6},{8,9},{9,8},{10,11... | collective-permute-start | bytes 786440 | tf_op jit(solution)/shard_map/ppermute | solution.py:23
  30.7 5.4 %collective-permute-start.7 = (bf16[96,256]{1,0:T(8,128)(2,1)S(1)}, bf16[96,256]{1,0:T(8,128)(2,1)S(1)}, u32[]{:S(2)}, u32[]{:S(2)}) collective-permute-start(bf16[96,256]{1,0:T(8,128)(2,1)S(1)} %get-tuple-element.78), channel_id=1, source_target_pairs={{0,8},{1,9},{2,10},{3,11},{4,12},{5,13},{6,14},{7,15},{8,0},{9,1},... | collective-permute-start | bytes 147464 | tf_op jit(solution)/shard_map/ppermute | solution.py:23
  36.1 12.0 %collective-permute-start.10 = (bf16[512,256]{1,0:T(8,128)(2,1)S(1)}, bf16[512,256]{1,0:T(8,128)(2,1)S(1)}, u32[]{:S(2)}, u32[]{:S(2)}) collective-permute-start(bf16[512,256]{1,0:T(8,128)(2,1)S(1)} %get-tuple-element.89), channel_id=1, source_target_pairs={{0,1},{1,0},{2,3},{3,2},{4,5},{5,4},{6,7},{7,6},{8,9},{9,8},{10,11... | collective-permute-start | bytes 786440 | tf_op jit(solution)/shard_map/ppermute | solution.py:23
  37.1 11.0 %collective-permute-start.11 = (bf16[512,256]{1,0:T(8,128)(2,1)S(1)}, bf16[512,256]{1,0:T(8,128)(2,1)S(1)}, u32[]{:S(2)}, u32[]{:S(2)}) collective-permute-start(bf16[512,256]{1,0:T(8,128)(2,1)S(1)} %get-tuple-element.90), channel_id=1, source_target_pairs={{0,15},{1,2},{2,1},{3,4},{4,3},{5,6},{6,5},{7,8},{8,7},{9,10},{10,... | collective-permute-start | bytes 786440 | tf_op jit(solution)/shard_map/ppermute | solution.py:28
  38.0 10.1 %collective-permute-start.8 = (bf16[192,256]{1,0:T(8,128)(2,1)S(1)}, bf16[192,256]{1,0:T(8,128)(2,1)S(1)}, u32[]{:S(2)}, u32[]{:S(2)}) collective-permute-start(bf16[192,256]{1,0:T(8,128)(2,1)S(1)} %constant_dynamic-update-slice_fusion), channel_id=1, source_target_pairs={{0,2},{1,3},{2,0},{3,1},{4,6},{5,7},{6,4},{7,5},{8,10},{9,11},{10,... | collective-permute-start | bytes 294920 | tf_op jit(solution)/shard_map/ppermute | solution.py:23
  49.7 7.4 %collective-permute-start.12 = (bf16[512,256]{1,0:T(8,128)(2,1)S(1)}, bf16[512,256]{1,0:T(8,128)(2,1)S(1)}, u32[]{:S(2)}, u32[]{:S(2)}) collective-permute-start(bf16[512,256]{1,0:T(8,128)(2,1)S(1)} %get-tuple-element.91), channel_id=1, source_target_pairs={{0,1},{1,0},{2,3},{3,2},{4,5},{5,4},{6,7},{7,6},{8,9},{9,8},{10,11... | collective-permute-start | bytes 786440 | tf_op jit(solution)/shard_map/ppermute | solution.py:23
  49.8 7.3 %collective-permute-start.9 = (bf16[384,256]{1,0:T(8,128)(2,1)S(1)}, bf16[384,256]{1,0:T(8,128)(2,1)S(1)}, u32[]{:S(2)}, u32[]{:S(2)}) collective-permute-start(bf16[384,256]{1,0:T(8,128)(2,1)S(1)} %pad_maximum_fusion.2), channel_id=1, source_target_pairs={{0,4},{1,5},{2,6},{3,7},{4,0},{5,1},{6,2},{7,3},{8,12},{9,13},{10,... | collective-permute-start | bytes 589832 | tf_op jit(solution)/shard_map/ppermute | solution.py:23
  57.1 12.3 %collective-permute-start.13 = (bf16[768,256]{1,0:T(8,128)(2,1)S(1)}, bf16[768,256]{1,0:T(8,128)(2,1)S(1)}, u32[]{:S(2)}, u32[]{:S(2)}) collective-permute-start(bf16[768,256]{1,0:T(8,128)(2,1)S(1)} %pad_maximum_fusion.half), channel_id=1, source_target_pairs={{0,1},{1,0},{2,3},{3,2},{4,5},{5,4},{6,7},{7,6},{8,9},{9,8},{10,11... | collective-permute-start | bytes 1179656 | tf_op jit(solution)/shard_map/ppermute | solution.py:23
  57.2 8.7 %collective-permute-start.14 = (bf16[512,256]{1,0:T(8,128)(2,1)S(1)}, bf16[512,256]{1,0:T(8,128)(2,1)S(1)}, u32[]{:S(2)}, u32[]{:S(2)}) collective-permute-start(bf16[512,256]{1,0:T(8,128)(2,1)S(1)} %get-tuple-element.97), channel_id=1, source_target_pairs={{0,15},{1,2},{2,1},{3,4},{4,3},{5,6},{6,5},{7,8},{8,7},{9,10},{10,... | collective-permute-start | bytes 786440 | tf_op jit(solution)/shard_map/ppermute | solution.py:28
  71.2 4.6 %collective-permute-start.15 = (f32[4,256]{1,0:T(4,128)S(1)}, f32[4,256]{1,0:T(4,128)S(1)}, u32[]{:S(2)}, u32[]{:S(2)}) collective-permute-start(f32[4,256]{1,0:T(4,128)S(1)} %get-tuple-element.102), channel_id=1, source_target_pairs={{0,8},{1,9},{2,10},{3,11},{4,12},{5,13},{6,14},{7,15},{8,0},{9,1},... | collective-permute-start | bytes 12296 | tf_op jit(solution)/shard_map/ppermute | solution.py:23
  75.7 3.6 %collective-permute-start.16 = (f32[4,256]{1,0:T(4,128)S(1)}, f32[4,256]{1,0:T(4,128)S(1)}, u32[]{:S(2)}, u32[]{:S(2)}) collective-permute-start(f32[4,256]{1,0:T(4,128)S(1)} %add.12), channel_id=1, source_target_pairs={{0,2},{1,3},{2,0},{3,1},{4,6},{5,7},{6,4},{7,5},{8,10},{9,11},{10,... | collective-permute-start | bytes 12296 | tf_op jit(solution)/shard_map/ppermute | solution.py:23
  79.3 3.6 %collective-permute-start.17 = (f32[4,256]{1,0:T(4,128)S(1)}, f32[4,256]{1,0:T(4,128)S(1)}, u32[]{:S(2)}, u32[]{:S(2)}) collective-permute-start(f32[4,256]{1,0:T(4,128)S(1)} %add.13), channel_id=1, source_target_pairs={{0,4},{1,5},{2,6},{3,7},{4,0},{5,1},{6,2},{7,3},{8,12},{9,13},{10,... | collective-permute-start | bytes 12296 | tf_op jit(solution)/shard_map/ppermute | solution.py:23
  83.0 3.9 %collective-permute-start.19 = (bf16[512,256]{1,0:T(8,128)(2,1)S(1)}, bf16[512,256]{1,0:T(8,128)(2,1)S(1)}, u32[]{:S(2)}, u32[]{:S(2)}) collective-permute-start(bf16[512,256]{1,0:T(8,128)(2,1)S(1)} %get-tuple-element.113), channel_id=1, source_target_pairs={{1,0},{2,1},{3,2},{4,3},{5,4},{6,5},{7,6},{8,7},{9,8},{10,9},{11,1... | collective-permute-start | bytes 786440 | tf_op jit(solution)/shard_map/ppermute | solution.py:19
  83.0 1.5 %collective-permute-start.18 = (f32[4,256]{1,0:T(4,128)S(1)}, f32[4,256]{1,0:T(4,128)S(1)}, u32[]{:S(2)}, u32[]{:S(2)}) collective-permute-start(f32[4,256]{1,0:T(4,128)S(1)} %add.14), channel_id=1, source_target_pairs={{0,1},{1,0},{2,3},{3,2},{4,5},{5,4},{6,7},{7,6},{8,9},{9,8},{10,11... | collective-permute-start | bytes 12296 | tf_op jit(solution)/shard_map/ppermute | solution.py:23

commit v11 on v9

--- a/solution.py
+++ b/solution.py
@@ -472,21 +472,21 @@
         load, part, near, far, weight, message, turned_high, turned_low, half, crossed_half, inverse, coarse, gram,
         scratch=[pltpu.VMEM((local_rows, columns), F32), pltpu.VMEM((nco, columns), BF16)],
     )
+    half = gather_half(shares_rounded, early[:1])
     part, near, far, sums = stage(
         bind(schur_load), [(faces, F32)] + halves + [sum_rows],
-        z_local, schur, basis_high, basis_low, z_coarse, sums,
-    )
-    half = gather_half(shares_rounded, early[:1])
+        after(z_local, half), schur, basis_high, basis_low, z_coarse, sums,
+    )
+    half = gather_half(half, early[1:], far)
     near, far = after((near, far), half)
     far, near = far_block(far), crossed(near, 1)
+    half = gather_half(half, late)
+    part = after(part, half)
     image, part, near, far = stage(
         bind(neumann_image), [(own, F32), (faces, F32)] + halves, part, near, far, weight, message, neumann
     )
-    half = gather_half(half, early[1:], far)
+    crossed_half = crossed(half, 1)
     far, near = far_block(far), crossed(near, 1)
-    half = gather_half(half, late, near, far)
-    crossed_half = crossed(half, 1)
-    part = after(part, half)
     y_local, product, quadratic, base = stage(
         bind(schur_image), products, image, part, near, far, weight, message, schur, turned_high, turned_low
     )

time: 80.6 us -> 82.2 us (1.020)
  waiting for transfers between devices: 33.5 us -> 36.4 us
  starting transfers between devices: 23.3 us -> 22 us
    ppermute x15, starting transfers between devices: 18.9 us -> 13.7 us  [crossed(): lax.ppermute(block, AXIS, [(i, i ^ bit) for i in range(lax.axis_size(AXIS...]
    ppermute x3, starting transfers between devices: 4.39 us -> 8.33 us  [far_block(): lax.ppermute(block, AXIS, [(i, (i + (1 if i % 2 else -1)) % n) for i in r...]
    ppermute x3, waiting for transfers between devices: 12.6 us -> 15.5 us  [far_block(): lax.ppermute(block, AXIS, [(i, (i + (1 if i % 2 else -1)) % n) for i in r...]
  transfers between devices with their start and end apart: 20 -> 20, of which waited for: 10 -> 11; matrix products, arithmetic and copies ran while one was open for 0% -> 0% of each run, Pallas kernels for 20% -> 20%
where the time goes in v11:
time: 82.2 us; the launch traced here: 82 us
  waiting for transfers between devices  36.4 us (44%)
  Pallas kernels  22.7 us (28%)
  starting transfers between devices  22 us (27%)
  between operations  0.85 us (1%)
    pallas_call x12, Pallas kernels, stage(): return call(*operands)  22.7 us
    ppermute x15, waiting for transfers between devices, crossed(): lax.ppermute(block, AXIS, [(i, i ^ bit) for i in range(lax.axis_size(AXIS...  20.9 us
    ppermute x3, waiting for transfers between devices, far_block(): lax.ppermute(block, AXIS, [(i, (i + (1 if i % 2 else -1)) % n) for i in r...  15.5 us
    ppermute x15, starting transfers between devices, crossed(): lax.ppermute(block, AXIS, [(i, i ^ bit) for i in range(lax.axis_size(AXIS...  13.7 us
    ppermute x3, starting transfers between devices, far_block(): lax.ppermute(block, AXIS, [(i, (i + (1 if i % 2 else -1)) % n) for i in r...  8.33 us
  transfers between devices with their start and end apart: 20, of which 11 were waited for; matrix products, arithmetic and copies ran while one was open for 0% of the time, Pallas kernels for 20%

profile of v11, /device:TPU:0, one launch (start us, length us, event | category | flops | bytes accessed | tf_op | source)
XLA Modules:
  0.0 82.0 jit_solution(13581329093839931755)
XLA Ops:
  0.6 1.5 %prepare.1 = (f32[1024,256]{1,0:T(8,128)S(1)}, bf16[64,512]{1,0:T(8,128)(2,1)S(1)}, f32[2,512]{1,0:T(2,128)S(1)}, bf16[64,1024]{1,0:T(8,128)(2,1)S(1)}, bf16[64,...) custom-call(f32[1024,256]{1,0:T(8,128)} %load.1, bf16[64,512]{1,0:T(8,128)(2,1)} %rows.1, f32[2,512]{1,0:T(2,128)} %weight.1, ...), custom_call_target="tpu_custom_call" | custom-call | tf_op jit(solution)/shard_map/prepare/pallas_call | solution.py:161
  2.1 4.1 %collective-permute-start = (bf16[64,256]{1,0:T(8,128)(2,1)S(1)}, bf16[64,256]{1,0:T(8,128)(2,1)S(1)}, u32[]{:S(2)}, u32[]{:S(2)}) collective-permute-start(bf16[64,256]{1,0:T(8,128)(2,1)S(1)} %get-tuple-element.61), channel_id=1, source_target_pairs={{0,8},{1,9},{2,10},{3,11},{4,12},{5,13},{6,14},{7,15},{8,0},{9,1},... | collective-permute-start | bytes 98312 | tf_op jit(solution)/shard_map/ppermute | solution.py:23
  6.3 0.3 halo_message.1
  6.5 2.0 %collective-permute-done = bf16[64,256]{1,0:T(8,128)(2,1)S(1)} collective-permute-done((bf16[64,256]{1,0:T(8,128)(2,1)S(1)}, bf16[64,256]{1,0:T(8,128)(2,1)S(1)}, u32[]{:S(2)}, u32[]{:S(2)}) %collective-permute-start) | collective-permute-done | bytes 32800 | tf_op jit(solution)/shard_map/ppermute | solution.py:23
  8.5 0.0 collective-permute-start.1
  8.5 1.8 %collective-permute-start.4 = (bf16[128,256]{1,0:T(8,128)(2,1)S(1)}, bf16[128,256]{1,0:T(8,128)(2,1)S(1)}, u32[]{:S(2)}, u32[]{:S(2)}) collective-permute-start(bf16[128,256]{1,0:T(8,128)(2,1)S(1)} %pad_maximum_fusion.5), channel_id=1, source_target_pairs={{0,2},{1,3},{2,0},{3,1},{4,6},{5,7},{6,4},{7,5},{8,10},{9,11},{10,... | collective-permute-start | bytes 196616 | tf_op jit(solution)/shard_map/ppermute | solution.py:23
  10.3 3.5 %fetch.1 = (bf16[2048,1024]{1,0:T(8,128)(2,1)S(1)}, bf16[2048,1024]{1,0:T(8,128)(2,1)S(1)}) custom-call(bf16[2048,1024]{1,0:T(8,128)(2,1)} %neumann, bf16[2048,1024]{1,0:T(8,128)(2,1)} %schur), custom_call_target="tpu_custom_call" | custom-call | tf_op jit(solution)/shard_map/fetch/pallas_call | solution.py:161
  13.8 0.0 collective-permute-done.4
  13.8 5.0 %collective-permute-start.5 = (bf16[256,256]{1,0:T(8,128)(2,1)S(1)}, bf16[256,256]{1,0:T(8,128)(2,1)S(1)}, u32[]{:S(2)}, u32[]{:S(2)}) collective-permute-start(bf16[256,256]{1,0:T(8,128)(2,1)S(1)} %pad_maximum_fusion.3), channel_id=1, source_target_pairs={{0,4},{1,5},{2,6},{3,7},{4,0},{5,1},{6,2},{7,3},{8,12},{9,13},{10,... | collective-permute-start | bytes 393224 | tf_op jit(solution)/shard_map/ppermute | solution.py:23
  18.8 0.0 collective-permute-done.1.message
  18.8 1.5 %neumann_load.1 = (f32[1536,256]{1,0:T(8,128)S(1)}, bf16[512,256]{1,0:T(8,128)(2,1)S(1)}, bf16[512,256]{1,0:T(8,128)(2,1)S(1)}) custom-call(f32[1024,256]{1,0:T(8,128)S(1)} %get-tuple-element.57.load, f32[2,512]{1,0:T(2,128)S(1)} %get-tuple-element.58.weight, bf16[720,256]{1,0:T(8,128)(2,1)S(1)} %collective-permute-done.1.message, ...), custom_call_target="tpu_custom_call" | custom-call | tf_op jit(solution)/shard_map/neumann_load/pallas_call | solution.py:161
  20.3 0.1 collective-permute-start.2
  20.4 2.4 %collective-permute-start.3 = (bf16[512,256]{1,0:T(8,128)(2,1)S(1)}, bf16[512,256]{1,0:T(8,128)(2,1)S(1)}, u32[]{:S(2)}, u32[]{:S(2)}) collective-permute-start(bf16[512,256]{1,0:T(8,128)(2,1)S(1)} %get-tuple-element.68), channel_id=1, source_target_pairs={{0,15},{1,2},{2,1},{3,4},{4,3},{5,6},{6,5},{7,8},{8,7},{9,10},{10,... | collective-permute-start | bytes 786440 | tf_op jit(solution)/shard_map/ppermute | solution.py:28
  22.8 1.9 %static_basis.1 = (bf16[2048,64]{1,0:T(8,128)(2,1)S(1)}, bf16[2048,64]{1,0:T(8,128)(2,1)S(1)}, bf16[128,1024]{1,0:T(8,128)(2,1)S(1)}, bf16[128,1024]{1,0:T(8,128)(2,1)S(1)}, f32[128,128]{1,0:T(8,128)S(1)}) custom-call(bf16[2048,1024]{1,0:T(8,128)(2,1)S(1)} %get-tuple-element.69.schur, bf16[720,256]{1,0:T(8,128)(2,1)S(1)} %collective-permute-done.1.message, ...), custom_call_target="tpu_custom_call" | custom-call | tf_op jit(solution)/shard_map/static_basis/pallas_call | solution.py:161
  24.7 0.0 collective-permute-done.5
  24.8 0.1 collective-permute-start.6
  24.8 0.0 collective-permute-done.2.near
  24.9 4.2 %collective-permute-done.3.far = bf16[512,256]{1,0:T(8,128)(2,1)S(1)} collective-permute-done((bf16[512,256]{1,0:T(8,128)(2,1)S(1)}, bf16[512,256]{1,0:T(8,128)(2,1)S(1)}, u32[]{:S(2)}, u32[]{:S(2)}) %collective-permute-start.3) | collective-permute-done | bytes 262176 | tf_op jit(solution)/shard_map/ppermute | solution.py:28
  29.1 0.0 collective-permute-done.6.crossed_half
  29.1 1.6 %coarse_load.1 = (f32[1536,256]{1,0:T(8,128)S(1)}, bf16[96,256]{1,0:T(8,128)(2,1)S(1)}, f32[96,256]{1,0:T(8,128)S(1)}, f32[96,256]{1,0:T(8,128)S(1)}, f32[8,256]{1,0:T(8,128)S(1)}) custom-call(f32[1024,256]{1,0:T(8,128)S(1)} %get-tuple-element.57.load, f32[1536,256]{1,0:T(8,128)S(1)} %get-tuple-element.66.part, ...), custom_call_target="tpu_custom_call" | custom-call | tf_op jit(solution)/shard_map/coarse_load/pallas_call | solution.py:161
  30.7 1.1 %collective-permute-start.7 = (bf16[96,256]{1,0:T(8,128)(2,1)S(1)}, bf16[96,256]{1,0:T(8,128)(2,1)S(1)}, u32[]{:S(2)}, u32[]{:S(2)}) collective-permute-start(bf16[96,256]{1,0:T(8,128)(2,1)S(1)} %get-tuple-element.77), channel_id=1, source_target_pairs={{0,8},{1,9},{2,10},{3,11},{4,12},{5,13},{6,14},{7,15},{8,0},{9,1},... | collective-permute-start | bytes 147464 | tf_op jit(solution)/shard_map/ppermute | solution.py:23
  31.8 4.3 %collective-permute-done.7 = bf16[96,256]{1,0:T(8,128)(2,1)S(1)} collective-permute-done((bf16[96,256]{1,0:T(8,128)(2,1)S(1)}, bf16[96,256]{1,0:T(8,128)(2,1)S(1)}, u32[]{:S(2)}, u32[]{:S(2)}) %collective-permute-start.7) | collective-permute-done | bytes 49184 | tf_op jit(solution)/shard_map/ppermute | solution.py:23
  36.1 0.8 %collective-permute-start.8 = (bf16[192,256]{1,0:T(8,128)(2,1)S(1)}, bf16[192,256]{1,0:T(8,128)(2,1)S(1)}, u32[]{:S(2)}, u32[]{:S(2)}) collective-permute-start(bf16[192,256]{1,0:T(8,128)(2,1)S(1)} %pad_maximum_fusion.4), channel_id=1, source_target_pairs={{0,2},{1,3},{2,0},{3,1},{4,6},{5,7},{6,4},{7,5},{8,10},{9,11},{10,... | collective-permute-start | bytes 294920 | tf_op jit(solution)/shard_map/ppermute | solution.py:23
  37.0 3.3 %schur_load.1 = (f32[1536,256]{1,0:T(8,128)S(1)}, bf16[512,256]{1,0:T(8,128)(2,1)S(1)}, bf16[512,256]{1,0:T(8,128)(2,1)S(1)}, f32[8,256]{1,0:T(8,128)S(1)}) custom-call(f32[1536,256]{1,0:T(8,128)S(1)} %get-tuple-element.79.local.z_local, bf16[2048,1024]{1,0:T(8,128)(2,1)S(1)} %get-tuple-element.69.schur, bf16[2048,64]{1,0:T(8,128)(2,1)S(1)} %get-tuple-element.80.basis_high, ...), custom_call_target="tpu_custom_call" | custom-call | tf_op jit(solution)/shard_map/schur_load/pallas_call | solution.py:161
  40.3 0.6 collective-permute-done.8
  40.9 0.1 collective-permute-start.9
  41.0 0.1 collective-permute-start.11
  41.0 4.0 %collective-permute-start.12 = (bf16[512,256]{1,0:T(8,128)(2,1)S(1)}, bf16[512,256]{1,0:T(8,128)(2,1)S(1)}, u32[]{:S(2)}, u32[]{:S(2)}) collective-permute-start(bf16[512,256]{1,0:T(8,128)(2,1)S(1)} %get-tuple-element.91), channel_id=1, source_target_pairs={{0,15},{1,2},{2,1},{3,4},{4,3},{5,6},{6,5},{7,8},{8,7},{9,10},{10,... | collective-permute-start | bytes 786440 | tf_op jit(solution)/shard_map/ppermute | solution.py:28
  45.0 1.9 %collective-permute-done.9 = bf16[384,256]{1,0:T(8,128)(2,1)S(1)} collective-permute-done((bf16[384,256]{1,0:T(8,128)(2,1)S(1)}, bf16[384,256]{1,0:T(8,128)(2,1)S(1)}, u32[]{:S(2)}, u32[]{:S(2)}) %collective-permute-start.9) | collective-permute-done | bytes 196640 | tf_op jit(solution)/shard_map/ppermute | solution.py:23
  46.9 0.1 collective-permute-start.10
  47.0 4.6 %collective-permute-done.12.far_in = bf16[512,256]{1,0:T(8,128)(2,1)S(1)} collective-permute-done((bf16[512,256]{1,0:T(8,128)(2,1)S(1)}, bf16[512,256]{1,0:T(8,128)(2,1)S(1)}, u32[]{:S(2)}, u32[]{:S(2)}) %collective-permute-start.12) | collective-permute-done | bytes 262176 | tf_op jit(solution)/shard_map/ppermute | solution.py:28
  51.5 1.5 %neumann_image.1 = (f32[1024,256]{1,0:T(8,128)S(1)}, f32[1536,256]{1,0:T(8,128)S(1)}, bf16[512,256]{1,0:T(8,128)(2,1)S(1)}, bf16[512,256]{1,0:T(8,128)(2,1)S(1)}) custom-call(f32[1536,256]{1,0:T(8,128)S(1)} %get-tuple-element.88.part_in, bf16[512,256]{1,0:T(8,128)(2,1)S(1)} %collective-permute-done.11.near_in, ...), custom_call_target="tpu_custom_call" | custom-call | tf_op jit(solution)/shard_map/neumann_image/pallas_call | solution.py:161
  53.1 0.1 collective-permute-start.13
  53.2 2.0 %collective-permute-start.14 = (bf16[512,256]{1,0:T(8,128)(2,1)S(1)}, bf16[512,256]{1,0:T(8,128)(2,1)S(1)}, u32[]{:S(2)}, u32[]{:S(2)}) collective-permute-start(bf16[512,256]{1,0:T(8,128)(2,1)S(1)} %get-tuple-element.95), channel_id=1, source_target_pairs={{0,15},{1,2},{2,1},{3,4},{4,3},{5,6},{6,5},{7,8},{8,7},{9,10},{10,... | collective-permute-start | bytes 786440 | tf_op jit(solution)/shard_map/ppermute | solution.py:28
  55.2 0.0 collective-permute-done.13.near
  55.2 6.7 %collective-permute-done.14.far = bf16[512,256]{1,0:T(8,128)(2,1)S(1)} collective-permute-done((bf16[512,256]{1,0:T(8,128)(2,1)S(1)}, bf16[512,256]{1,0:T(8,128)(2,1)S(1)}, u32[]{:S(2)}, u32[]{:S(2)}) %collective-permute-start.14) | collective-permute-done | bytes 262176 | tf_op jit(solution)/shard_map/ppermute | solution.py:28
  61.8 3.6 %schur_image.1 = (f32[1536,256]{1,0:T(8,128)S(1)}, f32[1536,256]{1,0:T(8,128)S(1)}, f32[8,256]{1,0:T(8,128)S(1)}, f32[128,256]{1,0:T(8,128)S(1)}) custom-call(f32[1024,256]{1,0:T(8,128)S(1)} %get-tuple-element.92.image, f32[1536,256]{1,0:T(8,128)S(1)} %get-tuple-element.93.part, bf16[512,256]{1,0:T(8,128)(2,1)S(1)} %collective-permute-done.13.near, ...), custom_call_target="tpu_custom_call" | custom-call | tf_op jit(solution)/shard_map/schur_image/pallas_call | solution.py:161
  65.4 0.0 collective-permute-done.10.crossed_half
  65.5 1.7 %coarse_image.1 = (f32[4,256]{1,0:T(4,128)S(1)}, f32[64,256]{1,0:T(8,128)S(1)}, f32[1024,256]{1,0:T(8,128)S(1)}, bf16[512,256]{1,0:T(8,128)(2,1)S(1)}) custom-call(bf16[768,256]{1,0:T(8,128)(2,1)S(1)} %pad_maximum_fusion.half, bf16[768,256]{1,0:T(8,128)(2,1)S(1)} %collective-permute-done.10.crossed_half, bf16[64,1024]{1,0:T(8,128)(2,1)S(1)} %get-tuple-element.60.inverse, ...), custom_call_target="tpu_custom_call" | custom-call | tf_op jit(solution)/shard_map/coarse_image/pallas_call | solution.py:161
  67.1 0.1 collective-permute-start.15
  67.2 0.7 complete.1
  67.9 3.8 %collective-permute-done.15 = f32[4,256]{1,0:T(4,128)S(1)} collective-permute-done((f32[4,256]{1,0:T(4,128)S(1)}, f32[4,256]{1,0:T(4,128)S(1)}, u32[]{:S(2)}, u32[]{:S(2)}) %collective-permute-start.15) | collective-permute-done | bytes 4128 | tf_op jit(solution)/shard_map/ppermute | solution.py:23
  71.7 0.3 collective-permute-start.16
  72.0 3.3 %collective-permute-done.16 = f32[4,256]{1,0:T(4,128)S(1)} collective-permute-done((f32[4,256]{1,0:T(4,128)S(1)}, f32[4,256]{1,0:T(4,128)S(1)}, u32[]{:S(2)}, u32[]{:S(2)}) %collective-permute-start.16) | collective-permute-done | bytes 4128 | tf_op jit(solution)/shard_map/ppermute | solution.py:23
  75.3 0.0 collective-permute-start.19
  75.3 3.9 %collective-permute-done.17 = f32[4,256]{1,0:T(4,128)S(1)} collective-permute-done((f32[4,256]{1,0:T(4,128)S(1)}, f32[4,256]{1,0:T(4,128)S(1)}, u32[]{:S(2)}, u32[]{:S(2)}) %collective-permute-start.17) | collective-permute-done | bytes 4128 | tf_op jit(solution)/shard_map/ppermute | solution.py:23
  79.3 1.2 %collective-permute-done.18 = f32[4,256]{1,0:T(4,128)S(1)} collective-permute-done((f32[4,256]{1,0:T(4,128)S(1)}, f32[4,256]{1,0:T(4,128)S(1)}, u32[]{:S(2)}, u32[]{:S(2)}) %collective-permute-start.18) | collective-permute-done | bytes 4128 | tf_op jit(solution)/shard_map/ppermute | solution.py:23
  80.4 1.6 %combine.1 = (f32[1024,256]{1,0:T(8,128)}, f32[1024,256]{1,0:T(8,128)}) custom-call(f32[4,256]{1,0:T(4,128)S(1)} %add.15.sums, f32[1024,256]{1,0:T(8,128)S(1)} %get-tuple-element.57.load, f32[1024,256]{1,0:T(8,128)S(1)} %get-tuple-element.108.z, f32[1024,256]{1,0:T(8,128)S(1)} %get-tuple-element.103.y, f32[1024,256]{1,0:T(8,128)S(1)} %get-tuple-element.92.image, ...), custom_call_target="tpu_custom_call" | custom-call | tf_op jit(solution)/shard_map/combine/pallas_call | solution.py:161
  (14 shorter events, 0.1 us)
Async XLA Ops:
  2.1 6.3 %collective-permute-start = (bf16[64,256]{1,0:T(8,128)(2,1)S(1)}, bf16[64,256]{1,0:T(8,128)(2,1)S(1)}, u32[]{:S(2)}, u32[]{:S(2)}) collective-permute-start(bf16[64,256]{1,0:T(8,128)(2,1)S(1)} %get-tuple-element.61), channel_id=1, source_target_pairs={{0,8},{1,9},{2,10},{3,11},{4,12},{5,13},{6,14},{7,15},{8,0},{9,1},... | collective-permute-start | bytes 98312 | tf_op jit(solution)/shard_map/ppermute | solution.py:23
  8.5 10.3 %collective-permute-start.1 = (bf16[720,256]{1,0:T(8,128)(2,1)S(1)}, bf16[720,256]{1,0:T(8,128)(2,1)S(1)}, u32[]{:S(2)}, u32[]{:S(2)}) collective-permute-start(bf16[720,256]{1,0:T(8,128)(2,1)S(1)} %halo_message.1), channel_id=1, source_target_pairs={{15,0},{0,1},{1,2},{2,3},{3,4},{4,5},{5,6},{6,7},{7,8},{8,9},{9,10... | collective-permute-start | bytes 1105928 | tf_op jit(solution)/shard_map/ppermute | solution.py:19
  8.5 5.3 %collective-permute-start.4 = (bf16[128,256]{1,0:T(8,128)(2,1)S(1)}, bf16[128,256]{1,0:T(8,128)(2,1)S(1)}, u32[]{:S(2)}, u32[]{:S(2)}) collective-permute-start(bf16[128,256]{1,0:T(8,128)(2,1)S(1)} %pad_maximum_fusion.5), channel_id=1, source_target_pairs={{0,2},{1,3},{2,0},{3,1},{4,6},{5,7},{6,4},{7,5},{8,10},{9,11},{10,... | collective-permute-start | bytes 196616 | tf_op jit(solution)/shard_map/ppermute | solution.py:23
  13.8 10.9 %collective-permute-start.5 = (bf16[256,256]{1,0:T(8,128)(2,1)S(1)}, bf16[256,256]{1,0:T(8,128)(2,1)S(1)}, u32[]{:S(2)}, u32[]{:S(2)}) collective-permute-start(bf16[256,256]{1,0:T(8,128)(2,1)S(1)} %pad_maximum_fusion.3), channel_id=1, source_target_pairs={{0,4},{1,5},{2,6},{3,7},{4,0},{5,1},{6,2},{7,3},{8,12},{9,13},{10,... | collective-permute-start | bytes 393224 | tf_op jit(solution)/shard_map/ppermute | solution.py:23
  20.3 4.5 %collective-permute-start.2 = (bf16[512,256]{1,0:T(8,128)(2,1)S(1)}, bf16[512,256]{1,0:T(8,128)(2,1)S(1)}, u32[]{:S(2)}, u32[]{:S(2)}) collective-permute-start(bf16[512,256]{1,0:T(8,128)(2,1)S(1)} %get-tuple-element.67), channel_id=1, source_target_pairs={{0,1},{1,0},{2,3},{3,2},{4,5},{5,4},{6,7},{7,6},{8,9},{9,8},{10,11... | collective-permute-start | bytes 786440 | tf_op jit(solution)/shard_map/ppermute | solution.py:23
  20.4 8.7 %collective-permute-start.3 = (bf16[512,256]{1,0:T(8,128)(2,1)S(1)}, bf16[512,256]{1,0:T(8,128)(2,1)S(1)}, u32[]{:S(2)}, u32[]{:S(2)}) collective-permute-start(bf16[512,256]{1,0:T(8,128)(2,1)S(1)} %get-tuple-element.68), channel_id=1, source_target_pairs={{0,15},{1,2},{2,1},{3,4},{4,3},{5,6},{6,5},{7,8},{8,7},{9,10},{10,... | collective-permute-start | bytes 786440 | tf_op jit(solution)/shard_map/ppermute | solution.py:28
  24.8 4.3 %collective-permute-start.6 = (bf16[512,256]{1,0:T(8,128)(2,1)S(1)}, bf16[512,256]{1,0:T(8,128)(2,1)S(1)}, u32[]{:S(2)}, u32[]{:S(2)}) collective-permute-start(bf16[512,256]{1,0:T(8,128)(2,1)S(1)} %pad_maximum_fusion.1.half), channel_id=1, source_target_pairs={{0,1},{1,0},{2,3},{3,2},{4,5},{5,4},{6,7},{7,6},{8,9},{9,8},{10,11... | collective-permute-start | bytes 786440 | tf_op jit(solution)/shard_map/ppermute | solution.py:23
  30.7 5.4 %collective-permute-start.7 = (bf16[96,256]{1,0:T(8,128)(2,1)S(1)}, bf16[96,256]{1,0:T(8,128)(2,1)S(1)}, u32[]{:S(2)}, u32[]{:S(2)}) collective-permute-start(bf16[96,256]{1,0:T(8,128)(2,1)S(1)} %get-tuple-element.77), channel_id=1, source_target_pairs={{0,8},{1,9},{2,10},{3,11},{4,12},{5,13},{6,14},{7,15},{8,0},{9,1},... | collective-permute-start | bytes 147464 | tf_op jit(solution)/shard_map/ppermute | solution.py:23
  36.1 4.7 %collective-permute-start.8 = (bf16[192,256]{1,0:T(8,128)(2,1)S(1)}, bf16[192,256]{1,0:T(8,128)(2,1)S(1)}, u32[]{:S(2)}, u32[]{:S(2)}) collective-permute-start(bf16[192,256]{1,0:T(8,128)(2,1)S(1)} %pad_maximum_fusion.4), channel_id=1, source_target_pairs={{0,2},{1,3},{2,0},{3,1},{4,6},{5,7},{6,4},{7,5},{8,10},{9,11},{10,... | collective-permute-start | bytes 294920 | tf_op jit(solution)/shard_map/ppermute | solution.py:23
  40.9 6.0 %collective-permute-start.9 = (bf16[384,256]{1,0:T(8,128)(2,1)S(1)}, bf16[384,256]{1,0:T(8,128)(2,1)S(1)}, u32[]{:S(2)}, u32[]{:S(2)}) collective-permute-start(bf16[384,256]{1,0:T(8,128)(2,1)S(1)} %pad_maximum_fusion.2), channel_id=1, source_target_pairs={{0,4},{1,5},{2,6},{3,7},{4,0},{5,1},{6,2},{7,3},{8,12},{9,13},{10,... | collective-permute-start | bytes 589832 | tf_op jit(solution)/shard_map/ppermute | solution.py:23
  41.0 6.0 %collective-permute-start.11 = (bf16[512,256]{1,0:T(8,128)(2,1)S(1)}, bf16[512,256]{1,0:T(8,128)(2,1)S(1)}, u32[]{:S(2)}, u32[]{:S(2)}) collective-permute-start(bf16[512,256]{1,0:T(8,128)(2,1)S(1)} %get-tuple-element.90), channel_id=1, source_target_pairs={{0,1},{1,0},{2,3},{3,2},{4,5},{5,4},{6,7},{7,6},{8,9},{9,8},{10,11... | collective-permute-start | bytes 786440 | tf_op jit(solution)/shard_map/ppermute | solution.py:23
  41.0 10.5 %collective-permute-start.12 = (bf16[512,256]{1,0:T(8,128)(2,1)S(1)}, bf16[512,256]{1,0:T(8,128)(2,1)S(1)}, u32[]{:S(2)}, u32[]{:S(2)}) collective-permute-start(bf16[512,256]{1,0:T(8,128)(2,1)S(1)} %get-tuple-element.91), channel_id=1, source_target_pairs={{0,15},{1,2},{2,1},{3,4},{4,3},{5,6},{6,5},{7,8},{8,7},{9,10},{10,... | collective-permute-start | bytes 786440 | tf_op jit(solution)/shard_map/ppermute | solution.py:28
  46.9 18.6 %collective-permute-start.10 = (bf16[768,256]{1,0:T(8,128)(2,1)S(1)}, bf16[768,256]{1,0:T(8,128)(2,1)S(1)}, u32[]{:S(2)}, u32[]{:S(2)}) collective-permute-start(bf16[768,256]{1,0:T(8,128)(2,1)S(1)} %pad_maximum_fusion.half), channel_id=1, source_target_pairs={{0,1},{1,0},{2,3},{3,2},{4,5},{5,4},{6,7},{7,6},{8,9},{9,8},{10,11... | collective-permute-start | bytes 1179656 | tf_op jit(solution)/shard_map/ppermute | solution.py:23
  53.1 2.1 %collective-permute-start.13 = (bf16[512,256]{1,0:T(8,128)(2,1)S(1)}, bf16[512,256]{1,0:T(8,128)(2,1)S(1)}, u32[]{:S(2)}, u32[]{:S(2)}) collective-permute-start(bf16[512,256]{1,0:T(8,128)(2,1)S(1)} %get-tuple-element.94), channel_id=1, source_target_pairs={{0,1},{1,0},{2,3},{3,2},{4,5},{5,4},{6,7},{7,6},{8,9},{9,8},{10,11... | collective-permute-start | bytes 786440 | tf_op jit(solution)/shard_map/ppermute | solution.py:23
  53.2 8.7 %collective-permute-start.14 = (bf16[512,256]{1,0:T(8,128)(2,1)S(1)}, bf16[512,256]{1,0:T(8,128)(2,1)S(1)}, u32[]{:S(2)}, u32[]{:S(2)}) collective-permute-start(bf16[512,256]{1,0:T(8,128)(2,1)S(1)} %get-tuple-element.95), channel_id=1, source_target_pairs={{0,15},{1,2},{2,1},{3,4},{4,3},{5,6},{6,5},{7,8},{8,7},{9,10},{10,... | collective-permute-start | bytes 786440 | tf_op jit(solution)/shard_map/ppermute | solution.py:28
  67.1 4.6 %collective-permute-start.15 = (f32[4,256]{1,0:T(4,128)S(1)}, f32[4,256]{1,0:T(4,128)S(1)}, u32[]{:S(2)}, u32[]{:S(2)}) collective-permute-start(f32[4,256]{1,0:T(4,128)S(1)} %get-tuple-element.100), channel_id=1, source_target_pairs={{0,8},{1,9},{2,10},{3,11},{4,12},{5,13},{6,14},{7,15},{8,0},{9,1},... | collective-permute-start | bytes 12296 | tf_op jit(solution)/shard_map/ppermute | solution.py:23
  71.7 3.6 %collective-permute-start.16 = (f32[4,256]{1,0:T(4,128)S(1)}, f32[4,256]{1,0:T(4,128)S(1)}, u32[]{:S(2)}, u32[]{:S(2)}) collective-permute-start(f32[4,256]{1,0:T(4,128)S(1)} %add.12), channel_id=1, source_target_pairs={{0,2},{1,3},{2,0},{3,1},{4,6},{5,7},{6,4},{7,5},{8,10},{9,11},{10,... | collective-permute-start | bytes 12296 | tf_op jit(solution)/shard_map/ppermute | solution.py:23
  75.3 5.1 %collective-permute-start.19 = (bf16[512,256]{1,0:T(8,128)(2,1)S(1)}, bf16[512,256]{1,0:T(8,128)(2,1)S(1)}, u32[]{:S(2)}, u32[]{:S(2)}) collective-permute-start(bf16[512,256]{1,0:T(8,128)(2,1)S(1)} %get-tuple-element.111), channel_id=1, source_target_pairs={{1,0},{2,1},{3,2},{4,3},{5,4},{6,5},{7,6},{8,7},{9,8},{10,9},{11,1... | collective-permute-start | bytes 786440 | tf_op jit(solution)/shard_map/ppermute | solution.py:19
  75.3 3.9 %collective-permute-start.17 = (f32[4,256]{1,0:T(4,128)S(1)}, f32[4,256]{1,0:T(4,128)S(1)}, u32[]{:S(2)}, u32[]{:S(2)}) collective-permute-start(f32[4,256]{1,0:T(4,128)S(1)} %add.13), channel_id=1, source_target_pairs={{0,4},{1,5},{2,6},{3,7},{4,0},{5,1},{6,2},{7,3},{8,12},{9,13},{10,... | collective-permute-start | bytes 12296 | tf_op jit(solution)/shard_map/ppermute | solution.py:23
  79.3 1.2 %collective-permute-start.18 = (f32[4,256]{1,0:T(4,128)S(1)}, f32[4,256]{1,0:T(4,128)S(1)}, u32[]{:S(2)}, u32[]{:S(2)}) collective-permute-start(f32[4,256]{1,0:T(4,128)S(1)} %add.14), channel_id=1, source_target_pairs={{0,1},{1,0},{2,3},{3,2},{4,5},{5,4},{6,7},{7,6},{8,9},{9,8},{10,11... | collective-permute-start | bytes 12296 | tf_op jit(solution)/shard_map/ppermute | solution.py:23

commit v12 on v9

--- a/solution.py
+++ b/solution.py
@@ -205,42 +205,74 @@
         copy.wait()
 
 
-def neumann_products(left, right, weights, neumann, part, near, far):
-    subs, nf = len(left), left[0].shape[0]
-    previous = None
-    for j in range(subs):
-        product = dot(rows_of(neumann, j, 2 * nf), jnp.concatenate([left[j], right[j]], axis=0))
-        first, second = product[:nf], product[nf:]
-        if j == 0:
-            part[:nf] = outer = first
-        else:
-            part[j * nf : (j + 1) * nf] = weights[j] * previous + (1.0 - weights[j]) * first
-        previous = second
-    part[subs * nf :] = previous
-    send(outer, previous, near, far)
-
-
-def neumann_load(halo, load, weight, message, neumann, part, near, far):
+def neumann_half(neumann, left, right, j, half, nf):
+    start = (2 * j + half) * nf
+    return dot(neumann[start : start + nf], jnp.concatenate([left[j](), right[j]()], axis=0))
+
+
+def neumann_outer(left, right, neumann, outer, near, far):
+    nf, last = near.shape[0], len(left) - 1
+    first = neumann_half(neumann, left, right, 0, 0, nf)
+    second = neumann_half(neumann, left, right, last, 1, nf)
+    outer[:nf], outer[nf:] = first, second
+    send(first, second, near, far)
+
+
+def neumann_inner(left, right, weights, neumann, inner, nf):
+    for j in range(1, len(left)):
+        before = neumann_half(neumann, left, right, j - 1, 1, nf)
+        after_it = neumann_half(neumann, left, right, j, 0, nf)
+        inner[(j - 1) * nf : j * nf] = weights(j) * before + (1.0 - weights(j)) * after_it
+
+
+def face_of(outer, inner, e, nf):
+    if e == 0:
+        return outer[:nf]
+    if e * nf > inner.shape[0]:
+        return outer[nf:]
+    return inner[(e - 1) * nf : e * nf]
+
+
+def load_sides(halo, load, weight, message):
     subs, nf = weight.shape
-    weights = [None] + [column_of(weight[j : j + 1]) for j in range(subs)]
-    left = [message[:nf]]
-    left += [((1.0 - weights[j]) * rows_of(load, j - 1, nf)).astype(BF16) for j in range(1, subs)]
-    right = [(weights[j + 1] * rows_of(load, j, nf)).astype(BF16) for j in range(subs)]
-    neumann_products(left, right, weights, neumann, part, near, far)
-
-
-def neumann_image(halo, part_in, near_in, far_in, weight, message, neumann, image, part, near, far):
+    own = lambda e: column_of(weight[e - 1 : e])
+    left = [lambda: message[:nf]]
+    left += [lambda j=j: ((1.0 - own(j)) * rows_of(load, j - 1, nf)).astype(BF16) for j in range(1, subs)]
+    right = [lambda j=j: (own(j + 1) * rows_of(load, j, nf)).astype(BF16) for j in range(subs)]
+    return left, right, own
+
+
+def load_outer(halo, load, weight, message, neumann, outer, near, far):
+    left, right, _ = load_sides(halo, load, weight, message)
+    neumann_outer(left, right, neumann, outer, near, far)
+
+
+def load_inner(halo, load, weight, message, neumann, inner):
+    left, right, own = load_sides(halo, load, weight, message)
+    neumann_inner(left, right, own, neumann, inner, halo.nf)
+
+
+def image_sides(halo, outer, inner, near, far, weight, message):
     subs, nf = weight.shape
-    weights = all_weights(halo, message, weight)
-    faces = [rows_of(part_in, e, nf) for e in range(subs + 1)]
-    from_next, from_previous = received(near_in, far_in)
-    faces[0] = faces[0] + from_previous
-    faces[subs] = faces[subs] + from_next
-    for e in range(1, subs + 1):
-        image[(e - 1) * nf : e * nf] = faces[e]
-    left = [((1.0 - weights[j]) * faces[j]).astype(BF16) for j in range(subs)]
-    right = [(weights[j + 1] * faces[j + 1]).astype(BF16) for j in range(subs)]
-    neumann_products(left, right, weights, neumann, part, near, far)
+    own = lambda e: column_of(weight[e - 1 : e]) if e else halo.weight(message)
+    from_next, from_previous = received(near, far)
+    face = lambda e: face_of(outer, inner, e, nf) + (from_previous if e == 0 else from_next if e == subs else 0.0)
+    left = [lambda j=j: ((1.0 - own(j)) * face(j)).astype(BF16) for j in range(subs)]
+    right = [lambda j=j: (own(j + 1) * face(j + 1)).astype(BF16) for j in range(subs)]
+    return left, right, own, face
+
+
+def image_outer(halo, outer_in, inner_in, near_in, far_in, weight, message, neumann, outer, near, far):
+    left, right, _, _ = image_sides(halo, outer_in, inner_in, near_in, far_in, weight, message)
+    neumann_outer(left, right, neumann, outer, near, far)
+
+
+def image_inner(halo, outer_in, inner_in, near_in, far_in, weight, message, neumann, image, inner):
+    nf = halo.nf
+    left, right, own, face = image_sides(halo, outer_in, inner_in, near_in, far_in, weight, message)
+    for e in range(1, len(left) + 1):
+        image[(e - 1) * nf : e * nf] = face(e)
+    neumann_inner(left, right, own, neumann, inner, nf)
 
 
 def static_basis(halo, schur, message, rows, basis_high, basis_low, turned_high, turned_low, gram):
@@ -259,14 +291,14 @@
             gram[wide, k * ncf : (k + 1) * ncf] = dot_nt(turned[0][:, half], pair[k]) + dot_nt(turned[1][:, half], pair[k])
 
 
-def complete_local(halo, part, near, far, weight, message, local):
+def complete_local(halo, outer, inner, near, far, weight, message, local):
     subs, nf = weight.shape
     weights = all_weights(halo, message, weight)
     from_next, from_previous = received(near, far)
-    local[:nf] = (1.0 - weights[0]) * part[:nf] + weights[0] * from_previous
+    local[:nf] = (1.0 - weights[0]) * outer[:nf] + weights[0] * from_previous
     for e in range(1, subs):
-        local[e * nf : (e + 1) * nf] = rows_of(part, e, nf)
-    local[subs * nf :] = weights[subs] * part[subs * nf :] + (1.0 - weights[subs]) * from_next
+        local[e * nf : (e + 1) * nf] = face_of(outer, inner, e, nf)
+    local[subs * nf :] = weights[subs] * outer[nf:] + (1.0 - weights[subs]) * from_next
 
 
 def project(halo, local, turned_high, turned_low, base):
@@ -288,23 +320,50 @@
     return faces, energy
 
 
-def schur_load(halo, local, schur, basis_high, basis_low, solution, sums_in, part, near, far, sums):
+def schur_half(halo, local, schur, j, half):
+    nf, columns = halo.nf, halo.columns
+    start = (2 * j + half) * nf
+    both = dot(schur[start : start + nf], jnp.concatenate(split(local[j * nf : (j + 2) * nf]), axis=1))
+    return both[:, :columns] + both[:, columns:]
+
+
+def basis_half(halo, basis_high, basis_low, solution, j, half):
     ncf, nf = halo.ncf, halo.nf
-    faces, energy = schur_faces(halo, local, schur)
-    x = [rows_of(solution, e, ncf) for e in range(len(faces))]
-    faces = add_basis(nf, x, basis_high, basis_low, faces)
-    for e, face in enumerate(faces):
-        part[e * nf : (e + 1) * nf] = face
-    send(faces[0], faces[-1], near, far)
+    here = slice((2 * j + half) * nf, (2 * j + half + 1) * nf)
+    return split_dot((basis_high[here], basis_low[here]), solution[j * ncf : (j + 2) * ncf])
+
+
+def schur_outer(halo, local, schur, basis_high, basis_low, solution, sums_in, outer, near, far, sums):
+    nf = halo.nf
+    last = schur.shape[0] // (2 * nf) - 1
+    energy = sums_in[1:2]
+    for here, face, j, half in ((slice(0, nf), 0, 0, 0), (slice(nf, 2 * nf), last + 1, last, 1)):
+        outer[here] = basis_half(halo, basis_high, basis_low, solution, j, half)
+        result = schur_half(halo, local, schur, j, half)
+        energy = energy + column_sum(local[face * nf : (face + 1) * nf] * result)
+        outer[here] += result
+    send(outer[:nf], outer[nf:], near, far)
     sums[0:1] = sums_in[0:1]
-    sums[1:2] = sums_in[1:2] + energy
+    sums[1:2] = energy
+
+
+def schur_inner(halo, local, schur, basis_high, basis_low, solution, inner, energies):
+    nf = halo.nf
+    for j in range(1, schur.shape[0] // (2 * nf)):
+        here = slice((j - 1) * nf, j * nf)
+        inner[here] = basis_half(halo, basis_high, basis_low, solution, j - 1, 1)
+        inner[here] += basis_half(halo, basis_high, basis_low, solution, j, 0)
+        result = schur_half(halo, local, schur, j - 1, 1)
+        result = result + schur_half(halo, local, schur, j, 0)
+        energies[j - 1 : j] = column_sum(local[j * nf : (j + 1) * nf] * result)
+        inner[here] += result
 
 
 def schur_image(
-    halo, image, part, near, far, weight, message, schur, turned_high, turned_low, local, product, quadratic, base
+    halo, image, outer, inner, near, far, weight, message, schur, turned_high, turned_low, local, product, quadratic, base
 ):
     nf = halo.nf
-    complete_local(halo, part, near, far, weight, message, local)
+    complete_local(halo, outer, inner, near, far, weight, message, local)
     project(halo, local, turned_high, turned_low, base)
     faces, energy = schur_faces(halo, local, schur)
     for e, face in enumerate(faces):
@@ -352,12 +411,12 @@
 
 
 def coarse_load(
-    halo, load, part, near, far, weight, message, turned_high, turned_low, half, crossed_half, inverse, coarse, gram,
+    halo, load, outer, inner, near, far, weight, message, turned_high, turned_low, half, crossed_half, inverse, coarse, gram,
     local, shares_rounded, shares, solution, sums, base, gathered,
 ):
     ncf, nf = halo.ncf, halo.nf
     subs = weight.shape[0]
-    complete_local(halo, part, near, far, weight, message, local)
+    complete_local(halo, outer, inner, near, far, weight, message, local)
     project(halo, local, turned_high, turned_low, base)
     for place, blocks, start, stop in placed(half, crossed_half):
         gathered[pl.ds(pl.multiple_of(place * subs * ncf, subs * ncf), subs * ncf)] = blocks[start:stop]
@@ -374,10 +433,9 @@
 
 
 def coarse_image(
-    halo, half, crossed_half, inverse, message, shares, base, gram, quadratic, basis_high, basis_low, product, sums_in,
-    sums, solution, part, back, gathered,
+    halo, half, crossed_half, inverse, message, shares, base, gram, quadratic, sums_in, energies, sums, solution, gathered
 ):
-    ncf, nf = halo.ncf, halo.nf
+    ncf = halo.ncf
     subs = inverse.shape[0] // ncf
     total = gathered.shape[0]
     for place, blocks, start, stop in placed(half, crossed_half):
@@ -389,22 +447,28 @@
     own = split_dot(inverse[...], everything)
     x = [split_dot(halo.inverse(message), everything)] + [own[j * ncf : (j + 1) * ncf] for j in range(subs)]
     _, energy = coarse_products(ncf, x, base, gram)
-    sums[0:2] = sums_in[0:2]
-    sums[2:3] = quadratic[1:2] + sum(column_sum(rows_of(shares, e, ncf) * x[e]) for e in range(subs + 1))
+    for e in range(subs + 1):
+        solution[e * ncf : (e + 1) * ncf] = x[e]
+    sums[0:1] = sums_in[0:1]
+    sums[1:2] = sums_in[1:2] + column_sum(energies[...])
+    sums[2:3] = quadratic[1:2] + column_sum(shares[...] * solution[...])
     sums[3:4] = quadratic[0:1] + energy
-    solution[...] = own
+
+
+def complete(
+    halo, z_local, z_coarse, y_local, y_coarse, rows, basis_high, basis_low, product, z, y, part, back
+):
+    ncf, nf = halo.ncf, halo.nf
+    subs = rows.shape[0] // ncf
+    x = [rows_of(y_coarse, e, ncf) for e in range(subs + 1)]
     faces = add_basis(nf, x, basis_high, basis_low, [rows_of(product, e, nf) for e in range(subs + 1)])
     for e in range(1, subs + 1):
         part[(e - 1) * nf : e * nf] = faces[e]
     back[...] = faces[0].astype(BF16)
-
-
-def complete(halo, z_local, z_coarse, y_local, y_coarse, rows, z, y):
-    ncf, nf = halo.ncf, halo.nf
-    for j in range(rows.shape[0] // ncf):
+    for j in range(subs):
         here, beside = slice(j * nf, (j + 1) * nf), slice((j + 1) * nf, (j + 2) * nf)
-        for local, coarse, whole in ((z_local, z_coarse[ncf:], z), (y_local, y_coarse[...], y)):
-            whole[here] = local[beside] + split_dot(rows_of(rows, j, ncf), rows_of(coarse, j, ncf), dot_tn)
+        for local, coarse, whole in ((z_local, z_coarse, z), (y_local, y_coarse, y)):
+            whole[here] = local[beside] + split_dot(rows_of(rows, j, ncf), rows_of(coarse, j + 1, ncf), dot_tn)
 
 
 def combine(halo, sums, load, z, y, image, part, from_next, solution, residual):
@@ -430,7 +494,6 @@
     bind = lambda kernel: functools.partial(kernel, halo)
     faces, own = ((subs + 1) * nf, columns), (subs * nf, columns)
     coarse_own, local_rows = (subs * ncf, columns), 2 * subs * ncf
-    halves = [((nf, columns), BF16)] * 2
     products = [(faces, F32), (faces, F32), ((8, columns), F32), ((local_rows, columns), F32)]
     semaphores = lambda count: [pltpu.SemaphoreType.DMA((count,))]
     described = lambda array: (array.shape, array.dtype)
@@ -449,53 +512,57 @@
         scratch=[pltpu.VMEM((halo.weight_count, columns), F32)],
     )
     half = gather_half(coarse_rounded, early[:1])
-    message = after(message, half)
     tied = after(tuple(map(outside, (neumann, schur))), message)
     neumann, schur = stage(
         bind(fetch), [described(array) for array in tied], *tied, scratch=semaphores(2), fetched=2
     )
     message = shifted(message, 1)
-    half = gather_half(half, early[1:], neumann)
-    part, near, far = stage(
-        bind(neumann_load), [(faces, F32)] + halves, load, weight, message, neumann
-    )
+    outside_faces = [((2 * nf, columns), F32)] + 2 * [((nf, columns), BF16)]
+    inside_faces = [(((subs - 1) * nf, columns), F32)]
+    outer, near, far = stage(bind(load_outer), outside_faces, load, weight, message, neumann)
+    (inner,) = stage(bind(load_inner), inside_faces, load, weight, after(message, far), neumann)
+    half = gather_half(half, early[1:], far)
     far, near = far_block(far), crossed(near, 1)
     long, wide = ((2 * subs * nf, 2 * ncf), BF16), ((local_rows, 2 * nf), BF16)
     basis_high, basis_low, turned_high, turned_low, gram = stage(
-        bind(static_basis), [long, long, wide, wide, ((local_rows, LANES), F32)], schur, after(message, part), rows
+        bind(static_basis), [long, long, wide, wide, ((local_rows, LANES), F32)], schur, after(message, inner), rows
     )
     half = gather_half(half, late, gram)
     crossed_half = crossed(half, 1)
     share_rows, sum_rows = ((subs + 1) * ncf, columns), ((8, columns), F32)
     z_local, shares_rounded, shares, z_coarse, sums = stage(
         bind(coarse_load), [(faces, F32), (share_rows, BF16), (share_rows, F32), (share_rows, F32), sum_rows],
-        load, part, near, far, weight, message, turned_high, turned_low, half, crossed_half, inverse, coarse, gram,
+        load, outer, inner, near, far, weight, message, turned_high, turned_low, half, crossed_half, inverse, coarse, gram,
         scratch=[pltpu.VMEM((local_rows, columns), F32), pltpu.VMEM((nco, columns), BF16)],
     )
-    part, near, far, sums = stage(
-        bind(schur_load), [(faces, F32)] + halves + [sum_rows],
-        z_local, schur, basis_high, basis_low, z_coarse, sums,
-    )
-    half = gather_half(shares_rounded, early[:1])
-    near, far = after((near, far), half)
+    outer, near, far, sums = stage(
+        bind(schur_outer), outside_faces + [sum_rows], z_local, schur, basis_high, basis_low, z_coarse, sums
+    )
+    inner, energies = stage(
+        bind(schur_inner), inside_faces + [((subs - 1, columns), F32)], z_local, schur, basis_high, basis_low, z_coarse
+    )
+    half = gather_half(shares_rounded, early[:1], inner)
     far, near = far_block(far), crossed(near, 1)
-    image, part, near, far = stage(
-        bind(neumann_image), [(own, F32), (faces, F32)] + halves, part, near, far, weight, message, neumann
-    )
+    operands = outer, inner, near, far, weight, message, neumann
+    outer, near, far = stage(bind(image_outer), outside_faces, *operands)
+    image, inner = stage(bind(image_inner), [(own, F32)] + inside_faces, after(operands[0], far), *operands[1:])
     half = gather_half(half, early[1:], far)
     far, near = far_block(far), crossed(near, 1)
-    half = gather_half(half, late, near, far)
+    half = gather_half(half, late, near, far, inner)
     crossed_half = crossed(half, 1)
-    part = after(part, half)
+    outer = after(outer, half)
     y_local, product, quadratic, base = stage(
-        bind(schur_image), products, image, part, near, far, weight, message, schur, turned_high, turned_low
-    )
-    sums, y_coarse, part, back = stage(
-        bind(coarse_image), [((4, columns), F32), (coarse_own, F32), (own, F32), ((nf, columns), BF16)],
-        half, crossed_half, inverse, message, shares, base, gram, quadratic, basis_high, basis_low, product, sums,
+        bind(schur_image), products, image, outer, inner, near, far, weight, message, schur, turned_high, turned_low
+    )
+    sums, y_coarse = stage(
+        bind(coarse_image), [((4, columns), F32), (share_rows, F32)],
+        half, crossed_half, inverse, message, shares, base, gram, quadratic, sums, energies,
         scratch=[pltpu.VMEM((nco, columns), F32)],
     )
-    z, y = stage(bind(complete), [(own, F32), (own, F32)], z_local, z_coarse, y_local, y_coarse, rows)
+    z, y, part, back = stage(
+        bind(complete), [(own, F32), (own, F32), (own, F32), ((nf, columns), BF16)],
+        z_local, z_coarse, y_local, y_coarse, rows, basis_high, basis_low, product,
+    )
     for k, bit in enumerate(steps):
         sums = sums + after(crossed(sums, bit), y)
         if k == len(early) - 1:

time: 80.6 us -> 74.4 us (0.923)
  waiting for transfers between devices: 33.5 us -> 24.1 us
  Pallas kernels: 22.7 us -> 24.4 us
  starting transfers between devices: 23.3 us -> 24.8 us
    ppermute x3, waiting for transfers between devices: 12.6 us -> 7.79 us  [far_block(): lax.ppermute(block, AXIS, [(i, (i + (1 if i % 2 else -1)) % n) for i in r...]
    ppermute x15, waiting for transfers between devices: 20.9 us -> 16.3 us  [crossed(): lax.ppermute(block, AXIS, [(i, i ^ bit) for i in range(lax.axis_size(AXIS...]
    pallas_call x12 -> x15, Pallas kernels: 22.7 us -> 24.4 us  [stage(): return call(*operands)]
    ppermute x2, starting transfers between devices: 0.01 us -> 1.28 us  [shifted(): lax.ppermute(block, AXIS, [((i - distance) % n, i) for i in range(n)])]
  transfers between devices with their start and end apart: 20 -> 20, of which waited for: 10 -> 10; matrix products, arithmetic and copies ran while one was open for 0% -> 0% of each run, Pallas kernels for 20% -> 25%
where the time goes in v12:
time: 74.4 us; the launch traced here: 74.3 us
  starting transfers between devices  24.8 us (33%)
  Pallas kernels  24.4 us (33%)
  waiting for transfers between devices  24.1 us (32%)
  between operations  0.85 us (1%)
    pallas_call x15, Pallas kernels, stage(): return call(*operands)  24.4 us
    ppermute x15, starting transfers between devices, crossed(): lax.ppermute(block, AXIS, [(i, i ^ bit) for i in range(lax.axis_size(AXIS...  18.7 us
    ppermute x15, waiting for transfers between devices, crossed(): lax.ppermute(block, AXIS, [(i, i ^ bit) for i in range(lax.axis_size(AXIS...  16.3 us
    ppermute x3, waiting for transfers between devices, far_block(): lax.ppermute(block, AXIS, [(i, (i + (1 if i % 2 else -1)) % n) for i in r...  7.79 us
    ppermute x3, starting transfers between devices, far_block(): lax.ppermute(block, AXIS, [(i, (i + (1 if i % 2 else -1)) % n) for i in r...  4.79 us
  transfers between devices with their start and end apart: 20, of which 10 were waited for; matrix products, arithmetic and copies ran while one was open for 0% of the time, Pallas kernels for 25%

profile of v12, /device:TPU:0, one launch (start us, length us, event | category | flops | bytes accessed | tf_op | source)
XLA Modules:
  0.0 74.3 jit_solution(15883372993022526160)
XLA Ops:
  0.6 1.5 %prepare.1 = (f32[1024,256]{1,0:T(8,128)S(1)}, bf16[64,512]{1,0:T(8,128)(2,1)S(1)}, f32[2,512]{1,0:T(2,128)S(1)}, bf16[64,1024]{1,0:T(8,128)(2,1)S(1)}, bf16[64,...) custom-call(f32[1024,256]{1,0:T(8,128)} %load.1, bf16[64,512]{1,0:T(8,128)(2,1)} %rows.1, f32[2,512]{1,0:T(2,128)} %weight.1, ...), custom_call_target="tpu_custom_call" | custom-call | tf_op jit(solution)/shard_map/prepare/pallas_call | solution.py:161
  2.2 0.3 halo_message.1
  2.4 0.5 collective-permute-start
  2.9 3.7 %collective-permute-start.3 = (bf16[64,256]{1,0:T(8,128)(2,1)S(1)}, bf16[64,256]{1,0:T(8,128)(2,1)S(1)}, u32[]{:S(2)}, u32[]{:S(2)}) collective-permute-start(bf16[64,256]{1,0:T(8,128)(2,1)S(1)} %get-tuple-element.75), channel_id=1, source_target_pairs={{0,8},{1,9},{2,10},{3,11},{4,12},{5,13},{6,14},{7,15},{8,0},{9,1},... | collective-permute-start | bytes 98312 | tf_op jit(solution)/shard_map/ppermute | solution.py:23
  6.6 1.9 %collective-permute-done.3 = bf16[64,256]{1,0:T(8,128)(2,1)S(1)} collective-permute-done((bf16[64,256]{1,0:T(8,128)(2,1)S(1)}, bf16[64,256]{1,0:T(8,128)(2,1)S(1)}, u32[]{:S(2)}, u32[]{:S(2)}) %collective-permute-start.3) | collective-permute-done | bytes 32800 | tf_op jit(solution)/shard_map/ppermute | solution.py:23
  8.5 6.5 %collective-permute-start.4 = (bf16[128,256]{1,0:T(8,128)(2,1)S(1)}, bf16[128,256]{1,0:T(8,128)(2,1)S(1)}, u32[]{:S(2)}, u32[]{:S(2)}) collective-permute-start(bf16[128,256]{1,0:T(8,128)(2,1)S(1)} %pad_maximum_fusion.4), channel_id=1, source_target_pairs={{0,2},{1,3},{2,0},{3,1},{4,6},{5,7},{6,4},{7,5},{8,10},{9,11},{10,... | collective-permute-start | bytes 196616 | tf_op jit(solution)/shard_map/ppermute | solution.py:23
  15.0 3.5 %fetch.1 = (bf16[2048,1024]{1,0:T(8,128)(2,1)S(1)}, bf16[2048,1024]{1,0:T(8,128)(2,1)S(1)}) custom-call(bf16[2048,1024]{1,0:T(8,128)(2,1)} %neumann, bf16[2048,1024]{1,0:T(8,128)(2,1)} %schur), custom_call_target="tpu_custom_call" | custom-call | tf_op jit(solution)/shard_map/fetch/pallas_call | solution.py:161
  18.5 1.0 %load_outer.1 = (f32[1024,256]{1,0:T(8,128)S(1)}, bf16[512,256]{1,0:T(8,128)(2,1)S(1)}, bf16[512,256]{1,0:T(8,128)(2,1)S(1)}) custom-call(f32[1024,256]{1,0:T(8,128)S(1)} %get-tuple-element.60.load, f32[2,512]{1,0:T(2,128)S(1)} %get-tuple-element.61.weight, bf16[720,256]{1,0:T(8,128)(2,1)S(1)} %collective-permute-done.message, ...), custom_call_target="tpu_custom_call" | custom-call | tf_op jit(solution)/shard_map/load_outer/pallas_call | solution.py:161
  19.6 0.0 collective-permute-done.4
  19.6 0.1 collective-permute-start.5
  19.7 1.1 %collective-permute-start.2 = (bf16[512,256]{1,0:T(8,128)(2,1)S(1)}, bf16[512,256]{1,0:T(8,128)(2,1)S(1)}, u32[]{:S(2)}, u32[]{:S(2)}) collective-permute-start(bf16[512,256]{1,0:T(8,128)(2,1)S(1)} %get-tuple-element.68), channel_id=1, source_target_pairs={{0,15},{1,2},{2,1},{3,4},{4,3},{5,6},{6,5},{7,8},{8,7},{9,10},{10,... | collective-permute-start | bytes 786440 | tf_op jit(solution)/shard_map/ppermute | solution.py:28
  20.8 1.0 %load_inner.1.inner = f32[512,256]{1,0:T(8,128)S(1)} custom-call(f32[1024,256]{1,0:T(8,128)S(1)} %get-tuple-element.60.load, f32[2,512]{1,0:T(2,128)S(1)} %get-tuple-element.61.weight, bf16[720,256]{1,0:T(8,128)(2,1)S(1)} %collective-permute-done.message, bf16[2048,1024]{1,0:T(8,128)(2,1)S(1)} %get-tuple-element.66.neumann), custom_call_target="tpu_custom_call" | custom-call | tf_op jit(solution)/shard_map/load_inner/pallas_call | solution.py:161
  21.8 0.1 collective-permute-start.1
  21.9 1.9 %static_basis.1 = (bf16[2048,64]{1,0:T(8,128)(2,1)S(1)}, bf16[2048,64]{1,0:T(8,128)(2,1)S(1)}, bf16[128,1024]{1,0:T(8,128)(2,1)S(1)}, bf16[128,1024]{1,0:T(8,128)(2,1)S(1)}, f32[128,128]{1,0:T(8,128)S(1)}) custom-call(bf16[2048,1024]{1,0:T(8,128)(2,1)S(1)} %get-tuple-element.71.schur, bf16[720,256]{1,0:T(8,128)(2,1)S(1)} %collective-permute-done.message, ...), custom_call_target="tpu_custom_call" | custom-call | tf_op jit(solution)/shard_map/static_basis/pallas_call | solution.py:161
  23.8 1.1 %collective-permute-done.5 = bf16[256,256]{1,0:T(8,128)(2,1)S(1)} collective-permute-done((bf16[256,256]{1,0:T(8,128)(2,1)S(1)}, bf16[256,256]{1,0:T(8,128)(2,1)S(1)}, u32[]{:S(2)}, u32[]{:S(2)}) %collective-permute-start.5) | collective-permute-done | bytes 131104 | tf_op jit(solution)/shard_map/ppermute | solution.py:23
  24.9 0.1 collective-permute-start.6
  25.0 3.3 %collective-permute-done.2.far = bf16[512,256]{1,0:T(8,128)(2,1)S(1)} collective-permute-done((bf16[512,256]{1,0:T(8,128)(2,1)S(1)}, bf16[512,256]{1,0:T(8,128)(2,1)S(1)}, u32[]{:S(2)}, u32[]{:S(2)}) %collective-permute-start.2) | collective-permute-done | bytes 262176 | tf_op jit(solution)/shard_map/ppermute | solution.py:28
  28.3 1.6 %coarse_load.1 = (f32[1536,256]{1,0:T(8,128)S(1)}, bf16[96,256]{1,0:T(8,128)(2,1)S(1)}, f32[96,256]{1,0:T(8,128)S(1)}, f32[96,256]{1,0:T(8,128)S(1)}, f32[8,256]{1,0:T(8,128)S(1)}) custom-call(f32[1024,256]{1,0:T(8,128)S(1)} %get-tuple-element.60.load, f32[1024,256]{1,0:T(8,128)S(1)} %get-tuple-element.67.outer, f32[512,256]{1,0:T(8,128)S(1)} %load_inner.1.inner, ...), custom_call_target="tpu_custom_call" | custom-call | tf_op jit(solution)/shard_map/coarse_load/pallas_call | solution.py:161
  30.0 0.1 collective-permute-start.7
  30.0 1.8 %schur_outer.1 = (f32[1024,256]{1,0:T(8,128)S(1)}, bf16[512,256]{1,0:T(8,128)(2,1)S(1)}, bf16[512,256]{1,0:T(8,128)(2,1)S(1)}, f32[8,256]{1,0:T(8,128)S(1)}) custom-call(f32[1536,256]{1,0:T(8,128)S(1)} %get-tuple-element.81.local.z_local, bf16[2048,1024]{1,0:T(8,128)(2,1)S(1)} %get-tuple-element.71.schur, bf16[2048,64]{1,0:T(8,128)(2,1)S(1)} %get-tuple-element.82.basis_high, ...), custom_call_target="tpu_custom_call" | custom-call | tf_op jit(solution)/shard_map/schur_outer/pallas_call | solution.py:161
  31.8 1.8 %collective-permute-start.10 = (bf16[512,256]{1,0:T(8,128)(2,1)S(1)}, bf16[512,256]{1,0:T(8,128)(2,1)S(1)}, u32[]{:S(2)}, u32[]{:S(2)}) collective-permute-start(bf16[512,256]{1,0:T(8,128)(2,1)S(1)} %get-tuple-element.90), channel_id=1, source_target_pairs={{0,15},{1,2},{2,1},{3,4},{4,3},{5,6},{6,5},{7,8},{8,7},{9,10},{10,... | collective-permute-start | bytes 786440 | tf_op jit(solution)/shard_map/ppermute | solution.py:28
  33.7 0.2 collective-permute-start.9
  33.8 1.8 %schur_inner.1 = (f32[512,256]{1,0:T(8,128)S(1)}, f32[1,256]{1,0:T(1,128)S(1)}) custom-call(f32[1536,256]{1,0:T(8,128)S(1)} %get-tuple-element.81.local.z_local, bf16[2048,1024]{1,0:T(8,128)(2,1)S(1)} %get-tuple-element.71.schur, bf16[2048,64]{1,0:T(8,128)(2,1)S(1)} %get-tuple-element.82.basis_high, bf16[2048,64]{1,0:T(8,128)(2,1)S(1)} %get-tuple-element.83.basis_low, ...), custom_call_target="tpu_custom_call" | custom-call | tf_op jit(solution)/shard_map/schur_inner/pallas_call | solution.py:161
  35.6 0.1 collective-permute-done.7
  35.7 0.4 collective-permute-start.8
  36.0 4.4 %collective-permute-done.10.far_in = bf16[512,256]{1,0:T(8,128)(2,1)S(1)} collective-permute-done((bf16[512,256]{1,0:T(8,128)(2,1)S(1)}, bf16[512,256]{1,0:T(8,128)(2,1)S(1)}, u32[]{:S(2)}, u32[]{:S(2)}) %collective-permute-start.10) | collective-permute-done | bytes 262176 | tf_op jit(solution)/shard_map/ppermute | solution.py:28
  40.5 0.0 collective-permute-done.9.near_in
  40.5 1.2 %image_outer.1 = (f32[1024,256]{1,0:T(8,128)S(1)}, bf16[512,256]{1,0:T(8,128)(2,1)S(1)}, bf16[512,256]{1,0:T(8,128)(2,1)S(1)}) custom-call(f32[1024,256]{1,0:T(8,128)S(1)} %get-tuple-element.94.outer_in, f32[512,256]{1,0:T(8,128)S(1)} %get-tuple-element.85.inner_in, bf16[512,256]{1,0:T(8,128)(2,1)S(1)} %collective-permute-done.9.near_in, ...), custom_call_target="tpu_custom_call" | custom-call | tf_op jit(solution)/shard_map/image_outer/pallas_call | solution.py:161
  41.7 1.8 %collective-permute-start.13 = (bf16[512,256]{1,0:T(8,128)(2,1)S(1)}, bf16[512,256]{1,0:T(8,128)(2,1)S(1)}, u32[]{:S(2)}, u32[]{:S(2)}) collective-permute-start(bf16[512,256]{1,0:T(8,128)(2,1)S(1)} %get-tuple-element.91), channel_id=1, source_target_pairs={{0,15},{1,2},{2,1},{3,4},{4,3},{5,6},{6,5},{7,8},{8,7},{9,10},{10,... | collective-permute-start | bytes 786440 | tf_op jit(solution)/shard_map/ppermute | solution.py:28
  43.5 1.2 %collective-permute-start.12 = (bf16[512,256]{1,0:T(8,128)(2,1)S(1)}, bf16[512,256]{1,0:T(8,128)(2,1)S(1)}, u32[]{:S(2)}, u32[]{:S(2)}) collective-permute-start(bf16[512,256]{1,0:T(8,128)(2,1)S(1)} %get-tuple-element.93), channel_id=1, source_target_pairs={{0,1},{1,0},{2,3},{3,2},{4,5},{5,4},{6,7},{7,6},{8,9},{9,8},{10,11... | collective-permute-start | bytes 786440 | tf_op jit(solution)/shard_map/ppermute | solution.py:23
  44.7 0.1 collective-permute-start.11
  44.8 1.2 %image_inner.1 = (f32[1024,256]{1,0:T(8,128)S(1)}, f32[512,256]{1,0:T(8,128)S(1)}) custom-call(f32[1024,256]{1,0:T(8,128)S(1)} %get-tuple-element.94.outer_in, f32[512,256]{1,0:T(8,128)S(1)} %get-tuple-element.85.inner_in, bf16[512,256]{1,0:T(8,128)(2,1)S(1)} %collective-permute-done.9.near_in, bf16[512,256]{1,0:T(8,128)(2,1)S(1)} %collective-permute-done.10.far_in, ...), custom_call_target="tpu_custom_call" | custom-call | tf_op jit(solution)/shard_map/image_inner/pallas_call | solution.py:161
  46.0 5.6 %collective-permute-done.11 = bf16[384,256]{1,0:T(8,128)(2,1)S(1)} collective-permute-done((bf16[384,256]{1,0:T(8,128)(2,1)S(1)}, bf16[384,256]{1,0:T(8,128)(2,1)S(1)}, u32[]{:S(2)}, u32[]{:S(2)}) %collective-permute-start.11) | collective-permute-done | bytes 196640 | tf_op jit(solution)/shard_map/ppermute | solution.py:23
  51.6 0.0 collective-permute-done.13.far
  51.6 0.2 collective-permute-start.14
  51.8 3.7 %schur_image.1 = (f32[1536,256]{1,0:T(8,128)S(1)}, f32[1536,256]{1,0:T(8,128)S(1)}, f32[8,256]{1,0:T(8,128)S(1)}, f32[128,256]{1,0:T(8,128)S(1)}) custom-call(f32[1024,256]{1,0:T(8,128)S(1)} %get-tuple-element.98.image, f32[1024,256]{1,0:T(8,128)S(1)} %get-tuple-element.100.outer, f32[512,256]{1,0:T(8,128)S(1)} %get-tuple-element.95.inner, ...), custom_call_target="tpu_custom_call" | custom-call | tf_op jit(solution)/shard_map/schur_image/pallas_call | solution.py:161
  55.5 0.8 %coarse_image.1 = (f32[4,256]{1,0:T(4,128)S(1)}, f32[96,256]{1,0:T(8,128)S(1)}) custom-call(bf16[768,256]{1,0:T(8,128)(2,1)S(1)} %constant_dynamic-update-slice_fusion.half, bf16[768,256]{1,0:T(8,128)(2,1)S(1)} %collective-permute-done.14.crossed_half, bf16[64,1024]{1,0:T(8,128)(2,1)S(1)} %get-tuple-element.63.inverse, ...), custom_call_target="tpu_custom_call" | custom-call | tf_op jit(solution)/shard_map/coarse_image/pallas_call | solution.py:161
  56.4 2.6 %collective-permute-start.15 = (f32[4,256]{1,0:T(4,128)S(1)}, f32[4,256]{1,0:T(4,128)S(1)}, u32[]{:S(2)}, u32[]{:S(2)}) collective-permute-start(f32[4,256]{1,0:T(4,128)S(1)} %get-tuple-element.105), channel_id=1, source_target_pairs={{0,8},{1,9},{2,10},{3,11},{4,12},{5,13},{6,14},{7,15},{8,0},{9,1},... | collective-permute-start | bytes 12296 | tf_op jit(solution)/shard_map/ppermute | solution.py:23
  58.9 1.5 %complete.1 = (f32[1024,256]{1,0:T(8,128)S(1)}, f32[1024,256]{1,0:T(8,128)S(1)}, f32[1024,256]{1,0:T(8,128)S(1)}, bf16[512,256]{1,0:T(8,128)(2,1)S(1)}) custom-call(f32[1536,256]{1,0:T(8,128)S(1)} %get-tuple-element.81.local.z_local, f32[96,256]{1,0:T(8,128)S(1)} %get-tuple-element.84.solution.z_coarse, f32[1536,256]{1,0:T(8,128)S(1)} %get-tuple-element.106.y_local, ...), custom_call_target="tpu_custom_call" | custom-call | tf_op jit(solution)/shard_map/complete/pallas_call | solution.py:161
  60.5 0.5 collective-permute-done.15
  61.0 3.2 %collective-permute-start.16 = (f32[4,256]{1,0:T(4,128)S(1)}, f32[4,256]{1,0:T(4,128)S(1)}, u32[]{:S(2)}, u32[]{:S(2)}) collective-permute-start(f32[4,256]{1,0:T(4,128)S(1)} %add.12), channel_id=1, source_target_pairs={{0,2},{1,3},{2,0},{3,1},{4,6},{5,7},{6,4},{7,5},{8,10},{9,11},{10,... | collective-permute-start | bytes 12296 | tf_op jit(solution)/shard_map/ppermute | solution.py:23
  64.1 1.6 %collective-permute-done.16 = f32[4,256]{1,0:T(4,128)S(1)} collective-permute-done((f32[4,256]{1,0:T(4,128)S(1)}, f32[4,256]{1,0:T(4,128)S(1)}, u32[]{:S(2)}, u32[]{:S(2)}) %collective-permute-start.16) | collective-permute-done | bytes 4128 | tf_op jit(solution)/shard_map/ppermute | solution.py:23
  65.7 0.8 %collective-permute-start.19 = (bf16[512,256]{1,0:T(8,128)(2,1)S(1)}, bf16[512,256]{1,0:T(8,128)(2,1)S(1)}, u32[]{:S(2)}, u32[]{:S(2)}) collective-permute-start(bf16[512,256]{1,0:T(8,128)(2,1)S(1)} %get-tuple-element.117), channel_id=1, source_target_pairs={{1,0},{2,1},{3,2},{4,3},{5,4},{6,5},{7,6},{8,7},{9,8},{10,9},{11,1... | collective-permute-start | bytes 786440 | tf_op jit(solution)/shard_map/ppermute | solution.py:19
  66.5 0.5 collective-permute-start.17
  67.0 4.4 %collective-permute-done.17 = f32[4,256]{1,0:T(4,128)S(1)} collective-permute-done((f32[4,256]{1,0:T(4,128)S(1)}, f32[4,256]{1,0:T(4,128)S(1)}, u32[]{:S(2)}, u32[]{:S(2)}) %collective-permute-start.17) | collective-permute-done | bytes 4128 | tf_op jit(solution)/shard_map/ppermute | solution.py:23
  71.5 0.0 collective-permute-start.18
  71.5 1.2 %collective-permute-done.18 = f32[4,256]{1,0:T(4,128)S(1)} collective-permute-done((f32[4,256]{1,0:T(4,128)S(1)}, f32[4,256]{1,0:T(4,128)S(1)}, u32[]{:S(2)}, u32[]{:S(2)}) %collective-permute-start.18) | collective-permute-done | bytes 4128 | tf_op jit(solution)/shard_map/ppermute | solution.py:23
  72.6 1.6 %combine.1 = (f32[1024,256]{1,0:T(8,128)}, f32[1024,256]{1,0:T(8,128)}) custom-call(f32[4,256]{1,0:T(4,128)S(1)} %add.15.sums, f32[1024,256]{1,0:T(8,128)S(1)} %get-tuple-element.60.load, f32[1024,256]{1,0:T(8,128)S(1)} %get-tuple-element.114.z, f32[1024,256]{1,0:T(8,128)S(1)} %get-tuple-element.109.y, f32[1024,256]{1,0:T(8,128)S(1)} %get-tuple-element.98.image, ...), custom_call_target="tpu_custom_call" | custom-call | tf_op jit(solution)/shard_map/combine/pallas_call | solution.py:161
  (20 shorter events, 0.1 us)
Async XLA Ops:
  2.4 16.1 %collective-permute-start = (bf16[720,256]{1,0:T(8,128)(2,1)S(1)}, bf16[720,256]{1,0:T(8,128)(2,1)S(1)}, u32[]{:S(2)}, u32[]{:S(2)}) collective-permute-start(bf16[720,256]{1,0:T(8,128)(2,1)S(1)} %halo_message.1), channel_id=1, source_target_pairs={{15,0},{0,1},{1,2},{2,3},{3,4},{4,5},{5,6},{6,7},{7,8},{8,9},{9,10... | collective-permute-start | bytes 1105928 | tf_op jit(solution)/shard_map/ppermute | solution.py:19
  2.9 5.6 %collective-permute-start.3 = (bf16[64,256]{1,0:T(8,128)(2,1)S(1)}, bf16[64,256]{1,0:T(8,128)(2,1)S(1)}, u32[]{:S(2)}, u32[]{:S(2)}) collective-permute-start(bf16[64,256]{1,0:T(8,128)(2,1)S(1)} %get-tuple-element.75), channel_id=1, source_target_pairs={{0,8},{1,9},{2,10},{3,11},{4,12},{5,13},{6,14},{7,15},{8,0},{9,1},... | collective-permute-start | bytes 98312 | tf_op jit(solution)/shard_map/ppermute | solution.py:23
  8.5 11.1 %collective-permute-start.4 = (bf16[128,256]{1,0:T(8,128)(2,1)S(1)}, bf16[128,256]{1,0:T(8,128)(2,1)S(1)}, u32[]{:S(2)}, u32[]{:S(2)}) collective-permute-start(bf16[128,256]{1,0:T(8,128)(2,1)S(1)} %pad_maximum_fusion.4), channel_id=1, source_target_pairs={{0,2},{1,3},{2,0},{3,1},{4,6},{5,7},{6,4},{7,5},{8,10},{9,11},{10,... | collective-permute-start | bytes 196616 | tf_op jit(solution)/shard_map/ppermute | solution.py:23
  19.6 5.3 %collective-permute-start.5 = (bf16[256,256]{1,0:T(8,128)(2,1)S(1)}, bf16[256,256]{1,0:T(8,128)(2,1)S(1)}, u32[]{:S(2)}, u32[]{:S(2)}) collective-permute-start(bf16[256,256]{1,0:T(8,128)(2,1)S(1)} %pad_maximum_fusion.2), channel_id=1, source_target_pairs={{0,4},{1,5},{2,6},{3,7},{4,0},{5,1},{6,2},{7,3},{8,12},{9,13},{10,... | collective-permute-start | bytes 393224 | tf_op jit(solution)/shard_map/ppermute | solution.py:23
  19.7 8.7 %collective-permute-start.2 = (bf16[512,256]{1,0:T(8,128)(2,1)S(1)}, bf16[512,256]{1,0:T(8,128)(2,1)S(1)}, u32[]{:S(2)}, u32[]{:S(2)}) collective-permute-start(bf16[512,256]{1,0:T(8,128)(2,1)S(1)} %get-tuple-element.68), channel_id=1, source_target_pairs={{0,15},{1,2},{2,1},{3,4},{4,3},{5,6},{6,5},{7,8},{8,7},{9,10},{10,... | collective-permute-start | bytes 786440 | tf_op jit(solution)/shard_map/ppermute | solution.py:28
  21.8 6.5 %collective-permute-start.1 = (bf16[512,256]{1,0:T(8,128)(2,1)S(1)}, bf16[512,256]{1,0:T(8,128)(2,1)S(1)}, u32[]{:S(2)}, u32[]{:S(2)}) collective-permute-start(bf16[512,256]{1,0:T(8,128)(2,1)S(1)} %get-tuple-element.70), channel_id=1, source_target_pairs={{0,1},{1,0},{2,3},{3,2},{4,5},{5,4},{6,7},{7,6},{8,9},{9,8},{10,11... | collective-permute-start | bytes 786440 | tf_op jit(solution)/shard_map/ppermute | solution.py:23
  24.9 3.4 %collective-permute-start.6 = (bf16[512,256]{1,0:T(8,128)(2,1)S(1)}, bf16[512,256]{1,0:T(8,128)(2,1)S(1)}, u32[]{:S(2)}, u32[]{:S(2)}) collective-permute-start(bf16[512,256]{1,0:T(8,128)(2,1)S(1)} %pad_maximum_fusion.half), channel_id=1, source_target_pairs={{0,1},{1,0},{2,3},{3,2},{4,5},{5,4},{6,7},{7,6},{8,9},{9,8},{10,11... | collective-permute-start | bytes 786440 | tf_op jit(solution)/shard_map/ppermute | solution.py:23
  30.0 5.7 %collective-permute-start.7 = (bf16[96,256]{1,0:T(8,128)(2,1)S(1)}, bf16[96,256]{1,0:T(8,128)(2,1)S(1)}, u32[]{:S(2)}, u32[]{:S(2)}) collective-permute-start(bf16[96,256]{1,0:T(8,128)(2,1)S(1)} %get-tuple-element.80), channel_id=1, source_target_pairs={{0,8},{1,9},{2,10},{3,11},{4,12},{5,13},{6,14},{7,15},{8,0},{9,1},... | collective-permute-start | bytes 147464 | tf_op jit(solution)/shard_map/ppermute | solution.py:23
  31.8 8.7 %collective-permute-start.10 = (bf16[512,256]{1,0:T(8,128)(2,1)S(1)}, bf16[512,256]{1,0:T(8,128)(2,1)S(1)}, u32[]{:S(2)}, u32[]{:S(2)}) collective-permute-start(bf16[512,256]{1,0:T(8,128)(2,1)S(1)} %get-tuple-element.90), channel_id=1, source_target_pairs={{0,15},{1,2},{2,1},{3,4},{4,3},{5,6},{6,5},{7,8},{8,7},{9,10},{10,... | collective-permute-start | bytes 786440 | tf_op jit(solution)/shard_map/ppermute | solution.py:28
  33.7 6.8 %collective-permute-start.9 = (bf16[512,256]{1,0:T(8,128)(2,1)S(1)}, bf16[512,256]{1,0:T(8,128)(2,1)S(1)}, u32[]{:S(2)}, u32[]{:S(2)}) collective-permute-start(bf16[512,256]{1,0:T(8,128)(2,1)S(1)} %get-tuple-element.89), channel_id=1, source_target_pairs={{0,1},{1,0},{2,3},{3,2},{4,5},{5,4},{6,7},{7,6},{8,9},{9,8},{10,11... | collective-permute-start | bytes 786440 | tf_op jit(solution)/shard_map/ppermute | solution.py:23
  35.7 7.8 %collective-permute-start.8 = (bf16[192,256]{1,0:T(8,128)(2,1)S(1)}, bf16[192,256]{1,0:T(8,128)(2,1)S(1)}, u32[]{:S(2)}, u32[]{:S(2)}) collective-permute-start(bf16[192,256]{1,0:T(8,128)(2,1)S(1)} %pad_maximum_fusion.3), channel_id=1, source_target_pairs={{0,2},{1,3},{2,0},{3,1},{4,6},{5,7},{6,4},{7,5},{8,10},{9,11},{10,... | collective-permute-start | bytes 294920 | tf_op jit(solution)/shard_map/ppermute | solution.py:23
  41.7 9.9 %collective-permute-start.13 = (bf16[512,256]{1,0:T(8,128)(2,1)S(1)}, bf16[512,256]{1,0:T(8,128)(2,1)S(1)}, u32[]{:S(2)}, u32[]{:S(2)}) collective-permute-start(bf16[512,256]{1,0:T(8,128)(2,1)S(1)} %get-tuple-element.91), channel_id=1, source_target_pairs={{0,15},{1,2},{2,1},{3,4},{4,3},{5,6},{6,5},{7,8},{8,7},{9,10},{10,... | collective-permute-start | bytes 786440 | tf_op jit(solution)/shard_map/ppermute | solution.py:28
  43.5 8.1 %collective-permute-start.12 = (bf16[512,256]{1,0:T(8,128)(2,1)S(1)}, bf16[512,256]{1,0:T(8,128)(2,1)S(1)}, u32[]{:S(2)}, u32[]{:S(2)}) collective-permute-start(bf16[512,256]{1,0:T(8,128)(2,1)S(1)} %get-tuple-element.93), channel_id=1, source_target_pairs={{0,1},{1,0},{2,3},{3,2},{4,5},{5,4},{6,7},{7,6},{8,9},{9,8},{10,11... | collective-permute-start | bytes 786440 | tf_op jit(solution)/shard_map/ppermute | solution.py:23
  44.7 6.9 %collective-permute-start.11 = (bf16[384,256]{1,0:T(8,128)(2,1)S(1)}, bf16[384,256]{1,0:T(8,128)(2,1)S(1)}, u32[]{:S(2)}, u32[]{:S(2)}) collective-permute-start(bf16[384,256]{1,0:T(8,128)(2,1)S(1)} %pad_maximum_fusion.1), channel_id=1, source_target_pairs={{0,4},{1,5},{2,6},{3,7},{4,0},{5,1},{6,2},{7,3},{8,12},{9,13},{10,... | collective-permute-start | bytes 589832 | tf_op jit(solution)/shard_map/ppermute | solution.py:23
  51.6 3.9 %collective-permute-start.14 = (bf16[768,256]{1,0:T(8,128)(2,1)S(1)}, bf16[768,256]{1,0:T(8,128)(2,1)S(1)}, u32[]{:S(2)}, u32[]{:S(2)}) collective-permute-start(bf16[768,256]{1,0:T(8,128)(2,1)S(1)} %constant_dynamic-update-slice_fusion.half), channel_id=1, source_target_pairs={{0,1},{1,0},{2,3},{3,2},{4,5},{5,4},{6,7},{7,6},{8,9},{9,8},{10,11... | collective-permute-start | bytes 1179656 | tf_op jit(solution)/shard_map/ppermute | solution.py:23
  56.4 4.6 %collective-permute-start.15 = (f32[4,256]{1,0:T(4,128)S(1)}, f32[4,256]{1,0:T(4,128)S(1)}, u32[]{:S(2)}, u32[]{:S(2)}) collective-permute-start(f32[4,256]{1,0:T(4,128)S(1)} %get-tuple-element.105), channel_id=1, source_target_pairs={{0,8},{1,9},{2,10},{3,11},{4,12},{5,13},{6,14},{7,15},{8,0},{9,1},... | collective-permute-start | bytes 12296 | tf_op jit(solution)/shard_map/ppermute | solution.py:23
  61.0 4.8 %collective-permute-start.16 = (f32[4,256]{1,0:T(4,128)S(1)}, f32[4,256]{1,0:T(4,128)S(1)}, u32[]{:S(2)}, u32[]{:S(2)}) collective-permute-start(f32[4,256]{1,0:T(4,128)S(1)} %add.12), channel_id=1, source_target_pairs={{0,2},{1,3},{2,0},{3,1},{4,6},{5,7},{6,4},{7,5},{8,10},{9,11},{10,... | collective-permute-start | bytes 12296 | tf_op jit(solution)/shard_map/ppermute | solution.py:23
  65.7 6.9 %collective-permute-start.19 = (bf16[512,256]{1,0:T(8,128)(2,1)S(1)}, bf16[512,256]{1,0:T(8,128)(2,1)S(1)}, u32[]{:S(2)}, u32[]{:S(2)}) collective-permute-start(bf16[512,256]{1,0:T(8,128)(2,1)S(1)} %get-tuple-element.117), channel_id=1, source_target_pairs={{1,0},{2,1},{3,2},{4,3},{5,4},{6,5},{7,6},{8,7},{9,8},{10,9},{11,1... | collective-permute-start | bytes 786440 | tf_op jit(solution)/shard_map/ppermute | solution.py:19
  66.5 4.9 %collective-permute-start.17 = (f32[4,256]{1,0:T(4,128)S(1)}, f32[4,256]{1,0:T(4,128)S(1)}, u32[]{:S(2)}, u32[]{:S(2)}) collective-permute-start(f32[4,256]{1,0:T(4,128)S(1)} %add.13), channel_id=1, source_target_pairs={{0,4},{1,5},{2,6},{3,7},{4,0},{5,1},{6,2},{7,3},{8,12},{9,13},{10,... | collective-permute-start | bytes 12296 | tf_op jit(solution)/shard_map/ppermute | solution.py:23
  71.5 1.2 %collective-permute-start.18 = (f32[4,256]{1,0:T(4,128)S(1)}, f32[4,256]{1,0:T(4,128)S(1)}, u32[]{:S(2)}, u32[]{:S(2)}) collective-permute-start(f32[4,256]{1,0:T(4,128)S(1)} %add.14), channel_id=1, source_target_pairs={{0,1},{1,0},{2,3},{3,2},{4,5},{5,4},{6,7},{7,6},{8,9},{9,8},{10,11... | collective-permute-start | bytes 12296 | tf_op jit(solution)/shard_map/ppermute | solution.py:23

commit v13 on v12

--- a/solution.py
+++ b/solution.py
@@ -511,12 +511,12 @@
         bind(halo_message), [((halo.height, columns), BF16)], load, weight, rows, inverse,
         scratch=[pltpu.VMEM((halo.weight_count, columns), F32)],
     )
-    half = gather_half(coarse_rounded, early[:1])
     tied = after(tuple(map(outside, (neumann, schur))), message)
     neumann, schur = stage(
         bind(fetch), [described(array) for array in tied], *tied, scratch=semaphores(2), fetched=2
     )
     message = shifted(message, 1)
+    half = gather_half(coarse_rounded, early[:1], neumann)
     outside_faces = [((2 * nf, columns), F32)] + 2 * [((nf, columns), BF16)]
     inside_faces = [(((subs - 1) * nf, columns), F32)]
     outer, near, far = stage(bind(load_outer), outside_faces, load, weight, message, neumann)
@@ -538,10 +538,10 @@
     outer, near, far, sums = stage(
         bind(schur_outer), outside_faces + [sum_rows], z_local, schur, basis_high, basis_low, z_coarse, sums
     )
+    half = gather_half(shares_rounded, early[:1], far)
     inner, energies = stage(
-        bind(schur_inner), inside_faces + [((subs - 1, columns), F32)], z_local, schur, basis_high, basis_low, z_coarse
-    )
-    half = gather_half(shares_rounded, early[:1], inner)
+        bind(schur_inner), inside_faces + [((subs - 1, columns), F32)], after(z_local, half), schur, basis_high, basis_low, z_coarse
+    )
     far, near = far_block(far), crossed(near, 1)
     operands = outer, inner, near, far, weight, message, neumann
     outer, near, far = stage(bind(image_outer), outside_faces, *operands)

time: 74.4 us -> 75.8 us (1.019)
  starting transfers between devices: 24.8 us -> 26.3 us
    ppermute x3, starting transfers between devices: 4.79 us -> 11.4 us  [far_block(): lax.ppermute(block, AXIS, [(i, (i + (1 if i % 2 else -1)) % n) for i in r...]
    ppermute x15, starting transfers between devices: 18.7 us -> 13.5 us  [crossed(): lax.ppermute(block, AXIS, [(i, i ^ bit) for i in range(lax.axis_size(AXIS...]
    ppermute x3, waiting for transfers between devices: 7.79 us -> 5.53 us  [far_block(): lax.ppermute(block, AXIS, [(i, (i + (1 if i % 2 else -1)) % n) for i in r...]
    ppermute x15, waiting for transfers between devices: 16.3 us -> 18.4 us  [crossed(): lax.ppermute(block, AXIS, [(i, i ^ bit) for i in range(lax.axis_size(AXIS...]
  transfers between devices with their start and end apart: 20 -> 20, of which waited for: 10 -> 8; matrix products, arithmetic and copies ran while one was open for 0% -> 0% of each run, Pallas kernels for 25% -> 25%
where the time goes in v13:
time: 75.8 us; the launch traced here: 75.6 us
  starting transfers between devices  26.3 us (35%)
  Pallas kernels  24.4 us (32%)
  waiting for transfers between devices  23.9 us (32%)
  between operations  0.88 us (1%)
    pallas_call x15, Pallas kernels, stage(): return call(*operands)  24.4 us
    ppermute x15, waiting for transfers between devices, crossed(): lax.ppermute(block, AXIS, [(i, i ^ bit) for i in range(lax.axis_size(AXIS...  18.4 us
    ppermute x15, starting transfers between devices, crossed(): lax.ppermute(block, AXIS, [(i, i ^ bit) for i in range(lax.axis_size(AXIS...  13.5 us
    ppermute x3, starting transfers between devices, far_block(): lax.ppermute(block, AXIS, [(i, (i + (1 if i % 2 else -1)) % n) for i in r...  11.4 us
    ppermute x3, waiting for transfers between devices, far_block(): lax.ppermute(block, AXIS, [(i, (i + (1 if i % 2 else -1)) % n) for i in r...  5.53 us
  transfers between devices with their start and end apart: 20, of which 8 were waited for; matrix products, arithmetic and copies ran while one was open for 0% of the time, Pallas kernels for 25%

profile of v13, /device:TPU:0, one launch (start us, length us, event | category | flops | bytes accessed | tf_op | source)
XLA Modules:
  0.0 75.6 jit_solution(11704227592192296916)
XLA Ops:
  0.6 1.5 %prepare.1 = (f32[1024,256]{1,0:T(8,128)S(1)}, bf16[64,512]{1,0:T(8,128)(2,1)S(1)}, f32[2,512]{1,0:T(2,128)S(1)}, bf16[64,1024]{1,0:T(8,128)(2,1)S(1)}, bf16[64,...) custom-call(f32[1024,256]{1,0:T(8,128)} %load.1, bf16[64,512]{1,0:T(8,128)(2,1)} %rows.1, f32[2,512]{1,0:T(2,128)} %weight.1, ...), custom_call_target="tpu_custom_call" | custom-call | tf_op jit(solution)/shard_map/prepare/pallas_call | solution.py:161
  2.2 0.3 halo_message.1
  2.4 0.5 collective-permute-start
  2.9 3.7 %collective-permute-start.3 = (bf16[64,256]{1,0:T(8,128)(2,1)S(1)}, bf16[64,256]{1,0:T(8,128)(2,1)S(1)}, u32[]{:S(2)}, u32[]{:S(2)}) collective-permute-start(bf16[64,256]{1,0:T(8,128)(2,1)S(1)} %get-tuple-element.77), channel_id=1, source_target_pairs={{0,8},{1,9},{2,10},{3,11},{4,12},{5,13},{6,14},{7,15},{8,0},{9,1},... | collective-permute-start | bytes 98312 | tf_op jit(solution)/shard_map/ppermute | solution.py:23
  6.6 3.5 %fetch.1 = (bf16[2048,1024]{1,0:T(8,128)(2,1)S(1)}, bf16[2048,1024]{1,0:T(8,128)(2,1)S(1)}) custom-call(bf16[2048,1024]{1,0:T(8,128)(2,1)} %neumann, bf16[2048,1024]{1,0:T(8,128)(2,1)} %schur), custom_call_target="tpu_custom_call" | custom-call | tf_op jit(solution)/shard_map/fetch/pallas_call | solution.py:161
  10.1 0.0 collective-permute-done.3
  10.1 4.9 %collective-permute-start.4 = (bf16[128,256]{1,0:T(8,128)(2,1)S(1)}, bf16[128,256]{1,0:T(8,128)(2,1)S(1)}, u32[]{:S(2)}, u32[]{:S(2)}) collective-permute-start(bf16[128,256]{1,0:T(8,128)(2,1)S(1)} %pad_maximum_fusion.2), channel_id=1, source_target_pairs={{0,2},{1,3},{2,0},{3,1},{4,6},{5,7},{6,4},{7,5},{8,10},{9,11},{10,... | collective-permute-start | bytes 196616 | tf_op jit(solution)/shard_map/ppermute | solution.py:23
  15.0 0.0 collective-permute-done.message
  15.0 1.0 %load_outer.1 = (f32[1024,256]{1,0:T(8,128)S(1)}, bf16[512,256]{1,0:T(8,128)(2,1)S(1)}, bf16[512,256]{1,0:T(8,128)(2,1)S(1)}) custom-call(f32[1024,256]{1,0:T(8,128)S(1)} %get-tuple-element.62.load, f32[2,512]{1,0:T(2,128)S(1)} %get-tuple-element.63.weight, bf16[720,256]{1,0:T(8,128)(2,1)S(1)} %collective-permute-done.message, ...), custom_call_target="tpu_custom_call" | custom-call | tf_op jit(solution)/shard_map/load_outer/pallas_call | solution.py:161
  16.1 1.3 %collective-permute-done.4 = bf16[128,256]{1,0:T(8,128)(2,1)S(1)} collective-permute-done((bf16[128,256]{1,0:T(8,128)(2,1)S(1)}, bf16[128,256]{1,0:T(8,128)(2,1)S(1)}, u32[]{:S(2)}, u32[]{:S(2)}) %collective-permute-start.4) | collective-permute-done | bytes 65568 | tf_op jit(solution)/shard_map/ppermute | solution.py:23
  17.4 0.1 collective-permute-start.5
  17.5 2.3 %collective-permute-start.2 = (bf16[512,256]{1,0:T(8,128)(2,1)S(1)}, bf16[512,256]{1,0:T(8,128)(2,1)S(1)}, u32[]{:S(2)}, u32[]{:S(2)}) collective-permute-start(bf16[512,256]{1,0:T(8,128)(2,1)S(1)} %get-tuple-element.70), channel_id=1, source_target_pairs={{0,15},{1,2},{2,1},{3,4},{4,3},{5,6},{6,5},{7,8},{8,7},{9,10},{10,... | collective-permute-start | bytes 786440 | tf_op jit(solution)/shard_map/ppermute | solution.py:28
  19.8 1.0 %load_inner.1.inner = f32[512,256]{1,0:T(8,128)S(1)} custom-call(f32[1024,256]{1,0:T(8,128)S(1)} %get-tuple-element.62.load, f32[2,512]{1,0:T(2,128)S(1)} %get-tuple-element.63.weight, bf16[720,256]{1,0:T(8,128)(2,1)S(1)} %collective-permute-done.message, bf16[2048,1024]{1,0:T(8,128)(2,1)S(1)} %get-tuple-element.68.neumann), custom_call_target="tpu_custom_call" | custom-call | tf_op jit(solution)/shard_map/load_inner/pallas_call | solution.py:161
  20.8 1.9 %static_basis.1 = (bf16[2048,64]{1,0:T(8,128)(2,1)S(1)}, bf16[2048,64]{1,0:T(8,128)(2,1)S(1)}, bf16[128,1024]{1,0:T(8,128)(2,1)S(1)}, bf16[128,1024]{1,0:T(8,128)(2,1)S(1)}, f32[128,128]{1,0:T(8,128)S(1)}) custom-call(bf16[2048,1024]{1,0:T(8,128)(2,1)S(1)} %get-tuple-element.73.schur, bf16[720,256]{1,0:T(8,128)(2,1)S(1)} %collective-permute-done.message, ...), custom_call_target="tpu_custom_call" | custom-call | tf_op jit(solution)/shard_map/static_basis/pallas_call | solution.py:161
  22.8 0.6 collective-permute-start.6
  23.4 0.0 collective-permute-done.1.near
  23.4 3.3 %collective-permute-done.2.far = bf16[512,256]{1,0:T(8,128)(2,1)S(1)} collective-permute-done((bf16[512,256]{1,0:T(8,128)(2,1)S(1)}, bf16[512,256]{1,0:T(8,128)(2,1)S(1)}, u32[]{:S(2)}, u32[]{:S(2)}) %collective-permute-start.2) | collective-permute-done | bytes 262176 | tf_op jit(solution)/shard_map/ppermute | solution.py:28
  26.7 1.6 %coarse_load.1 = (f32[1536,256]{1,0:T(8,128)S(1)}, bf16[96,256]{1,0:T(8,128)(2,1)S(1)}, f32[96,256]{1,0:T(8,128)S(1)}, f32[96,256]{1,0:T(8,128)S(1)}, f32[8,256]{1,0:T(8,128)S(1)}) custom-call(f32[1024,256]{1,0:T(8,128)S(1)} %get-tuple-element.62.load, f32[1024,256]{1,0:T(8,128)S(1)} %get-tuple-element.69.outer, f32[512,256]{1,0:T(8,128)S(1)} %load_inner.1.inner, ...), custom_call_target="tpu_custom_call" | custom-call | tf_op jit(solution)/shard_map/coarse_load/pallas_call | solution.py:161
  28.3 0.1 collective-permute-start.7
  28.4 1.8 %schur_outer.1 = (f32[1024,256]{1,0:T(8,128)S(1)}, bf16[512,256]{1,0:T(8,128)(2,1)S(1)}, bf16[512,256]{1,0:T(8,128)(2,1)S(1)}, f32[8,256]{1,0:T(8,128)S(1)}) custom-call(f32[1536,256]{1,0:T(8,128)S(1)} %get-tuple-element.92.local.z_local, bf16[2048,1024]{1,0:T(8,128)(2,1)S(1)} %get-tuple-element.73.schur, bf16[2048,64]{1,0:T(8,128)(2,1)S(1)} %get-tuple-element.85.basis_high, ...), custom_call_target="tpu_custom_call" | custom-call | tf_op jit(solution)/shard_map/schur_outer/pallas_call | solution.py:161
  30.1 0.5 collective-permute-start.9
  30.6 4.6 %collective-permute-start.10 = (bf16[512,256]{1,0:T(8,128)(2,1)S(1)}, bf16[512,256]{1,0:T(8,128)(2,1)S(1)}, u32[]{:S(2)}, u32[]{:S(2)}) collective-permute-start(bf16[512,256]{1,0:T(8,128)(2,1)S(1)} %get-tuple-element.89), channel_id=1, source_target_pairs={{0,15},{1,2},{2,1},{3,4},{4,3},{5,6},{6,5},{7,8},{8,7},{9,10},{10,... | collective-permute-start | bytes 786440 | tf_op jit(solution)/shard_map/ppermute | solution.py:28
  35.2 0.1 collective-permute-start.8
  35.3 1.8 %schur_inner.1 = (f32[512,256]{1,0:T(8,128)S(1)}, f32[1,256]{1,0:T(1,128)S(1)}) custom-call(f32[1536,256]{1,0:T(8,128)S(1)} %get-tuple-element.92.local.z_local, bf16[2048,1024]{1,0:T(8,128)(2,1)S(1)} %get-tuple-element.73.schur, bf16[2048,64]{1,0:T(8,128)(2,1)S(1)} %get-tuple-element.85.basis_high, bf16[2048,64]{1,0:T(8,128)(2,1)S(1)} %get-tuple-element.86.basis_low, ...), custom_call_target="tpu_custom_call" | custom-call | tf_op jit(solution)/shard_map/schur_inner/pallas_call | solution.py:161
  37.1 0.0 collective-permute-done.9.near_in
  37.1 2.3 %collective-permute-done.10.far_in = bf16[512,256]{1,0:T(8,128)(2,1)S(1)} collective-permute-done((bf16[512,256]{1,0:T(8,128)(2,1)S(1)}, bf16[512,256]{1,0:T(8,128)(2,1)S(1)}, u32[]{:S(2)}, u32[]{:S(2)}) %collective-permute-start.10) | collective-permute-done | bytes 262176 | tf_op jit(solution)/shard_map/ppermute | solution.py:28
  39.4 1.1 %image_outer.1 = (f32[1024,256]{1,0:T(8,128)S(1)}, bf16[512,256]{1,0:T(8,128)(2,1)S(1)}, bf16[512,256]{1,0:T(8,128)(2,1)S(1)}) custom-call(f32[1024,256]{1,0:T(8,128)S(1)} %get-tuple-element.98.outer_in, f32[512,256]{1,0:T(8,128)S(1)} %get-tuple-element.93.inner_in, bf16[512,256]{1,0:T(8,128)(2,1)S(1)} %collective-permute-done.9.near_in, ...), custom_call_target="tpu_custom_call" | custom-call | tf_op jit(solution)/shard_map/image_outer/pallas_call | solution.py:161
  40.5 4.5 %collective-permute-start.13 = (bf16[512,256]{1,0:T(8,128)(2,1)S(1)}, bf16[512,256]{1,0:T(8,128)(2,1)S(1)}, u32[]{:S(2)}, u32[]{:S(2)}) collective-permute-start(bf16[512,256]{1,0:T(8,128)(2,1)S(1)} %get-tuple-element.95), channel_id=1, source_target_pairs={{0,15},{1,2},{2,1},{3,4},{4,3},{5,6},{6,5},{7,8},{8,7},{9,10},{10,... | collective-permute-start | bytes 786440 | tf_op jit(solution)/shard_map/ppermute | solution.py:28
  45.0 0.0 collective-permute-done.8
  45.0 0.0 collective-permute-start.12
  45.1 0.1 collective-permute-start.11
  45.1 1.2 %image_inner.1 = (f32[1024,256]{1,0:T(8,128)S(1)}, f32[512,256]{1,0:T(8,128)S(1)}) custom-call(f32[1024,256]{1,0:T(8,128)S(1)} %get-tuple-element.98.outer_in, f32[512,256]{1,0:T(8,128)S(1)} %get-tuple-element.93.inner_in, bf16[512,256]{1,0:T(8,128)(2,1)S(1)} %collective-permute-done.9.near_in, bf16[512,256]{1,0:T(8,128)(2,1)S(1)} %collective-permute-done.10.far_in, ...), custom_call_target="tpu_custom_call" | custom-call | tf_op jit(solution)/shard_map/image_inner/pallas_call | solution.py:161
  46.3 6.7 %collective-permute-done.11 = bf16[384,256]{1,0:T(8,128)(2,1)S(1)} collective-permute-done((bf16[384,256]{1,0:T(8,128)(2,1)S(1)}, bf16[384,256]{1,0:T(8,128)(2,1)S(1)}, u32[]{:S(2)}, u32[]{:S(2)}) %collective-permute-start.11) | collective-permute-done | bytes 196640 | tf_op jit(solution)/shard_map/ppermute | solution.py:23
  53.1 0.1 collective-permute-start.14
  53.2 3.7 %schur_image.1 = (f32[1536,256]{1,0:T(8,128)S(1)}, f32[1536,256]{1,0:T(8,128)S(1)}, f32[8,256]{1,0:T(8,128)S(1)}, f32[128,256]{1,0:T(8,128)S(1)}) custom-call(f32[1024,256]{1,0:T(8,128)S(1)} %get-tuple-element.102.image, f32[1024,256]{1,0:T(8,128)S(1)} %get-tuple-element.104.outer, f32[512,256]{1,0:T(8,128)S(1)} %get-tuple-element.99.inner, ...), custom_call_target="tpu_custom_call" | custom-call | tf_op jit(solution)/shard_map/schur_image/pallas_call | solution.py:161
  56.9 0.0 collective-permute-done.14.crossed_half
  56.9 0.8 %coarse_image.1 = (f32[4,256]{1,0:T(4,128)S(1)}, f32[96,256]{1,0:T(8,128)S(1)}) custom-call(bf16[768,256]{1,0:T(8,128)(2,1)S(1)} %constant_dynamic-update-slice_fusion.6.half, bf16[768,256]{1,0:T(8,128)(2,1)S(1)} %collective-permute-done.14.crossed_half, bf16[64,1024]{1,0:T(8,128)(2,1)S(1)} %get-tuple-element.65.inverse, ...), custom_call_target="tpu_custom_call" | custom-call | tf_op jit(solution)/shard_map/coarse_image/pallas_call | solution.py:161
  57.7 1.5 %collective-permute-start.15 = (f32[4,256]{1,0:T(4,128)S(1)}, f32[4,256]{1,0:T(4,128)S(1)}, u32[]{:S(2)}, u32[]{:S(2)}) collective-permute-start(f32[4,256]{1,0:T(4,128)S(1)} %get-tuple-element.109), channel_id=1, source_target_pairs={{0,8},{1,9},{2,10},{3,11},{4,12},{5,13},{6,14},{7,15},{8,0},{9,1},... | collective-permute-start | bytes 12296 | tf_op jit(solution)/shard_map/ppermute | solution.py:23
  59.3 1.5 %complete.1 = (f32[1024,256]{1,0:T(8,128)S(1)}, f32[1024,256]{1,0:T(8,128)S(1)}, f32[1024,256]{1,0:T(8,128)S(1)}, bf16[512,256]{1,0:T(8,128)(2,1)S(1)}) custom-call(f32[1536,256]{1,0:T(8,128)S(1)} %get-tuple-element.92.local.z_local, f32[96,256]{1,0:T(8,128)S(1)} %get-tuple-element.87.solution.z_coarse, f32[1536,256]{1,0:T(8,128)S(1)} %get-tuple-element.110.y_local, ...), custom_call_target="tpu_custom_call" | custom-call | tf_op jit(solution)/shard_map/complete/pallas_call | solution.py:161
  60.8 1.5 %collective-permute-done.15 = f32[4,256]{1,0:T(4,128)S(1)} collective-permute-done((f32[4,256]{1,0:T(4,128)S(1)}, f32[4,256]{1,0:T(4,128)S(1)}, u32[]{:S(2)}, u32[]{:S(2)}) %collective-permute-start.15) | collective-permute-done | bytes 4128 | tf_op jit(solution)/shard_map/ppermute | solution.py:23
  62.3 0.4 collective-permute-start.16
  62.7 3.2 %collective-permute-done.16 = f32[4,256]{1,0:T(4,128)S(1)} collective-permute-done((f32[4,256]{1,0:T(4,128)S(1)}, f32[4,256]{1,0:T(4,128)S(1)}, u32[]{:S(2)}, u32[]{:S(2)}) %collective-permute-start.16) | collective-permute-done | bytes 4128 | tf_op jit(solution)/shard_map/ppermute | solution.py:23
  65.9 0.9 %collective-permute-start.19 = (bf16[512,256]{1,0:T(8,128)(2,1)S(1)}, bf16[512,256]{1,0:T(8,128)(2,1)S(1)}, u32[]{:S(2)}, u32[]{:S(2)}) collective-permute-start(bf16[512,256]{1,0:T(8,128)(2,1)S(1)} %get-tuple-element.121), channel_id=1, source_target_pairs={{1,0},{2,1},{3,2},{4,3},{5,4},{6,5},{7,6},{8,7},{9,8},{10,9},{11,1... | collective-permute-start | bytes 786440 | tf_op jit(solution)/shard_map/ppermute | solution.py:19
  66.8 1.6 %collective-permute-start.17 = (f32[4,256]{1,0:T(4,128)S(1)}, f32[4,256]{1,0:T(4,128)S(1)}, u32[]{:S(2)}, u32[]{:S(2)}) collective-permute-start(f32[4,256]{1,0:T(4,128)S(1)} %add.13), channel_id=1, source_target_pairs={{0,4},{1,5},{2,6},{3,7},{4,0},{5,1},{6,2},{7,3},{8,12},{9,13},{10,... | collective-permute-start | bytes 12296 | tf_op jit(solution)/shard_map/ppermute | solution.py:23
  68.4 4.4 %collective-permute-done.17 = f32[4,256]{1,0:T(4,128)S(1)} collective-permute-done((f32[4,256]{1,0:T(4,128)S(1)}, f32[4,256]{1,0:T(4,128)S(1)}, u32[]{:S(2)}, u32[]{:S(2)}) %collective-permute-start.17) | collective-permute-done | bytes 4128 | tf_op jit(solution)/shard_map/ppermute | solution.py:23
  72.8 1.2 %collective-permute-done.18 = f32[4,256]{1,0:T(4,128)S(1)} collective-permute-done((f32[4,256]{1,0:T(4,128)S(1)}, f32[4,256]{1,0:T(4,128)S(1)}, u32[]{:S(2)}, u32[]{:S(2)}) %collective-permute-start.18) | collective-permute-done | bytes 4128 | tf_op jit(solution)/shard_map/ppermute | solution.py:23
  74.0 0.0 collective-permute-done.19.from_next
  74.0 1.6 %combine.1 = (f32[1024,256]{1,0:T(8,128)}, f32[1024,256]{1,0:T(8,128)}) custom-call(f32[4,256]{1,0:T(4,128)S(1)} %add.15.sums, f32[1024,256]{1,0:T(8,128)S(1)} %get-tuple-element.62.load, f32[1024,256]{1,0:T(8,128)S(1)} %get-tuple-element.118.z, f32[1024,256]{1,0:T(8,128)S(1)} %get-tuple-element.113.y, f32[1024,256]{1,0:T(8,128)S(1)} %get-tuple-element.102.image, ...), custom_call_target="tpu_custom_call" | custom-call | tf_op jit(solution)/shard_map/combine/pallas_call | solution.py:161
  (22 shorter events, 0.1 us)
Async XLA Ops:
  2.4 12.6 %collective-permute-start = (bf16[720,256]{1,0:T(8,128)(2,1)S(1)}, bf16[720,256]{1,0:T(8,128)(2,1)S(1)}, u32[]{:S(2)}, u32[]{:S(2)}) collective-permute-start(bf16[720,256]{1,0:T(8,128)(2,1)S(1)} %halo_message.1), channel_id=1, source_target_pairs={{15,0},{0,1},{1,2},{2,3},{3,4},{4,5},{5,6},{6,7},{7,8},{8,9},{9,10... | collective-permute-start | bytes 1105928 | tf_op jit(solution)/shard_map/ppermute | solution.py:19
  2.9 7.2 %collective-permute-start.3 = (bf16[64,256]{1,0:T(8,128)(2,1)S(1)}, bf16[64,256]{1,0:T(8,128)(2,1)S(1)}, u32[]{:S(2)}, u32[]{:S(2)}) collective-permute-start(bf16[64,256]{1,0:T(8,128)(2,1)S(1)} %get-tuple-element.77), channel_id=1, source_target_pairs={{0,8},{1,9},{2,10},{3,11},{4,12},{5,13},{6,14},{7,15},{8,0},{9,1},... | collective-permute-start | bytes 98312 | tf_op jit(solution)/shard_map/ppermute | solution.py:23
  10.1 7.3 %collective-permute-start.4 = (bf16[128,256]{1,0:T(8,128)(2,1)S(1)}, bf16[128,256]{1,0:T(8,128)(2,1)S(1)}, u32[]{:S(2)}, u32[]{:S(2)}) collective-permute-start(bf16[128,256]{1,0:T(8,128)(2,1)S(1)} %pad_maximum_fusion.2), channel_id=1, source_target_pairs={{0,2},{1,3},{2,0},{3,1},{4,6},{5,7},{6,4},{7,5},{8,10},{9,11},{10,... | collective-permute-start | bytes 196616 | tf_op jit(solution)/shard_map/ppermute | solution.py:23
  17.4 5.4 %collective-permute-start.5 = (bf16[256,256]{1,0:T(8,128)(2,1)S(1)}, bf16[256,256]{1,0:T(8,128)(2,1)S(1)}, u32[]{:S(2)}, u32[]{:S(2)}) collective-permute-start(bf16[256,256]{1,0:T(8,128)(2,1)S(1)} %pad_maximum_fusion.1), channel_id=1, source_target_pairs={{0,4},{1,5},{2,6},{3,7},{4,0},{5,1},{6,2},{7,3},{8,12},{9,13},{10,... | collective-permute-start | bytes 393224 | tf_op jit(solution)/shard_map/ppermute | solution.py:23
  17.5 9.1 %collective-permute-start.2 = (bf16[512,256]{1,0:T(8,128)(2,1)S(1)}, bf16[512,256]{1,0:T(8,128)(2,1)S(1)}, u32[]{:S(2)}, u32[]{:S(2)}) collective-permute-start(bf16[512,256]{1,0:T(8,128)(2,1)S(1)} %get-tuple-element.70), channel_id=1, source_target_pairs={{0,15},{1,2},{2,1},{3,4},{4,3},{5,6},{6,5},{7,8},{8,7},{9,10},{10,... | collective-permute-start | bytes 786440 | tf_op jit(solution)/shard_map/ppermute | solution.py:28
  19.8 3.6 %collective-permute-start.1 = (bf16[512,256]{1,0:T(8,128)(2,1)S(1)}, bf16[512,256]{1,0:T(8,128)(2,1)S(1)}, u32[]{:S(2)}, u32[]{:S(2)}) collective-permute-start(bf16[512,256]{1,0:T(8,128)(2,1)S(1)} %get-tuple-element.72), channel_id=1, source_target_pairs={{0,1},{1,0},{2,3},{3,2},{4,5},{5,4},{6,7},{7,6},{8,9},{9,8},{10,11... | collective-permute-start | bytes 786440 | tf_op jit(solution)/shard_map/ppermute | solution.py:23
  22.8 3.8 %collective-permute-start.6 = (bf16[512,256]{1,0:T(8,128)(2,1)S(1)}, bf16[512,256]{1,0:T(8,128)(2,1)S(1)}, u32[]{:S(2)}, u32[]{:S(2)}) collective-permute-start(bf16[512,256]{1,0:T(8,128)(2,1)S(1)} %constant_dynamic-update-slice_fusion.half), channel_id=1, source_target_pairs={{0,1},{1,0},{2,3},{3,2},{4,5},{5,4},{6,7},{7,6},{8,9},{9,8},{10,11... | collective-permute-start | bytes 786440 | tf_op jit(solution)/shard_map/ppermute | solution.py:23
  28.3 7.0 %collective-permute-start.7 = (bf16[96,256]{1,0:T(8,128)(2,1)S(1)}, bf16[96,256]{1,0:T(8,128)(2,1)S(1)}, u32[]{:S(2)}, u32[]{:S(2)}) collective-permute-start(bf16[96,256]{1,0:T(8,128)(2,1)S(1)} %get-tuple-element.83), channel_id=1, source_target_pairs={{0,8},{1,9},{2,10},{3,11},{4,12},{5,13},{6,14},{7,15},{8,0},{9,1},... | collective-permute-start | bytes 147464 | tf_op jit(solution)/shard_map/ppermute | solution.py:23
  30.1 7.0 %collective-permute-start.9 = (bf16[512,256]{1,0:T(8,128)(2,1)S(1)}, bf16[512,256]{1,0:T(8,128)(2,1)S(1)}, u32[]{:S(2)}, u32[]{:S(2)}) collective-permute-start(bf16[512,256]{1,0:T(8,128)(2,1)S(1)} %get-tuple-element.94), channel_id=1, source_target_pairs={{0,1},{1,0},{2,3},{3,2},{4,5},{5,4},{6,7},{7,6},{8,9},{9,8},{10,11... | collective-permute-start | bytes 786440 | tf_op jit(solution)/shard_map/ppermute | solution.py:23
  30.6 8.8 %collective-permute-start.10 = (bf16[512,256]{1,0:T(8,128)(2,1)S(1)}, bf16[512,256]{1,0:T(8,128)(2,1)S(1)}, u32[]{:S(2)}, u32[]{:S(2)}) collective-permute-start(bf16[512,256]{1,0:T(8,128)(2,1)S(1)} %get-tuple-element.89), channel_id=1, source_target_pairs={{0,15},{1,2},{2,1},{3,4},{4,3},{5,6},{6,5},{7,8},{8,7},{9,10},{10,... | collective-permute-start | bytes 786440 | tf_op jit(solution)/shard_map/ppermute | solution.py:28
  35.2 9.8 %collective-permute-start.8 = (bf16[192,256]{1,0:T(8,128)(2,1)S(1)}, bf16[192,256]{1,0:T(8,128)(2,1)S(1)}, u32[]{:S(2)}, u32[]{:S(2)}) collective-permute-start(bf16[192,256]{1,0:T(8,128)(2,1)S(1)} %get-tuple-element.122), channel_id=1, source_target_pairs={{0,2},{1,3},{2,0},{3,1},{4,6},{5,7},{6,4},{7,5},{8,10},{9,11},{10,... | collective-permute-start | bytes 294920 | tf_op jit(solution)/shard_map/ppermute | solution.py:23
  40.5 12.5 %collective-permute-start.13 = (bf16[512,256]{1,0:T(8,128)(2,1)S(1)}, bf16[512,256]{1,0:T(8,128)(2,1)S(1)}, u32[]{:S(2)}, u32[]{:S(2)}) collective-permute-start(bf16[512,256]{1,0:T(8,128)(2,1)S(1)} %get-tuple-element.95), channel_id=1, source_target_pairs={{0,15},{1,2},{2,1},{3,4},{4,3},{5,6},{6,5},{7,8},{8,7},{9,10},{10,... | collective-permute-start | bytes 786440 | tf_op jit(solution)/shard_map/ppermute | solution.py:28
  45.0 8.0 %collective-permute-start.12 = (bf16[512,256]{1,0:T(8,128)(2,1)S(1)}, bf16[512,256]{1,0:T(8,128)(2,1)S(1)}, u32[]{:S(2)}, u32[]{:S(2)}) collective-permute-start(bf16[512,256]{1,0:T(8,128)(2,1)S(1)} %get-tuple-element.97), channel_id=1, source_target_pairs={{0,1},{1,0},{2,3},{3,2},{4,5},{5,4},{6,7},{7,6},{8,9},{9,8},{10,11... | collective-permute-start | bytes 786440 | tf_op jit(solution)/shard_map/ppermute | solution.py:23
  45.1 8.0 %collective-permute-start.11 = (bf16[384,256]{1,0:T(8,128)(2,1)S(1)}, bf16[384,256]{1,0:T(8,128)(2,1)S(1)}, u32[]{:S(2)}, u32[]{:S(2)}) collective-permute-start(bf16[384,256]{1,0:T(8,128)(2,1)S(1)} %pad_maximum_fusion), channel_id=1, source_target_pairs={{0,4},{1,5},{2,6},{3,7},{4,0},{5,1},{6,2},{7,3},{8,12},{9,13},{10,... | collective-permute-start | bytes 589832 | tf_op jit(solution)/shard_map/ppermute | solution.py:23
  53.1 3.8 %collective-permute-start.14 = (bf16[768,256]{1,0:T(8,128)(2,1)S(1)}, bf16[768,256]{1,0:T(8,128)(2,1)S(1)}, u32[]{:S(2)}, u32[]{:S(2)}) collective-permute-start(bf16[768,256]{1,0:T(8,128)(2,1)S(1)} %constant_dynamic-update-slice_fusion.6.half), channel_id=1, source_target_pairs={{0,1},{1,0},{2,3},{3,2},{4,5},{5,4},{6,7},{7,6},{8,9},{9,8},{10,11... | collective-permute-start | bytes 1179656 | tf_op jit(solution)/shard_map/ppermute | solution.py:23
  57.7 4.6 %collective-permute-start.15 = (f32[4,256]{1,0:T(4,128)S(1)}, f32[4,256]{1,0:T(4,128)S(1)}, u32[]{:S(2)}, u32[]{:S(2)}) collective-permute-start(f32[4,256]{1,0:T(4,128)S(1)} %get-tuple-element.109), channel_id=1, source_target_pairs={{0,8},{1,9},{2,10},{3,11},{4,12},{5,13},{6,14},{7,15},{8,0},{9,1},... | collective-permute-start | bytes 12296 | tf_op jit(solution)/shard_map/ppermute | solution.py:23
  62.3 3.6 %collective-permute-start.16 = (f32[4,256]{1,0:T(4,128)S(1)}, f32[4,256]{1,0:T(4,128)S(1)}, u32[]{:S(2)}, u32[]{:S(2)}) collective-permute-start(f32[4,256]{1,0:T(4,128)S(1)} %add.12), channel_id=1, source_target_pairs={{0,2},{1,3},{2,0},{3,1},{4,6},{5,7},{6,4},{7,5},{8,10},{9,11},{10,... | collective-permute-start | bytes 12296 | tf_op jit(solution)/shard_map/ppermute | solution.py:23
  65.9 8.0 %collective-permute-start.19 = (bf16[512,256]{1,0:T(8,128)(2,1)S(1)}, bf16[512,256]{1,0:T(8,128)(2,1)S(1)}, u32[]{:S(2)}, u32[]{:S(2)}) collective-permute-start(bf16[512,256]{1,0:T(8,128)(2,1)S(1)} %get-tuple-element.121), channel_id=1, source_target_pairs={{1,0},{2,1},{3,2},{4,3},{5,4},{6,5},{7,6},{8,7},{9,8},{10,9},{11,1... | collective-permute-start | bytes 786440 | tf_op jit(solution)/shard_map/ppermute | solution.py:19
  66.8 6.0 %collective-permute-start.17 = (f32[4,256]{1,0:T(4,128)S(1)}, f32[4,256]{1,0:T(4,128)S(1)}, u32[]{:S(2)}, u32[]{:S(2)}) collective-permute-start(f32[4,256]{1,0:T(4,128)S(1)} %add.13), channel_id=1, source_target_pairs={{0,4},{1,5},{2,6},{3,7},{4,0},{5,1},{6,2},{7,3},{8,12},{9,13},{10,... | collective-permute-start | bytes 12296 | tf_op jit(solution)/shard_map/ppermute | solution.py:23
  72.8 1.2 %collective-permute-start.18 = (f32[4,256]{1,0:T(4,128)S(1)}, f32[4,256]{1,0:T(4,128)S(1)}, u32[]{:S(2)}, u32[]{:S(2)}) collective-permute-start(f32[4,256]{1,0:T(4,128)S(1)} %add.14), channel_id=1, source_target_pairs={{0,1},{1,0},{2,3},{3,2},{4,5},{5,4},{6,7},{7,6},{8,9},{9,8},{10,11... | collective-permute-start | bytes 12296 | tf_op jit(solution)/shard_map/ppermute | solution.py:23

commit v14 on v12

--- a/solution.py
+++ b/solution.py
@@ -511,12 +511,12 @@
         bind(halo_message), [((halo.height, columns), BF16)], load, weight, rows, inverse,
         scratch=[pltpu.VMEM((halo.weight_count, columns), F32)],
     )
-    half = gather_half(coarse_rounded, early[:1])
     tied = after(tuple(map(outside, (neumann, schur))), message)
     neumann, schur = stage(
         bind(fetch), [described(array) for array in tied], *tied, scratch=semaphores(2), fetched=2
     )
     message = shifted(message, 1)
+    half = gather_half(coarse_rounded, early[:1], neumann)
     outside_faces = [((2 * nf, columns), F32)] + 2 * [((nf, columns), BF16)]
     inside_faces = [(((subs - 1) * nf, columns), F32)]
     outer, near, far = stage(bind(load_outer), outside_faces, load, weight, message, neumann)
@@ -563,7 +563,7 @@
         bind(complete), [(own, F32), (own, F32), (own, F32), ((nf, columns), BF16)],
         z_local, z_coarse, y_local, y_coarse, rows, basis_high, basis_low, product,
     )
-    for k, bit in enumerate(steps):
+    for k, bit in enumerate(early + steps[-1:] + late):
         sums = sums + after(crossed(sums, bit), y)
         if k == len(early) - 1:
             back = shifted(after(back, sums), -1)

time: 74.4 us -> 71.5 us (0.961)
  waiting for transfers between devices: 24.1 us -> 18.6 us
  starting transfers between devices: 24.8 us -> 27.3 us
    ppermute x15, waiting for transfers between devices: 16.3 us -> 11.9 us  [crossed(): lax.ppermute(block, AXIS, [(i, i ^ bit) for i in range(lax.axis_size(AXIS...]
    ppermute x15, starting transfers between devices: 18.7 us -> 19.9 us  [crossed(): lax.ppermute(block, AXIS, [(i, i ^ bit) for i in range(lax.axis_size(AXIS...]
    ppermute x3, starting transfers between devices: 4.79 us -> 5.89 us  [far_block(): lax.ppermute(block, AXIS, [(i, (i + (1 if i % 2 else -1)) % n) for i in r...]
    ppermute x3, waiting for transfers between devices: 7.79 us -> 6.71 us  [far_block(): lax.ppermute(block, AXIS, [(i, (i + (1 if i % 2 else -1)) % n) for i in r...]
  transfers between devices with their start and end apart: 20 -> 20, of which waited for: 10 -> 9; matrix products, arithmetic and copies ran while one was open for 0% -> 0% of each run, Pallas kernels for 25% -> 26%
where the time goes in v14:
time: 71.5 us; the launch traced here: 71.3 us
  starting transfers between devices  27.3 us (38%)
  Pallas kernels  24.4 us (34%)
  waiting for transfers between devices  18.6 us (26%)
  between operations  0.85 us (1%)
    pallas_call x15, Pallas kernels, stage(): return call(*operands)  24.4 us
    ppermute x15, starting transfers between devices, crossed(): lax.ppermute(block, AXIS, [(i, i ^ bit) for i in range(lax.axis_size(AXIS...  19.9 us
    ppermute x15, waiting for transfers between devices, crossed(): lax.ppermute(block, AXIS, [(i, i ^ bit) for i in range(lax.axis_size(AXIS...  11.9 us
    ppermute x3, waiting for transfers between devices, far_block(): lax.ppermute(block, AXIS, [(i, (i + (1 if i % 2 else -1)) % n) for i in r...  6.71 us
    ppermute x3, starting transfers between devices, far_block(): lax.ppermute(block, AXIS, [(i, (i + (1 if i % 2 else -1)) % n) for i in r...  5.89 us
    ppermute x2, starting transfers between devices, shifted(): lax.ppermute(block, AXIS, [((i - distance) % n, i) for i in range(n)])  1.52 us
  transfers between devices with their start and end apart: 20, of which 9 were waited for; matrix products, arithmetic and copies ran while one was open for 0% of the time, Pallas kernels for 26%

profile of v14, /device:TPU:0, one launch (start us, length us, event | category | flops | bytes accessed | tf_op | source)
XLA Modules:
  0.0 71.3 jit_solution(17635071417513409377)
XLA Ops:
  0.6 1.5 %prepare.1 = (f32[1024,256]{1,0:T(8,128)S(1)}, bf16[64,512]{1,0:T(8,128)(2,1)S(1)}, f32[2,512]{1,0:T(2,128)S(1)}, bf16[64,1024]{1,0:T(8,128)(2,1)S(1)}, bf16[64,...) custom-call(f32[1024,256]{1,0:T(8,128)} %load.1, bf16[64,512]{1,0:T(8,128)(2,1)} %rows.1, f32[2,512]{1,0:T(2,128)} %weight.1, ...), custom_call_target="tpu_custom_call" | custom-call | tf_op jit(solution)/shard_map/prepare/pallas_call | solution.py:161
  2.2 0.3 halo_message.1
  2.4 0.5 collective-permute-start
  2.9 3.7 %collective-permute-start.3 = (bf16[64,256]{1,0:T(8,128)(2,1)S(1)}, bf16[64,256]{1,0:T(8,128)(2,1)S(1)}, u32[]{:S(2)}, u32[]{:S(2)}) collective-permute-start(bf16[64,256]{1,0:T(8,128)(2,1)S(1)} %get-tuple-element.76), channel_id=1, source_target_pairs={{0,8},{1,9},{2,10},{3,11},{4,12},{5,13},{6,14},{7,15},{8,0},{9,1},... | collective-permute-start | bytes 98312 | tf_op jit(solution)/shard_map/ppermute | solution.py:23
  6.6 3.5 %fetch.1 = (bf16[2048,1024]{1,0:T(8,128)(2,1)S(1)}, bf16[2048,1024]{1,0:T(8,128)(2,1)S(1)}) custom-call(bf16[2048,1024]{1,0:T(8,128)(2,1)} %neumann, bf16[2048,1024]{1,0:T(8,128)(2,1)} %schur), custom_call_target="tpu_custom_call" | custom-call | tf_op jit(solution)/shard_map/fetch/pallas_call | solution.py:161
  10.1 0.0 collective-permute-done.3
  10.1 4.9 %collective-permute-start.4 = (bf16[128,256]{1,0:T(8,128)(2,1)S(1)}, bf16[128,256]{1,0:T(8,128)(2,1)S(1)}, u32[]{:S(2)}, u32[]{:S(2)}) collective-permute-start(bf16[128,256]{1,0:T(8,128)(2,1)S(1)} %pad_maximum_fusion.3), channel_id=1, source_target_pairs={{0,2},{1,3},{2,0},{3,1},{4,6},{5,7},{6,4},{7,5},{8,10},{9,11},{10,... | collective-permute-start | bytes 196616 | tf_op jit(solution)/shard_map/ppermute | solution.py:23
  15.0 0.0 collective-permute-done.message
  15.0 1.0 %load_outer.1 = (f32[1024,256]{1,0:T(8,128)S(1)}, bf16[512,256]{1,0:T(8,128)(2,1)S(1)}, bf16[512,256]{1,0:T(8,128)(2,1)S(1)}) custom-call(f32[1024,256]{1,0:T(8,128)S(1)} %get-tuple-element.61.load, f32[2,512]{1,0:T(2,128)S(1)} %get-tuple-element.62.weight, bf16[720,256]{1,0:T(8,128)(2,1)S(1)} %collective-permute-done.message, ...), custom_call_target="tpu_custom_call" | custom-call | tf_op jit(solution)/shard_map/load_outer/pallas_call | solution.py:161
  16.1 1.3 %collective-permute-done.4 = bf16[128,256]{1,0:T(8,128)(2,1)S(1)} collective-permute-done((bf16[128,256]{1,0:T(8,128)(2,1)S(1)}, bf16[128,256]{1,0:T(8,128)(2,1)S(1)}, u32[]{:S(2)}, u32[]{:S(2)}) %collective-permute-start.4) | collective-permute-done | bytes 65568 | tf_op jit(solution)/shard_map/ppermute | solution.py:23
  17.4 0.1 collective-permute-start.5
  17.5 2.3 %collective-permute-start.2 = (bf16[512,256]{1,0:T(8,128)(2,1)S(1)}, bf16[512,256]{1,0:T(8,128)(2,1)S(1)}, u32[]{:S(2)}, u32[]{:S(2)}) collective-permute-start(bf16[512,256]{1,0:T(8,128)(2,1)S(1)} %get-tuple-element.69), channel_id=1, source_target_pairs={{0,15},{1,2},{2,1},{3,4},{4,3},{5,6},{6,5},{7,8},{8,7},{9,10},{10,... | collective-permute-start | bytes 786440 | tf_op jit(solution)/shard_map/ppermute | solution.py:28
  19.8 1.0 %load_inner.1.inner = f32[512,256]{1,0:T(8,128)S(1)} custom-call(f32[1024,256]{1,0:T(8,128)S(1)} %get-tuple-element.61.load, f32[2,512]{1,0:T(2,128)S(1)} %get-tuple-element.62.weight, bf16[720,256]{1,0:T(8,128)(2,1)S(1)} %collective-permute-done.message, bf16[2048,1024]{1,0:T(8,128)(2,1)S(1)} %get-tuple-element.67.neumann), custom_call_target="tpu_custom_call" | custom-call | tf_op jit(solution)/shard_map/load_inner/pallas_call | solution.py:161
  20.8 0.1 collective-permute-start.1
  20.9 1.9 %static_basis.1 = (bf16[2048,64]{1,0:T(8,128)(2,1)S(1)}, bf16[2048,64]{1,0:T(8,128)(2,1)S(1)}, bf16[128,1024]{1,0:T(8,128)(2,1)S(1)}, bf16[128,1024]{1,0:T(8,128)(2,1)S(1)}, f32[128,128]{1,0:T(8,128)S(1)}) custom-call(bf16[2048,1024]{1,0:T(8,128)(2,1)S(1)} %get-tuple-element.72.schur, bf16[720,256]{1,0:T(8,128)(2,1)S(1)} %collective-permute-done.message, ...), custom_call_target="tpu_custom_call" | custom-call | tf_op jit(solution)/shard_map/static_basis/pallas_call | solution.py:161
  22.9 0.6 collective-permute-start.6
  23.5 3.2 %collective-permute-done.2.far = bf16[512,256]{1,0:T(8,128)(2,1)S(1)} collective-permute-done((bf16[512,256]{1,0:T(8,128)(2,1)S(1)}, bf16[512,256]{1,0:T(8,128)(2,1)S(1)}, u32[]{:S(2)}, u32[]{:S(2)}) %collective-permute-start.2) | collective-permute-done | bytes 262176 | tf_op jit(solution)/shard_map/ppermute | solution.py:28
  26.7 1.6 %coarse_load.1 = (f32[1536,256]{1,0:T(8,128)S(1)}, bf16[96,256]{1,0:T(8,128)(2,1)S(1)}, f32[96,256]{1,0:T(8,128)S(1)}, f32[96,256]{1,0:T(8,128)S(1)}, f32[8,256]{1,0:T(8,128)S(1)}) custom-call(f32[1024,256]{1,0:T(8,128)S(1)} %get-tuple-element.61.load, f32[1024,256]{1,0:T(8,128)S(1)} %get-tuple-element.68.outer, f32[512,256]{1,0:T(8,128)S(1)} %load_inner.1.inner, ...), custom_call_target="tpu_custom_call" | custom-call | tf_op jit(solution)/shard_map/coarse_load/pallas_call | solution.py:161
  28.3 0.1 collective-permute-start.7
  28.4 1.8 %schur_outer.1 = (f32[1024,256]{1,0:T(8,128)S(1)}, bf16[512,256]{1,0:T(8,128)(2,1)S(1)}, bf16[512,256]{1,0:T(8,128)(2,1)S(1)}, f32[8,256]{1,0:T(8,128)S(1)}) custom-call(f32[1536,256]{1,0:T(8,128)S(1)} %get-tuple-element.83.local.z_local, bf16[2048,1024]{1,0:T(8,128)(2,1)S(1)} %get-tuple-element.72.schur, bf16[2048,64]{1,0:T(8,128)(2,1)S(1)} %get-tuple-element.84.basis_high, ...), custom_call_target="tpu_custom_call" | custom-call | tf_op jit(solution)/shard_map/schur_outer/pallas_call | solution.py:161
  30.1 1.8 %collective-permute-start.10 = (bf16[512,256]{1,0:T(8,128)(2,1)S(1)}, bf16[512,256]{1,0:T(8,128)(2,1)S(1)}, u32[]{:S(2)}, u32[]{:S(2)}) collective-permute-start(bf16[512,256]{1,0:T(8,128)(2,1)S(1)} %get-tuple-element.92), channel_id=1, source_target_pairs={{0,15},{1,2},{2,1},{3,4},{4,3},{5,6},{6,5},{7,8},{8,7},{9,10},{10,... | collective-permute-start | bytes 786440 | tf_op jit(solution)/shard_map/ppermute | solution.py:28
  31.9 1.8 %schur_inner.1 = (f32[512,256]{1,0:T(8,128)S(1)}, f32[1,256]{1,0:T(1,128)S(1)}) custom-call(f32[1536,256]{1,0:T(8,128)S(1)} %get-tuple-element.83.local.z_local, bf16[2048,1024]{1,0:T(8,128)(2,1)S(1)} %get-tuple-element.72.schur, bf16[2048,64]{1,0:T(8,128)(2,1)S(1)} %get-tuple-element.84.basis_high, bf16[2048,64]{1,0:T(8,128)(2,1)S(1)} %get-tuple-element.85.basis_low, ...), custom_call_target="tpu_custom_call" | custom-call | tf_op jit(solution)/shard_map/schur_inner/pallas_call | solution.py:161
  33.7 0.2 collective-permute-done.7
  34.0 1.3 %collective-permute-start.8 = (bf16[192,256]{1,0:T(8,128)(2,1)S(1)}, bf16[192,256]{1,0:T(8,128)(2,1)S(1)}, u32[]{:S(2)}, u32[]{:S(2)}) collective-permute-start(bf16[192,256]{1,0:T(8,128)(2,1)S(1)} %pad_maximum_fusion.2), channel_id=1, source_target_pairs={{0,2},{1,3},{2,0},{3,1},{4,6},{5,7},{6,4},{7,5},{8,10},{9,11},{10,... | collective-permute-start | bytes 294920 | tf_op jit(solution)/shard_map/ppermute | solution.py:23
  35.3 3.5 %collective-permute-done.10.far_in = bf16[512,256]{1,0:T(8,128)(2,1)S(1)} collective-permute-done((bf16[512,256]{1,0:T(8,128)(2,1)S(1)}, bf16[512,256]{1,0:T(8,128)(2,1)S(1)}, u32[]{:S(2)}, u32[]{:S(2)}) %collective-permute-start.10) | collective-permute-done | bytes 262176 | tf_op jit(solution)/shard_map/ppermute | solution.py:28
  38.8 1.1 %image_outer.1 = (f32[1024,256]{1,0:T(8,128)S(1)}, bf16[512,256]{1,0:T(8,128)(2,1)S(1)}, bf16[512,256]{1,0:T(8,128)(2,1)S(1)}) custom-call(f32[1024,256]{1,0:T(8,128)S(1)} %get-tuple-element.96.outer_in, f32[512,256]{1,0:T(8,128)S(1)} %get-tuple-element.87.inner_in, bf16[512,256]{1,0:T(8,128)(2,1)S(1)} %collective-permute-done.9.near_in, ...), custom_call_target="tpu_custom_call" | custom-call | tf_op jit(solution)/shard_map/image_outer/pallas_call | solution.py:161
  40.0 1.8 %collective-permute-start.13 = (bf16[512,256]{1,0:T(8,128)(2,1)S(1)}, bf16[512,256]{1,0:T(8,128)(2,1)S(1)}, u32[]{:S(2)}, u32[]{:S(2)}) collective-permute-start(bf16[512,256]{1,0:T(8,128)(2,1)S(1)} %get-tuple-element.93), channel_id=1, source_target_pairs={{0,15},{1,2},{2,1},{3,4},{4,3},{5,6},{6,5},{7,8},{8,7},{9,10},{10,... | collective-permute-start | bytes 786440 | tf_op jit(solution)/shard_map/ppermute | solution.py:28
  41.8 1.0 %collective-permute-start.12 = (bf16[512,256]{1,0:T(8,128)(2,1)S(1)}, bf16[512,256]{1,0:T(8,128)(2,1)S(1)}, u32[]{:S(2)}, u32[]{:S(2)}) collective-permute-start(bf16[512,256]{1,0:T(8,128)(2,1)S(1)} %get-tuple-element.95), channel_id=1, source_target_pairs={{0,1},{1,0},{2,3},{3,2},{4,5},{5,4},{6,7},{7,6},{8,9},{9,8},{10,11... | collective-permute-start | bytes 786440 | tf_op jit(solution)/shard_map/ppermute | solution.py:23
  42.8 1.7 %collective-permute-start.11 = (bf16[384,256]{1,0:T(8,128)(2,1)S(1)}, bf16[384,256]{1,0:T(8,128)(2,1)S(1)}, u32[]{:S(2)}, u32[]{:S(2)}) collective-permute-start(bf16[384,256]{1,0:T(8,128)(2,1)S(1)} %pad_maximum_fusion), channel_id=1, source_target_pairs={{0,4},{1,5},{2,6},{3,7},{4,0},{5,1},{6,2},{7,3},{8,12},{9,13},{10,... | collective-permute-start | bytes 589832 | tf_op jit(solution)/shard_map/ppermute | solution.py:23
  44.4 1.2 %image_inner.1 = (f32[1024,256]{1,0:T(8,128)S(1)}, f32[512,256]{1,0:T(8,128)S(1)}) custom-call(f32[1024,256]{1,0:T(8,128)S(1)} %get-tuple-element.96.outer_in, f32[512,256]{1,0:T(8,128)S(1)} %get-tuple-element.87.inner_in, bf16[512,256]{1,0:T(8,128)(2,1)S(1)} %collective-permute-done.9.near_in, bf16[512,256]{1,0:T(8,128)(2,1)S(1)} %collective-permute-done.10.far_in, ...), custom_call_target="tpu_custom_call" | custom-call | tf_op jit(solution)/shard_map/image_inner/pallas_call | solution.py:161
  45.6 4.3 %collective-permute-done.11 = bf16[384,256]{1,0:T(8,128)(2,1)S(1)} collective-permute-done((bf16[384,256]{1,0:T(8,128)(2,1)S(1)}, bf16[384,256]{1,0:T(8,128)(2,1)S(1)}, u32[]{:S(2)}, u32[]{:S(2)}) %collective-permute-start.11) | collective-permute-done | bytes 196640 | tf_op jit(solution)/shard_map/ppermute | solution.py:23
  49.9 0.0 collective-permute-done.13.far
  49.9 0.1 collective-permute-start.14
  50.0 3.7 %schur_image.1 = (f32[1536,256]{1,0:T(8,128)S(1)}, f32[1536,256]{1,0:T(8,128)S(1)}, f32[8,256]{1,0:T(8,128)S(1)}, f32[128,256]{1,0:T(8,128)S(1)}) custom-call(f32[1024,256]{1,0:T(8,128)S(1)} %get-tuple-element.100.image, f32[1024,256]{1,0:T(8,128)S(1)} %get-tuple-element.102.outer, f32[512,256]{1,0:T(8,128)S(1)} %get-tuple-element.97.inner, ...), custom_call_target="tpu_custom_call" | custom-call | tf_op jit(solution)/shard_map/schur_image/pallas_call | solution.py:161
  53.7 0.0 collective-permute-done.14.crossed_half
  53.7 0.8 %coarse_image.1 = (f32[4,256]{1,0:T(4,128)S(1)}, f32[96,256]{1,0:T(8,128)S(1)}) custom-call(bf16[768,256]{1,0:T(8,128)(2,1)S(1)} %constant_dynamic-update-slice_fusion.4.half, bf16[768,256]{1,0:T(8,128)(2,1)S(1)} %collective-permute-done.14.crossed_half, bf16[64,1024]{1,0:T(8,128)(2,1)S(1)} %get-tuple-element.64.inverse, ...), custom_call_target="tpu_custom_call" | custom-call | tf_op jit(solution)/shard_map/coarse_image/pallas_call | solution.py:161
  54.6 2.7 %collective-permute-start.15 = (f32[4,256]{1,0:T(4,128)S(1)}, f32[4,256]{1,0:T(4,128)S(1)}, u32[]{:S(2)}, u32[]{:S(2)}) collective-permute-start(f32[4,256]{1,0:T(4,128)S(1)} %get-tuple-element.107), channel_id=1, source_target_pairs={{0,8},{1,9},{2,10},{3,11},{4,12},{5,13},{6,14},{7,15},{8,0},{9,1},... | collective-permute-start | bytes 12296 | tf_op jit(solution)/shard_map/ppermute | solution.py:23
  57.2 1.5 %complete.1 = (f32[1024,256]{1,0:T(8,128)S(1)}, f32[1024,256]{1,0:T(8,128)S(1)}, f32[1024,256]{1,0:T(8,128)S(1)}, bf16[512,256]{1,0:T(8,128)(2,1)S(1)}) custom-call(f32[1536,256]{1,0:T(8,128)S(1)} %get-tuple-element.83.local.z_local, f32[96,256]{1,0:T(8,128)S(1)} %get-tuple-element.86.solution.z_coarse, f32[1536,256]{1,0:T(8,128)S(1)} %get-tuple-element.108.y_local, ...), custom_call_target="tpu_custom_call" | custom-call | tf_op jit(solution)/shard_map/complete/pallas_call | solution.py:161
  58.7 0.4 collective-permute-done.15
  59.1 3.0 %collective-permute-start.16 = (f32[4,256]{1,0:T(4,128)S(1)}, f32[4,256]{1,0:T(4,128)S(1)}, u32[]{:S(2)}, u32[]{:S(2)}) collective-permute-start(f32[4,256]{1,0:T(4,128)S(1)} %add.12), channel_id=1, source_target_pairs={{0,2},{1,3},{2,0},{3,1},{4,6},{5,7},{6,4},{7,5},{8,10},{9,11},{10,... | collective-permute-start | bytes 12296 | tf_op jit(solution)/shard_map/ppermute | solution.py:23
  62.2 1.6 %collective-permute-done.16 = f32[4,256]{1,0:T(4,128)S(1)} collective-permute-done((f32[4,256]{1,0:T(4,128)S(1)}, f32[4,256]{1,0:T(4,128)S(1)}, u32[]{:S(2)}, u32[]{:S(2)}) %collective-permute-start.16) | collective-permute-done | bytes 4128 | tf_op jit(solution)/shard_map/ppermute | solution.py:23
  63.8 1.0 %collective-permute-start.19 = (bf16[512,256]{1,0:T(8,128)(2,1)S(1)}, bf16[512,256]{1,0:T(8,128)(2,1)S(1)}, u32[]{:S(2)}, u32[]{:S(2)}) collective-permute-start(bf16[512,256]{1,0:T(8,128)(2,1)S(1)} %get-tuple-element.119), channel_id=1, source_target_pairs={{1,0},{2,1},{3,2},{4,3},{5,4},{6,5},{7,6},{8,7},{9,8},{10,9},{11,1... | collective-permute-start | bytes 786440 | tf_op jit(solution)/shard_map/ppermute | solution.py:19
  64.8 0.0 collective-permute-start.17
  64.8 1.2 %collective-permute-done.17 = f32[4,256]{1,0:T(4,128)S(1)} collective-permute-done((f32[4,256]{1,0:T(4,128)S(1)}, f32[4,256]{1,0:T(4,128)S(1)}, u32[]{:S(2)}, u32[]{:S(2)}) %collective-permute-start.17) | collective-permute-done | bytes 4128 | tf_op jit(solution)/shard_map/ppermute | solution.py:23
  66.0 0.8 %collective-permute-start.18 = (f32[4,256]{1,0:T(4,128)S(1)}, f32[4,256]{1,0:T(4,128)S(1)}, u32[]{:S(2)}, u32[]{:S(2)}) collective-permute-start(f32[4,256]{1,0:T(4,128)S(1)} %add.14), channel_id=1, source_target_pairs={{0,4},{1,5},{2,6},{3,7},{4,0},{5,1},{6,2},{7,3},{8,12},{9,13},{10,... | collective-permute-start | bytes 12296 | tf_op jit(solution)/shard_map/ppermute | solution.py:23
  66.8 2.9 %collective-permute-done.18 = f32[4,256]{1,0:T(4,128)S(1)} collective-permute-done((f32[4,256]{1,0:T(4,128)S(1)}, f32[4,256]{1,0:T(4,128)S(1)}, u32[]{:S(2)}, u32[]{:S(2)}) %collective-permute-start.18) | collective-permute-done | bytes 4128 | tf_op jit(solution)/shard_map/ppermute | solution.py:23
  69.7 0.0 collective-permute-done.19.from_next
  69.7 1.6 %combine.1 = (f32[1024,256]{1,0:T(8,128)}, f32[1024,256]{1,0:T(8,128)}) custom-call(f32[4,256]{1,0:T(4,128)S(1)} %add.15.sums, f32[1024,256]{1,0:T(8,128)S(1)} %get-tuple-element.61.load, f32[1024,256]{1,0:T(8,128)S(1)} %get-tuple-element.116.z, f32[1024,256]{1,0:T(8,128)S(1)} %get-tuple-element.111.y, f32[1024,256]{1,0:T(8,128)S(1)} %get-tuple-element.100.image, ...), custom_call_target="tpu_custom_call" | custom-call | tf_op jit(solution)/shard_map/combine/pallas_call | solution.py:161
  (23 shorter events, 0.1 us)
Async XLA Ops:
  2.4 12.6 %collective-permute-start = (bf16[720,256]{1,0:T(8,128)(2,1)S(1)}, bf16[720,256]{1,0:T(8,128)(2,1)S(1)}, u32[]{:S(2)}, u32[]{:S(2)}) collective-permute-start(bf16[720,256]{1,0:T(8,128)(2,1)S(1)} %halo_message.1), channel_id=1, source_target_pairs={{15,0},{0,1},{1,2},{2,3},{3,4},{4,5},{5,6},{6,7},{7,8},{8,9},{9,10... | collective-permute-start | bytes 1105928 | tf_op jit(solution)/shard_map/ppermute | solution.py:19
  2.9 7.2 %collective-permute-start.3 = (bf16[64,256]{1,0:T(8,128)(2,1)S(1)}, bf16[64,256]{1,0:T(8,128)(2,1)S(1)}, u32[]{:S(2)}, u32[]{:S(2)}) collective-permute-start(bf16[64,256]{1,0:T(8,128)(2,1)S(1)} %get-tuple-element.76), channel_id=1, source_target_pairs={{0,8},{1,9},{2,10},{3,11},{4,12},{5,13},{6,14},{7,15},{8,0},{9,1},... | collective-permute-start | bytes 98312 | tf_op jit(solution)/shard_map/ppermute | solution.py:23
  10.1 7.3 %collective-permute-start.4 = (bf16[128,256]{1,0:T(8,128)(2,1)S(1)}, bf16[128,256]{1,0:T(8,128)(2,1)S(1)}, u32[]{:S(2)}, u32[]{:S(2)}) collective-permute-start(bf16[128,256]{1,0:T(8,128)(2,1)S(1)} %pad_maximum_fusion.3), channel_id=1, source_target_pairs={{0,2},{1,3},{2,0},{3,1},{4,6},{5,7},{6,4},{7,5},{8,10},{9,11},{10,... | collective-permute-start | bytes 196616 | tf_op jit(solution)/shard_map/ppermute | solution.py:23
  17.4 5.5 %collective-permute-start.5 = (bf16[256,256]{1,0:T(8,128)(2,1)S(1)}, bf16[256,256]{1,0:T(8,128)(2,1)S(1)}, u32[]{:S(2)}, u32[]{:S(2)}) collective-permute-start(bf16[256,256]{1,0:T(8,128)(2,1)S(1)} %pad_maximum_fusion.1), channel_id=1, source_target_pairs={{0,4},{1,5},{2,6},{3,7},{4,0},{5,1},{6,2},{7,3},{8,12},{9,13},{10,... | collective-permute-start | bytes 393224 | tf_op jit(solution)/shard_map/ppermute | solution.py:23
  17.5 9.1 %collective-permute-start.2 = (bf16[512,256]{1,0:T(8,128)(2,1)S(1)}, bf16[512,256]{1,0:T(8,128)(2,1)S(1)}, u32[]{:S(2)}, u32[]{:S(2)}) collective-permute-start(bf16[512,256]{1,0:T(8,128)(2,1)S(1)} %get-tuple-element.69), channel_id=1, source_target_pairs={{0,15},{1,2},{2,1},{3,4},{4,3},{5,6},{6,5},{7,8},{8,7},{9,10},{10,... | collective-permute-start | bytes 786440 | tf_op jit(solution)/shard_map/ppermute | solution.py:28
  20.8 5.8 %collective-permute-start.1 = (bf16[512,256]{1,0:T(8,128)(2,1)S(1)}, bf16[512,256]{1,0:T(8,128)(2,1)S(1)}, u32[]{:S(2)}, u32[]{:S(2)}) collective-permute-start(bf16[512,256]{1,0:T(8,128)(2,1)S(1)} %get-tuple-element.71), channel_id=1, source_target_pairs={{0,1},{1,0},{2,3},{3,2},{4,5},{5,4},{6,7},{7,6},{8,9},{9,8},{10,11... | collective-permute-start | bytes 786440 | tf_op jit(solution)/shard_map/ppermute | solution.py:23
  22.9 3.8 %collective-permute-start.6 = (bf16[512,256]{1,0:T(8,128)(2,1)S(1)}, bf16[512,256]{1,0:T(8,128)(2,1)S(1)}, u32[]{:S(2)}, u32[]{:S(2)}) collective-permute-start(bf16[512,256]{1,0:T(8,128)(2,1)S(1)} %constant_dynamic-update-slice_fusion.half), channel_id=1, source_target_pairs={{0,1},{1,0},{2,3},{3,2},{4,5},{5,4},{6,7},{7,6},{8,9},{9,8},{10,11... | collective-permute-start | bytes 786440 | tf_op jit(solution)/shard_map/ppermute | solution.py:23
  28.3 5.7 %collective-permute-start.7 = (bf16[96,256]{1,0:T(8,128)(2,1)S(1)}, bf16[96,256]{1,0:T(8,128)(2,1)S(1)}, u32[]{:S(2)}, u32[]{:S(2)}) collective-permute-start(bf16[96,256]{1,0:T(8,128)(2,1)S(1)} %get-tuple-element.82), channel_id=1, source_target_pairs={{0,8},{1,9},{2,10},{3,11},{4,12},{5,13},{6,14},{7,15},{8,0},{9,1},... | collective-permute-start | bytes 147464 | tf_op jit(solution)/shard_map/ppermute | solution.py:23
  30.1 8.7 %collective-permute-start.10 = (bf16[512,256]{1,0:T(8,128)(2,1)S(1)}, bf16[512,256]{1,0:T(8,128)(2,1)S(1)}, u32[]{:S(2)}, u32[]{:S(2)}) collective-permute-start(bf16[512,256]{1,0:T(8,128)(2,1)S(1)} %get-tuple-element.92), channel_id=1, source_target_pairs={{0,15},{1,2},{2,1},{3,4},{4,3},{5,6},{6,5},{7,8},{8,7},{9,10},{10,... | collective-permute-start | bytes 786440 | tf_op jit(solution)/shard_map/ppermute | solution.py:28
  31.9 6.9 %collective-permute-start.9 = (bf16[512,256]{1,0:T(8,128)(2,1)S(1)}, bf16[512,256]{1,0:T(8,128)(2,1)S(1)}, u32[]{:S(2)}, u32[]{:S(2)}) collective-permute-start(bf16[512,256]{1,0:T(8,128)(2,1)S(1)} %get-tuple-element.91), channel_id=1, source_target_pairs={{0,1},{1,0},{2,3},{3,2},{4,5},{5,4},{6,7},{7,6},{8,9},{9,8},{10,11... | collective-permute-start | bytes 786440 | tf_op jit(solution)/shard_map/ppermute | solution.py:23
  34.0 7.8 %collective-permute-start.8 = (bf16[192,256]{1,0:T(8,128)(2,1)S(1)}, bf16[192,256]{1,0:T(8,128)(2,1)S(1)}, u32[]{:S(2)}, u32[]{:S(2)}) collective-permute-start(bf16[192,256]{1,0:T(8,128)(2,1)S(1)} %pad_maximum_fusion.2), channel_id=1, source_target_pairs={{0,2},{1,3},{2,0},{3,1},{4,6},{5,7},{6,4},{7,5},{8,10},{9,11},{10,... | collective-permute-start | bytes 294920 | tf_op jit(solution)/shard_map/ppermute | solution.py:23
  40.0 9.9 %collective-permute-start.13 = (bf16[512,256]{1,0:T(8,128)(2,1)S(1)}, bf16[512,256]{1,0:T(8,128)(2,1)S(1)}, u32[]{:S(2)}, u32[]{:S(2)}) collective-permute-start(bf16[512,256]{1,0:T(8,128)(2,1)S(1)} %get-tuple-element.93), channel_id=1, source_target_pairs={{0,15},{1,2},{2,1},{3,4},{4,3},{5,6},{6,5},{7,8},{8,7},{9,10},{10,... | collective-permute-start | bytes 786440 | tf_op jit(solution)/shard_map/ppermute | solution.py:28
  41.8 8.1 %collective-permute-start.12 = (bf16[512,256]{1,0:T(8,128)(2,1)S(1)}, bf16[512,256]{1,0:T(8,128)(2,1)S(1)}, u32[]{:S(2)}, u32[]{:S(2)}) collective-permute-start(bf16[512,256]{1,0:T(8,128)(2,1)S(1)} %get-tuple-element.95), channel_id=1, source_target_pairs={{0,1},{1,0},{2,3},{3,2},{4,5},{5,4},{6,7},{7,6},{8,9},{9,8},{10,11... | collective-permute-start | bytes 786440 | tf_op jit(solution)/shard_map/ppermute | solution.py:23
  42.8 7.1 %collective-permute-start.11 = (bf16[384,256]{1,0:T(8,128)(2,1)S(1)}, bf16[384,256]{1,0:T(8,128)(2,1)S(1)}, u32[]{:S(2)}, u32[]{:S(2)}) collective-permute-start(bf16[384,256]{1,0:T(8,128)(2,1)S(1)} %pad_maximum_fusion), channel_id=1, source_target_pairs={{0,4},{1,5},{2,6},{3,7},{4,0},{5,1},{6,2},{7,3},{8,12},{9,13},{10,... | collective-permute-start | bytes 589832 | tf_op jit(solution)/shard_map/ppermute | solution.py:23
  49.9 3.8 %collective-permute-start.14 = (bf16[768,256]{1,0:T(8,128)(2,1)S(1)}, bf16[768,256]{1,0:T(8,128)(2,1)S(1)}, u32[]{:S(2)}, u32[]{:S(2)}) collective-permute-start(bf16[768,256]{1,0:T(8,128)(2,1)S(1)} %constant_dynamic-update-slice_fusion.4.half), channel_id=1, source_target_pairs={{0,1},{1,0},{2,3},{3,2},{4,5},{5,4},{6,7},{7,6},{8,9},{9,8},{10,11... | collective-permute-start | bytes 1179656 | tf_op jit(solution)/shard_map/ppermute | solution.py:23
  54.6 4.6 %collective-permute-start.15 = (f32[4,256]{1,0:T(4,128)S(1)}, f32[4,256]{1,0:T(4,128)S(1)}, u32[]{:S(2)}, u32[]{:S(2)}) collective-permute-start(f32[4,256]{1,0:T(4,128)S(1)} %get-tuple-element.107), channel_id=1, source_target_pairs={{0,8},{1,9},{2,10},{3,11},{4,12},{5,13},{6,14},{7,15},{8,0},{9,1},... | collective-permute-start | bytes 12296 | tf_op jit(solution)/shard_map/ppermute | solution.py:23
  59.1 4.6 %collective-permute-start.16 = (f32[4,256]{1,0:T(4,128)S(1)}, f32[4,256]{1,0:T(4,128)S(1)}, u32[]{:S(2)}, u32[]{:S(2)}) collective-permute-start(f32[4,256]{1,0:T(4,128)S(1)} %add.12), channel_id=1, source_target_pairs={{0,2},{1,3},{2,0},{3,1},{4,6},{5,7},{6,4},{7,5},{8,10},{9,11},{10,... | collective-permute-start | bytes 12296 | tf_op jit(solution)/shard_map/ppermute | solution.py:23
  63.8 5.9 %collective-permute-start.19 = (bf16[512,256]{1,0:T(8,128)(2,1)S(1)}, bf16[512,256]{1,0:T(8,128)(2,1)S(1)}, u32[]{:S(2)}, u32[]{:S(2)}) collective-permute-start(bf16[512,256]{1,0:T(8,128)(2,1)S(1)} %get-tuple-element.119), channel_id=1, source_target_pairs={{1,0},{2,1},{3,2},{4,3},{5,4},{6,5},{7,6},{8,7},{9,8},{10,9},{11,1... | collective-permute-start | bytes 786440 | tf_op jit(solution)/shard_map/ppermute | solution.py:19
  64.8 1.2 %collective-permute-start.17 = (f32[4,256]{1,0:T(4,128)S(1)}, f32[4,256]{1,0:T(4,128)S(1)}, u32[]{:S(2)}, u32[]{:S(2)}) collective-permute-start(f32[4,256]{1,0:T(4,128)S(1)} %add.13), channel_id=1, source_target_pairs={{0,1},{1,0},{2,3},{3,2},{4,5},{5,4},{6,7},{7,6},{8,9},{9,8},{10,11... | collective-permute-start | bytes 12296 | tf_op jit(solution)/shard_map/ppermute | solution.py:23
  66.0 3.7 %collective-permute-start.18 = (f32[4,256]{1,0:T(4,128)S(1)}, f32[4,256]{1,0:T(4,128)S(1)}, u32[]{:S(2)}, u32[]{:S(2)}) collective-permute-start(f32[4,256]{1,0:T(4,128)S(1)} %add.14), channel_id=1, source_target_pairs={{0,4},{1,5},{2,6},{3,7},{4,0},{5,1},{6,2},{7,3},{8,12},{9,13},{10,... | collective-permute-start | bytes 12296 | tf_op jit(solution)/shard_map/ppermute | solution.py:23

commit v15 on v14

--- a/solution.py
+++ b/solution.py
@@ -146,13 +146,14 @@
     return [halo.weight(message)] + [column_of(weight[j : j + 1]) for j in range(weight.shape[0])]
 
 
-def stage(kernel, shapes, *operands, scratch=(), fetched=0):
+def stage(kernel, shapes, *operands, scratch=(), fetched=0, outputs=pltpu.VMEM):
     out = [jax.ShapeDtypeStruct(shape, dtype) for shape, dtype in shapes]
     params = pltpu.CompilerParams(vmem_limit_bytes=VMEM_BYTES)
     spaces = [pltpu.HBM] * fetched + [pltpu.VMEM] * (len(operands) - fetched)
     call = pl.pallas_call(
         kernel,
         out_shape=out,
+        out_specs=[pl.BlockSpec(memory_space=outputs)] * len(out),
         in_specs=[pl.BlockSpec(memory_space=space) for space in spaces],
         scratch_shapes=list(scratch),
         compiler_params=params,
@@ -471,18 +472,30 @@
             whole[here] = local[beside] + split_dot(rows_of(rows, j, ncf), rows_of(coarse, j + 1, ncf), dot_tn)
 
 
-def combine(halo, sums, load, z, y, image, part, from_next, solution, residual):
+def combine(halo, sums, load, z, y, image, part, from_next, solution, residual, solution_here, residual_here, done):
     nf = halo.nf
+    subs = load.shape[0] // nf
     a, b, c, d = (sums[k : k + 1] for k in range(4))
     step = a / b
     grow = step * (c / b)
     next_step = (grow - 1.0) / ((d - c * (c / b)) * (step / b))
     s = step + next_step * grow
     t = step * next_step
-    solution[...] = s * z[...] - t * y[...]
-    last = load.shape[0] - nf
-    residual[:last] = load[:last] - s * image[:last] + t * part[:last]
-    residual[last:] = load[last:] - s * image[last:] + t * (part[last:] + from_next[...].astype(F32))
+    copies = []
+
+    def copy_out(here, source, target):
+        copies.append(pltpu.make_async_copy(source.at[here], target.at[here], done.at[len(copies)]))
+        copies[-1].start()
+
+    for j in range(subs):
+        here = slice(j * nf, (j + 1) * nf)
+        solution_here[here] = s * z[here] - t * y[here]
+        copy_out(pl.ds(j * nf, nf), solution_here, solution)
+        last = part[here] + from_next[...].astype(F32) if j == subs - 1 else part[here]
+        residual_here[here] = load[here] - s * image[here] + t * last
+        copy_out(pl.ds(j * nf, nf), residual_here, residual)
+    for copy in copies:
+        copy.wait()
 
 
 def shards(right_side, face_weight, schur, neumann, constraint, coarse_inverse):
@@ -563,11 +576,14 @@
         bind(complete), [(own, F32), (own, F32), (own, F32), ((nf, columns), BF16)],
         z_local, z_coarse, y_local, y_coarse, rows, basis_high, basis_low, product,
     )
-    for k, bit in enumerate(early + steps[-1:] + late):
+    for k, bit in enumerate(early[:1] + steps[-1:] + early[1:] + late):
         sums = sums + after(crossed(sums, bit), y)
-        if k == len(early) - 1:
+        if k == 0:
             back = shifted(after(back, sums), -1)
-    return stage(bind(combine), [(own, F32), (own, F32)], sums, load, z, y, image, part, back)
+    return stage(
+        bind(combine), [(own, F32), (own, F32)], sums, load, z, y, image, part, back,
+        scratch=[pltpu.VMEM(own, F32)] * 2 + semaphores(2 * subs), outputs=pltpu.HBM,
+    )
 
 
 def solution(mesh):

time: 71.5 us -> 72 us (level)
  waiting for transfers between devices: 18.6 us -> 19.7 us
    ppermute x15, starting transfers between devices: 19.9 us -> 17.7 us  [crossed(): lax.ppermute(block, AXIS, [(i, i ^ bit) for i in range(lax.axis_size(AXIS...]
    ppermute x2, starting transfers between devices: 1.52 us -> 3.22 us  [shifted(): lax.ppermute(block, AXIS, [((i - distance) % n, i) for i in range(n)])]
    ppermute x15, waiting for transfers between devices: 11.9 us -> 13 us  [crossed(): lax.ppermute(block, AXIS, [(i, i ^ bit) for i in range(lax.axis_size(AXIS...]
where the time goes in v15:
time: 72 us; the launch traced here: 71.8 us
  starting transfers between devices  26.8 us (37%)
  Pallas kernels  24.2 us (34%)
  waiting for transfers between devices  19.7 us (27%)
  between operations  1.01 us (1%)
    pallas_call x15, Pallas kernels, stage(): return call(*operands)  24.2 us
    ppermute x15, starting transfers between devices, crossed(): lax.ppermute(block, AXIS, [(i, i ^ bit) for i in range(lax.axis_size(AXIS...  17.7 us
    ppermute x15, waiting for transfers between devices, crossed(): lax.ppermute(block, AXIS, [(i, i ^ bit) for i in range(lax.axis_size(AXIS...  13 us
    ppermute x3, waiting for transfers between devices, far_block(): lax.ppermute(block, AXIS, [(i, (i + (1 if i % 2 else -1)) % n) for i in r...  6.71 us
    ppermute x3, starting transfers between devices, far_block(): lax.ppermute(block, AXIS, [(i, (i + (1 if i % 2 else -1)) % n) for i in r...  5.89 us
    ppermute x2, starting transfers between devices, shifted(): lax.ppermute(block, AXIS, [((i - distance) % n, i) for i in range(n)])  3.22 us
  transfers between devices with their start and end apart: 20, of which 9 were waited for; matrix products, arithmetic and copies ran while one was open for 0% of the time, Pallas kernels for 26%

profile of v15, /device:TPU:0, one launch (start us, length us, event | category | flops | bytes accessed | tf_op | source)
XLA Modules:
  0.0 71.8 jit_solution(1471915746814876552)
XLA Ops:
  0.6 1.5 %prepare.1 = (f32[1024,256]{1,0:T(8,128)S(1)}, bf16[64,512]{1,0:T(8,128)(2,1)S(1)}, f32[2,512]{1,0:T(2,128)S(1)}, bf16[64,1024]{1,0:T(8,128)(2,1)S(1)}, bf16[64,...) custom-call(f32[1024,256]{1,0:T(8,128)} %load.1, bf16[64,512]{1,0:T(8,128)(2,1)} %rows.1, f32[2,512]{1,0:T(2,128)} %weight.1, ...), custom_call_target="tpu_custom_call" | custom-call | tf_op jit(solution)/shard_map/prepare/pallas_call | solution.py:162
  2.2 0.3 halo_message.1
  2.4 0.5 collective-permute-start
  2.9 3.7 %collective-permute-start.3 = (bf16[64,256]{1,0:T(8,128)(2,1)S(1)}, bf16[64,256]{1,0:T(8,128)(2,1)S(1)}, u32[]{:S(2)}, u32[]{:S(2)}) collective-permute-start(bf16[64,256]{1,0:T(8,128)(2,1)S(1)} %get-tuple-element.76), channel_id=1, source_target_pairs={{0,8},{1,9},{2,10},{3,11},{4,12},{5,13},{6,14},{7,15},{8,0},{9,1},... | collective-permute-start | bytes 98312 | tf_op jit(solution)/shard_map/ppermute | solution.py:23
  6.6 3.5 %fetch.1 = (bf16[2048,1024]{1,0:T(8,128)(2,1)S(1)}, bf16[2048,1024]{1,0:T(8,128)(2,1)S(1)}) custom-call(bf16[2048,1024]{1,0:T(8,128)(2,1)} %neumann, bf16[2048,1024]{1,0:T(8,128)(2,1)} %schur), custom_call_target="tpu_custom_call" | custom-call | tf_op jit(solution)/shard_map/fetch/pallas_call | solution.py:162
  10.1 4.9 %collective-permute-start.4 = (bf16[128,256]{1,0:T(8,128)(2,1)S(1)}, bf16[128,256]{1,0:T(8,128)(2,1)S(1)}, u32[]{:S(2)}, u32[]{:S(2)}) collective-permute-start(bf16[128,256]{1,0:T(8,128)(2,1)S(1)} %pad_maximum_fusion.3), channel_id=1, source_target_pairs={{0,2},{1,3},{2,0},{3,1},{4,6},{5,7},{6,4},{7,5},{8,10},{9,11},{10,... | collective-permute-start | bytes 196616 | tf_op jit(solution)/shard_map/ppermute | solution.py:23
  15.0 1.0 %load_outer.1 = (f32[1024,256]{1,0:T(8,128)S(1)}, bf16[512,256]{1,0:T(8,128)(2,1)S(1)}, bf16[512,256]{1,0:T(8,128)(2,1)S(1)}) custom-call(f32[1024,256]{1,0:T(8,128)S(1)} %get-tuple-element.61.load, f32[2,512]{1,0:T(2,128)S(1)} %get-tuple-element.62.weight, bf16[720,256]{1,0:T(8,128)(2,1)S(1)} %collective-permute-done.message, ...), custom_call_target="tpu_custom_call" | custom-call | tf_op jit(solution)/shard_map/load_outer/pallas_call | solution.py:162
  16.1 1.3 %collective-permute-done.4 = bf16[128,256]{1,0:T(8,128)(2,1)S(1)} collective-permute-done((bf16[128,256]{1,0:T(8,128)(2,1)S(1)}, bf16[128,256]{1,0:T(8,128)(2,1)S(1)}, u32[]{:S(2)}, u32[]{:S(2)}) %collective-permute-start.4) | collective-permute-done | bytes 65568 | tf_op jit(solution)/shard_map/ppermute | solution.py:23
  17.4 0.1 collective-permute-start.5
  17.5 2.3 %collective-permute-start.2 = (bf16[512,256]{1,0:T(8,128)(2,1)S(1)}, bf16[512,256]{1,0:T(8,128)(2,1)S(1)}, u32[]{:S(2)}, u32[]{:S(2)}) collective-permute-start(bf16[512,256]{1,0:T(8,128)(2,1)S(1)} %get-tuple-element.69), channel_id=1, source_target_pairs={{0,15},{1,2},{2,1},{3,4},{4,3},{5,6},{6,5},{7,8},{8,7},{9,10},{10,... | collective-permute-start | bytes 786440 | tf_op jit(solution)/shard_map/ppermute | solution.py:28
  19.8 1.0 %load_inner.1.inner = f32[512,256]{1,0:T(8,128)S(1)} custom-call(f32[1024,256]{1,0:T(8,128)S(1)} %get-tuple-element.61.load, f32[2,512]{1,0:T(2,128)S(1)} %get-tuple-element.62.weight, bf16[720,256]{1,0:T(8,128)(2,1)S(1)} %collective-permute-done.message, bf16[2048,1024]{1,0:T(8,128)(2,1)S(1)} %get-tuple-element.67.neumann), custom_call_target="tpu_custom_call" | custom-call | tf_op jit(solution)/shard_map/load_inner/pallas_call | solution.py:162
  20.8 0.1 collective-permute-start.1
  20.9 1.9 %static_basis.1 = (bf16[2048,64]{1,0:T(8,128)(2,1)S(1)}, bf16[2048,64]{1,0:T(8,128)(2,1)S(1)}, bf16[128,1024]{1,0:T(8,128)(2,1)S(1)}, bf16[128,1024]{1,0:T(8,128)(2,1)S(1)}, f32[128,128]{1,0:T(8,128)S(1)}) custom-call(bf16[2048,1024]{1,0:T(8,128)(2,1)S(1)} %get-tuple-element.72.schur, bf16[720,256]{1,0:T(8,128)(2,1)S(1)} %collective-permute-done.message, ...), custom_call_target="tpu_custom_call" | custom-call | tf_op jit(solution)/shard_map/static_basis/pallas_call | solution.py:162
  22.9 0.0 collective-permute-done.5
  22.9 0.6 collective-permute-start.6
  23.5 3.2 %collective-permute-done.2.far = bf16[512,256]{1,0:T(8,128)(2,1)S(1)} collective-permute-done((bf16[512,256]{1,0:T(8,128)(2,1)S(1)}, bf16[512,256]{1,0:T(8,128)(2,1)S(1)}, u32[]{:S(2)}, u32[]{:S(2)}) %collective-permute-start.2) | collective-permute-done | bytes 262176 | tf_op jit(solution)/shard_map/ppermute | solution.py:28
  26.7 0.0 collective-permute-done.1.near
  26.7 0.0 collective-permute-done.6.crossed_half
  26.7 1.6 %coarse_load.1 = (f32[1536,256]{1,0:T(8,128)S(1)}, bf16[96,256]{1,0:T(8,128)(2,1)S(1)}, f32[96,256]{1,0:T(8,128)S(1)}, f32[96,256]{1,0:T(8,128)S(1)}, f32[8,256]{1,0:T(8,128)S(1)}) custom-call(f32[1024,256]{1,0:T(8,128)S(1)} %get-tuple-element.61.load, f32[1024,256]{1,0:T(8,128)S(1)} %get-tuple-element.68.outer, f32[512,256]{1,0:T(8,128)S(1)} %load_inner.1.inner, ...), custom_call_target="tpu_custom_call" | custom-call | tf_op jit(solution)/shard_map/coarse_load/pallas_call | solution.py:162
  28.3 0.1 collective-permute-start.7
  28.4 1.8 %schur_outer.1 = (f32[1024,256]{1,0:T(8,128)S(1)}, bf16[512,256]{1,0:T(8,128)(2,1)S(1)}, bf16[512,256]{1,0:T(8,128)(2,1)S(1)}, f32[8,256]{1,0:T(8,128)S(1)}) custom-call(f32[1536,256]{1,0:T(8,128)S(1)} %get-tuple-element.83.local.z_local, bf16[2048,1024]{1,0:T(8,128)(2,1)S(1)} %get-tuple-element.72.schur, bf16[2048,64]{1,0:T(8,128)(2,1)S(1)} %get-tuple-element.84.basis_high, ...), custom_call_target="tpu_custom_call" | custom-call | tf_op jit(solution)/shard_map/schur_outer/pallas_call | solution.py:162
  30.1 1.8 %collective-permute-start.10 = (bf16[512,256]{1,0:T(8,128)(2,1)S(1)}, bf16[512,256]{1,0:T(8,128)(2,1)S(1)}, u32[]{:S(2)}, u32[]{:S(2)}) collective-permute-start(bf16[512,256]{1,0:T(8,128)(2,1)S(1)} %get-tuple-element.92), channel_id=1, source_target_pairs={{0,15},{1,2},{2,1},{3,4},{4,3},{5,6},{6,5},{7,8},{8,7},{9,10},{10,... | collective-permute-start | bytes 786440 | tf_op jit(solution)/shard_map/ppermute | solution.py:28
  31.9 0.0 collective-permute-start.9
  31.9 1.8 %schur_inner.1 = (f32[512,256]{1,0:T(8,128)S(1)}, f32[1,256]{1,0:T(1,128)S(1)}) custom-call(f32[1536,256]{1,0:T(8,128)S(1)} %get-tuple-element.83.local.z_local, bf16[2048,1024]{1,0:T(8,128)(2,1)S(1)} %get-tuple-element.72.schur, bf16[2048,64]{1,0:T(8,128)(2,1)S(1)} %get-tuple-element.84.basis_high, bf16[2048,64]{1,0:T(8,128)(2,1)S(1)} %get-tuple-element.85.basis_low, ...), custom_call_target="tpu_custom_call" | custom-call | tf_op jit(solution)/shard_map/schur_inner/pallas_call | solution.py:162
  33.7 0.2 collective-permute-done.7
  34.0 1.3 %collective-permute-start.8 = (bf16[192,256]{1,0:T(8,128)(2,1)S(1)}, bf16[192,256]{1,0:T(8,128)(2,1)S(1)}, u32[]{:S(2)}, u32[]{:S(2)}) collective-permute-start(bf16[192,256]{1,0:T(8,128)(2,1)S(1)} %pad_maximum_fusion.2), channel_id=1, source_target_pairs={{0,2},{1,3},{2,0},{3,1},{4,6},{5,7},{6,4},{7,5},{8,10},{9,11},{10,... | collective-permute-start | bytes 294920 | tf_op jit(solution)/shard_map/ppermute | solution.py:23
  35.3 3.5 %collective-permute-done.10.far_in = bf16[512,256]{1,0:T(8,128)(2,1)S(1)} collective-permute-done((bf16[512,256]{1,0:T(8,128)(2,1)S(1)}, bf16[512,256]{1,0:T(8,128)(2,1)S(1)}, u32[]{:S(2)}, u32[]{:S(2)}) %collective-permute-start.10) | collective-permute-done | bytes 262176 | tf_op jit(solution)/shard_map/ppermute | solution.py:28
  38.8 1.1 %image_outer.1 = (f32[1024,256]{1,0:T(8,128)S(1)}, bf16[512,256]{1,0:T(8,128)(2,1)S(1)}, bf16[512,256]{1,0:T(8,128)(2,1)S(1)}) custom-call(f32[1024,256]{1,0:T(8,128)S(1)} %get-tuple-element.96.outer_in, f32[512,256]{1,0:T(8,128)S(1)} %get-tuple-element.87.inner_in, bf16[512,256]{1,0:T(8,128)(2,1)S(1)} %collective-permute-done.9.near_in, ...), custom_call_target="tpu_custom_call" | custom-call | tf_op jit(solution)/shard_map/image_outer/pallas_call | solution.py:162
  40.0 1.8 %collective-permute-start.13 = (bf16[512,256]{1,0:T(8,128)(2,1)S(1)}, bf16[512,256]{1,0:T(8,128)(2,1)S(1)}, u32[]{:S(2)}, u32[]{:S(2)}) collective-permute-start(bf16[512,256]{1,0:T(8,128)(2,1)S(1)} %get-tuple-element.93), channel_id=1, source_target_pairs={{0,15},{1,2},{2,1},{3,4},{4,3},{5,6},{6,5},{7,8},{8,7},{9,10},{10,... | collective-permute-start | bytes 786440 | tf_op jit(solution)/shard_map/ppermute | solution.py:28
  41.8 0.0 collective-permute-done.8
  41.8 1.0 %collective-permute-start.12 = (bf16[512,256]{1,0:T(8,128)(2,1)S(1)}, bf16[512,256]{1,0:T(8,128)(2,1)S(1)}, u32[]{:S(2)}, u32[]{:S(2)}) collective-permute-start(bf16[512,256]{1,0:T(8,128)(2,1)S(1)} %get-tuple-element.95), channel_id=1, source_target_pairs={{0,1},{1,0},{2,3},{3,2},{4,5},{5,4},{6,7},{7,6},{8,9},{9,8},{10,11... | collective-permute-start | bytes 786440 | tf_op jit(solution)/shard_map/ppermute | solution.py:23
  42.8 1.7 %collective-permute-start.11 = (bf16[384,256]{1,0:T(8,128)(2,1)S(1)}, bf16[384,256]{1,0:T(8,128)(2,1)S(1)}, u32[]{:S(2)}, u32[]{:S(2)}) collective-permute-start(bf16[384,256]{1,0:T(8,128)(2,1)S(1)} %pad_maximum_fusion), channel_id=1, source_target_pairs={{0,4},{1,5},{2,6},{3,7},{4,0},{5,1},{6,2},{7,3},{8,12},{9,13},{10,... | collective-permute-start | bytes 589832 | tf_op jit(solution)/shard_map/ppermute | solution.py:23
  44.4 1.2 %image_inner.1 = (f32[1024,256]{1,0:T(8,128)S(1)}, f32[512,256]{1,0:T(8,128)S(1)}) custom-call(f32[1024,256]{1,0:T(8,128)S(1)} %get-tuple-element.96.outer_in, f32[512,256]{1,0:T(8,128)S(1)} %get-tuple-element.87.inner_in, bf16[512,256]{1,0:T(8,128)(2,1)S(1)} %collective-permute-done.9.near_in, bf16[512,256]{1,0:T(8,128)(2,1)S(1)} %collective-permute-done.10.far_in, ...), custom_call_target="tpu_custom_call" | custom-call | tf_op jit(solution)/shard_map/image_inner/pallas_call | solution.py:162
  45.6 4.3 %collective-permute-done.11 = bf16[384,256]{1,0:T(8,128)(2,1)S(1)} collective-permute-done((bf16[384,256]{1,0:T(8,128)(2,1)S(1)}, bf16[384,256]{1,0:T(8,128)(2,1)S(1)}, u32[]{:S(2)}, u32[]{:S(2)}) %collective-permute-start.11) | collective-permute-done | bytes 196640 | tf_op jit(solution)/shard_map/ppermute | solution.py:23
  49.9 0.0 collective-permute-done.12.near
  49.9 0.1 collective-permute-start.14
  50.0 3.7 %schur_image.1 = (f32[1536,256]{1,0:T(8,128)S(1)}, f32[1536,256]{1,0:T(8,128)S(1)}, f32[8,256]{1,0:T(8,128)S(1)}, f32[128,256]{1,0:T(8,128)S(1)}) custom-call(f32[1024,256]{1,0:T(8,128)S(1)} %get-tuple-element.100.image, f32[1024,256]{1,0:T(8,128)S(1)} %get-tuple-element.102.outer, f32[512,256]{1,0:T(8,128)S(1)} %get-tuple-element.97.inner, ...), custom_call_target="tpu_custom_call" | custom-call | tf_op jit(solution)/shard_map/schur_image/pallas_call | solution.py:162
  53.7 0.8 %coarse_image.1 = (f32[4,256]{1,0:T(4,128)S(1)}, f32[96,256]{1,0:T(8,128)S(1)}) custom-call(bf16[768,256]{1,0:T(8,128)(2,1)S(1)} %constant_dynamic-update-slice_fusion.4.half, bf16[768,256]{1,0:T(8,128)(2,1)S(1)} %collective-permute-done.14.crossed_half, bf16[64,1024]{1,0:T(8,128)(2,1)S(1)} %get-tuple-element.64.inverse, ...), custom_call_target="tpu_custom_call" | custom-call | tf_op jit(solution)/shard_map/coarse_image/pallas_call | solution.py:162
  54.6 2.7 %collective-permute-start.15 = (f32[4,256]{1,0:T(4,128)S(1)}, f32[4,256]{1,0:T(4,128)S(1)}, u32[]{:S(2)}, u32[]{:S(2)}) collective-permute-start(f32[4,256]{1,0:T(4,128)S(1)} %get-tuple-element.107), channel_id=1, source_target_pairs={{0,8},{1,9},{2,10},{3,11},{4,12},{5,13},{6,14},{7,15},{8,0},{9,1},... | collective-permute-start | bytes 12296 | tf_op jit(solution)/shard_map/ppermute | solution.py:23
  57.2 1.5 %complete.1 = (f32[1024,256]{1,0:T(8,128)S(1)}, f32[1024,256]{1,0:T(8,128)S(1)}, f32[1024,256]{1,0:T(8,128)S(1)}, bf16[512,256]{1,0:T(8,128)(2,1)S(1)}) custom-call(f32[1536,256]{1,0:T(8,128)S(1)} %get-tuple-element.83.local.z_local, f32[96,256]{1,0:T(8,128)S(1)} %get-tuple-element.86.solution.z_coarse, f32[1536,256]{1,0:T(8,128)S(1)} %get-tuple-element.108.y_local, ...), custom_call_target="tpu_custom_call" | custom-call | tf_op jit(solution)/shard_map/complete/pallas_call | solution.py:162
  58.7 0.4 collective-permute-done.15
  59.1 2.7 %collective-permute-start.19 = (bf16[512,256]{1,0:T(8,128)(2,1)S(1)}, bf16[512,256]{1,0:T(8,128)(2,1)S(1)}, u32[]{:S(2)}, u32[]{:S(2)}) collective-permute-start(bf16[512,256]{1,0:T(8,128)(2,1)S(1)} %get-tuple-element.119), channel_id=1, source_target_pairs={{1,0},{2,1},{3,2},{4,3},{5,4},{6,5},{7,6},{8,7},{9,8},{10,9},{11,1... | collective-permute-start | bytes 786440 | tf_op jit(solution)/shard_map/ppermute | solution.py:19
  61.8 1.2 %collective-permute-done.16 = f32[4,256]{1,0:T(4,128)S(1)} collective-permute-done((f32[4,256]{1,0:T(4,128)S(1)}, f32[4,256]{1,0:T(4,128)S(1)}, u32[]{:S(2)}, u32[]{:S(2)}) %collective-permute-start.16) | collective-permute-done | bytes 4128 | tf_op jit(solution)/shard_map/ppermute | solution.py:23
  63.0 0.7 collective-permute-start.17
  63.7 2.9 %collective-permute-done.17 = f32[4,256]{1,0:T(4,128)S(1)} collective-permute-done((f32[4,256]{1,0:T(4,128)S(1)}, f32[4,256]{1,0:T(4,128)S(1)}, u32[]{:S(2)}, u32[]{:S(2)}) %collective-permute-start.17) | collective-permute-done | bytes 4128 | tf_op jit(solution)/shard_map/ppermute | solution.py:23
  66.6 0.9 %collective-permute-start.18 = (f32[4,256]{1,0:T(4,128)S(1)}, f32[4,256]{1,0:T(4,128)S(1)}, u32[]{:S(2)}, u32[]{:S(2)}) collective-permute-start(f32[4,256]{1,0:T(4,128)S(1)} %add.14), channel_id=1, source_target_pairs={{0,4},{1,5},{2,6},{3,7},{4,0},{5,1},{6,2},{7,3},{8,12},{9,13},{10,... | collective-permute-start | bytes 12296 | tf_op jit(solution)/shard_map/ppermute | solution.py:23
  67.6 2.7 %collective-permute-done.18 = f32[4,256]{1,0:T(4,128)S(1)} collective-permute-done((f32[4,256]{1,0:T(4,128)S(1)}, f32[4,256]{1,0:T(4,128)S(1)}, u32[]{:S(2)}, u32[]{:S(2)}) %collective-permute-start.18) | collective-permute-done | bytes 4128 | tf_op jit(solution)/shard_map/ppermute | solution.py:23
  70.2 1.4 %combine.1 = (f32[1024,256]{1,0:T(8,128)}, f32[1024,256]{1,0:T(8,128)}) custom-call(f32[4,256]{1,0:T(4,128)S(1)} %add.15.sums, f32[1024,256]{1,0:T(8,128)S(1)} %get-tuple-element.61.load, f32[1024,256]{1,0:T(8,128)S(1)} %get-tuple-element.116.z, f32[1024,256]{1,0:T(8,128)S(1)} %get-tuple-element.111.y, f32[1024,256]{1,0:T(8,128)S(1)} %get-tuple-element.100.image, ...), custom_call_target="tpu_custom_call" | custom-call | tf_op jit(solution)/shard_map/combine/pallas_call | solution.py:162
  (23 shorter events, 0.1 us)
Async XLA Ops:
  2.4 12.6 %collective-permute-start = (bf16[720,256]{1,0:T(8,128)(2,1)S(1)}, bf16[720,256]{1,0:T(8,128)(2,1)S(1)}, u32[]{:S(2)}, u32[]{:S(2)}) collective-permute-start(bf16[720,256]{1,0:T(8,128)(2,1)S(1)} %halo_message.1), channel_id=1, source_target_pairs={{15,0},{0,1},{1,2},{2,3},{3,4},{4,5},{5,6},{6,7},{7,8},{8,9},{9,10... | collective-permute-start | bytes 1105928 | tf_op jit(solution)/shard_map/ppermute | solution.py:19
  2.9 7.2 %collective-permute-start.3 = (bf16[64,256]{1,0:T(8,128)(2,1)S(1)}, bf16[64,256]{1,0:T(8,128)(2,1)S(1)}, u32[]{:S(2)}, u32[]{:S(2)}) collective-permute-start(bf16[64,256]{1,0:T(8,128)(2,1)S(1)} %get-tuple-element.76), channel_id=1, source_target_pairs={{0,8},{1,9},{2,10},{3,11},{4,12},{5,13},{6,14},{7,15},{8,0},{9,1},... | collective-permute-start | bytes 98312 | tf_op jit(solution)/shard_map/ppermute | solution.py:23
  10.1 7.3 %collective-permute-start.4 = (bf16[128,256]{1,0:T(8,128)(2,1)S(1)}, bf16[128,256]{1,0:T(8,128)(2,1)S(1)}, u32[]{:S(2)}, u32[]{:S(2)}) collective-permute-start(bf16[128,256]{1,0:T(8,128)(2,1)S(1)} %pad_maximum_fusion.3), channel_id=1, source_target_pairs={{0,2},{1,3},{2,0},{3,1},{4,6},{5,7},{6,4},{7,5},{8,10},{9,11},{10,... | collective-permute-start | bytes 196616 | tf_op jit(solution)/shard_map/ppermute | solution.py:23
  17.4 5.5 %collective-permute-start.5 = (bf16[256,256]{1,0:T(8,128)(2,1)S(1)}, bf16[256,256]{1,0:T(8,128)(2,1)S(1)}, u32[]{:S(2)}, u32[]{:S(2)}) collective-permute-start(bf16[256,256]{1,0:T(8,128)(2,1)S(1)} %pad_maximum_fusion.1), channel_id=1, source_target_pairs={{0,4},{1,5},{2,6},{3,7},{4,0},{5,1},{6,2},{7,3},{8,12},{9,13},{10,... | collective-permute-start | bytes 393224 | tf_op jit(solution)/shard_map/ppermute | solution.py:23
  17.5 9.1 %collective-permute-start.2 = (bf16[512,256]{1,0:T(8,128)(2,1)S(1)}, bf16[512,256]{1,0:T(8,128)(2,1)S(1)}, u32[]{:S(2)}, u32[]{:S(2)}) collective-permute-start(bf16[512,256]{1,0:T(8,128)(2,1)S(1)} %get-tuple-element.69), channel_id=1, source_target_pairs={{0,15},{1,2},{2,1},{3,4},{4,3},{5,6},{6,5},{7,8},{8,7},{9,10},{10,... | collective-permute-start | bytes 786440 | tf_op jit(solution)/shard_map/ppermute | solution.py:28
  20.8 5.8 %collective-permute-start.1 = (bf16[512,256]{1,0:T(8,128)(2,1)S(1)}, bf16[512,256]{1,0:T(8,128)(2,1)S(1)}, u32[]{:S(2)}, u32[]{:S(2)}) collective-permute-start(bf16[512,256]{1,0:T(8,128)(2,1)S(1)} %get-tuple-element.71), channel_id=1, source_target_pairs={{0,1},{1,0},{2,3},{3,2},{4,5},{5,4},{6,7},{7,6},{8,9},{9,8},{10,11... | collective-permute-start | bytes 786440 | tf_op jit(solution)/shard_map/ppermute | solution.py:23
  22.9 3.8 %collective-permute-start.6 = (bf16[512,256]{1,0:T(8,128)(2,1)S(1)}, bf16[512,256]{1,0:T(8,128)(2,1)S(1)}, u32[]{:S(2)}, u32[]{:S(2)}) collective-permute-start(bf16[512,256]{1,0:T(8,128)(2,1)S(1)} %constant_dynamic-update-slice_fusion.half), channel_id=1, source_target_pairs={{0,1},{1,0},{2,3},{3,2},{4,5},{5,4},{6,7},{7,6},{8,9},{9,8},{10,11... | collective-permute-start | bytes 786440 | tf_op jit(solution)/shard_map/ppermute | solution.py:23
  28.3 5.7 %collective-permute-start.7 = (bf16[96,256]{1,0:T(8,128)(2,1)S(1)}, bf16[96,256]{1,0:T(8,128)(2,1)S(1)}, u32[]{:S(2)}, u32[]{:S(2)}) collective-permute-start(bf16[96,256]{1,0:T(8,128)(2,1)S(1)} %get-tuple-element.82), channel_id=1, source_target_pairs={{0,8},{1,9},{2,10},{3,11},{4,12},{5,13},{6,14},{7,15},{8,0},{9,1},... | collective-permute-start | bytes 147464 | tf_op jit(solution)/shard_map/ppermute | solution.py:23
  30.1 8.7 %collective-permute-start.10 = (bf16[512,256]{1,0:T(8,128)(2,1)S(1)}, bf16[512,256]{1,0:T(8,128)(2,1)S(1)}, u32[]{:S(2)}, u32[]{:S(2)}) collective-permute-start(bf16[512,256]{1,0:T(8,128)(2,1)S(1)} %get-tuple-element.92), channel_id=1, source_target_pairs={{0,15},{1,2},{2,1},{3,4},{4,3},{5,6},{6,5},{7,8},{8,7},{9,10},{10,... | collective-permute-start | bytes 786440 | tf_op jit(solution)/shard_map/ppermute | solution.py:28
  31.9 6.9 %collective-permute-start.9 = (bf16[512,256]{1,0:T(8,128)(2,1)S(1)}, bf16[512,256]{1,0:T(8,128)(2,1)S(1)}, u32[]{:S(2)}, u32[]{:S(2)}) collective-permute-start(bf16[512,256]{1,0:T(8,128)(2,1)S(1)} %get-tuple-element.91), channel_id=1, source_target_pairs={{0,1},{1,0},{2,3},{3,2},{4,5},{5,4},{6,7},{7,6},{8,9},{9,8},{10,11... | collective-permute-start | bytes 786440 | tf_op jit(solution)/shard_map/ppermute | solution.py:23
  34.0 7.8 %collective-permute-start.8 = (bf16[192,256]{1,0:T(8,128)(2,1)S(1)}, bf16[192,256]{1,0:T(8,128)(2,1)S(1)}, u32[]{:S(2)}, u32[]{:S(2)}) collective-permute-start(bf16[192,256]{1,0:T(8,128)(2,1)S(1)} %pad_maximum_fusion.2), channel_id=1, source_target_pairs={{0,2},{1,3},{2,0},{3,1},{4,6},{5,7},{6,4},{7,5},{8,10},{9,11},{10,... | collective-permute-start | bytes 294920 | tf_op jit(solution)/shard_map/ppermute | solution.py:23
  40.0 9.9 %collective-permute-start.13 = (bf16[512,256]{1,0:T(8,128)(2,1)S(1)}, bf16[512,256]{1,0:T(8,128)(2,1)S(1)}, u32[]{:S(2)}, u32[]{:S(2)}) collective-permute-start(bf16[512,256]{1,0:T(8,128)(2,1)S(1)} %get-tuple-element.93), channel_id=1, source_target_pairs={{0,15},{1,2},{2,1},{3,4},{4,3},{5,6},{6,5},{7,8},{8,7},{9,10},{10,... | collective-permute-start | bytes 786440 | tf_op jit(solution)/shard_map/ppermute | solution.py:28
  41.8 8.1 %collective-permute-start.12 = (bf16[512,256]{1,0:T(8,128)(2,1)S(1)}, bf16[512,256]{1,0:T(8,128)(2,1)S(1)}, u32[]{:S(2)}, u32[]{:S(2)}) collective-permute-start(bf16[512,256]{1,0:T(8,128)(2,1)S(1)} %get-tuple-element.95), channel_id=1, source_target_pairs={{0,1},{1,0},{2,3},{3,2},{4,5},{5,4},{6,7},{7,6},{8,9},{9,8},{10,11... | collective-permute-start | bytes 786440 | tf_op jit(solution)/shard_map/ppermute | solution.py:23
  42.8 7.1 %collective-permute-start.11 = (bf16[384,256]{1,0:T(8,128)(2,1)S(1)}, bf16[384,256]{1,0:T(8,128)(2,1)S(1)}, u32[]{:S(2)}, u32[]{:S(2)}) collective-permute-start(bf16[384,256]{1,0:T(8,128)(2,1)S(1)} %pad_maximum_fusion), channel_id=1, source_target_pairs={{0,4},{1,5},{2,6},{3,7},{4,0},{5,1},{6,2},{7,3},{8,12},{9,13},{10,... | collective-permute-start | bytes 589832 | tf_op jit(solution)/shard_map/ppermute | solution.py:23
  49.9 3.8 %collective-permute-start.14 = (bf16[768,256]{1,0:T(8,128)(2,1)S(1)}, bf16[768,256]{1,0:T(8,128)(2,1)S(1)}, u32[]{:S(2)}, u32[]{:S(2)}) collective-permute-start(bf16[768,256]{1,0:T(8,128)(2,1)S(1)} %constant_dynamic-update-slice_fusion.4.half), channel_id=1, source_target_pairs={{0,1},{1,0},{2,3},{3,2},{4,5},{5,4},{6,7},{7,6},{8,9},{9,8},{10,11... | collective-permute-start | bytes 1179656 | tf_op jit(solution)/shard_map/ppermute | solution.py:23
  54.6 4.6 %collective-permute-start.15 = (f32[4,256]{1,0:T(4,128)S(1)}, f32[4,256]{1,0:T(4,128)S(1)}, u32[]{:S(2)}, u32[]{:S(2)}) collective-permute-start(f32[4,256]{1,0:T(4,128)S(1)} %get-tuple-element.107), channel_id=1, source_target_pairs={{0,8},{1,9},{2,10},{3,11},{4,12},{5,13},{6,14},{7,15},{8,0},{9,1},... | collective-permute-start | bytes 12296 | tf_op jit(solution)/shard_map/ppermute | solution.py:23
  59.1 11.1 %collective-permute-start.19 = (bf16[512,256]{1,0:T(8,128)(2,1)S(1)}, bf16[512,256]{1,0:T(8,128)(2,1)S(1)}, u32[]{:S(2)}, u32[]{:S(2)}) collective-permute-start(bf16[512,256]{1,0:T(8,128)(2,1)S(1)} %get-tuple-element.119), channel_id=1, source_target_pairs={{1,0},{2,1},{3,2},{4,3},{5,4},{6,5},{7,6},{8,7},{9,8},{10,9},{11,1... | collective-permute-start | bytes 786440 | tf_op jit(solution)/shard_map/ppermute | solution.py:19
  61.8 1.2 %collective-permute-start.16 = (f32[4,256]{1,0:T(4,128)S(1)}, f32[4,256]{1,0:T(4,128)S(1)}, u32[]{:S(2)}, u32[]{:S(2)}) collective-permute-start(f32[4,256]{1,0:T(4,128)S(1)} %add.12), channel_id=1, source_target_pairs={{0,1},{1,0},{2,3},{3,2},{4,5},{5,4},{6,7},{7,6},{8,9},{9,8},{10,11... | collective-permute-start | bytes 12296 | tf_op jit(solution)/shard_map/ppermute | solution.py:23
  63.0 3.6 %collective-permute-start.17 = (f32[4,256]{1,0:T(4,128)S(1)}, f32[4,256]{1,0:T(4,128)S(1)}, u32[]{:S(2)}, u32[]{:S(2)}) collective-permute-start(f32[4,256]{1,0:T(4,128)S(1)} %add.13), channel_id=1, source_target_pairs={{0,2},{1,3},{2,0},{3,1},{4,6},{5,7},{6,4},{7,5},{8,10},{9,11},{10,... | collective-permute-start | bytes 12296 | tf_op jit(solution)/shard_map/ppermute | solution.py:23
  66.6 3.6 %collective-permute-start.18 = (f32[4,256]{1,0:T(4,128)S(1)}, f32[4,256]{1,0:T(4,128)S(1)}, u32[]{:S(2)}, u32[]{:S(2)}) collective-permute-start(f32[4,256]{1,0:T(4,128)S(1)} %add.14), channel_id=1, source_target_pairs={{0,4},{1,5},{2,6},{3,7},{4,0},{5,1},{6,2},{7,3},{8,12},{9,13},{10,... | collective-permute-start | bytes 12296 | tf_op jit(solution)/shard_map/ppermute | solution.py:23

commit v16 on v15

--- a/solution.py
+++ b/solution.py
@@ -551,11 +551,11 @@
     outer, near, far, sums = stage(
         bind(schur_outer), outside_faces + [sum_rows], z_local, schur, basis_high, basis_low, z_coarse, sums
     )
+    half = gather_half(shares_rounded, early[:1], far)
     inner, energies = stage(
-        bind(schur_inner), inside_faces + [((subs - 1, columns), F32)], z_local, schur, basis_high, basis_low, z_coarse
-    )
-    half = gather_half(shares_rounded, early[:1], inner)
-    far, near = far_block(far), crossed(near, 1)
+        bind(schur_inner), inside_faces + [((subs - 1, columns), F32)], after(z_local, half), schur, basis_high, basis_low, z_coarse
+    )
+    far, near = far_block(far), crossed(after(near, half), 1)
     operands = outer, inner, near, far, weight, message, neumann
     outer, near, far = stage(bind(image_outer), outside_faces, *operands)
     image, inner = stage(bind(image_inner), [(own, F32)] + inside_faces, after(operands[0], far), *operands[1:])
@@ -576,9 +576,9 @@
         bind(complete), [(own, F32), (own, F32), (own, F32), ((nf, columns), BF16)],
         z_local, z_coarse, y_local, y_coarse, rows, basis_high, basis_low, product,
     )
-    for k, bit in enumerate(early[:1] + steps[-1:] + early[1:] + late):
+    for k, bit in enumerate(early + steps[-1:] + late):
         sums = sums + after(crossed(sums, bit), y)
-        if k == 0:
+        if k == len(early) - 1:
             back = shifted(after(back, sums), -1)
     return stage(
         bind(combine), [(own, F32), (own, F32)], sums, load, z, y, image, part, back,

time: 72 us -> 71.4 us (level)
    ppermute x15, starting transfers between devices: 17.7 us -> 19.4 us  [crossed(): lax.ppermute(block, AXIS, [(i, i ^ bit) for i in range(lax.axis_size(AXIS...]
    ppermute x2, starting transfers between devices: 3.22 us -> 1.52 us  [shifted(): lax.ppermute(block, AXIS, [((i - distance) % n, i) for i in range(n)])]
    ppermute x3, waiting for transfers between devices: 6.71 us -> 5.41 us  [far_block(): lax.ppermute(block, AXIS, [(i, (i + (1 if i % 2 else -1)) % n) for i in r...]
where the time goes in v16:
time: 71.4 us; the launch traced here: 71.3 us
  starting transfers between devices  26.9 us (38%)
  Pallas kernels  24.2 us (34%)
  waiting for transfers between devices  19.1 us (27%)
  between operations  1.02 us (1%)
    pallas_call x15, Pallas kernels, stage(): return call(*operands)  24.2 us
    ppermute x15, starting transfers between devices, crossed(): lax.ppermute(block, AXIS, [(i, i ^ bit) for i in range(lax.axis_size(AXIS...  19.4 us
    ppermute x15, waiting for transfers between devices, crossed(): lax.ppermute(block, AXIS, [(i, i ^ bit) for i in range(lax.axis_size(AXIS...  13.7 us
    ppermute x3, starting transfers between devices, far_block(): lax.ppermute(block, AXIS, [(i, (i + (1 if i % 2 else -1)) % n) for i in r...  5.9 us
    ppermute x3, waiting for transfers between devices, far_block(): lax.ppermute(block, AXIS, [(i, (i + (1 if i % 2 else -1)) % n) for i in r...  5.41 us
    ppermute x2, starting transfers between devices, shifted(): lax.ppermute(block, AXIS, [((i - distance) % n, i) for i in range(n)])  1.52 us
  transfers between devices with their start and end apart: 20, of which 9 were waited for; matrix products, arithmetic and copies ran while one was open for 0% of the time, Pallas kernels for 26%

profile of v16, /device:TPU:0, one launch (start us, length us, event | category | flops | bytes accessed | tf_op | source)
XLA Modules:
  0.0 71.3 jit_solution(9142987156356578624)
XLA Ops:
  0.6 1.5 %prepare.1 = (f32[1024,256]{1,0:T(8,128)S(1)}, bf16[64,512]{1,0:T(8,128)(2,1)S(1)}, f32[2,512]{1,0:T(2,128)S(1)}, bf16[64,1024]{1,0:T(8,128)(2,1)S(1)}, bf16[64,...) custom-call(f32[1024,256]{1,0:T(8,128)} %load.1, bf16[64,512]{1,0:T(8,128)(2,1)} %rows.1, f32[2,512]{1,0:T(2,128)} %weight.1, ...), custom_call_target="tpu_custom_call" | custom-call | tf_op jit(solution)/shard_map/prepare/pallas_call | solution.py:162
  2.2 0.3 halo_message.1
  2.4 0.5 collective-permute-start
  2.9 3.7 %collective-permute-start.3 = (bf16[64,256]{1,0:T(8,128)(2,1)S(1)}, bf16[64,256]{1,0:T(8,128)(2,1)S(1)}, u32[]{:S(2)}, u32[]{:S(2)}) collective-permute-start(bf16[64,256]{1,0:T(8,128)(2,1)S(1)} %get-tuple-element.78), channel_id=1, source_target_pairs={{0,8},{1,9},{2,10},{3,11},{4,12},{5,13},{6,14},{7,15},{8,0},{9,1},... | collective-permute-start | bytes 98312 | tf_op jit(solution)/shard_map/ppermute | solution.py:23
  6.6 3.5 %fetch.1 = (bf16[2048,1024]{1,0:T(8,128)(2,1)S(1)}, bf16[2048,1024]{1,0:T(8,128)(2,1)S(1)}) custom-call(bf16[2048,1024]{1,0:T(8,128)(2,1)} %neumann, bf16[2048,1024]{1,0:T(8,128)(2,1)} %schur), custom_call_target="tpu_custom_call" | custom-call | tf_op jit(solution)/shard_map/fetch/pallas_call | solution.py:162
  10.1 0.0 collective-permute-done.3
  10.1 4.9 %collective-permute-start.4 = (bf16[128,256]{1,0:T(8,128)(2,1)S(1)}, bf16[128,256]{1,0:T(8,128)(2,1)S(1)}, u32[]{:S(2)}, u32[]{:S(2)}) collective-permute-start(bf16[128,256]{1,0:T(8,128)(2,1)S(1)} %pad_maximum_fusion.2), channel_id=1, source_target_pairs={{0,2},{1,3},{2,0},{3,1},{4,6},{5,7},{6,4},{7,5},{8,10},{9,11},{10,... | collective-permute-start | bytes 196616 | tf_op jit(solution)/shard_map/ppermute | solution.py:23
  15.0 0.0 collective-permute-done.message
  15.0 1.0 %load_outer.1 = (f32[1024,256]{1,0:T(8,128)S(1)}, bf16[512,256]{1,0:T(8,128)(2,1)S(1)}, bf16[512,256]{1,0:T(8,128)(2,1)S(1)}) custom-call(f32[1024,256]{1,0:T(8,128)S(1)} %get-tuple-element.63.load, f32[2,512]{1,0:T(2,128)S(1)} %get-tuple-element.64.weight, bf16[720,256]{1,0:T(8,128)(2,1)S(1)} %collective-permute-done.message, ...), custom_call_target="tpu_custom_call" | custom-call | tf_op jit(solution)/shard_map/load_outer/pallas_call | solution.py:162
  16.1 1.3 %collective-permute-done.4 = bf16[128,256]{1,0:T(8,128)(2,1)S(1)} collective-permute-done((bf16[128,256]{1,0:T(8,128)(2,1)S(1)}, bf16[128,256]{1,0:T(8,128)(2,1)S(1)}, u32[]{:S(2)}, u32[]{:S(2)}) %collective-permute-start.4) | collective-permute-done | bytes 65568 | tf_op jit(solution)/shard_map/ppermute | solution.py:23
  17.4 0.1 collective-permute-start.5
  17.5 2.3 %collective-permute-start.2 = (bf16[512,256]{1,0:T(8,128)(2,1)S(1)}, bf16[512,256]{1,0:T(8,128)(2,1)S(1)}, u32[]{:S(2)}, u32[]{:S(2)}) collective-permute-start(bf16[512,256]{1,0:T(8,128)(2,1)S(1)} %get-tuple-element.71), channel_id=1, source_target_pairs={{0,15},{1,2},{2,1},{3,4},{4,3},{5,6},{6,5},{7,8},{8,7},{9,10},{10,... | collective-permute-start | bytes 786440 | tf_op jit(solution)/shard_map/ppermute | solution.py:28
  19.8 0.0 collective-permute-start.1
  19.8 1.0 %load_inner.1.inner = f32[512,256]{1,0:T(8,128)S(1)} custom-call(f32[1024,256]{1,0:T(8,128)S(1)} %get-tuple-element.63.load, f32[2,512]{1,0:T(2,128)S(1)} %get-tuple-element.64.weight, bf16[720,256]{1,0:T(8,128)(2,1)S(1)} %collective-permute-done.message, bf16[2048,1024]{1,0:T(8,128)(2,1)S(1)} %get-tuple-element.69.neumann), custom_call_target="tpu_custom_call" | custom-call | tf_op jit(solution)/shard_map/load_inner/pallas_call | solution.py:162
  20.8 1.9 %static_basis.1 = (bf16[2048,64]{1,0:T(8,128)(2,1)S(1)}, bf16[2048,64]{1,0:T(8,128)(2,1)S(1)}, bf16[128,1024]{1,0:T(8,128)(2,1)S(1)}, bf16[128,1024]{1,0:T(8,128)(2,1)S(1)}, f32[128,128]{1,0:T(8,128)S(1)}) custom-call(bf16[2048,1024]{1,0:T(8,128)(2,1)S(1)} %get-tuple-element.74.schur, bf16[720,256]{1,0:T(8,128)(2,1)S(1)} %collective-permute-done.message, ...), custom_call_target="tpu_custom_call" | custom-call | tf_op jit(solution)/shard_map/static_basis/pallas_call | solution.py:162
  22.8 0.0 collective-permute-done.5
  22.8 0.6 collective-permute-start.6
  23.4 3.3 %collective-permute-done.2.far = bf16[512,256]{1,0:T(8,128)(2,1)S(1)} collective-permute-done((bf16[512,256]{1,0:T(8,128)(2,1)S(1)}, bf16[512,256]{1,0:T(8,128)(2,1)S(1)}, u32[]{:S(2)}, u32[]{:S(2)}) %collective-permute-start.2) | collective-permute-done | bytes 262176 | tf_op jit(solution)/shard_map/ppermute | solution.py:28
  26.7 0.0 collective-permute-done.6.crossed_half
  26.7 1.6 %coarse_load.1 = (f32[1536,256]{1,0:T(8,128)S(1)}, bf16[96,256]{1,0:T(8,128)(2,1)S(1)}, f32[96,256]{1,0:T(8,128)S(1)}, f32[96,256]{1,0:T(8,128)S(1)}, f32[8,256]{1,0:T(8,128)S(1)}) custom-call(f32[1024,256]{1,0:T(8,128)S(1)} %get-tuple-element.63.load, f32[1024,256]{1,0:T(8,128)S(1)} %get-tuple-element.70.outer, f32[512,256]{1,0:T(8,128)S(1)} %load_inner.1.inner, ...), custom_call_target="tpu_custom_call" | custom-call | tf_op jit(solution)/shard_map/coarse_load/pallas_call | solution.py:162
  28.3 0.1 collective-permute-start.7
  28.4 1.8 %schur_outer.1 = (f32[1024,256]{1,0:T(8,128)S(1)}, bf16[512,256]{1,0:T(8,128)(2,1)S(1)}, bf16[512,256]{1,0:T(8,128)(2,1)S(1)}, f32[8,256]{1,0:T(8,128)S(1)}) custom-call(f32[1536,256]{1,0:T(8,128)S(1)} %get-tuple-element.93.local.z_local, bf16[2048,1024]{1,0:T(8,128)(2,1)S(1)} %get-tuple-element.74.schur, bf16[2048,64]{1,0:T(8,128)(2,1)S(1)} %get-tuple-element.86.basis_high, ...), custom_call_target="tpu_custom_call" | custom-call | tf_op jit(solution)/shard_map/schur_outer/pallas_call | solution.py:162
  30.2 1.8 %collective-permute-start.10 = (bf16[512,256]{1,0:T(8,128)(2,1)S(1)}, bf16[512,256]{1,0:T(8,128)(2,1)S(1)}, u32[]{:S(2)}, u32[]{:S(2)}) collective-permute-start(bf16[512,256]{1,0:T(8,128)(2,1)S(1)} %get-tuple-element.90), channel_id=1, source_target_pairs={{0,15},{1,2},{2,1},{3,4},{4,3},{5,6},{6,5},{7,8},{8,7},{9,10},{10,... | collective-permute-start | bytes 786440 | tf_op jit(solution)/shard_map/ppermute | solution.py:28
  32.0 2.0 %collective-permute-done.7 = bf16[96,256]{1,0:T(8,128)(2,1)S(1)} collective-permute-done((bf16[96,256]{1,0:T(8,128)(2,1)S(1)}, bf16[96,256]{1,0:T(8,128)(2,1)S(1)}, u32[]{:S(2)}, u32[]{:S(2)}) %collective-permute-start.7) | collective-permute-done | bytes 49184 | tf_op jit(solution)/shard_map/ppermute | solution.py:23
  34.0 0.1 collective-permute-start.9
  34.1 0.8 %collective-permute-start.8 = (bf16[192,256]{1,0:T(8,128)(2,1)S(1)}, bf16[192,256]{1,0:T(8,128)(2,1)S(1)}, u32[]{:S(2)}, u32[]{:S(2)}) collective-permute-start(bf16[192,256]{1,0:T(8,128)(2,1)S(1)} %get-tuple-element.124), channel_id=1, source_target_pairs={{0,2},{1,3},{2,0},{3,1},{4,6},{5,7},{6,4},{7,5},{8,10},{9,11},{10,... | collective-permute-start | bytes 294920 | tf_op jit(solution)/shard_map/ppermute | solution.py:23
  34.9 1.8 %schur_inner.1 = (f32[512,256]{1,0:T(8,128)S(1)}, f32[1,256]{1,0:T(1,128)S(1)}) custom-call(f32[1536,256]{1,0:T(8,128)S(1)} %get-tuple-element.93.local.z_local, bf16[2048,1024]{1,0:T(8,128)(2,1)S(1)} %get-tuple-element.74.schur, bf16[2048,64]{1,0:T(8,128)(2,1)S(1)} %get-tuple-element.86.basis_high, bf16[2048,64]{1,0:T(8,128)(2,1)S(1)} %get-tuple-element.87.basis_low, ...), custom_call_target="tpu_custom_call" | custom-call | tf_op jit(solution)/shard_map/schur_inner/pallas_call | solution.py:162
  36.7 2.1 %collective-permute-done.10.far_in = bf16[512,256]{1,0:T(8,128)(2,1)S(1)} collective-permute-done((bf16[512,256]{1,0:T(8,128)(2,1)S(1)}, bf16[512,256]{1,0:T(8,128)(2,1)S(1)}, u32[]{:S(2)}, u32[]{:S(2)}) %collective-permute-start.10) | collective-permute-done | bytes 262176 | tf_op jit(solution)/shard_map/ppermute | solution.py:28
  38.8 0.0 collective-permute-done.9.near_in
  38.8 1.1 %image_outer.1 = (f32[1024,256]{1,0:T(8,128)S(1)}, bf16[512,256]{1,0:T(8,128)(2,1)S(1)}, bf16[512,256]{1,0:T(8,128)(2,1)S(1)}) custom-call(f32[1024,256]{1,0:T(8,128)S(1)} %get-tuple-element.100.outer_in, f32[512,256]{1,0:T(8,128)S(1)} %get-tuple-element.94.inner_in, bf16[512,256]{1,0:T(8,128)(2,1)S(1)} %collective-permute-done.9.near_in, ...), custom_call_target="tpu_custom_call" | custom-call | tf_op jit(solution)/shard_map/image_outer/pallas_call | solution.py:162
  40.0 1.8 %collective-permute-start.13 = (bf16[512,256]{1,0:T(8,128)(2,1)S(1)}, bf16[512,256]{1,0:T(8,128)(2,1)S(1)}, u32[]{:S(2)}, u32[]{:S(2)}) collective-permute-start(bf16[512,256]{1,0:T(8,128)(2,1)S(1)} %get-tuple-element.97), channel_id=1, source_target_pairs={{0,15},{1,2},{2,1},{3,4},{4,3},{5,6},{6,5},{7,8},{8,7},{9,10},{10,... | collective-permute-start | bytes 786440 | tf_op jit(solution)/shard_map/ppermute | solution.py:28
  41.8 1.0 %collective-permute-start.12 = (bf16[512,256]{1,0:T(8,128)(2,1)S(1)}, bf16[512,256]{1,0:T(8,128)(2,1)S(1)}, u32[]{:S(2)}, u32[]{:S(2)}) collective-permute-start(bf16[512,256]{1,0:T(8,128)(2,1)S(1)} %get-tuple-element.99), channel_id=1, source_target_pairs={{0,1},{1,0},{2,3},{3,2},{4,5},{5,4},{6,7},{7,6},{8,9},{9,8},{10,11... | collective-permute-start | bytes 786440 | tf_op jit(solution)/shard_map/ppermute | solution.py:23
  42.8 1.7 %collective-permute-start.11 = (bf16[384,256]{1,0:T(8,128)(2,1)S(1)}, bf16[384,256]{1,0:T(8,128)(2,1)S(1)}, u32[]{:S(2)}, u32[]{:S(2)}) collective-permute-start(bf16[384,256]{1,0:T(8,128)(2,1)S(1)} %pad_maximum_fusion), channel_id=1, source_target_pairs={{0,4},{1,5},{2,6},{3,7},{4,0},{5,1},{6,2},{7,3},{8,12},{9,13},{10,... | collective-permute-start | bytes 589832 | tf_op jit(solution)/shard_map/ppermute | solution.py:23
  44.4 1.2 %image_inner.1 = (f32[1024,256]{1,0:T(8,128)S(1)}, f32[512,256]{1,0:T(8,128)S(1)}) custom-call(f32[1024,256]{1,0:T(8,128)S(1)} %get-tuple-element.100.outer_in, f32[512,256]{1,0:T(8,128)S(1)} %get-tuple-element.94.inner_in, bf16[512,256]{1,0:T(8,128)(2,1)S(1)} %collective-permute-done.9.near_in, bf16[512,256]{1,0:T(8,128)(2,1)S(1)} %collective-permute-done.10.far_in, ...), custom_call_target="tpu_custom_call" | custom-call | tf_op jit(solution)/shard_map/image_inner/pallas_call | solution.py:162
  45.6 4.3 %collective-permute-done.11 = bf16[384,256]{1,0:T(8,128)(2,1)S(1)} collective-permute-done((bf16[384,256]{1,0:T(8,128)(2,1)S(1)}, bf16[384,256]{1,0:T(8,128)(2,1)S(1)}, u32[]{:S(2)}, u32[]{:S(2)}) %collective-permute-start.11) | collective-permute-done | bytes 196640 | tf_op jit(solution)/shard_map/ppermute | solution.py:23
  49.9 0.1 collective-permute-start.14
  50.0 3.7 %schur_image.1 = (f32[1536,256]{1,0:T(8,128)S(1)}, f32[1536,256]{1,0:T(8,128)S(1)}, f32[8,256]{1,0:T(8,128)S(1)}, f32[128,256]{1,0:T(8,128)S(1)}) custom-call(f32[1024,256]{1,0:T(8,128)S(1)} %get-tuple-element.104.image, f32[1024,256]{1,0:T(8,128)S(1)} %get-tuple-element.106.outer, f32[512,256]{1,0:T(8,128)S(1)} %get-tuple-element.101.inner, ...), custom_call_target="tpu_custom_call" | custom-call | tf_op jit(solution)/shard_map/schur_image/pallas_call | solution.py:162
  53.7 0.8 %coarse_image.1 = (f32[4,256]{1,0:T(4,128)S(1)}, f32[96,256]{1,0:T(8,128)S(1)}) custom-call(bf16[768,256]{1,0:T(8,128)(2,1)S(1)} %constant_dynamic-update-slice_fusion.6.half, bf16[768,256]{1,0:T(8,128)(2,1)S(1)} %collective-permute-done.14.crossed_half, bf16[64,1024]{1,0:T(8,128)(2,1)S(1)} %get-tuple-element.66.inverse, ...), custom_call_target="tpu_custom_call" | custom-call | tf_op jit(solution)/shard_map/coarse_image/pallas_call | solution.py:162
  54.6 2.7 %collective-permute-start.15 = (f32[4,256]{1,0:T(4,128)S(1)}, f32[4,256]{1,0:T(4,128)S(1)}, u32[]{:S(2)}, u32[]{:S(2)}) collective-permute-start(f32[4,256]{1,0:T(4,128)S(1)} %get-tuple-element.111), channel_id=1, source_target_pairs={{0,8},{1,9},{2,10},{3,11},{4,12},{5,13},{6,14},{7,15},{8,0},{9,1},... | collective-permute-start | bytes 12296 | tf_op jit(solution)/shard_map/ppermute | solution.py:23
  57.2 1.5 %complete.1 = (f32[1024,256]{1,0:T(8,128)S(1)}, f32[1024,256]{1,0:T(8,128)S(1)}, f32[1024,256]{1,0:T(8,128)S(1)}, bf16[512,256]{1,0:T(8,128)(2,1)S(1)}) custom-call(f32[1536,256]{1,0:T(8,128)S(1)} %get-tuple-element.93.local.z_local, f32[96,256]{1,0:T(8,128)S(1)} %get-tuple-element.88.solution.z_coarse, f32[1536,256]{1,0:T(8,128)S(1)} %get-tuple-element.112.y_local, ...), custom_call_target="tpu_custom_call" | custom-call | tf_op jit(solution)/shard_map/complete/pallas_call | solution.py:162
  58.8 0.4 collective-permute-done.15
  59.1 3.0 %collective-permute-start.16 = (f32[4,256]{1,0:T(4,128)S(1)}, f32[4,256]{1,0:T(4,128)S(1)}, u32[]{:S(2)}, u32[]{:S(2)}) collective-permute-start(f32[4,256]{1,0:T(4,128)S(1)} %add.12), channel_id=1, source_target_pairs={{0,2},{1,3},{2,0},{3,1},{4,6},{5,7},{6,4},{7,5},{8,10},{9,11},{10,... | collective-permute-start | bytes 12296 | tf_op jit(solution)/shard_map/ppermute | solution.py:23
  62.2 1.6 %collective-permute-done.16 = f32[4,256]{1,0:T(4,128)S(1)} collective-permute-done((f32[4,256]{1,0:T(4,128)S(1)}, f32[4,256]{1,0:T(4,128)S(1)}, u32[]{:S(2)}, u32[]{:S(2)}) %collective-permute-start.16) | collective-permute-done | bytes 4128 | tf_op jit(solution)/shard_map/ppermute | solution.py:23
  63.8 1.0 %collective-permute-start.19 = (bf16[512,256]{1,0:T(8,128)(2,1)S(1)}, bf16[512,256]{1,0:T(8,128)(2,1)S(1)}, u32[]{:S(2)}, u32[]{:S(2)}) collective-permute-start(bf16[512,256]{1,0:T(8,128)(2,1)S(1)} %get-tuple-element.123), channel_id=1, source_target_pairs={{1,0},{2,1},{3,2},{4,3},{5,4},{6,5},{7,6},{8,7},{9,8},{10,9},{11,1... | collective-permute-start | bytes 786440 | tf_op jit(solution)/shard_map/ppermute | solution.py:19
  64.8 1.2 %collective-permute-done.17 = f32[4,256]{1,0:T(4,128)S(1)} collective-permute-done((f32[4,256]{1,0:T(4,128)S(1)}, f32[4,256]{1,0:T(4,128)S(1)}, u32[]{:S(2)}, u32[]{:S(2)}) %collective-permute-start.17) | collective-permute-done | bytes 4128 | tf_op jit(solution)/shard_map/ppermute | solution.py:23
  66.0 0.8 %collective-permute-start.18 = (f32[4,256]{1,0:T(4,128)S(1)}, f32[4,256]{1,0:T(4,128)S(1)}, u32[]{:S(2)}, u32[]{:S(2)}) collective-permute-start(f32[4,256]{1,0:T(4,128)S(1)} %add.14), channel_id=1, source_target_pairs={{0,4},{1,5},{2,6},{3,7},{4,0},{5,1},{6,2},{7,3},{8,12},{9,13},{10,... | collective-permute-start | bytes 12296 | tf_op jit(solution)/shard_map/ppermute | solution.py:23
  66.8 2.9 %collective-permute-done.18 = f32[4,256]{1,0:T(4,128)S(1)} collective-permute-done((f32[4,256]{1,0:T(4,128)S(1)}, f32[4,256]{1,0:T(4,128)S(1)}, u32[]{:S(2)}, u32[]{:S(2)}) %collective-permute-start.18) | collective-permute-done | bytes 4128 | tf_op jit(solution)/shard_map/ppermute | solution.py:23
  69.7 1.4 %combine.1 = (f32[1024,256]{1,0:T(8,128)}, f32[1024,256]{1,0:T(8,128)}) custom-call(f32[4,256]{1,0:T(4,128)S(1)} %add.15.sums, f32[1024,256]{1,0:T(8,128)S(1)} %get-tuple-element.63.load, f32[1024,256]{1,0:T(8,128)S(1)} %get-tuple-element.120.z, f32[1024,256]{1,0:T(8,128)S(1)} %get-tuple-element.115.y, f32[1024,256]{1,0:T(8,128)S(1)} %get-tuple-element.104.image, ...), custom_call_target="tpu_custom_call" | custom-call | tf_op jit(solution)/shard_map/combine/pallas_call | solution.py:162
  (22 shorter events, 0.1 us)
Async XLA Ops:
  2.4 12.6 %collective-permute-start = (bf16[720,256]{1,0:T(8,128)(2,1)S(1)}, bf16[720,256]{1,0:T(8,128)(2,1)S(1)}, u32[]{:S(2)}, u32[]{:S(2)}) collective-permute-start(bf16[720,256]{1,0:T(8,128)(2,1)S(1)} %halo_message.1), channel_id=1, source_target_pairs={{15,0},{0,1},{1,2},{2,3},{3,4},{4,5},{5,6},{6,7},{7,8},{8,9},{9,10... | collective-permute-start | bytes 1105928 | tf_op jit(solution)/shard_map/ppermute | solution.py:19
  2.9 7.2 %collective-permute-start.3 = (bf16[64,256]{1,0:T(8,128)(2,1)S(1)}, bf16[64,256]{1,0:T(8,128)(2,1)S(1)}, u32[]{:S(2)}, u32[]{:S(2)}) collective-permute-start(bf16[64,256]{1,0:T(8,128)(2,1)S(1)} %get-tuple-element.78), channel_id=1, source_target_pairs={{0,8},{1,9},{2,10},{3,11},{4,12},{5,13},{6,14},{7,15},{8,0},{9,1},... | collective-permute-start | bytes 98312 | tf_op jit(solution)/shard_map/ppermute | solution.py:23
  10.1 7.3 %collective-permute-start.4 = (bf16[128,256]{1,0:T(8,128)(2,1)S(1)}, bf16[128,256]{1,0:T(8,128)(2,1)S(1)}, u32[]{:S(2)}, u32[]{:S(2)}) collective-permute-start(bf16[128,256]{1,0:T(8,128)(2,1)S(1)} %pad_maximum_fusion.2), channel_id=1, source_target_pairs={{0,2},{1,3},{2,0},{3,1},{4,6},{5,7},{6,4},{7,5},{8,10},{9,11},{10,... | collective-permute-start | bytes 196616 | tf_op jit(solution)/shard_map/ppermute | solution.py:23
  17.4 5.4 %collective-permute-start.5 = (bf16[256,256]{1,0:T(8,128)(2,1)S(1)}, bf16[256,256]{1,0:T(8,128)(2,1)S(1)}, u32[]{:S(2)}, u32[]{:S(2)}) collective-permute-start(bf16[256,256]{1,0:T(8,128)(2,1)S(1)} %pad_maximum_fusion.1), channel_id=1, source_target_pairs={{0,4},{1,5},{2,6},{3,7},{4,0},{5,1},{6,2},{7,3},{8,12},{9,13},{10,... | collective-permute-start | bytes 393224 | tf_op jit(solution)/shard_map/ppermute | solution.py:23
  17.5 9.1 %collective-permute-start.2 = (bf16[512,256]{1,0:T(8,128)(2,1)S(1)}, bf16[512,256]{1,0:T(8,128)(2,1)S(1)}, u32[]{:S(2)}, u32[]{:S(2)}) collective-permute-start(bf16[512,256]{1,0:T(8,128)(2,1)S(1)} %get-tuple-element.71), channel_id=1, source_target_pairs={{0,15},{1,2},{2,1},{3,4},{4,3},{5,6},{6,5},{7,8},{8,7},{9,10},{10,... | collective-permute-start | bytes 786440 | tf_op jit(solution)/shard_map/ppermute | solution.py:28
  19.8 3.6 %collective-permute-start.1 = (bf16[512,256]{1,0:T(8,128)(2,1)S(1)}, bf16[512,256]{1,0:T(8,128)(2,1)S(1)}, u32[]{:S(2)}, u32[]{:S(2)}) collective-permute-start(bf16[512,256]{1,0:T(8,128)(2,1)S(1)} %get-tuple-element.73), channel_id=1, source_target_pairs={{0,1},{1,0},{2,3},{3,2},{4,5},{5,4},{6,7},{7,6},{8,9},{9,8},{10,11... | collective-permute-start | bytes 786440 | tf_op jit(solution)/shard_map/ppermute | solution.py:23
  22.8 3.8 %collective-permute-start.6 = (bf16[512,256]{1,0:T(8,128)(2,1)S(1)}, bf16[512,256]{1,0:T(8,128)(2,1)S(1)}, u32[]{:S(2)}, u32[]{:S(2)}) collective-permute-start(bf16[512,256]{1,0:T(8,128)(2,1)S(1)} %constant_dynamic-update-slice_fusion.half), channel_id=1, source_target_pairs={{0,1},{1,0},{2,3},{3,2},{4,5},{5,4},{6,7},{7,6},{8,9},{9,8},{10,11... | collective-permute-start | bytes 786440 | tf_op jit(solution)/shard_map/ppermute | solution.py:23
  28.3 5.7 %collective-permute-start.7 = (bf16[96,256]{1,0:T(8,128)(2,1)S(1)}, bf16[96,256]{1,0:T(8,128)(2,1)S(1)}, u32[]{:S(2)}, u32[]{:S(2)}) collective-permute-start(bf16[96,256]{1,0:T(8,128)(2,1)S(1)} %get-tuple-element.84), channel_id=1, source_target_pairs={{0,8},{1,9},{2,10},{3,11},{4,12},{5,13},{6,14},{7,15},{8,0},{9,1},... | collective-permute-start | bytes 147464 | tf_op jit(solution)/shard_map/ppermute | solution.py:23
  30.2 8.7 %collective-permute-start.10 = (bf16[512,256]{1,0:T(8,128)(2,1)S(1)}, bf16[512,256]{1,0:T(8,128)(2,1)S(1)}, u32[]{:S(2)}, u32[]{:S(2)}) collective-permute-start(bf16[512,256]{1,0:T(8,128)(2,1)S(1)} %get-tuple-element.90), channel_id=1, source_target_pairs={{0,15},{1,2},{2,1},{3,4},{4,3},{5,6},{6,5},{7,8},{8,7},{9,10},{10,... | collective-permute-start | bytes 786440 | tf_op jit(solution)/shard_map/ppermute | solution.py:28
  34.0 4.9 %collective-permute-start.9 = (bf16[512,256]{1,0:T(8,128)(2,1)S(1)}, bf16[512,256]{1,0:T(8,128)(2,1)S(1)}, u32[]{:S(2)}, u32[]{:S(2)}) collective-permute-start(bf16[512,256]{1,0:T(8,128)(2,1)S(1)} %get-tuple-element.96), channel_id=1, source_target_pairs={{0,1},{1,0},{2,3},{3,2},{4,5},{5,4},{6,7},{7,6},{8,9},{9,8},{10,11... | collective-permute-start | bytes 786440 | tf_op jit(solution)/shard_map/ppermute | solution.py:23
  34.1 7.7 %collective-permute-start.8 = (bf16[192,256]{1,0:T(8,128)(2,1)S(1)}, bf16[192,256]{1,0:T(8,128)(2,1)S(1)}, u32[]{:S(2)}, u32[]{:S(2)}) collective-permute-start(bf16[192,256]{1,0:T(8,128)(2,1)S(1)} %get-tuple-element.124), channel_id=1, source_target_pairs={{0,2},{1,3},{2,0},{3,1},{4,6},{5,7},{6,4},{7,5},{8,10},{9,11},{10,... | collective-permute-start | bytes 294920 | tf_op jit(solution)/shard_map/ppermute | solution.py:23
  40.0 9.9 %collective-permute-start.13 = (bf16[512,256]{1,0:T(8,128)(2,1)S(1)}, bf16[512,256]{1,0:T(8,128)(2,1)S(1)}, u32[]{:S(2)}, u32[]{:S(2)}) collective-permute-start(bf16[512,256]{1,0:T(8,128)(2,1)S(1)} %get-tuple-element.97), channel_id=1, source_target_pairs={{0,15},{1,2},{2,1},{3,4},{4,3},{5,6},{6,5},{7,8},{8,7},{9,10},{10,... | collective-permute-start | bytes 786440 | tf_op jit(solution)/shard_map/ppermute | solution.py:28
  41.8 8.1 %collective-permute-start.12 = (bf16[512,256]{1,0:T(8,128)(2,1)S(1)}, bf16[512,256]{1,0:T(8,128)(2,1)S(1)}, u32[]{:S(2)}, u32[]{:S(2)}) collective-permute-start(bf16[512,256]{1,0:T(8,128)(2,1)S(1)} %get-tuple-element.99), channel_id=1, source_target_pairs={{0,1},{1,0},{2,3},{3,2},{4,5},{5,4},{6,7},{7,6},{8,9},{9,8},{10,11... | collective-permute-start | bytes 786440 | tf_op jit(solution)/shard_map/ppermute | solution.py:23
  42.8 7.1 %collective-permute-start.11 = (bf16[384,256]{1,0:T(8,128)(2,1)S(1)}, bf16[384,256]{1,0:T(8,128)(2,1)S(1)}, u32[]{:S(2)}, u32[]{:S(2)}) collective-permute-start(bf16[384,256]{1,0:T(8,128)(2,1)S(1)} %pad_maximum_fusion), channel_id=1, source_target_pairs={{0,4},{1,5},{2,6},{3,7},{4,0},{5,1},{6,2},{7,3},{8,12},{9,13},{10,... | collective-permute-start | bytes 589832 | tf_op jit(solution)/shard_map/ppermute | solution.py:23
  49.9 3.8 %collective-permute-start.14 = (bf16[768,256]{1,0:T(8,128)(2,1)S(1)}, bf16[768,256]{1,0:T(8,128)(2,1)S(1)}, u32[]{:S(2)}, u32[]{:S(2)}) collective-permute-start(bf16[768,256]{1,0:T(8,128)(2,1)S(1)} %constant_dynamic-update-slice_fusion.6.half), channel_id=1, source_target_pairs={{0,1},{1,0},{2,3},{3,2},{4,5},{5,4},{6,7},{7,6},{8,9},{9,8},{10,11... | collective-permute-start | bytes 1179656 | tf_op jit(solution)/shard_map/ppermute | solution.py:23
  54.6 4.6 %collective-permute-start.15 = (f32[4,256]{1,0:T(4,128)S(1)}, f32[4,256]{1,0:T(4,128)S(1)}, u32[]{:S(2)}, u32[]{:S(2)}) collective-permute-start(f32[4,256]{1,0:T(4,128)S(1)} %get-tuple-element.111), channel_id=1, source_target_pairs={{0,8},{1,9},{2,10},{3,11},{4,12},{5,13},{6,14},{7,15},{8,0},{9,1},... | collective-permute-start | bytes 12296 | tf_op jit(solution)/shard_map/ppermute | solution.py:23
  59.1 4.6 %collective-permute-start.16 = (f32[4,256]{1,0:T(4,128)S(1)}, f32[4,256]{1,0:T(4,128)S(1)}, u32[]{:S(2)}, u32[]{:S(2)}) collective-permute-start(f32[4,256]{1,0:T(4,128)S(1)} %add.12), channel_id=1, source_target_pairs={{0,2},{1,3},{2,0},{3,1},{4,6},{5,7},{6,4},{7,5},{8,10},{9,11},{10,... | collective-permute-start | bytes 12296 | tf_op jit(solution)/shard_map/ppermute | solution.py:23
  63.8 5.9 %collective-permute-start.19 = (bf16[512,256]{1,0:T(8,128)(2,1)S(1)}, bf16[512,256]{1,0:T(8,128)(2,1)S(1)}, u32[]{:S(2)}, u32[]{:S(2)}) collective-permute-start(bf16[512,256]{1,0:T(8,128)(2,1)S(1)} %get-tuple-element.123), channel_id=1, source_target_pairs={{1,0},{2,1},{3,2},{4,3},{5,4},{6,5},{7,6},{8,7},{9,8},{10,9},{11,1... | collective-permute-start | bytes 786440 | tf_op jit(solution)/shard_map/ppermute | solution.py:19
  64.8 1.2 %collective-permute-start.17 = (f32[4,256]{1,0:T(4,128)S(1)}, f32[4,256]{1,0:T(4,128)S(1)}, u32[]{:S(2)}, u32[]{:S(2)}) collective-permute-start(f32[4,256]{1,0:T(4,128)S(1)} %add.13), channel_id=1, source_target_pairs={{0,1},{1,0},{2,3},{3,2},{4,5},{5,4},{6,7},{7,6},{8,9},{9,8},{10,11... | collective-permute-start | bytes 12296 | tf_op jit(solution)/shard_map/ppermute | solution.py:23
  66.0 3.7 %collective-permute-start.18 = (f32[4,256]{1,0:T(4,128)S(1)}, f32[4,256]{1,0:T(4,128)S(1)}, u32[]{:S(2)}, u32[]{:S(2)}) collective-permute-start(f32[4,256]{1,0:T(4,128)S(1)} %add.14), channel_id=1, source_target_pairs={{0,4},{1,5},{2,6},{3,7},{4,0},{5,1},{6,2},{7,3},{8,12},{9,13},{10,... | collective-permute-start | bytes 12296 | tf_op jit(solution)/shard_map/ppermute | solution.py:23

commit v17 on v15

--- a/solution.py
+++ b/solution.py
@@ -576,9 +576,9 @@
         bind(complete), [(own, F32), (own, F32), (own, F32), ((nf, columns), BF16)],
         z_local, z_coarse, y_local, y_coarse, rows, basis_high, basis_low, product,
     )
-    for k, bit in enumerate(early[:1] + steps[-1:] + early[1:] + late):
+    for k, bit in enumerate(early + steps[-1:] + late):
         sums = sums + after(crossed(sums, bit), y)
-        if k == 0:
+        if k == len(early) - 1:
             back = shifted(after(back, sums), -1)
     return stage(
         bind(combine), [(own, F32), (own, F32)], sums, load, z, y, image, part, back,

time: 72 us -> 71.4 us (level)
  waiting for transfers between devices: 19.7 us -> 18.6 us
    ppermute x15, starting transfers between devices: 17.7 us -> 19.9 us  [crossed(): lax.ppermute(block, AXIS, [(i, i ^ bit) for i in range(lax.axis_size(AXIS...]
    ppermute x2, starting transfers between devices: 3.22 us -> 1.52 us  [shifted(): lax.ppermute(block, AXIS, [((i - distance) % n, i) for i in range(n)])]
    ppermute x15, waiting for transfers between devices: 13 us -> 11.9 us  [crossed(): lax.ppermute(block, AXIS, [(i, i ^ bit) for i in range(lax.axis_size(AXIS...]
where the time goes in v17:
time: 71.4 us; the launch traced here: 71.3 us
  starting transfers between devices  27.3 us (38%)
  Pallas kernels  24.2 us (34%)
  waiting for transfers between devices  18.6 us (26%)
  between operations  1.01 us (1%)
    pallas_call x15, Pallas kernels, stage(): return call(*operands)  24.2 us
    ppermute x15, starting transfers between devices, crossed(): lax.ppermute(block, AXIS, [(i, i ^ bit) for i in range(lax.axis_size(AXIS...  19.9 us
    ppermute x15, waiting for transfers between devices, crossed(): lax.ppermute(block, AXIS, [(i, i ^ bit) for i in range(lax.axis_size(AXIS...  11.9 us
    ppermute x3, waiting for transfers between devices, far_block(): lax.ppermute(block, AXIS, [(i, (i + (1 if i % 2 else -1)) % n) for i in r...  6.71 us
    ppermute x3, starting transfers between devices, far_block(): lax.ppermute(block, AXIS, [(i, (i + (1 if i % 2 else -1)) % n) for i in r...  5.89 us
    ppermute x2, starting transfers between devices, shifted(): lax.ppermute(block, AXIS, [((i - distance) % n, i) for i in range(n)])  1.52 us
  transfers between devices with their start and end apart: 20, of which 9 were waited for; matrix products, arithmetic and copies ran while one was open for 0% of the time, Pallas kernels for 26%

profile of v17, /device:TPU:0, one launch (start us, length us, event | category | flops | bytes accessed | tf_op | source)
XLA Modules:
  0.0 71.3 jit_solution(15825412603581520733)
XLA Ops:
  0.6 1.5 %prepare.1 = (f32[1024,256]{1,0:T(8,128)S(1)}, bf16[64,512]{1,0:T(8,128)(2,1)S(1)}, f32[2,512]{1,0:T(2,128)S(1)}, bf16[64,1024]{1,0:T(8,128)(2,1)S(1)}, bf16[64,...) custom-call(f32[1024,256]{1,0:T(8,128)} %load.1, bf16[64,512]{1,0:T(8,128)(2,1)} %rows.1, f32[2,512]{1,0:T(2,128)} %weight.1, ...), custom_call_target="tpu_custom_call" | custom-call | tf_op jit(solution)/shard_map/prepare/pallas_call | solution.py:162
  2.2 0.3 halo_message.1
  2.4 0.5 collective-permute-start
  2.9 3.7 %collective-permute-start.3 = (bf16[64,256]{1,0:T(8,128)(2,1)S(1)}, bf16[64,256]{1,0:T(8,128)(2,1)S(1)}, u32[]{:S(2)}, u32[]{:S(2)}) collective-permute-start(bf16[64,256]{1,0:T(8,128)(2,1)S(1)} %get-tuple-element.76), channel_id=1, source_target_pairs={{0,8},{1,9},{2,10},{3,11},{4,12},{5,13},{6,14},{7,15},{8,0},{9,1},... | collective-permute-start | bytes 98312 | tf_op jit(solution)/shard_map/ppermute | solution.py:23
  6.6 3.5 %fetch.1 = (bf16[2048,1024]{1,0:T(8,128)(2,1)S(1)}, bf16[2048,1024]{1,0:T(8,128)(2,1)S(1)}) custom-call(bf16[2048,1024]{1,0:T(8,128)(2,1)} %neumann, bf16[2048,1024]{1,0:T(8,128)(2,1)} %schur), custom_call_target="tpu_custom_call" | custom-call | tf_op jit(solution)/shard_map/fetch/pallas_call | solution.py:162
  10.1 4.9 %collective-permute-start.4 = (bf16[128,256]{1,0:T(8,128)(2,1)S(1)}, bf16[128,256]{1,0:T(8,128)(2,1)S(1)}, u32[]{:S(2)}, u32[]{:S(2)}) collective-permute-start(bf16[128,256]{1,0:T(8,128)(2,1)S(1)} %pad_maximum_fusion.3), channel_id=1, source_target_pairs={{0,2},{1,3},{2,0},{3,1},{4,6},{5,7},{6,4},{7,5},{8,10},{9,11},{10,... | collective-permute-start | bytes 196616 | tf_op jit(solution)/shard_map/ppermute | solution.py:23
  15.0 1.0 %load_outer.1 = (f32[1024,256]{1,0:T(8,128)S(1)}, bf16[512,256]{1,0:T(8,128)(2,1)S(1)}, bf16[512,256]{1,0:T(8,128)(2,1)S(1)}) custom-call(f32[1024,256]{1,0:T(8,128)S(1)} %get-tuple-element.61.load, f32[2,512]{1,0:T(2,128)S(1)} %get-tuple-element.62.weight, bf16[720,256]{1,0:T(8,128)(2,1)S(1)} %collective-permute-done.message, ...), custom_call_target="tpu_custom_call" | custom-call | tf_op jit(solution)/shard_map/load_outer/pallas_call | solution.py:162
  16.1 1.3 %collective-permute-done.4 = bf16[128,256]{1,0:T(8,128)(2,1)S(1)} collective-permute-done((bf16[128,256]{1,0:T(8,128)(2,1)S(1)}, bf16[128,256]{1,0:T(8,128)(2,1)S(1)}, u32[]{:S(2)}, u32[]{:S(2)}) %collective-permute-start.4) | collective-permute-done | bytes 65568 | tf_op jit(solution)/shard_map/ppermute | solution.py:23
  17.4 0.1 collective-permute-start.5
  17.5 2.3 %collective-permute-start.2 = (bf16[512,256]{1,0:T(8,128)(2,1)S(1)}, bf16[512,256]{1,0:T(8,128)(2,1)S(1)}, u32[]{:S(2)}, u32[]{:S(2)}) collective-permute-start(bf16[512,256]{1,0:T(8,128)(2,1)S(1)} %get-tuple-element.69), channel_id=1, source_target_pairs={{0,15},{1,2},{2,1},{3,4},{4,3},{5,6},{6,5},{7,8},{8,7},{9,10},{10,... | collective-permute-start | bytes 786440 | tf_op jit(solution)/shard_map/ppermute | solution.py:28
  19.8 1.0 %load_inner.1.inner = f32[512,256]{1,0:T(8,128)S(1)} custom-call(f32[1024,256]{1,0:T(8,128)S(1)} %get-tuple-element.61.load, f32[2,512]{1,0:T(2,128)S(1)} %get-tuple-element.62.weight, bf16[720,256]{1,0:T(8,128)(2,1)S(1)} %collective-permute-done.message, bf16[2048,1024]{1,0:T(8,128)(2,1)S(1)} %get-tuple-element.67.neumann), custom_call_target="tpu_custom_call" | custom-call | tf_op jit(solution)/shard_map/load_inner/pallas_call | solution.py:162
  20.8 0.1 collective-permute-start.1
  20.9 1.9 %static_basis.1 = (bf16[2048,64]{1,0:T(8,128)(2,1)S(1)}, bf16[2048,64]{1,0:T(8,128)(2,1)S(1)}, bf16[128,1024]{1,0:T(8,128)(2,1)S(1)}, bf16[128,1024]{1,0:T(8,128)(2,1)S(1)}, f32[128,128]{1,0:T(8,128)S(1)}) custom-call(bf16[2048,1024]{1,0:T(8,128)(2,1)S(1)} %get-tuple-element.72.schur, bf16[720,256]{1,0:T(8,128)(2,1)S(1)} %collective-permute-done.message, ...), custom_call_target="tpu_custom_call" | custom-call | tf_op jit(solution)/shard_map/static_basis/pallas_call | solution.py:162
  22.9 0.0 collective-permute-done.5
  22.9 0.6 collective-permute-start.6
  23.5 3.2 %collective-permute-done.2.far = bf16[512,256]{1,0:T(8,128)(2,1)S(1)} collective-permute-done((bf16[512,256]{1,0:T(8,128)(2,1)S(1)}, bf16[512,256]{1,0:T(8,128)(2,1)S(1)}, u32[]{:S(2)}, u32[]{:S(2)}) %collective-permute-start.2) | collective-permute-done | bytes 262176 | tf_op jit(solution)/shard_map/ppermute | solution.py:28
  26.7 0.0 collective-permute-done.1.near
  26.7 0.0 collective-permute-done.6.crossed_half
  26.7 1.6 %coarse_load.1 = (f32[1536,256]{1,0:T(8,128)S(1)}, bf16[96,256]{1,0:T(8,128)(2,1)S(1)}, f32[96,256]{1,0:T(8,128)S(1)}, f32[96,256]{1,0:T(8,128)S(1)}, f32[8,256]{1,0:T(8,128)S(1)}) custom-call(f32[1024,256]{1,0:T(8,128)S(1)} %get-tuple-element.61.load, f32[1024,256]{1,0:T(8,128)S(1)} %get-tuple-element.68.outer, f32[512,256]{1,0:T(8,128)S(1)} %load_inner.1.inner, ...), custom_call_target="tpu_custom_call" | custom-call | tf_op jit(solution)/shard_map/coarse_load/pallas_call | solution.py:162
  28.3 0.1 collective-permute-start.7
  28.4 1.8 %schur_outer.1 = (f32[1024,256]{1,0:T(8,128)S(1)}, bf16[512,256]{1,0:T(8,128)(2,1)S(1)}, bf16[512,256]{1,0:T(8,128)(2,1)S(1)}, f32[8,256]{1,0:T(8,128)S(1)}) custom-call(f32[1536,256]{1,0:T(8,128)S(1)} %get-tuple-element.83.local.z_local, bf16[2048,1024]{1,0:T(8,128)(2,1)S(1)} %get-tuple-element.72.schur, bf16[2048,64]{1,0:T(8,128)(2,1)S(1)} %get-tuple-element.84.basis_high, ...), custom_call_target="tpu_custom_call" | custom-call | tf_op jit(solution)/shard_map/schur_outer/pallas_call | solution.py:162
  30.1 1.8 %collective-permute-start.10 = (bf16[512,256]{1,0:T(8,128)(2,1)S(1)}, bf16[512,256]{1,0:T(8,128)(2,1)S(1)}, u32[]{:S(2)}, u32[]{:S(2)}) collective-permute-start(bf16[512,256]{1,0:T(8,128)(2,1)S(1)} %get-tuple-element.92), channel_id=1, source_target_pairs={{0,15},{1,2},{2,1},{3,4},{4,3},{5,6},{6,5},{7,8},{8,7},{9,10},{10,... | collective-permute-start | bytes 786440 | tf_op jit(solution)/shard_map/ppermute | solution.py:28
  31.9 0.0 collective-permute-start.9
  31.9 1.8 %schur_inner.1 = (f32[512,256]{1,0:T(8,128)S(1)}, f32[1,256]{1,0:T(1,128)S(1)}) custom-call(f32[1536,256]{1,0:T(8,128)S(1)} %get-tuple-element.83.local.z_local, bf16[2048,1024]{1,0:T(8,128)(2,1)S(1)} %get-tuple-element.72.schur, bf16[2048,64]{1,0:T(8,128)(2,1)S(1)} %get-tuple-element.84.basis_high, bf16[2048,64]{1,0:T(8,128)(2,1)S(1)} %get-tuple-element.85.basis_low, ...), custom_call_target="tpu_custom_call" | custom-call | tf_op jit(solution)/shard_map/schur_inner/pallas_call | solution.py:162
  33.7 0.2 collective-permute-done.7
  34.0 1.3 %collective-permute-start.8 = (bf16[192,256]{1,0:T(8,128)(2,1)S(1)}, bf16[192,256]{1,0:T(8,128)(2,1)S(1)}, u32[]{:S(2)}, u32[]{:S(2)}) collective-permute-start(bf16[192,256]{1,0:T(8,128)(2,1)S(1)} %pad_maximum_fusion.2), channel_id=1, source_target_pairs={{0,2},{1,3},{2,0},{3,1},{4,6},{5,7},{6,4},{7,5},{8,10},{9,11},{10,... | collective-permute-start | bytes 294920 | tf_op jit(solution)/shard_map/ppermute | solution.py:23
  35.3 3.5 %collective-permute-done.10.far_in = bf16[512,256]{1,0:T(8,128)(2,1)S(1)} collective-permute-done((bf16[512,256]{1,0:T(8,128)(2,1)S(1)}, bf16[512,256]{1,0:T(8,128)(2,1)S(1)}, u32[]{:S(2)}, u32[]{:S(2)}) %collective-permute-start.10) | collective-permute-done | bytes 262176 | tf_op jit(solution)/shard_map/ppermute | solution.py:28
  38.8 1.1 %image_outer.1 = (f32[1024,256]{1,0:T(8,128)S(1)}, bf16[512,256]{1,0:T(8,128)(2,1)S(1)}, bf16[512,256]{1,0:T(8,128)(2,1)S(1)}) custom-call(f32[1024,256]{1,0:T(8,128)S(1)} %get-tuple-element.96.outer_in, f32[512,256]{1,0:T(8,128)S(1)} %get-tuple-element.87.inner_in, bf16[512,256]{1,0:T(8,128)(2,1)S(1)} %collective-permute-done.9.near_in, ...), custom_call_target="tpu_custom_call" | custom-call | tf_op jit(solution)/shard_map/image_outer/pallas_call | solution.py:162
  40.0 1.8 %collective-permute-start.13 = (bf16[512,256]{1,0:T(8,128)(2,1)S(1)}, bf16[512,256]{1,0:T(8,128)(2,1)S(1)}, u32[]{:S(2)}, u32[]{:S(2)}) collective-permute-start(bf16[512,256]{1,0:T(8,128)(2,1)S(1)} %get-tuple-element.93), channel_id=1, source_target_pairs={{0,15},{1,2},{2,1},{3,4},{4,3},{5,6},{6,5},{7,8},{8,7},{9,10},{10,... | collective-permute-start | bytes 786440 | tf_op jit(solution)/shard_map/ppermute | solution.py:28
  41.8 0.0 collective-permute-done.8
  41.8 1.0 %collective-permute-start.12 = (bf16[512,256]{1,0:T(8,128)(2,1)S(1)}, bf16[512,256]{1,0:T(8,128)(2,1)S(1)}, u32[]{:S(2)}, u32[]{:S(2)}) collective-permute-start(bf16[512,256]{1,0:T(8,128)(2,1)S(1)} %get-tuple-element.95), channel_id=1, source_target_pairs={{0,1},{1,0},{2,3},{3,2},{4,5},{5,4},{6,7},{7,6},{8,9},{9,8},{10,11... | collective-permute-start | bytes 786440 | tf_op jit(solution)/shard_map/ppermute | solution.py:23
  42.8 1.7 %collective-permute-start.11 = (bf16[384,256]{1,0:T(8,128)(2,1)S(1)}, bf16[384,256]{1,0:T(8,128)(2,1)S(1)}, u32[]{:S(2)}, u32[]{:S(2)}) collective-permute-start(bf16[384,256]{1,0:T(8,128)(2,1)S(1)} %pad_maximum_fusion), channel_id=1, source_target_pairs={{0,4},{1,5},{2,6},{3,7},{4,0},{5,1},{6,2},{7,3},{8,12},{9,13},{10,... | collective-permute-start | bytes 589832 | tf_op jit(solution)/shard_map/ppermute | solution.py:23
  44.4 1.2 %image_inner.1 = (f32[1024,256]{1,0:T(8,128)S(1)}, f32[512,256]{1,0:T(8,128)S(1)}) custom-call(f32[1024,256]{1,0:T(8,128)S(1)} %get-tuple-element.96.outer_in, f32[512,256]{1,0:T(8,128)S(1)} %get-tuple-element.87.inner_in, bf16[512,256]{1,0:T(8,128)(2,1)S(1)} %collective-permute-done.9.near_in, bf16[512,256]{1,0:T(8,128)(2,1)S(1)} %collective-permute-done.10.far_in, ...), custom_call_target="tpu_custom_call" | custom-call | tf_op jit(solution)/shard_map/image_inner/pallas_call | solution.py:162
  45.6 4.3 %collective-permute-done.11 = bf16[384,256]{1,0:T(8,128)(2,1)S(1)} collective-permute-done((bf16[384,256]{1,0:T(8,128)(2,1)S(1)}, bf16[384,256]{1,0:T(8,128)(2,1)S(1)}, u32[]{:S(2)}, u32[]{:S(2)}) %collective-permute-start.11) | collective-permute-done | bytes 196640 | tf_op jit(solution)/shard_map/ppermute | solution.py:23
  49.9 0.0 collective-permute-done.12.near
  49.9 0.1 collective-permute-start.14
  50.0 3.7 %schur_image.1 = (f32[1536,256]{1,0:T(8,128)S(1)}, f32[1536,256]{1,0:T(8,128)S(1)}, f32[8,256]{1,0:T(8,128)S(1)}, f32[128,256]{1,0:T(8,128)S(1)}) custom-call(f32[1024,256]{1,0:T(8,128)S(1)} %get-tuple-element.100.image, f32[1024,256]{1,0:T(8,128)S(1)} %get-tuple-element.102.outer, f32[512,256]{1,0:T(8,128)S(1)} %get-tuple-element.97.inner, ...), custom_call_target="tpu_custom_call" | custom-call | tf_op jit(solution)/shard_map/schur_image/pallas_call | solution.py:162
  53.7 0.8 %coarse_image.1 = (f32[4,256]{1,0:T(4,128)S(1)}, f32[96,256]{1,0:T(8,128)S(1)}) custom-call(bf16[768,256]{1,0:T(8,128)(2,1)S(1)} %constant_dynamic-update-slice_fusion.4.half, bf16[768,256]{1,0:T(8,128)(2,1)S(1)} %collective-permute-done.14.crossed_half, bf16[64,1024]{1,0:T(8,128)(2,1)S(1)} %get-tuple-element.64.inverse, ...), custom_call_target="tpu_custom_call" | custom-call | tf_op jit(solution)/shard_map/coarse_image/pallas_call | solution.py:162
  54.6 2.7 %collective-permute-start.15 = (f32[4,256]{1,0:T(4,128)S(1)}, f32[4,256]{1,0:T(4,128)S(1)}, u32[]{:S(2)}, u32[]{:S(2)}) collective-permute-start(f32[4,256]{1,0:T(4,128)S(1)} %get-tuple-element.107), channel_id=1, source_target_pairs={{0,8},{1,9},{2,10},{3,11},{4,12},{5,13},{6,14},{7,15},{8,0},{9,1},... | collective-permute-start | bytes 12296 | tf_op jit(solution)/shard_map/ppermute | solution.py:23
  57.2 1.5 %complete.1 = (f32[1024,256]{1,0:T(8,128)S(1)}, f32[1024,256]{1,0:T(8,128)S(1)}, f32[1024,256]{1,0:T(8,128)S(1)}, bf16[512,256]{1,0:T(8,128)(2,1)S(1)}) custom-call(f32[1536,256]{1,0:T(8,128)S(1)} %get-tuple-element.83.local.z_local, f32[96,256]{1,0:T(8,128)S(1)} %get-tuple-element.86.solution.z_coarse, f32[1536,256]{1,0:T(8,128)S(1)} %get-tuple-element.108.y_local, ...), custom_call_target="tpu_custom_call" | custom-call | tf_op jit(solution)/shard_map/complete/pallas_call | solution.py:162
  58.7 0.4 collective-permute-done.15
  59.1 3.0 %collective-permute-start.16 = (f32[4,256]{1,0:T(4,128)S(1)}, f32[4,256]{1,0:T(4,128)S(1)}, u32[]{:S(2)}, u32[]{:S(2)}) collective-permute-start(f32[4,256]{1,0:T(4,128)S(1)} %add.12), channel_id=1, source_target_pairs={{0,2},{1,3},{2,0},{3,1},{4,6},{5,7},{6,4},{7,5},{8,10},{9,11},{10,... | collective-permute-start | bytes 12296 | tf_op jit(solution)/shard_map/ppermute | solution.py:23
  62.2 1.6 %collective-permute-done.16 = f32[4,256]{1,0:T(4,128)S(1)} collective-permute-done((f32[4,256]{1,0:T(4,128)S(1)}, f32[4,256]{1,0:T(4,128)S(1)}, u32[]{:S(2)}, u32[]{:S(2)}) %collective-permute-start.16) | collective-permute-done | bytes 4128 | tf_op jit(solution)/shard_map/ppermute | solution.py:23
  63.8 1.0 %collective-permute-start.19 = (bf16[512,256]{1,0:T(8,128)(2,1)S(1)}, bf16[512,256]{1,0:T(8,128)(2,1)S(1)}, u32[]{:S(2)}, u32[]{:S(2)}) collective-permute-start(bf16[512,256]{1,0:T(8,128)(2,1)S(1)} %get-tuple-element.119), channel_id=1, source_target_pairs={{1,0},{2,1},{3,2},{4,3},{5,4},{6,5},{7,6},{8,7},{9,8},{10,9},{11,1... | collective-permute-start | bytes 786440 | tf_op jit(solution)/shard_map/ppermute | solution.py:19
  64.8 1.2 %collective-permute-done.17 = f32[4,256]{1,0:T(4,128)S(1)} collective-permute-done((f32[4,256]{1,0:T(4,128)S(1)}, f32[4,256]{1,0:T(4,128)S(1)}, u32[]{:S(2)}, u32[]{:S(2)}) %collective-permute-start.17) | collective-permute-done | bytes 4128 | tf_op jit(solution)/shard_map/ppermute | solution.py:23
  66.0 0.8 %collective-permute-start.18 = (f32[4,256]{1,0:T(4,128)S(1)}, f32[4,256]{1,0:T(4,128)S(1)}, u32[]{:S(2)}, u32[]{:S(2)}) collective-permute-start(f32[4,256]{1,0:T(4,128)S(1)} %add.14), channel_id=1, source_target_pairs={{0,4},{1,5},{2,6},{3,7},{4,0},{5,1},{6,2},{7,3},{8,12},{9,13},{10,... | collective-permute-start | bytes 12296 | tf_op jit(solution)/shard_map/ppermute | solution.py:23
  66.8 2.9 %collective-permute-done.18 = f32[4,256]{1,0:T(4,128)S(1)} collective-permute-done((f32[4,256]{1,0:T(4,128)S(1)}, f32[4,256]{1,0:T(4,128)S(1)}, u32[]{:S(2)}, u32[]{:S(2)}) %collective-permute-start.18) | collective-permute-done | bytes 4128 | tf_op jit(solution)/shard_map/ppermute | solution.py:23
  69.7 1.4 %combine.1 = (f32[1024,256]{1,0:T(8,128)}, f32[1024,256]{1,0:T(8,128)}) custom-call(f32[4,256]{1,0:T(4,128)S(1)} %add.15.sums, f32[1024,256]{1,0:T(8,128)S(1)} %get-tuple-element.61.load, f32[1024,256]{1,0:T(8,128)S(1)} %get-tuple-element.116.z, f32[1024,256]{1,0:T(8,128)S(1)} %get-tuple-element.111.y, f32[1024,256]{1,0:T(8,128)S(1)} %get-tuple-element.100.image, ...), custom_call_target="tpu_custom_call" | custom-call | tf_op jit(solution)/shard_map/combine/pallas_call | solution.py:162
  (23 shorter events, 0.1 us)
Async XLA Ops:
  2.4 12.6 %collective-permute-start = (bf16[720,256]{1,0:T(8,128)(2,1)S(1)}, bf16[720,256]{1,0:T(8,128)(2,1)S(1)}, u32[]{:S(2)}, u32[]{:S(2)}) collective-permute-start(bf16[720,256]{1,0:T(8,128)(2,1)S(1)} %halo_message.1), channel_id=1, source_target_pairs={{15,0},{0,1},{1,2},{2,3},{3,4},{4,5},{5,6},{6,7},{7,8},{8,9},{9,10... | collective-permute-start | bytes 1105928 | tf_op jit(solution)/shard_map/ppermute | solution.py:19
  2.9 7.2 %collective-permute-start.3 = (bf16[64,256]{1,0:T(8,128)(2,1)S(1)}, bf16[64,256]{1,0:T(8,128)(2,1)S(1)}, u32[]{:S(2)}, u32[]{:S(2)}) collective-permute-start(bf16[64,256]{1,0:T(8,128)(2,1)S(1)} %get-tuple-element.76), channel_id=1, source_target_pairs={{0,8},{1,9},{2,10},{3,11},{4,12},{5,13},{6,14},{7,15},{8,0},{9,1},... | collective-permute-start | bytes 98312 | tf_op jit(solution)/shard_map/ppermute | solution.py:23
  10.1 7.3 %collective-permute-start.4 = (bf16[128,256]{1,0:T(8,128)(2,1)S(1)}, bf16[128,256]{1,0:T(8,128)(2,1)S(1)}, u32[]{:S(2)}, u32[]{:S(2)}) collective-permute-start(bf16[128,256]{1,0:T(8,128)(2,1)S(1)} %pad_maximum_fusion.3), channel_id=1, source_target_pairs={{0,2},{1,3},{2,0},{3,1},{4,6},{5,7},{6,4},{7,5},{8,10},{9,11},{10,... | collective-permute-start | bytes 196616 | tf_op jit(solution)/shard_map/ppermute | solution.py:23
  17.4 5.5 %collective-permute-start.5 = (bf16[256,256]{1,0:T(8,128)(2,1)S(1)}, bf16[256,256]{1,0:T(8,128)(2,1)S(1)}, u32[]{:S(2)}, u32[]{:S(2)}) collective-permute-start(bf16[256,256]{1,0:T(8,128)(2,1)S(1)} %pad_maximum_fusion.1), channel_id=1, source_target_pairs={{0,4},{1,5},{2,6},{3,7},{4,0},{5,1},{6,2},{7,3},{8,12},{9,13},{10,... | collective-permute-start | bytes 393224 | tf_op jit(solution)/shard_map/ppermute | solution.py:23
  17.5 9.1 %collective-permute-start.2 = (bf16[512,256]{1,0:T(8,128)(2,1)S(1)}, bf16[512,256]{1,0:T(8,128)(2,1)S(1)}, u32[]{:S(2)}, u32[]{:S(2)}) collective-permute-start(bf16[512,256]{1,0:T(8,128)(2,1)S(1)} %get-tuple-element.69), channel_id=1, source_target_pairs={{0,15},{1,2},{2,1},{3,4},{4,3},{5,6},{6,5},{7,8},{8,7},{9,10},{10,... | collective-permute-start | bytes 786440 | tf_op jit(solution)/shard_map/ppermute | solution.py:28
  20.8 5.8 %collective-permute-start.1 = (bf16[512,256]{1,0:T(8,128)(2,1)S(1)}, bf16[512,256]{1,0:T(8,128)(2,1)S(1)}, u32[]{:S(2)}, u32[]{:S(2)}) collective-permute-start(bf16[512,256]{1,0:T(8,128)(2,1)S(1)} %get-tuple-element.71), channel_id=1, source_target_pairs={{0,1},{1,0},{2,3},{3,2},{4,5},{5,4},{6,7},{7,6},{8,9},{9,8},{10,11... | collective-permute-start | bytes 786440 | tf_op jit(solution)/shard_map/ppermute | solution.py:23
  22.9 3.8 %collective-permute-start.6 = (bf16[512,256]{1,0:T(8,128)(2,1)S(1)}, bf16[512,256]{1,0:T(8,128)(2,1)S(1)}, u32[]{:S(2)}, u32[]{:S(2)}) collective-permute-start(bf16[512,256]{1,0:T(8,128)(2,1)S(1)} %constant_dynamic-update-slice_fusion.half), channel_id=1, source_target_pairs={{0,1},{1,0},{2,3},{3,2},{4,5},{5,4},{6,7},{7,6},{8,9},{9,8},{10,11... | collective-permute-start | bytes 786440 | tf_op jit(solution)/shard_map/ppermute | solution.py:23
  28.3 5.7 %collective-permute-start.7 = (bf16[96,256]{1,0:T(8,128)(2,1)S(1)}, bf16[96,256]{1,0:T(8,128)(2,1)S(1)}, u32[]{:S(2)}, u32[]{:S(2)}) collective-permute-start(bf16[96,256]{1,0:T(8,128)(2,1)S(1)} %get-tuple-element.82), channel_id=1, source_target_pairs={{0,8},{1,9},{2,10},{3,11},{4,12},{5,13},{6,14},{7,15},{8,0},{9,1},... | collective-permute-start | bytes 147464 | tf_op jit(solution)/shard_map/ppermute | solution.py:23
  30.1 8.7 %collective-permute-start.10 = (bf16[512,256]{1,0:T(8,128)(2,1)S(1)}, bf16[512,256]{1,0:T(8,128)(2,1)S(1)}, u32[]{:S(2)}, u32[]{:S(2)}) collective-permute-start(bf16[512,256]{1,0:T(8,128)(2,1)S(1)} %get-tuple-element.92), channel_id=1, source_target_pairs={{0,15},{1,2},{2,1},{3,4},{4,3},{5,6},{6,5},{7,8},{8,7},{9,10},{10,... | collective-permute-start | bytes 786440 | tf_op jit(solution)/shard_map/ppermute | solution.py:28
  31.9 6.9 %collective-permute-start.9 = (bf16[512,256]{1,0:T(8,128)(2,1)S(1)}, bf16[512,256]{1,0:T(8,128)(2,1)S(1)}, u32[]{:S(2)}, u32[]{:S(2)}) collective-permute-start(bf16[512,256]{1,0:T(8,128)(2,1)S(1)} %get-tuple-element.91), channel_id=1, source_target_pairs={{0,1},{1,0},{2,3},{3,2},{4,5},{5,4},{6,7},{7,6},{8,9},{9,8},{10,11... | collective-permute-start | bytes 786440 | tf_op jit(solution)/shard_map/ppermute | solution.py:23
  34.0 7.8 %collective-permute-start.8 = (bf16[192,256]{1,0:T(8,128)(2,1)S(1)}, bf16[192,256]{1,0:T(8,128)(2,1)S(1)}, u32[]{:S(2)}, u32[]{:S(2)}) collective-permute-start(bf16[192,256]{1,0:T(8,128)(2,1)S(1)} %pad_maximum_fusion.2), channel_id=1, source_target_pairs={{0,2},{1,3},{2,0},{3,1},{4,6},{5,7},{6,4},{7,5},{8,10},{9,11},{10,... | collective-permute-start | bytes 294920 | tf_op jit(solution)/shard_map/ppermute | solution.py:23
  40.0 9.9 %collective-permute-start.13 = (bf16[512,256]{1,0:T(8,128)(2,1)S(1)}, bf16[512,256]{1,0:T(8,128)(2,1)S(1)}, u32[]{:S(2)}, u32[]{:S(2)}) collective-permute-start(bf16[512,256]{1,0:T(8,128)(2,1)S(1)} %get-tuple-element.93), channel_id=1, source_target_pairs={{0,15},{1,2},{2,1},{3,4},{4,3},{5,6},{6,5},{7,8},{8,7},{9,10},{10,... | collective-permute-start | bytes 786440 | tf_op jit(solution)/shard_map/ppermute | solution.py:28
  41.8 8.1 %collective-permute-start.12 = (bf16[512,256]{1,0:T(8,128)(2,1)S(1)}, bf16[512,256]{1,0:T(8,128)(2,1)S(1)}, u32[]{:S(2)}, u32[]{:S(2)}) collective-permute-start(bf16[512,256]{1,0:T(8,128)(2,1)S(1)} %get-tuple-element.95), channel_id=1, source_target_pairs={{0,1},{1,0},{2,3},{3,2},{4,5},{5,4},{6,7},{7,6},{8,9},{9,8},{10,11... | collective-permute-start | bytes 786440 | tf_op jit(solution)/shard_map/ppermute | solution.py:23
  42.8 7.1 %collective-permute-start.11 = (bf16[384,256]{1,0:T(8,128)(2,1)S(1)}, bf16[384,256]{1,0:T(8,128)(2,1)S(1)}, u32[]{:S(2)}, u32[]{:S(2)}) collective-permute-start(bf16[384,256]{1,0:T(8,128)(2,1)S(1)} %pad_maximum_fusion), channel_id=1, source_target_pairs={{0,4},{1,5},{2,6},{3,7},{4,0},{5,1},{6,2},{7,3},{8,12},{9,13},{10,... | collective-permute-start | bytes 589832 | tf_op jit(solution)/shard_map/ppermute | solution.py:23
  49.9 3.8 %collective-permute-start.14 = (bf16[768,256]{1,0:T(8,128)(2,1)S(1)}, bf16[768,256]{1,0:T(8,128)(2,1)S(1)}, u32[]{:S(2)}, u32[]{:S(2)}) collective-permute-start(bf16[768,256]{1,0:T(8,128)(2,1)S(1)} %constant_dynamic-update-slice_fusion.4.half), channel_id=1, source_target_pairs={{0,1},{1,0},{2,3},{3,2},{4,5},{5,4},{6,7},{7,6},{8,9},{9,8},{10,11... | collective-permute-start | bytes 1179656 | tf_op jit(solution)/shard_map/ppermute | solution.py:23
  54.6 4.6 %collective-permute-start.15 = (f32[4,256]{1,0:T(4,128)S(1)}, f32[4,256]{1,0:T(4,128)S(1)}, u32[]{:S(2)}, u32[]{:S(2)}) collective-permute-start(f32[4,256]{1,0:T(4,128)S(1)} %get-tuple-element.107), channel_id=1, source_target_pairs={{0,8},{1,9},{2,10},{3,11},{4,12},{5,13},{6,14},{7,15},{8,0},{9,1},... | collective-permute-start | bytes 12296 | tf_op jit(solution)/shard_map/ppermute | solution.py:23
  59.1 4.6 %collective-permute-start.16 = (f32[4,256]{1,0:T(4,128)S(1)}, f32[4,256]{1,0:T(4,128)S(1)}, u32[]{:S(2)}, u32[]{:S(2)}) collective-permute-start(f32[4,256]{1,0:T(4,128)S(1)} %add.12), channel_id=1, source_target_pairs={{0,2},{1,3},{2,0},{3,1},{4,6},{5,7},{6,4},{7,5},{8,10},{9,11},{10,... | collective-permute-start | bytes 12296 | tf_op jit(solution)/shard_map/ppermute | solution.py:23
  63.8 5.9 %collective-permute-start.19 = (bf16[512,256]{1,0:T(8,128)(2,1)S(1)}, bf16[512,256]{1,0:T(8,128)(2,1)S(1)}, u32[]{:S(2)}, u32[]{:S(2)}) collective-permute-start(bf16[512,256]{1,0:T(8,128)(2,1)S(1)} %get-tuple-element.119), channel_id=1, source_target_pairs={{1,0},{2,1},{3,2},{4,3},{5,4},{6,5},{7,6},{8,7},{9,8},{10,9},{11,1... | collective-permute-start | bytes 786440 | tf_op jit(solution)/shard_map/ppermute | solution.py:19
  64.8 1.2 %collective-permute-start.17 = (f32[4,256]{1,0:T(4,128)S(1)}, f32[4,256]{1,0:T(4,128)S(1)}, u32[]{:S(2)}, u32[]{:S(2)}) collective-permute-start(f32[4,256]{1,0:T(4,128)S(1)} %add.13), channel_id=1, source_target_pairs={{0,1},{1,0},{2,3},{3,2},{4,5},{5,4},{6,7},{7,6},{8,9},{9,8},{10,11... | collective-permute-start | bytes 12296 | tf_op jit(solution)/shard_map/ppermute | solution.py:23
  66.0 3.7 %collective-permute-start.18 = (f32[4,256]{1,0:T(4,128)S(1)}, f32[4,256]{1,0:T(4,128)S(1)}, u32[]{:S(2)}, u32[]{:S(2)}) collective-permute-start(f32[4,256]{1,0:T(4,128)S(1)} %add.14), channel_id=1, source_target_pairs={{0,4},{1,5},{2,6},{3,7},{4,0},{5,1},{6,2},{7,3},{8,12},{9,13},{10,... | collective-permute-start | bytes 12296 | tf_op jit(solution)/shard_map/ppermute | solution.py:23
